TPU v7x, 128 devices: a whole 4x4x4 slice. The times are simulated.
128 devices in a mesh: lib: 16 (over z, y), lmk: 8 (over x, core).
Axes of the slice: x: 4, y: 4, z: 4, core: 2. Of those that a mesh axis runs over, the one named last changes fastest.
Arguments:
- library_bits: bfloat16 [12288, 2048], P('lib'), may hold values from 0 to 1, as said below
- library_count: int32 [12288], P('lib'), may hold values from 1 to 2048, as said below
- landmark_bits: bfloat16 [8192, 2048], P('lmk'), may hold values from 0 to 1, as said below
- landmark_count: int32 [8192], P('lmk'), may hold values from 1 to 2048, as said below
- inverse_root: bfloat16 [8192, 8192], P('lib', 'lmk'), may hold values from -0.09375 to 0.09375
Outputs:
- features: float32 [12288, 8192], P('lib', 'lmk')
Inputs may be any that keep to these rules, and one draw needn't show every extreme that they name: `library_bits`: every entry is 0 or 1; every fingerprint has at least one set bit, one has all 2048 set and one has exactly one. `library_count`: the number of ones in the same row of library_bits. `landmark_bits`: every entry is 0 or 1; every fingerprint has at least one set bit, one has all 2048 set and one has exactly one. `landmark_count`: the number of ones in the same row of landmark_bits.
All inputs are finite; a program needn't handle non-finite values.
Results may differ from a plain program's by a relative error of at most 0.0027.
Values may be sent and summed in bfloat16 or wider, within the bound.
No kernel may reach another device: no remote copies, remote signals or barrier semaphores. Data moves between devices by JAX's collectives and lax.ppermute only.
A program may use at most 128 MiB of HBM per device.

v0:
```python
import jax
import jax.numpy as jnp
from jax import lax
from jax.sharding import PartitionSpec as P


def tversky(row_bits, row_count, col_bits, col_count):
    common = lax.dot_general(
        row_bits, col_bits, (((1,), (1,)), ((), ())), preferred_element_type=jnp.float32
    )
    scale_sum = (
        0.9 * row_count.astype(jnp.float32)[:, None] + 0.1 * col_count.astype(jnp.float32)[None, :]
    )
    return (common / scale_sum).astype(jnp.bfloat16)


def shards(library_bits, library_count, landmark_bits, landmark_count, inverse_root):
    block = tversky(library_bits, library_count, landmark_bits, landmark_count)
    row_kernel = lax.all_gather(block, "lmk", axis=1, tiled=True)
    return jnp.dot(
        row_kernel,
        lax.all_gather(inverse_root, "lib", axis=0, tiled=True),
        preferred_element_type=jnp.float32,
    )


def solution(mesh):
    placed = (P("lib", None), P("lib"), P("lmk", None), P("lmk"), P("lib", "lmk"))
    return jax.shard_map(
        shards, mesh=mesh, in_specs=placed, out_specs=P("lib", "lmk"), check_vma=False
    )
```

profile of v0, /device:TPU:1, one launch (start us, length us, event | category | flops | bytes accessed | tf_op | source)
XLA Modules:
  0.0 226.9 jit_solution(4323188477653373957)
XLA Ops:
  6.5 0.0 copy-start
  6.5 0.0 all-gather.3.cloned.1.call-start
  6.5 0.8 convert_multiply_fusion.1
  7.4 0.8 convert_multiply_fusion
  8.2 0.3 copy-done
  8.4 6.7 %divide_convert_fusion = bf16[768,1024]{1,0:T(8,128)(2,1)} fusion(bf16[768,2048]{1,0:T(8,128)(2,1)S(1)} %copy-done, bf16[1024,2048]{1,0:T(8,128)(2,1)} %param.7, f32[1024]{0:T(1024)S(1)} %convert_multiply_fusion, f32[768]{0:T(1024)S(1)} %convert_multiply_fusion.1), kind=kOutput, calls=%fused_computation | convolution fusion | flops 3223584768 | bytes 8920064 | tf_op jit(solution)/shard_map/dot_general | solution.py:8
  15.2 0.0 all-gather.3.cloned.1.call-update
  15.2 0.0 all-gather.5.cloned.1.call-start
  15.3 0.7 all-gather.5.cloned.1.call-update
  16.0 70.3 %all-gather.3.cloned.1.call-done = bf16[768,8192]{1,0:T(8,128)(2,1)} async-done(((bf16[768,1024]{1,0:T(8,128)(2,1)}), bf16[768,8192]{1,0:T(8,128)(2,1)}) %all-gather.3.cloned.1.call-update) | async-done | bytes 12582928 | tf_op jit(solution)/shard_map/all_gather | solution.py:19
  86.3 113.6 %all-gather.5.cloned.1.call-done = bf16[8192,1024]{1,0:T(8,128)(2,1)} async-done(((bf16[512,1024]{1,0:T(8,128)(2,1)}), bf16[8192,1024]{1,0:T(8,128)(2,1)}) %all-gather.5.cloned.1.call-update) | async-done | bytes 16777232 | tf_op jit(solution)/shard_map/all_gather | solution.py:22
  199.9 20.2 %fusion = f32[768,1024]{1,0:T(8,128)} fusion(bf16[768,8192]{1,0:T(8,128)(2,1)} %all-gather.3.cloned.1.call-done, bf16[8192,1024]{1,0:T(8,128)(2,1)} %all-gather.5.cloned.1.call-done), kind=kOutput, calls=%fused_computation.3 | convolution fusion | flops 12884901888 | bytes 32505856 | tf_op jit(solution)/shard_map/dot_general | solution.py:20
Async XLA Ops:
  6.5 1.9 copy-start
  6.5 79.7 %all-gather.3.cloned.1.call-start = ((), (), s32[]{:S(2)}) async-start(), calls=%async_computation | async-start | bytes 14155776 | tf_op jit(solution)/shard_map/all_gather | solution.py:19
  15.2 184.7 %all-gather.5.cloned.1.call-start = ((), (), s32[]{:S(2)}) async-start(), calls=%async_computation.1 | async-start | bytes 17825792 | tf_op jit(solution)/shard_map/all_gather | solution.py:22
Sparse Core Ops, SparseCore 0:
  15.3 70.8 all-gather.2
  88.4 111.4 all-gather.4
where the time goes:
time: 227 us
  waiting for transfers between devices  185 us (81%)
  matrix products  26.9 us (12%)
  between operations  13.4 us (6%)
    all_gather x1, waiting for transfers between devices, shards(): lax.all_gather(inverse_root, 'lib', axis=0, tiled=True)  114 us
    all_gather x1, waiting for transfers between devices, shards(): row_kernel = lax.all_gather(block, 'lmk', axis=1, tiled=True)  70.3 us
    dot_general x1, matrix products, shards(): jnp.dot(row_kernel, lax.all_gather(inverse_root, 'lib', axis=0, tiled=Tru...  20.2 us
    dot_general x1, matrix products, tversky(): lax.dot_general(row_bits, col_bits, (((1,), (1,)), ((), ())), preferred_e...  6.74 us
  transfers between devices with their start and end apart: 2, of which 2 were waited for; matrix products, arithmetic and copies ran while one was open for 0% of the time, Pallas kernels for 0%

commit v1 on v0

v1 whole, which is shorter than its diff:
```python
import functools

import jax
import jax.numpy as jnp
from jax import lax
from jax.experimental import pallas as pl
from jax.experimental.pallas import tpu as pltpu
from jax.sharding import PartitionSpec as P

AXES = ("lib", "lmk")
NZ, NY, NX, NC = 4, 4, 4, 2


def ring_pairs(axis):
    pairs = []
    for z in range(NZ):
        for y in range(NY):
            for x in range(NX):
                for c in range(NC):
                    step = 1 if c == 0 else -1
                    tz = (z + step) % NZ if axis == "z" else z
                    ty = (y + step) % NY if axis == "y" else y
                    pairs.append((((z * NY + y) * NX + x) * NC + c, ((tz * NY + ty) * NX + x) * NC + c))
    return pairs


def ring(block, axis):
    got = []
    for _ in range(3):
        block = lax.ppermute(block, AXES, ring_pairs(axis))
        got.append(block)
    return got


def tversky(row_bits, row_count, col_bits, col_count):
    common = lax.dot_general(
        row_bits, col_bits, (((1,), (1,)), ((), ())), preferred_element_type=jnp.float32
    )
    scale_sum = (
        0.9 * row_count.astype(jnp.float32)[:, None] + 0.1 * col_count.astype(jnp.float32)[None, :]
    )
    return (common / scale_sum).astype(jnp.bfloat16)


def group_kernel(stages, n_r, has_acc, col0, width, offs, k_ref, *refs):
    r_refs = refs[:n_r]
    refs = refs[n_r:]
    if has_acc:
        acc_ref, refs = refs[0], refs[1:]
    out_ref, kbuf, rbuf, acc, k_sems, r_sems, o_sems = refs
    rows = acc.shape[0]
    tile = 256
    if has_acc:
        acc_in = pltpu.make_async_copy(acc_ref.at[:, pl.ds(col0, width)], acc, o_sems.at[0])
        acc_in.start()
    pos, nk, nr, plan = 0, 0, 0, []
    for stage in stages:
        copies, start = [], pos
        for ki, n, parts in stage:
            off = pl.multiple_of(offs[ki], 256)
            copies.append(pltpu.make_async_copy(k_ref.at[:, pl.ds(off, n)], kbuf.at[:, pl.ds(pos, n)], k_sems.at[nk]))
            nk += 1
            for ri, row0, column, columns in parts:
                copies.append(
                    pltpu.make_async_copy(
                        r_refs[ri].at[pl.ds(row0, n), :],
                        rbuf.at[pl.ds(pos, n), pl.ds(column, columns)],
                        r_sems.at[nr],
                    )
                )
                nr += 1
            pos += n
        for cp in copies:
            cp.start()
        plan.append((start, pos, copies))
    if has_acc:
        acc_in.wait()
    outs = []
    for s, (lo, hi, copies) in enumerate(plan):
        for cp in copies:
            cp.wait()
        for t in range(0, rows, tile):
            part = jnp.dot(kbuf[t : t + tile, lo:hi], rbuf[lo:hi, :], preferred_element_type=jnp.float32)
            if s == 0 and not has_acc:
                acc[t : t + tile, :] = part
            else:
                acc[t : t + tile, :] += part
            if s == len(plan) - 1:
                cp = pltpu.make_async_copy(
                    acc.at[pl.ds(t, tile), :], out_ref.at[pl.ds(t, tile), pl.ds(col0, width)], o_sems.at[1 + t // tile]
                )
                cp.start()
                outs.append(cp)
    for cp in outs:
        cp.wait()


def group(stages, rs, offs, k, acc, col0, width, out_cols=1024):
    rows = k.shape[0]
    depth = sum(n for st in stages for _, n, _ in st)
    n_k = sum(len(st) for st in stages)
    n_r = sum(len(p) for st in stages for _, _, p in st)
    has_acc = acc is not None
    args = [offs, k, *rs] + ([acc] if has_acc else [])
    any_spec = pl.BlockSpec(memory_space=pl.ANY)
    return pl.pallas_call(
        functools.partial(group_kernel, stages, len(rs), has_acc, col0, width),
        out_shape=jax.ShapeDtypeStruct((rows, out_cols), jnp.float32),
        in_specs=[pl.BlockSpec(memory_space=pltpu.SMEM)] + [any_spec] * (len(args) - 1),
        out_specs=any_spec,
        scratch_shapes=[
            pltpu.VMEM((rows, depth), jnp.bfloat16),
            pltpu.VMEM((depth, width), jnp.bfloat16),
            pltpu.VMEM((rows, width), jnp.float32),
            pltpu.SemaphoreType.DMA((n_k,)),
            pltpu.SemaphoreType.DMA((n_r,)),
            pltpu.SemaphoreType.DMA((1 + -(-rows // 256),)),
        ],
        input_output_aliases={len(args) - 1: 0} if has_acc else {},
        compiler_params=pltpu.CompilerParams(vmem_limit_bytes=40 * 2**20),
        cost_estimate=pl.CostEstimate(
            flops=2 * rows * depth * width,
            bytes_accessed=2 * depth * (rows + width) + 4 * rows * width,
            transcendentals=0,
        ),
    )(*args)


def shards(library_bits, library_count, landmark_bits, landmark_count, inverse_root):
    block = tversky(library_bits, library_count, landmark_bits, landmark_count)
    k = lax.all_gather(block, "lmk", axis=1, tiled=True)

    lib = lax.axis_index("lib")
    z, y = lib // NY, lib % NY
    step = 1 - 2 * (lax.axis_index("lmk") % NC)
    offs = jnp.stack(
        [(((z - i * step) % NZ) * NY + (y - j * step) % NY) * 512 for i in range(4) for j in range(4)]
    ).astype(jnp.int32)
    offs = jnp.concatenate([offs, offs + 256])

    half = inverse_root.shape[1] // 2
    top = inverse_root.shape[0] // 2
    sides = []
    for s in range(2):
        own = inverse_root[:, s * half : (s + 1) * half]
        ys, zs = ring(own, "y"), ring(own, "z")
        a = ring(jnp.concatenate([b[:top] for b in ys]), "z")
        b = ring(jnp.concatenate([b[top:] for b in zs]), "y")
        sides.append((own, ys, zs, a, b))

    def a_stage(i, pick):
        return [(4 * i + j, top, [(p, (j - 1) * top, col, half) for p, col in pick]) for j in (1, 2, 3)]

    def b_stage(j, pick):
        return [(16 + 4 * i + j, top, [(p, (i - 1) * top, col, half) for p, col in pick]) for i in (1, 2, 3)]

    both = lambda i: [(i, 0), (i + 1, half)]
    rs, units = [inverse_root], [(0, 512, [(0, 0, 0, 2 * half)])]
    for d in range(3):
        for which, index in ((1, d + 1), (2, 4 * (d + 1))):
            units.append((index, 512, [(len(rs), 0, 0, half), (len(rs) + 1, 0, half, half)]))
            rs += [sides[0][which][d], sides[1][which][d]]
    stages = [units[:1], units[1:3], units[3:5], units[5:7]]
    p = len(rs)
    rs += [sides[0][3][0], sides[1][3][0], sides[0][4][0], sides[1][4][0]]
    stages += [a_stage(1, both(p)), b_stage(1, both(p + 2))]
    out = group(stages, rs, offs, k, None, 0, 2 * half)
    rs = [sides[0][3][1], sides[1][3][1], sides[0][4][1], sides[1][4][1]]
    out = group([a_stage(2, both(0)), b_stage(2, both(2))], rs, offs, k, out, 0, 2 * half)
    for s in range(2):
        rs = [sides[s][3][2], sides[s][4][2]]
        out = group([a_stage(3, [(0, 0)]), b_stage(3, [(1, 0)])], rs, offs, k, out, s * half, half)
    return out


def solution(mesh):
    placed = (P("lib", None), P("lib"), P("lmk", None), P("lmk"), P("lib", "lmk"))
    return jax.shard_map(
        shards, mesh=mesh, in_specs=placed, out_specs=P("lib", "lmk"), check_vma=False
    )
```

time: 227 us -> 151 us (0.67)
  waiting for transfers between devices: 185 us -> 28.2 us
  starting transfers between devices: 0.04 us -> 48.1 us
  Pallas kernels: 0 us -> 29.3 us
  local copies, waits for them, and re-layouts: 0.26 us -> 22 us
  matrix products: 26.9 us -> 6.74 us
    all_gather x2 -> x1, waiting for transfers between devices: 184 us -> 0.01 us  [shards(): k = lax.all_gather(block, 'lmk', axis=1, tiled=True)]
    ppermute x0 -> x24, starting transfers between devices: none -> 48.1 us  [ring(): block = lax.ppermute(block, AXES, ring_pairs(axis))]
    pallas_call x0 -> x4, Pallas kernels: none -> 29.3 us  [group(): pl.pallas_call(functools.partial(group_kernel, stages, len(rs), has_acc,...]
    ppermute x0 -> x24, waiting for transfers between devices: none -> 28.2 us  [ring(): block = lax.ppermute(block, AXES, ring_pairs(axis))]
    dot_general x1 -> x0, matrix products: 20.2 us -> none  [shards(): jnp.dot(row_kernel, lax.all_gather(inverse_root, 'lib', axis=0, tiled=Tru...]
    unnamed x2 -> x54, local copies, waits for them, and re-layouts: 0.26 us -> 20.3 us
  transfers between devices with their start and end apart: 2 -> 25, of which waited for: 2 -> 12; matrix products, arithmetic and copies ran while one was open for 0% -> 1% of each run, Pallas kernels for 0% -> 16%
where the time goes in v1:
time: 151 us; the launch traced here: 150 us
  starting transfers between devices  48.1 us (32%)
  Pallas kernels  29.3 us (19%)
  waiting for transfers between devices  28.2 us (19%)
  local copies, waits for them, and re-layouts  22 us (15%)
  between operations  13.7 us (9%)
  matrix products  6.74 us (4%)
  other arithmetic  1.86 us (1%)
    ppermute x24, starting transfers between devices, ring(): block = lax.ppermute(block, AXES, ring_pairs(axis))  48.1 us
    pallas_call x4, Pallas kernels, group(): pl.pallas_call(functools.partial(group_kernel, stages, len(rs), has_acc,...  29.3 us
    ppermute x24, waiting for transfers between devices, ring(): block = lax.ppermute(block, AXES, ring_pairs(axis))  28.2 us
    unnamed x54, local copies, waits for them, and re-layouts  20.3 us
    dot_general x1, matrix products, tversky(): lax.dot_general(row_bits, col_bits, (((1,), (1,)), ((), ())), preferred_e...  6.74 us
  transfers between devices with their start and end apart: 25, of which 12 were waited for; matrix products, arithmetic and copies ran while one was open for 1% of the time, Pallas kernels for 16%

profile of v1, /device:TPU:1, one launch (start us, length us, event | category | flops | bytes accessed | tf_op | source)
XLA Modules:
  0.0 149.9 jit_solution(8860929957205365403)
XLA Ops:
  6.5 0.8 convert_multiply_fusion
  7.4 0.8 convert_multiply_fusion.1
  8.4 6.7 %divide_convert_fusion = bf16[768,1024]{1,0:T(8,128)(2,1)} fusion(bf16[768,2048]{1,0:T(8,128)(2,1)S(1)} %copy-done, bf16[1024,2048]{1,0:T(8,128)(2,1)} %param.7, f32[1024]{0:T(1024)S(1)} %convert_multiply_fusion, f32[768]{0:T(1024)S(1)} %convert_multiply_fusion.1), kind=kOutput, calls=%fused_computation | convolution fusion | flops 3223584768 | bytes 8920064 | tf_op jit(solution)/shard_map/dot_general | solution.py:36
  15.2 1.3 fusion
  16.5 3.6 %collective-permute-start.12 = (bf16[512,512]{1,0:T(8,128)(2,1)S(1)}, bf16[512,512]{1,0:T(8,128)(2,1)S(1)}, u32[]{:S(2)}, u32[]{:S(2)}) collective-permute-start(bf16[512,512]{1,0:T(8,128)(2,1)S(1)} %get-tuple-element.5), channel_id=1, source_target_pairs={{0,8},{1,25},{2,10},{3,27},{4,12},{5,29},{6,14},{7,31},{8,16},{9,1... | collective-permute-start | bytes 1572872 | tf_op jit(solution)/shard_map/ppermute | solution.py:30
  20.1 3.8 %collective-permute-start.18 = (bf16[512,512]{1,0:T(8,128)(2,1)S(1)}, bf16[512,512]{1,0:T(8,128)(2,1)S(1)}, u32[]{:S(2)}, u32[]{:S(2)}) collective-permute-start(bf16[512,512]{1,0:T(8,128)(2,1)S(1)} %get-tuple-element.5), channel_id=1, source_target_pairs={{0,32},{1,97},{2,34},{3,99},{4,36},{5,101},{6,38},{7,103},{8,40},{... | collective-permute-start | bytes 1572872 | tf_op jit(solution)/shard_map/ppermute | solution.py:30
  24.5 1.8 %collective-permute-done.12.refs_1_ = bf16[512,512]{1,0:T(8,128)(2,1)S(1)} collective-permute-done((bf16[512,512]{1,0:T(8,128)(2,1)S(1)}, bf16[512,512]{1,0:T(8,128)(2,1)S(1)}, u32[]{:S(2)}, u32[]{:S(2)}) %collective-permute-start.12) | collective-permute-done | bytes 524320 | tf_op jit(solution)/shard_map/ppermute | solution.py:30
  26.2 3.4 %collective-permute-start.13 = (bf16[512,512]{1,0:T(8,128)(2,1)S(1)}, bf16[512,512]{1,0:T(8,128)(2,1)S(1)}, u32[]{:S(2)}, u32[]{:S(2)}) collective-permute-start(bf16[512,512]{1,0:T(8,128)(2,1)S(1)} %collective-permute-done.12.refs_1_), channel_id=1, source_target_pairs={{0,8},{1,25},{2,10},{3,27},{4,12},{5,29},{6,14},{7,31},{8,16},{9,1... | collective-permute-start | bytes 1572872 | tf_op jit(solution)/shard_map/ppermute | solution.py:30
  30.0 3.4 %collective-permute-start.19 = (bf16[512,512]{1,0:T(8,128)(2,1)S(1)}, bf16[512,512]{1,0:T(8,128)(2,1)S(1)}, u32[]{:S(2)}, u32[]{:S(2)}) collective-permute-start(bf16[512,512]{1,0:T(8,128)(2,1)S(1)} %collective-permute-done.18.refs_3_), channel_id=1, source_target_pairs={{0,32},{1,97},{2,34},{3,99},{4,36},{5,101},{6,38},{7,103},{8,40},{... | collective-permute-start | bytes 1572872 | tf_op jit(solution)/shard_map/ppermute | solution.py:30
  33.4 2.2 %collective-permute-done.6.refs_4_ = bf16[512,512]{1,0:T(8,128)(2,1)S(1)} collective-permute-done((bf16[512,512]{1,0:T(8,128)(2,1)S(1)}, bf16[512,512]{1,0:T(8,128)(2,1)S(1)}, u32[]{:S(2)}, u32[]{:S(2)}) %collective-permute-start.6) | collective-permute-done | bytes 524320 | tf_op jit(solution)/shard_map/ppermute | solution.py:30
  35.6 3.5 %collective-permute-start.7 = (bf16[512,512]{1,0:T(8,128)(2,1)S(1)}, bf16[512,512]{1,0:T(8,128)(2,1)S(1)}, u32[]{:S(2)}, u32[]{:S(2)}) collective-permute-start(bf16[512,512]{1,0:T(8,128)(2,1)S(1)} %collective-permute-done.6.refs_4_), channel_id=1, source_target_pairs={{0,32},{1,97},{2,34},{3,99},{4,36},{5,101},{6,38},{7,103},{8,40},{... | collective-permute-start | bytes 1572872 | tf_op jit(solution)/shard_map/ppermute | solution.py:30
  39.6 1.4 collective-permute-start.14
  41.2 3.5 %collective-permute-start.20 = (bf16[512,512]{1,0:T(8,128)(2,1)S(1)}, bf16[512,512]{1,0:T(8,128)(2,1)S(1)}, u32[]{:S(2)}, u32[]{:S(2)}) collective-permute-start(bf16[512,512]{1,0:T(8,128)(2,1)S(1)} %collective-permute-done.19.refs_7_), channel_id=1, source_target_pairs={{0,32},{1,97},{2,34},{3,99},{4,36},{5,101},{6,38},{7,103},{8,40},{... | collective-permute-start | bytes 1572872 | tf_op jit(solution)/shard_map/ppermute | solution.py:30
  44.8 2.1 %collective-permute-done.7.refs_8_ = bf16[512,512]{1,0:T(8,128)(2,1)S(1)} collective-permute-done((bf16[512,512]{1,0:T(8,128)(2,1)S(1)}, bf16[512,512]{1,0:T(8,128)(2,1)S(1)}, u32[]{:S(2)}, u32[]{:S(2)}) %collective-permute-start.7) | collective-permute-done | bytes 524320 | tf_op jit(solution)/shard_map/ppermute | solution.py:30
  46.9 3.5 %collective-permute-start.8 = (bf16[512,512]{1,0:T(8,128)(2,1)S(1)}, bf16[512,512]{1,0:T(8,128)(2,1)S(1)}, u32[]{:S(2)}, u32[]{:S(2)}) collective-permute-start(bf16[512,512]{1,0:T(8,128)(2,1)S(1)} %collective-permute-done.7.refs_8_), channel_id=1, source_target_pairs={{0,32},{1,97},{2,34},{3,99},{4,36},{5,101},{6,38},{7,103},{8,40},{... | collective-permute-start | bytes 1572872 | tf_op jit(solution)/shard_map/ppermute | solution.py:30
  51.2 0.8 copy-done.15
  52.0 1.1 collective-permute-done.14.refs_9_
  53.2 0.8 copy-done.19
  54.3 2.8 %collective-permute-start.21 = (bf16[768,512]{1,0:T(8,128)(2,1)S(1)}, bf16[768,512]{1,0:T(8,128)(2,1)}, u32[]{:S(2)}, u32[]{:S(2)}) collective-permute-start(bf16[768,512]{1,0:T(8,128)(2,1)S(1)} %pad_maximum_fusion.3), channel_id=1, source_target_pairs={{0,8},{1,25},{2,10},{3,27},{4,12},{5,29},{6,14},{7,31},{8,16},{9,1... | collective-permute-start | bytes 2359304 | tf_op jit(solution)/shard_map/ppermute | solution.py:30
  57.1 1.0 collective-permute-done.8.refs_12_
  58.2 0.5 collective-permute-start.9
  58.9 3.5 %collective-permute-start.3 = (bf16[768,512]{1,0:T(8,128)(2,1)S(1)}, bf16[768,512]{1,0:T(8,128)(2,1)}, u32[]{:S(2)}, u32[]{:S(2)}) collective-permute-start(bf16[768,512]{1,0:T(8,128)(2,1)S(1)} %pad_maximum_fusion), channel_id=1, source_target_pairs={{0,32},{1,97},{2,34},{3,99},{4,36},{5,101},{6,38},{7,103},{8,40},{... | collective-permute-start | bytes 2359304 | tf_op jit(solution)/shard_map/ppermute | solution.py:30
  62.4 4.1 %collective-permute-done.15.refs_13_ = bf16[768,512]{1,0:T(8,128)(2,1)} collective-permute-done((bf16[768,512]{1,0:T(8,128)(2,1)S(1)}, bf16[768,512]{1,0:T(8,128)(2,1)}, u32[]{:S(2)}, u32[]{:S(2)}) %collective-permute-start.15) | collective-permute-done | bytes 786464 | tf_op jit(solution)/shard_map/ppermute | solution.py:30
  66.5 3.5 %collective-permute-start.16 = (bf16[768,512]{1,0:T(8,128)(2,1)}, bf16[768,512]{1,0:T(8,128)(2,1)}, u32[]{:S(2)}, u32[]{:S(2)}) collective-permute-start(bf16[768,512]{1,0:T(8,128)(2,1)} %collective-permute-done.15.refs_13_), channel_id=1, source_target_pairs={{0,32},{1,97},{2,34},{3,99},{4,36},{5,101},{6,38},{7,103},{8,40},{... | collective-permute-start | bytes 2359304 | tf_op jit(solution)/shard_map/ppermute | solution.py:30
  70.5 5.2 %collective-permute-done.9.refs_16_ = bf16[768,512]{1,0:T(8,128)(2,1)} collective-permute-done((bf16[768,512]{1,0:T(8,128)(2,1)S(1)}, bf16[768,512]{1,0:T(8,128)(2,1)}, u32[]{:S(2)}, u32[]{:S(2)}) %collective-permute-start.9) | collective-permute-done | bytes 786464 | tf_op jit(solution)/shard_map/ppermute | solution.py:30
  75.7 2.3 %collective-permute-start.10 = (bf16[768,512]{1,0:T(8,128)(2,1)}, bf16[768,512]{1,0:T(8,128)(2,1)}, u32[]{:S(2)}, u32[]{:S(2)}) collective-permute-start(bf16[768,512]{1,0:T(8,128)(2,1)} %collective-permute-done.9.refs_16_), channel_id=1, source_target_pairs={{0,8},{1,25},{2,10},{3,27},{4,12},{5,29},{6,14},{7,31},{8,16},{9,1... | collective-permute-start | bytes 2359304 | tf_op jit(solution)/shard_map/ppermute | solution.py:30
  78.7 4.8 %collective-permute-done.16.refs_0_ = bf16[768,512]{1,0:T(8,128)(2,1)} collective-permute-done((bf16[768,512]{1,0:T(8,128)(2,1)}, bf16[768,512]{1,0:T(8,128)(2,1)}, u32[]{:S(2)}, u32[]{:S(2)}) %collective-permute-start.16) | collective-permute-done | bytes 786464 | tf_op jit(solution)/shard_map/ppermute | solution.py:30
  83.5 3.4 %collective-permute-start.17 = (bf16[768,512]{1,0:T(8,128)(2,1)}, bf16[768,512]{1,0:T(8,128)(2,1)}, u32[]{:S(2)}, u32[]{:S(2)}) collective-permute-start(bf16[768,512]{1,0:T(8,128)(2,1)} %collective-permute-done.16.refs_0_), channel_id=1, source_target_pairs={{0,32},{1,97},{2,34},{3,99},{4,36},{5,101},{6,38},{7,103},{8,40},{... | collective-permute-start | bytes 2359304 | tf_op jit(solution)/shard_map/ppermute | solution.py:30
  87.4 5.2 %collective-permute-done.10.refs_3_ = bf16[768,512]{1,0:T(8,128)(2,1)} collective-permute-done((bf16[768,512]{1,0:T(8,128)(2,1)}, bf16[768,512]{1,0:T(8,128)(2,1)}, u32[]{:S(2)}, u32[]{:S(2)}) %collective-permute-start.10) | collective-permute-done | bytes 786464 | tf_op jit(solution)/shard_map/ppermute | solution.py:30
  92.5 2.3 %collective-permute-start.11 = (bf16[768,512]{1,0:T(8,128)(2,1)}, bf16[768,512]{1,0:T(8,128)(2,1)}, u32[]{:S(2)}, u32[]{:S(2)}) collective-permute-start(bf16[768,512]{1,0:T(8,128)(2,1)} %collective-permute-done.10.refs_3_), channel_id=1, source_target_pairs={{0,8},{1,25},{2,10},{3,27},{4,12},{5,29},{6,14},{7,31},{8,16},{9,1... | collective-permute-start | bytes 2359304 | tf_op jit(solution)/shard_map/ppermute | solution.py:30
  95.3 1.2 copy-done.2
  96.5 1.0 copy-done.4
  97.6 1.0 copy-done.6
  98.6 1.0 copy-done.8
  99.7 1.0 copy-done.10
  100.7 1.0 copy-done.12
  101.8 1.0 copy-done.14
  102.8 1.0 copy-done.16
  103.8 1.0 copy-done.18
  104.9 1.0 copy-done.20
  105.9 1.0 copy-done.22
  107.0 1.0 copy-done.24
  108.0 1.0 copy-done.26
  109.0 12.1 %shard_map.55.refs_4_ = f32[768,1024]{1,0:T(8,128)} custom-call(s32[32]{0:T(128)S(1)} %concatenate.16.offs, bf16[768,8192]{1,0:T(8,128)(2,1)} %all-gather.2.cloned.1.call-done.k_ref, bf16[512,1024]{1,0:T(8,128)(2,1)S(1)} %copy-done.2, bf16[512,512]{1,0:T(8,128)(2,1)S(1)} %copy-done.4, bf16[512,512]{1,0:T(8,128)(2,1)S(1)} %copy-done.10, ...), custom_call_target="tpu_custom_call" | custom-call | flops 8053063680 | bytes 21495808 | tf_op jit(solution)/shard_map/pallas_call | solution.py:106
  121.2 7.9 %shard_map.56.refs_2_ = f32[768,1024]{1,0:T(8,128)} custom-call(s32[32]{0:T(128)S(1)} %concatenate.16.offs, bf16[768,8192]{1,0:T(8,128)(2,1)} %all-gather.2.cloned.1.call-done.k_ref, bf16[768,512]{1,0:T(8,128)(2,1)} %collective-permute-done.16.refs_0_, bf16[768,512]{1,0:T(8,128)(2,1)} %collective-permute-done.4.refs_1_, ...), custom_call_target="tpu_custom_call", output_to_operand_aliasing={{}: (6, {})} | custom-call | flops 2415919104 | bytes 8650752 | tf_op jit(solution)/shard_map/pallas_call | solution.py:106
  129.1 4.6 %copy-done.1 = bf16[768,8192]{1,0:T(8,128)(2,1)S(1)} copy-done((bf16[768,8192]{1,0:T(8,128)(2,1)S(1)}, bf16[768,8192]{1,0:T(8,128)(2,1)}, u32[]{:S(2)}) %copy-start.1) | copy-done | bytes 12582936
  133.7 4.6 %shard_map.57.refs_2_ = f32[768,1024]{1,0:T(8,128)} custom-call(s32[32]{0:T(128)S(1)} %concatenate.16.offs, bf16[768,8192]{1,0:T(8,128)(2,1)S(1)} %copy-done.1, bf16[768,512]{1,0:T(8,128)(2,1)} %collective-permute-done.17.refs_0_, bf16[768,512]{1,0:T(8,128)(2,1)} %collective-permute-done.23.refs_1_, ...), custom_call_target="tpu_custom_call", output_to_operand_aliasing={{}: (4, {})} | custom-call | flops 1207959552 | bytes 5505024 | tf_op jit(solution)/shard_map/pallas_call | solution.py:106
  138.4 4.6 %shard_map.58 = f32[768,1024]{1,0:T(8,128)} custom-call(s32[32]{0:T(128)S(1)} %concatenate.16.offs, bf16[768,8192]{1,0:T(8,128)(2,1)S(1)} %copy-done.1, bf16[768,512]{1,0:T(8,128)(2,1)} %collective-permute-done.5.refs_0_, bf16[768,512]{1,0:T(8,128)(2,1)} %collective-permute-done.11.refs_1_, ...), custom_call_target="tpu_custom_call", output_to_operand_aliasing={{}: (4, {})} | custom-call | flops 1207959552 | bytes 5505024 | tf_op jit(solution)/shard_map/pallas_call | solution.py:106
  (84 shorter events, 5.3 us)
Async XLA Ops:
  6.5 1.9 %copy-start = (bf16[768,2048]{1,0:T(8,128)(2,1)S(1)}, bf16[768,2048]{1,0:T(8,128)(2,1)}, u32[]{:S(2)}) copy-start(bf16[768,2048]{1,0:T(8,128)(2,1)} %param.5) | copy-start | bytes 9437188
  6.5 88.8 %all-gather.2.cloned.1.call-start = ((), (), s32[]{:S(2)}) async-start(), calls=%async_computation | async-start | bytes 14155776 | tf_op jit(solution)/shard_map/all_gather | solution.py:131
  16.5 9.8 %collective-permute-start.12 = (bf16[512,512]{1,0:T(8,128)(2,1)S(1)}, bf16[512,512]{1,0:T(8,128)(2,1)S(1)}, u32[]{:S(2)}, u32[]{:S(2)}) collective-permute-start(bf16[512,512]{1,0:T(8,128)(2,1)S(1)} %get-tuple-element.5), channel_id=1, source_target_pairs={{0,8},{1,25},{2,10},{3,27},{4,12},{5,29},{6,14},{7,31},{8,16},{9,1... | collective-permute-start | bytes 1572872 | tf_op jit(solution)/shard_map/ppermute | solution.py:30
  20.1 9.9 %collective-permute-start.18 = (bf16[512,512]{1,0:T(8,128)(2,1)S(1)}, bf16[512,512]{1,0:T(8,128)(2,1)S(1)}, u32[]{:S(2)}, u32[]{:S(2)}) collective-permute-start(bf16[512,512]{1,0:T(8,128)(2,1)S(1)} %get-tuple-element.5), channel_id=1, source_target_pairs={{0,32},{1,97},{2,34},{3,99},{4,36},{5,101},{6,38},{7,103},{8,40},{... | collective-permute-start | bytes 1572872 | tf_op jit(solution)/shard_map/ppermute | solution.py:30
  23.9 11.7 %collective-permute-start.6 = (bf16[512,512]{1,0:T(8,128)(2,1)S(1)}, bf16[512,512]{1,0:T(8,128)(2,1)S(1)}, u32[]{:S(2)}, u32[]{:S(2)}) collective-permute-start(bf16[512,512]{1,0:T(8,128)(2,1)S(1)} %get-tuple-element.6), channel_id=1, source_target_pairs={{0,32},{1,97},{2,34},{3,99},{4,36},{5,101},{6,38},{7,103},{8,40},{... | collective-permute-start | bytes 1572872 | tf_op jit(solution)/shard_map/ppermute | solution.py:30
  24.0 15.1 %collective-permute-start = (bf16[512,512]{1,0:T(8,128)(2,1)S(1)}, bf16[512,512]{1,0:T(8,128)(2,1)S(1)}, u32[]{:S(2)}, u32[]{:S(2)}) collective-permute-start(bf16[512,512]{1,0:T(8,128)(2,1)S(1)} %get-tuple-element.6), channel_id=1, source_target_pairs={{0,8},{1,25},{2,10},{3,27},{4,12},{5,29},{6,14},{7,31},{8,16},{9,1... | collective-permute-start | bytes 1572872 | tf_op jit(solution)/shard_map/ppermute | solution.py:30
  26.2 24.8 %copy-start.3 = (bf16[512,512]{1,0:T(8,128)(2,1)}, bf16[512,512]{1,0:T(8,128)(2,1)S(1)}, u32[]{:S(2)}) copy-start(bf16[512,512]{1,0:T(8,128)(2,1)S(1)} %collective-permute-done.12.refs_1_) | copy-start | bytes 1572868
  26.2 13.4 %collective-permute-start.13 = (bf16[512,512]{1,0:T(8,128)(2,1)S(1)}, bf16[512,512]{1,0:T(8,128)(2,1)S(1)}, u32[]{:S(2)}, u32[]{:S(2)}) collective-permute-start(bf16[512,512]{1,0:T(8,128)(2,1)S(1)} %collective-permute-done.12.refs_1_), channel_id=1, source_target_pairs={{0,8},{1,25},{2,10},{3,27},{4,12},{5,29},{6,14},{7,31},{8,16},{9,1... | collective-permute-start | bytes 1572872 | tf_op jit(solution)/shard_map/ppermute | solution.py:30
  30.0 21.0 %copy-start.5 = (bf16[512,512]{1,0:T(8,128)(2,1)}, bf16[512,512]{1,0:T(8,128)(2,1)S(1)}, u32[]{:S(2)}) copy-start(bf16[512,512]{1,0:T(8,128)(2,1)S(1)} %collective-permute-done.18.refs_3_) | copy-start | bytes 1572868
  30.0 11.2 %collective-permute-start.19 = (bf16[512,512]{1,0:T(8,128)(2,1)S(1)}, bf16[512,512]{1,0:T(8,128)(2,1)S(1)}, u32[]{:S(2)}, u32[]{:S(2)}) collective-permute-start(bf16[512,512]{1,0:T(8,128)(2,1)S(1)} %collective-permute-done.18.refs_3_), channel_id=1, source_target_pairs={{0,32},{1,97},{2,34},{3,99},{4,36},{5,101},{6,38},{7,103},{8,40},{... | collective-permute-start | bytes 1572872 | tf_op jit(solution)/shard_map/ppermute | solution.py:30
  35.6 15.4 %copy-start.7 = (bf16[512,512]{1,0:T(8,128)(2,1)}, bf16[512,512]{1,0:T(8,128)(2,1)S(1)}, u32[]{:S(2)}) copy-start(bf16[512,512]{1,0:T(8,128)(2,1)S(1)} %collective-permute-done.6.refs_4_) | copy-start | bytes 1572868
  35.6 11.2 %collective-permute-start.7 = (bf16[512,512]{1,0:T(8,128)(2,1)S(1)}, bf16[512,512]{1,0:T(8,128)(2,1)S(1)}, u32[]{:S(2)}, u32[]{:S(2)}) collective-permute-start(bf16[512,512]{1,0:T(8,128)(2,1)S(1)} %collective-permute-done.6.refs_4_), channel_id=1, source_target_pairs={{0,32},{1,97},{2,34},{3,99},{4,36},{5,101},{6,38},{7,103},{8,40},{... | collective-permute-start | bytes 1572872 | tf_op jit(solution)/shard_map/ppermute | solution.py:30
  39.1 11.9 %copy-start.9 = (bf16[512,512]{1,0:T(8,128)(2,1)}, bf16[512,512]{1,0:T(8,128)(2,1)S(1)}, u32[]{:S(2)}) copy-start(bf16[512,512]{1,0:T(8,128)(2,1)S(1)} %collective-permute-done.refs_2_) | copy-start | bytes 1572868
  39.1 11.2 %collective-permute-start.1 = (bf16[512,512]{1,0:T(8,128)(2,1)S(1)}, bf16[512,512]{1,0:T(8,128)(2,1)S(1)}, u32[]{:S(2)}, u32[]{:S(2)}) collective-permute-start(bf16[512,512]{1,0:T(8,128)(2,1)S(1)} %collective-permute-done.refs_2_), channel_id=1, source_target_pairs={{0,8},{1,25},{2,10},{3,27},{4,12},{5,29},{6,14},{7,31},{8,16},{9,1... | collective-permute-start | bytes 1572872 | tf_op jit(solution)/shard_map/ppermute | solution.py:30
  39.6 11.4 %copy-start.11 = (bf16[512,512]{1,0:T(8,128)(2,1)}, bf16[512,512]{1,0:T(8,128)(2,1)S(1)}, u32[]{:S(2)}) copy-start(bf16[512,512]{1,0:T(8,128)(2,1)S(1)} %collective-permute-done.13.refs_5_) | copy-start | bytes 1572868
  39.6 13.6 %collective-permute-start.14 = (bf16[512,512]{1,0:T(8,128)(2,1)S(1)}, bf16[512,512]{1,0:T(8,128)(2,1)S(1)}, u32[]{:S(2)}, u32[]{:S(2)}) collective-permute-start(bf16[512,512]{1,0:T(8,128)(2,1)S(1)} %collective-permute-done.13.refs_5_), channel_id=1, source_target_pairs={{0,8},{1,25},{2,10},{3,27},{4,12},{5,29},{6,14},{7,31},{8,16},{9,1... | collective-permute-start | bytes 1572872 | tf_op jit(solution)/shard_map/ppermute | solution.py:30
  41.2 9.8 %copy-start.13 = (bf16[512,512]{1,0:T(8,128)(2,1)}, bf16[512,512]{1,0:T(8,128)(2,1)S(1)}, u32[]{:S(2)}) copy-start(bf16[512,512]{1,0:T(8,128)(2,1)S(1)} %collective-permute-done.19.refs_7_) | copy-start | bytes 1572868
  41.2 13.0 %collective-permute-start.20 = (bf16[512,512]{1,0:T(8,128)(2,1)S(1)}, bf16[512,512]{1,0:T(8,128)(2,1)S(1)}, u32[]{:S(2)}, u32[]{:S(2)}) collective-permute-start(bf16[512,512]{1,0:T(8,128)(2,1)S(1)} %collective-permute-done.19.refs_7_), channel_id=1, source_target_pairs={{0,32},{1,97},{2,34},{3,99},{4,36},{5,101},{6,38},{7,103},{8,40},{... | collective-permute-start | bytes 1572872 | tf_op jit(solution)/shard_map/ppermute | solution.py:30
  46.9 11.2 %collective-permute-start.8 = (bf16[512,512]{1,0:T(8,128)(2,1)S(1)}, bf16[512,512]{1,0:T(8,128)(2,1)S(1)}, u32[]{:S(2)}, u32[]{:S(2)}) collective-permute-start(bf16[512,512]{1,0:T(8,128)(2,1)S(1)} %collective-permute-done.7.refs_8_), channel_id=1, source_target_pairs={{0,32},{1,97},{2,34},{3,99},{4,36},{5,101},{6,38},{7,103},{8,40},{... | collective-permute-start | bytes 1572872 | tf_op jit(solution)/shard_map/ppermute | solution.py:30
  50.4 8.4 %collective-permute-start.2 = (bf16[512,512]{1,0:T(8,128)(2,1)S(1)}, bf16[512,512]{1,0:T(8,128)(2,1)S(1)}, u32[]{:S(2)}, u32[]{:S(2)}) collective-permute-start(bf16[512,512]{1,0:T(8,128)(2,1)S(1)} %collective-permute-done.1.refs_6_), channel_id=1, source_target_pairs={{0,8},{1,25},{2,10},{3,27},{4,12},{5,29},{6,14},{7,31},{8,16},{9,1... | collective-permute-start | bytes 1572872 | tf_op jit(solution)/shard_map/ppermute | solution.py:30
  54.1 12.4 %collective-permute-start.15 = (bf16[768,512]{1,0:T(8,128)(2,1)S(1)}, bf16[768,512]{1,0:T(8,128)(2,1)}, u32[]{:S(2)}, u32[]{:S(2)}) collective-permute-start(bf16[768,512]{1,0:T(8,128)(2,1)S(1)} %pad_maximum_fusion.2), channel_id=1, source_target_pairs={{0,32},{1,97},{2,34},{3,99},{4,36},{5,101},{6,38},{7,103},{8,40},{... | collective-permute-start | bytes 2359304 | tf_op jit(solution)/shard_map/ppermute | solution.py:30
  54.2 3.9 %copy-start.21 = (bf16[512,512]{1,0:T(8,128)(2,1)}, bf16[512,512]{1,0:T(8,128)(2,1)S(1)}, u32[]{:S(2)}) copy-start(bf16[512,512]{1,0:T(8,128)(2,1)S(1)} %collective-permute-done.20.refs_11_) | copy-start | bytes 1572868
  54.3 15.7 %collective-permute-start.21 = (bf16[768,512]{1,0:T(8,128)(2,1)S(1)}, bf16[768,512]{1,0:T(8,128)(2,1)}, u32[]{:S(2)}, u32[]{:S(2)}) collective-permute-start(bf16[768,512]{1,0:T(8,128)(2,1)S(1)} %pad_maximum_fusion.3), channel_id=1, source_target_pairs={{0,8},{1,25},{2,10},{3,27},{4,12},{5,29},{6,14},{7,31},{8,16},{9,1... | collective-permute-start | bytes 2359304 | tf_op jit(solution)/shard_map/ppermute | solution.py:30
  58.2 17.5 %collective-permute-start.9 = (bf16[768,512]{1,0:T(8,128)(2,1)S(1)}, bf16[768,512]{1,0:T(8,128)(2,1)}, u32[]{:S(2)}, u32[]{:S(2)}) collective-permute-start(bf16[768,512]{1,0:T(8,128)(2,1)S(1)} %pad_maximum_fusion.1), channel_id=1, source_target_pairs={{0,8},{1,25},{2,10},{3,27},{4,12},{5,29},{6,14},{7,31},{8,16},{9,1... | collective-permute-start | bytes 2359304 | tf_op jit(solution)/shard_map/ppermute | solution.py:30
  58.8 3.6 %copy-start.25 = (bf16[512,512]{1,0:T(8,128)(2,1)}, bf16[512,512]{1,0:T(8,128)(2,1)S(1)}, u32[]{:S(2)}) copy-start(bf16[512,512]{1,0:T(8,128)(2,1)S(1)} %collective-permute-done.2.refs_10_) | copy-start | bytes 1572868
  58.9 19.1 %collective-permute-start.3 = (bf16[768,512]{1,0:T(8,128)(2,1)S(1)}, bf16[768,512]{1,0:T(8,128)(2,1)}, u32[]{:S(2)}, u32[]{:S(2)}) collective-permute-start(bf16[768,512]{1,0:T(8,128)(2,1)S(1)} %pad_maximum_fusion), channel_id=1, source_target_pairs={{0,32},{1,97},{2,34},{3,99},{4,36},{5,101},{6,38},{7,103},{8,40},{... | collective-permute-start | bytes 2359304 | tf_op jit(solution)/shard_map/ppermute | solution.py:30
  66.5 17.0 %collective-permute-start.16 = (bf16[768,512]{1,0:T(8,128)(2,1)}, bf16[768,512]{1,0:T(8,128)(2,1)}, u32[]{:S(2)}, u32[]{:S(2)}) collective-permute-start(bf16[768,512]{1,0:T(8,128)(2,1)} %collective-permute-done.15.refs_13_), channel_id=1, source_target_pairs={{0,32},{1,97},{2,34},{3,99},{4,36},{5,101},{6,38},{7,103},{8,40},{... | collective-permute-start | bytes 2359304 | tf_op jit(solution)/shard_map/ppermute | solution.py:30
  70.0 16.9 %collective-permute-start.22 = (bf16[768,512]{1,0:T(8,128)(2,1)}, bf16[768,512]{1,0:T(8,128)(2,1)}, u32[]{:S(2)}, u32[]{:S(2)}) collective-permute-start(bf16[768,512]{1,0:T(8,128)(2,1)} %collective-permute-done.21.refs_15_), channel_id=1, source_target_pairs={{0,8},{1,25},{2,10},{3,27},{4,12},{5,29},{6,14},{7,31},{8,16},{9,1... | collective-permute-start | bytes 2359304 | tf_op jit(solution)/shard_map/ppermute | solution.py:30
  75.7 16.9 %collective-permute-start.10 = (bf16[768,512]{1,0:T(8,128)(2,1)}, bf16[768,512]{1,0:T(8,128)(2,1)}, u32[]{:S(2)}, u32[]{:S(2)}) collective-permute-start(bf16[768,512]{1,0:T(8,128)(2,1)} %collective-permute-done.9.refs_16_), channel_id=1, source_target_pairs={{0,8},{1,25},{2,10},{3,27},{4,12},{5,29},{6,14},{7,31},{8,16},{9,1... | collective-permute-start | bytes 2359304 | tf_op jit(solution)/shard_map/ppermute | solution.py:30
  78.0 16.9 %collective-permute-start.4 = (bf16[768,512]{1,0:T(8,128)(2,1)}, bf16[768,512]{1,0:T(8,128)(2,1)}, u32[]{:S(2)}, u32[]{:S(2)}) collective-permute-start(bf16[768,512]{1,0:T(8,128)(2,1)} %collective-permute-done.3.refs_14_), channel_id=1, source_target_pairs={{0,32},{1,97},{2,34},{3,99},{4,36},{5,101},{6,38},{7,103},{8,40},{... | collective-permute-start | bytes 2359304 | tf_op jit(solution)/shard_map/ppermute | solution.py:30
  83.5 45.6 %collective-permute-start.17 = (bf16[768,512]{1,0:T(8,128)(2,1)}, bf16[768,512]{1,0:T(8,128)(2,1)}, u32[]{:S(2)}, u32[]{:S(2)}) collective-permute-start(bf16[768,512]{1,0:T(8,128)(2,1)} %collective-permute-done.16.refs_0_), channel_id=1, source_target_pairs={{0,32},{1,97},{2,34},{3,99},{4,36},{5,101},{6,38},{7,103},{8,40},{... | collective-permute-start | bytes 2359304 | tf_op jit(solution)/shard_map/ppermute | solution.py:30
  86.9 42.2 %collective-permute-start.23 = (bf16[768,512]{1,0:T(8,128)(2,1)}, bf16[768,512]{1,0:T(8,128)(2,1)}, u32[]{:S(2)}, u32[]{:S(2)}) collective-permute-start(bf16[768,512]{1,0:T(8,128)(2,1)} %collective-permute-done.22.refs_2_), channel_id=1, source_target_pairs={{0,8},{1,25},{2,10},{3,27},{4,12},{5,29},{6,14},{7,31},{8,16},{9,1... | collective-permute-start | bytes 2359304 | tf_op jit(solution)/shard_map/ppermute | solution.py:30
  92.5 45.8 %collective-permute-start.11 = (bf16[768,512]{1,0:T(8,128)(2,1)}, bf16[768,512]{1,0:T(8,128)(2,1)}, u32[]{:S(2)}, u32[]{:S(2)}) collective-permute-start(bf16[768,512]{1,0:T(8,128)(2,1)} %collective-permute-done.10.refs_3_), channel_id=1, source_target_pairs={{0,8},{1,25},{2,10},{3,27},{4,12},{5,29},{6,14},{7,31},{8,16},{9,1... | collective-permute-start | bytes 2359304 | tf_op jit(solution)/shard_map/ppermute | solution.py:30
  94.8 43.5 %collective-permute-start.5 = (bf16[768,512]{1,0:T(8,128)(2,1)}, bf16[768,512]{1,0:T(8,128)(2,1)}, u32[]{:S(2)}, u32[]{:S(2)}) collective-permute-start(bf16[768,512]{1,0:T(8,128)(2,1)} %collective-permute-done.4.refs_1_), channel_id=1, source_target_pairs={{0,32},{1,97},{2,34},{3,99},{4,36},{5,101},{6,38},{7,103},{8,40},{... | collective-permute-start | bytes 2359304 | tf_op jit(solution)/shard_map/ppermute | solution.py:30
  95.3 1.2 copy-start.2
  96.5 1.0 copy-start.4
  97.6 1.0 copy-start.6
  98.6 1.0 copy-start.8
  99.7 1.0 copy-start.10
  100.7 1.0 copy-start.12
  101.8 1.0 copy-start.14
  102.8 1.0 copy-start.16
  103.8 1.0 copy-start.18
  104.9 1.0 copy-start.20
  105.9 1.0 copy-start.22
  107.0 1.0 copy-start.24
  108.0 1.0 copy-start.26
  129.1 4.6 %copy-start.1 = (bf16[768,8192]{1,0:T(8,128)(2,1)S(1)}, bf16[768,8192]{1,0:T(8,128)(2,1)}, u32[]{:S(2)}) copy-start(bf16[768,8192]{1,0:T(8,128)(2,1)} %all-gather.2.cloned.1.call-done.k_ref) | copy-start | bytes 37748740
  (4 other events, 3.3 us)
Sparse Core Ops, SparseCore 0:
  15.3 70.8 all-gather.1

commit v2 on v0

v2 whole, which is shorter than its diff:
```python
import functools

import jax
import jax.numpy as jnp
from jax import lax
from jax.experimental import pallas as pl
from jax.experimental.pallas import tpu as pltpu
from jax.sharding import PartitionSpec as P

AXES = ("lib", "lmk")
NZ, NY, NX, NC = 4, 4, 4, 2
TILE = 256
TIES = [5, 5, 5, 5, 5, 12, 9, 9, 9, 9, 9]
TAIL = 5 * 10**10
X1 = 4
X2 = 6
TV = 8 * 10**9


def pairs_of(move):
    pairs = []
    for z in range(NZ):
        for y in range(NY):
            for x in range(NX):
                for c in range(NC):
                    tz, ty, tx, tc = move(z, y, x, c, 1 if c == 0 else -1)
                    to = ((tz % NZ * NY + ty % NY) * NX + tx % NX) * NC + tc
                    pairs.append((((z * NY + y) * NX + x) * NC + c, to))
    return pairs


PAIRS = {
    "z": pairs_of(lambda z, y, x, c, s: (z + s, y, x, c)),
    "y": pairs_of(lambda z, y, x, c, s: (z, y + s, x, c)),
    "x": pairs_of(lambda z, y, x, c, s: (z, y, x + s, c)),
    "core": pairs_of(lambda z, y, x, c, s: (z, y, x, 1 - c)),
}


def send(block, axis):
    return lax.ppermute(block, AXES, PAIRS[axis])


def vmem(x):
    return pltpu.with_memory_space_constraint(x, pltpu.VMEM)


def hbm(x):
    return pltpu.with_memory_space_constraint(x, pltpu.HBM)


def position():
    lib, lmk = lax.axis_index("lib"), lax.axis_index("lmk")
    return lib // NY, lib % NY, lmk // NC, lmk % NC


def root_index(i, j):
    z, y, _, c = position()
    back = 3 + 2 * c
    return (z + i * back) % NZ * NY + (y + j * back) % NY


def kernel_index(i):
    _, _, x, c = position()
    return (x + i * (3 + 2 * c)) % NX * 4


VM = pl.BlockSpec(memory_space=pltpu.VMEM)
ANY = pl.BlockSpec(memory_space=pl.ANY)


def params(mib):
    return pltpu.CompilerParams(vmem_limit_bytes=mib * 2**20)


def cost(flops, bytes_accessed=0):
    return pl.CostEstimate(flops=flops, bytes_accessed=bytes_accessed, transcendentals=0)


def tversky_kernel(row_bits, row_scale, col_bits, got_bits, out, rbuf, cbuf, sems):
    core = position()[3]
    copies = [
        pltpu.make_async_copy(row_bits.at[pl.ds(t * TILE, TILE), :], rbuf.at[pl.ds(t * TILE, TILE), :], sems.at[t])
        for t in range(3)
    ] + [
        pltpu.make_async_copy(
            col_bits.at[pl.ds(pl.multiple_of(h * 512 + core * 256, 256), 256), :],
            cbuf.at[pl.ds(h * 256, 256), :],
            sems.at[3 + h],
        )
        for h in range(2)
    ]
    for at in (0, 3, 4, 1, 2):
        copies[at].start()
    copies[3].wait()
    copies[4].wait()
    ones = jnp.ones((8, row_bits.shape[1]), jnp.bfloat16)
    nt = (((1,), (1,)), ((), ()))
    for part, bits in enumerate((cbuf, got_bits)):
        count = lax.dot_general(ones, bits[...], nt, preferred_element_type=jnp.float32)[:1, :]
        col_scale = 0.1 * count
        first = 2 * (core if part == 0 else 1 - core)
        for t in range(3):
            if part == 0:
                copies[t].wait()
            rows = slice(t * TILE, (t + 1) * TILE)
            common = lax.dot_general(rbuf[rows, :], bits[...], nt, preferred_element_type=jnp.float32)
            k = (common / (row_scale[rows, :] + col_scale)).astype(jnp.bfloat16)
            for h in range(2):
                out[first + h, rows, :] = k[:, h * 256 : (h + 1) * 256]


def tversky(row_bits, row_count, col_bits, got_bits):
    row_scale = 0.9 * row_count.astype(jnp.float32)[:, None]
    rows = row_bits.shape[0]
    return pl.pallas_call(
        tversky_kernel,
        out_shape=pltpu.VMEM((4, rows, 256), jnp.bfloat16),
        in_specs=[ANY, VM, ANY, VM],
        out_specs=VM,
        scratch_shapes=[
            pltpu.VMEM(row_bits.shape, jnp.bfloat16),
            pltpu.VMEM((512, row_bits.shape[1]), jnp.bfloat16),
            pltpu.SemaphoreType.DMA((5,)),
        ],
        compiler_params=params(12),
        cost_estimate=cost(TV),
    )(hbm(row_bits), vmem(row_scale), hbm(col_bits), vmem(got_bits))


def tie_kernel(*refs):
    pass


def tie(*arrays, flops):
    return pl.pallas_call(
        tie_kernel,
        out_shape=tuple(pltpu.VMEM(a.shape, a.dtype) for a in arrays),
        in_specs=[VM] * len(arrays),
        out_specs=(VM,) * len(arrays),
        input_output_aliases={i: i for i in range(len(arrays))},
        compiler_params=params(1),
        cost_estimate=cost(flops),
    )(*map(vmem, arrays))


def place_kernel(hops, has_full, *refs):
    n = len(hops)
    blocks, full, sems = refs[:n], refs[n + has_full], refs[n + has_full + 1]
    copies = [
        pltpu.make_async_copy(b, full.at[pl.ds(kernel_index(i), 4)], sems.at[at])
        for at, (i, b) in enumerate(zip(hops, blocks))
    ]
    for cp in copies:
        cp.start()
    for cp in copies:
        cp.wait()


def place(hops, blocks, full=None):
    args = [*map(vmem, blocks)] + ([] if full is None else [vmem(full)])
    return pl.pallas_call(
        functools.partial(place_kernel, hops, full is not None),
        out_shape=pltpu.VMEM((16, *blocks[0].shape[1:]), blocks[0].dtype),
        in_specs=[VM] * len(args),
        out_specs=VM,
        scratch_shapes=[pltpu.SemaphoreType.DMA((len(hops),))],
        input_output_aliases={} if full is None else {len(hops): 0},
        compiler_params=params(1),
        cost_estimate=cost(10**6),
    )(*args)


def partial_kernel(terms, n_r, n_acc, hops, k, *refs):
    rs, accs, outs = refs[:n_r], refs[n_r : n_r + n_acc], refs[n_r + n_acc :]
    z, _, x, c = position()
    ahead = (x - z) * (1 - 2 * c) + 4

    def tile(t, carry):
        rows = pl.ds(t * TILE, TILE)
        for o, halves in enumerate(terms):
            if not n_acc:
                outs[o][rows, :] = jnp.zeros((TILE, 1024), jnp.float32)
            for i in range(4):
                hop = (ahead + i) % 4
                with_hop = (hop >= hops[0]) & (hop <= hops[-1])

                @pl.when(with_hop)
                def _():
                    for half, pieces in enumerate(halves):
                        cols = slice(half * 512, (half + 1) * 512)
                        total = outs[o][rows, cols]
                        for r, row0, col0, at in pieces:
                            if at[0] == i:
                                total += jnp.dot(
                                    k[root_index(*at), rows, :],
                                    rs[r][row0 : row0 + 256, col0 : col0 + 512],
                                    preferred_element_type=jnp.float32,
                                )
                        outs[o][rows, cols] = total

        return carry

    lax.fori_loop(0, outs[0].shape[0] // TILE, tile, 0)


def group_kernel(terms, n_r, n_acc, k, *refs):
    rs, accs, outs = refs[:n_r], refs[n_r : n_r + n_acc], refs[n_r + n_acc :]

    def tile(t, carry):
        rows = pl.ds(t * TILE, TILE)
        for o, halves in enumerate(terms):
            for half, pieces in enumerate(halves):
                cols = slice(half * 512, (half + 1) * 512)
                total = accs[o][rows, cols] if n_acc else None
                for r, row0, col0, at in pieces:
                    part = jnp.dot(
                        k[root_index(*at), rows, :],
                        rs[r][row0 : row0 + 256, col0 : col0 + 512],
                        preferred_element_type=jnp.float32,
                    )
                    total = part if total is None else total + part
                outs[o][rows, cols] = total
        return carry

    lax.fori_loop(0, outs[0].shape[0] // TILE, tile, 0)


def group(terms, rs, k, accs, hops=None):
    rows = k.shape[1]
    args = [*map(vmem, (k, *rs, *accs))]
    first = 1 + len(rs)
    return pl.pallas_call(
        functools.partial(group_kernel, terms, len(rs), len(accs))
        if hops is None
        else functools.partial(partial_kernel, terms, len(rs), len(accs), hops),
        out_shape=tuple(pltpu.VMEM((rows, 1024), jnp.float32) for _ in terms),
        in_specs=[VM] * len(args),
        out_specs=tuple(VM for _ in terms),
        input_output_aliases={first + i: i for i in range(len(accs))},
        compiler_params=params(8),
        cost_estimate=cost(10**6),
    )(*args)


def last_kernel(halves, n_r, k, *refs):
    rs, (acc, other, out, buf, sems) = refs[:n_r], refs[n_r:]
    copies = []
    for t in range(acc.shape[0] // TILE):
        rows = slice(t * TILE, (t + 1) * TILE)
        for half, pieces in enumerate(halves):
            cols = slice(half * 512, (half + 1) * 512)
            total = acc[rows, cols] + other[rows, cols]
            for r, row0, col0, at in pieces:
                total += jnp.dot(
                    k[root_index(*at), rows, :],
                    rs[r][row0 : row0 + 256, col0 : col0 + 512],
                    preferred_element_type=jnp.float32,
                )
            buf[rows, cols] = total
        cp = pltpu.make_async_copy(buf.at[pl.ds(t * TILE, TILE), :], out.at[pl.ds(t * TILE, TILE), :], sems.at[t])
        cp.start()
        copies.append(cp)
    for cp in copies:
        cp.wait()


def last(halves, rs, k, acc, other):
    rows = k.shape[1]
    args = [*map(vmem, (k, *rs, acc, other))]
    return pl.pallas_call(
        functools.partial(last_kernel, halves, len(rs)),
        out_shape=jax.ShapeDtypeStruct((rows, 1024), jnp.float32),
        in_specs=[VM] * len(args),
        out_specs=ANY,
        scratch_shapes=[pltpu.VMEM((rows, 1024), jnp.float32), pltpu.SemaphoreType.DMA((rows // TILE,))],
        compiler_params=params(8),
        cost_estimate=cost(10**6),
    )(*args)


def shards(library_bits, library_count, landmark_bits, landmark_count, inverse_root):
    core = lax.axis_index("lmk") % NC
    mine = lax.dynamic_slice_in_dim(inverse_root, core * 256, 256, 0)
    theirs = send(lax.dynamic_slice_in_dim(inverse_root, (1 - core) * 256, 256, 0), "core")
    blocks = landmark_bits.reshape(2, 512, -1)
    bits = send(lax.dynamic_slice_in_dim(blocks, (1 - core) * 256, 256, 1).reshape(512, -1), "core")
    own = [theirs, mine]
    first = [[[], []] for _ in range(2)]
    second = [[[], []] for _ in range(2)]
    for s in range(2):
        first[s][0].append(send(own[s], "y"))
        first[s][1].append(send(own[s], "z"))
    ks = [tversky(library_bits, library_count, landmark_bits, bits)]

    def second_terms(hop, p):
        return [[(p, 256 * m, 0, (hop, m + 1)) for m in range(3)], [(p + 1, 256 * m, 0, (m + 1, hop)) for m in range(3)]]

    accs = None
    for step in range(11):
        s, hop = step % 2, step // 2
        rings = (first if hop < 3 else second)[s]
        ready = [rings[0][hop % 3], rings[1][hop % 3]]
        if step == 8:
            k = place([0, 1, 2], ks[:3])
            rs, terms = [], []
            for o in range(2):
                p = len(rs)
                rs += [own[o], *first[o][0], *first[o][1], second[o][0][0], second[o][1][0]]
                where = [(0, 0), (0, 1), (0, 2), (0, 3), (1, 0), (2, 0), (3, 0)]
                more = second_terms(1, p + 7)
                terms.append([[(p + n, 0, 512 * h, at) for n, at in enumerate(where)] + more[h] for h in range(2)])
            accs = group(terms, rs, k, [], (0, 2))
        if step == 0:
            token = jnp.zeros((16, 128), jnp.bfloat16)
        if step in (X1, X2):
            tied = tie(token, *ready, ks[-1], flops=TIES[step] * 10**9)
            ks[-1] = tied[-1]
        else:
            tied = tie(token, *ready, flops=TIES[step] * 10**9)
        token = tied[0]
        rings[0][hop % 3], rings[1][hop % 3] = done = tied[1:3]
        if hop < 2:
            rings[0].append(send(done[0], "y"))
            rings[1].append(send(done[1], "z"))
        elif hop == 2:
            left = jnp.concatenate([q[:, :512] for q in rings[0]])
            right = jnp.concatenate([q[:, 512:] for q in rings[1]])
            second[s][0].append(send(left, "z"))
            second[s][1].append(send(right, "y"))
        elif hop < 5:
            rings[0].append(send(done[0], "z"))
            rings[1].append(send(done[1], "y"))
        if step in (0, X1, X2):
            ks.append(send(ks[-1], "x"))
    k = place([3], ks[3:], k)
    accs = group(terms, rs, k, accs, (3, 3))
    rs = [second[s][a][1] for s in range(2) for a in range(2)]
    accs = group([second_terms(2, 0), second_terms(2, 2)], rs, k, accs)
    (theirs,) = group([second_terms(3, 0)], [second[0][0][2], second[0][1][2]], k, accs[:1])
    other = send(theirs, "core")
    tail = tie(second[1][0][2], second[1][1][2], flops=TAIL)
    return last(second_terms(3, 0), tail, k, accs[1], other)


def solution(mesh):
    placed = (P("lib", None), P("lib"), P("lmk", None), P("lmk"), P("lib", "lmk"))
    return jax.shard_map(
        shards, mesh=mesh, in_specs=placed, out_specs=P("lib", "lmk"), check_vma=False
    )
```

time: 227 us -> 110 us (0.48)
  waiting for transfers between devices: 185 us -> 38.5 us
  starting transfers between devices: 0.04 us -> 39.6 us
  Pallas kernels: 0 us -> 27.5 us
  matrix products: 26.9 us -> 0 us
  between operations: 13.4 us -> 0.43 us
  local copies, waits for them, and re-layouts: 0.26 us -> 3.7 us
    all_gather x2 -> x0, waiting for transfers between devices: 184 us -> none  [the longest x1 114 us: shards(): lax.all_gather(inverse_root, 'lib', axis=0, tiled=True)]
    ppermute x0 -> x30, starting transfers between devices: none -> 39.6 us  [send(): return lax.ppermute(block, AXES, PAIRS[axis])]
    ppermute x0 -> x30, waiting for transfers between devices: none -> 38.5 us  [send(): return lax.ppermute(block, AXES, PAIRS[axis])]
    pallas_call x0 -> x20, Pallas kernels: none -> 27.5 us  [the longest x4 17.6 us: group(): pl.pallas_call(functools.partial(group_kernel, terms, len(rs), len(accs))...]
    dot_general x2 -> x0, matrix products: 26.9 us -> none  [the longest x1 20.2 us: shards(): jnp.dot(row_kernel, lax.all_gather(inverse_root, 'lib', axis=0, tiled=Tru...]
    dynamic_slice x0 -> x2, local copies, waits for them, and re-layouts: none -> 3.32 us  [the longest x1 3.25 us: shards(): lax.dynamic_slice_in_dim(blocks, (1 - core) * 256, 256, 1).reshape(512, -1)]
  transfers between devices with their start and end apart: 2 -> 30, of which waited for: 2 -> 15; matrix products, arithmetic and copies ran while one was open for 0% -> 1% of each run, Pallas kernels for 0% -> 23%
where the time goes in v2:
time: 110 us
  starting transfers between devices  39.6 us (36%)
  waiting for transfers between devices  38.5 us (35%)
  Pallas kernels  27.5 us (25%)
  local copies, waits for them, and re-layouts  3.7 us (3%)
    ppermute x30, starting transfers between devices, send(): return lax.ppermute(block, AXES, PAIRS[axis])  39.6 us
    ppermute x30, waiting for transfers between devices, send(): return lax.ppermute(block, AXES, PAIRS[axis])  38.5 us
    pallas_call x4, Pallas kernels, group(): pl.pallas_call(functools.partial(group_kernel, terms, len(rs), len(accs))...  17.6 us
    pallas_call x1, Pallas kernels, tversky(): pl.pallas_call(tversky_kernel, out_shape=pltpu.VMEM((4, rows, 256), jnp.b...  6.98 us
    dynamic_slice x1, local copies, waits for them, and re-layouts, shards(): lax.dynamic_slice_in_dim(blocks, (1 - core) * 256, 256, 1).reshape(512, -1)  3.25 us
    pallas_call x1, Pallas kernels, last(): pl.pallas_call(functools.partial(last_kernel, halves, len(rs)), out_shape...  2.39 us
  transfers between devices with their start and end apart: 30, of which 15 were waited for; matrix products, arithmetic and copies ran while one was open for 1% of the time, Pallas kernels for 23%

profile of v2, /device:TPU:1, one launch (start us, length us, event | category | flops | bytes accessed | tf_op | source)
XLA Modules:
  0.0 109.9 jit_solution(684882921335475438)
XLA Ops:
  0.0 3.2 %constant_dynamic-slice_fusion = bf16[2,256,2048]{2,1,0:T(8,128)(2,1)} fusion(bf16[2,512,2048]{2,1,0:T(8,128)(2,1)} %bitcast.2, s32[]{:T(128)S(6)} %select_n.15), kind=kLoop, calls=%fused_computation.5 | loop fusion | bytes 4194308 | tf_op jit(solution)/shard_map/dynamic_slice | solution.py:287
  3.3 1.4 %collective-permute-start.11 = (bf16[512,2048]{1,0:T(8,128)(2,1)}, bf16[512,2048]{1,0:T(8,128)(2,1)S(1)}, u32[]{:S(2)}, u32[]{:S(2)}) collective-permute-start(bf16[512,2048]{1,0:T(8,128)(2,1)} %bitcast.1), channel_id=1, source_target_pairs={{0,1},{1,0},{2,3},{3,2},{4,5},{5,4},{6,7},{7,6},{8,9},{9,8},{10,11... | collective-permute-start | bytes 6291464 | tf_op jit(solution)/shard_map/ppermute | solution.py:41
  4.8 2.9 %collective-permute-start.3 = (bf16[256,1024]{1,0:T(8,128)(2,1)S(1)}, bf16[256,1024]{1,0:T(8,128)(2,1)S(1)}, u32[]{:S(2)}, u32[]{:S(2)}) collective-permute-start(bf16[256,1024]{1,0:T(8,128)(2,1)S(1)} %get-tuple-element.89.refs_9_), channel_id=1, source_target_pairs={{0,8},{1,25},{2,10},{3,27},{4,12},{5,29},{6,14},{7,31},{8,16},{9,1... | collective-permute-start | bytes 1572872 | tf_op jit(solution)/shard_map/ppermute | solution.py:41
  7.7 3.8 %collective-permute-start.4 = (bf16[256,1024]{1,0:T(8,128)(2,1)S(1)}, bf16[256,1024]{1,0:T(8,128)(2,1)S(1)}, u32[]{:S(2)}, u32[]{:S(2)}) collective-permute-start(bf16[256,1024]{1,0:T(8,128)(2,1)S(1)} %get-tuple-element.89.refs_9_), channel_id=1, source_target_pairs={{0,32},{1,97},{2,34},{3,99},{4,36},{5,101},{6,38},{7,103},{8,40},{... | collective-permute-start | bytes 1572872 | tf_op jit(solution)/shard_map/ppermute | solution.py:41
  11.5 0.2 mul.20.row_scale
  11.7 0.5 collective-permute-start.1
  12.2 3.4 %collective-permute-start.2 = (bf16[256,1024]{1,0:T(8,128)(2,1)S(1)}, bf16[256,1024]{1,0:T(8,128)(2,1)S(1)}, u32[]{:S(2)}, u32[]{:S(2)}) collective-permute-start(bf16[256,1024]{1,0:T(8,128)(2,1)S(1)} %collective-permute-done.refs_0_), channel_id=1, source_target_pairs={{0,32},{1,97},{2,34},{3,99},{4,36},{5,101},{6,38},{7,103},{8,40},{... | collective-permute-start | bytes 1572872 | tf_op jit(solution)/shard_map/ppermute | solution.py:41
  15.7 7.0 %shard_map.50.refs_0_ = bf16[4,768,256]{2,1,0:T(8,128)(2,1)S(1)} custom-call(bf16[768,2048]{1,0:T(8,128)(2,1)} %row_bits.1, f32[768,1]{1,0:T(8,128)S(1)} %mul.20.row_scale, bf16[1024,2048]{1,0:T(8,128)(2,1)} %col_bits.1, bf16[512,2048]{1,0:T(8,128)(2,1)S(1)} %collective-permute-done.11.got_bits), custom_call_target="tpu_custom_call" | custom-call | flops 8000000000 | tf_op jit(solution)/shard_map/pallas_call | solution.py:116
  22.6 2.5 %collective-permute-start.12 = (bf16[4,768,256]{2,1,0:T(8,128)(2,1)S(1)}, bf16[4,768,256]{2,1,0:T(8,128)(2,1)S(1)}, u32[]{:S(2)}, u32[]{:S(2)}) collective-permute-start(bf16[4,768,256]{2,1,0:T(8,128)(2,1)S(1)} %shard_map.50.refs_0_), channel_id=1, source_target_pairs={{0,2},{1,7},{2,4},{3,1},{4,6},{5,3},{6,0},{7,5},{8,10},{9,15},{10,... | collective-permute-start | bytes 4718600 | tf_op jit(solution)/shard_map/ppermute | solution.py:41
  25.2 0.5 collective-permute-start.5
  25.7 1.1 collective-permute-start.6
  26.8 0.2 collective-permute-start.7
  27.1 6.5 %collective-permute-done.5.refs_1_ = bf16[256,1024]{1,0:T(8,128)(2,1)S(1)} collective-permute-done((bf16[256,1024]{1,0:T(8,128)(2,1)S(1)}, bf16[256,1024]{1,0:T(8,128)(2,1)S(1)}, u32[]{:S(2)}, u32[]{:S(2)}) %collective-permute-start.5) | collective-permute-done | bytes 524320 | tf_op jit(solution)/shard_map/ppermute | solution.py:41
  33.6 0.5 collective-permute-done.6.refs_2_
  34.1 1.2 %collective-permute-start.9 = (bf16[256,1024]{1,0:T(8,128)(2,1)S(1)}, bf16[256,1024]{1,0:T(8,128)(2,1)S(1)}, u32[]{:S(2)}, u32[]{:S(2)}) collective-permute-start(bf16[256,1024]{1,0:T(8,128)(2,1)S(1)} %get-tuple-element.55.refs_2_), channel_id=1, source_target_pairs={{0,8},{1,25},{2,10},{3,27},{4,12},{5,29},{6,14},{7,31},{8,16},{9,1... | collective-permute-start | bytes 1572872 | tf_op jit(solution)/shard_map/ppermute | solution.py:41
  35.3 1.2 %collective-permute-start.10 = (bf16[256,1024]{1,0:T(8,128)(2,1)S(1)}, bf16[256,1024]{1,0:T(8,128)(2,1)S(1)}, u32[]{:S(2)}, u32[]{:S(2)}) collective-permute-start(bf16[256,1024]{1,0:T(8,128)(2,1)S(1)} %get-tuple-element.56.refs_5_), channel_id=1, source_target_pairs={{0,32},{1,97},{2,34},{3,99},{4,36},{5,101},{6,38},{7,103},{8,40},{... | collective-permute-start | bytes 1572872 | tf_op jit(solution)/shard_map/ppermute | solution.py:41
  36.7 2.5 %collective-permute-done.7.refs_1_ = bf16[256,1024]{1,0:T(8,128)(2,1)S(1)} collective-permute-done((bf16[256,1024]{1,0:T(8,128)(2,1)S(1)}, bf16[256,1024]{1,0:T(8,128)(2,1)S(1)}, u32[]{:S(2)}, u32[]{:S(2)}) %collective-permute-start.7) | collective-permute-done | bytes 524320 | tf_op jit(solution)/shard_map/ppermute | solution.py:41
  39.2 0.5 collective-permute-done.8.refs_2_
  39.7 1.2 %collective-permute-start.13 = (bf16[256,1024]{1,0:T(8,128)(2,1)S(1)}, bf16[256,1024]{1,0:T(8,128)(2,1)S(1)}, u32[]{:S(2)}, u32[]{:S(2)}) collective-permute-start(bf16[256,1024]{1,0:T(8,128)(2,1)S(1)} %get-tuple-element.58.refs_11_), channel_id=1, source_target_pairs={{0,8},{1,25},{2,10},{3,27},{4,12},{5,29},{6,14},{7,31},{8,16},{9,1... | collective-permute-start | bytes 1572872 | tf_op jit(solution)/shard_map/ppermute | solution.py:41
  40.9 1.3 %collective-permute-start.14 = (bf16[256,1024]{1,0:T(8,128)(2,1)S(1)}, bf16[256,1024]{1,0:T(8,128)(2,1)S(1)}, u32[]{:S(2)}, u32[]{:S(2)}) collective-permute-start(bf16[256,1024]{1,0:T(8,128)(2,1)S(1)} %get-tuple-element.59.refs_14_), channel_id=1, source_target_pairs={{0,32},{1,97},{2,34},{3,99},{4,36},{5,101},{6,38},{7,103},{8,40},{... | collective-permute-start | bytes 1572872 | tf_op jit(solution)/shard_map/ppermute | solution.py:41
  42.3 2.6 %collective-permute-done.9.refs_1_ = bf16[256,1024]{1,0:T(8,128)(2,1)S(1)} collective-permute-done((bf16[256,1024]{1,0:T(8,128)(2,1)S(1)}, bf16[256,1024]{1,0:T(8,128)(2,1)S(1)}, u32[]{:S(2)}, u32[]{:S(2)}) %collective-permute-start.9) | collective-permute-done | bytes 524320 | tf_op jit(solution)/shard_map/ppermute | solution.py:41
  44.8 0.5 collective-permute-done.10.refs_2_
  45.3 1.4 %collective-permute-start.17 = (bf16[4,768,256]{2,1,0:T(8,128)(2,1)S(1)}, bf16[4,768,256]{2,1,0:T(8,128)(2,1)S(1)}, u32[]{:S(2)}, u32[]{:S(2)}) collective-permute-start(bf16[4,768,256]{2,1,0:T(8,128)(2,1)S(1)} %get-tuple-element.63.refs_1_), channel_id=1, source_target_pairs={{0,2},{1,7},{2,4},{3,1},{4,6},{5,3},{6,0},{7,5},{8,10},{9,15},{10,... | collective-permute-start | bytes 4718600 | tf_op jit(solution)/shard_map/ppermute | solution.py:41
  46.8 3.5 %collective-permute-start.15 = (bf16[768,512]{1,0:T(8,128)(2,1)S(1)}, bf16[768,512]{1,0:T(8,128)(2,1)S(1)}, u32[]{:S(2)}, u32[]{:S(2)}) collective-permute-start(bf16[768,512]{1,0:T(8,128)(2,1)S(1)} %pad_maximum_fusion), channel_id=1, source_target_pairs={{0,32},{1,97},{2,34},{3,99},{4,36},{5,101},{6,38},{7,103},{8,40},{... | collective-permute-start | bytes 2359304 | tf_op jit(solution)/shard_map/ppermute | solution.py:41
  50.5 0.5 collective-permute-done.14.refs_2_
  51.0 2.3 %collective-permute-start.19 = (bf16[768,512]{1,0:T(8,128)(2,1)S(1)}, bf16[768,512]{1,0:T(8,128)(2,1)S(1)}, u32[]{:S(2)}, u32[]{:S(2)}) collective-permute-start(bf16[768,512]{1,0:T(8,128)(2,1)S(1)} %pad_maximum_fusion.2), channel_id=1, source_target_pairs={{0,32},{1,97},{2,34},{3,99},{4,36},{5,101},{6,38},{7,103},{8,40},{... | collective-permute-start | bytes 2359304 | tf_op jit(solution)/shard_map/ppermute | solution.py:41
  53.4 0.3 collective-permute-start.20
  53.7 5.7 %collective-permute-done.15.refs_1_ = bf16[768,512]{1,0:T(8,128)(2,1)S(1)} collective-permute-done((bf16[768,512]{1,0:T(8,128)(2,1)S(1)}, bf16[768,512]{1,0:T(8,128)(2,1)S(1)}, u32[]{:S(2)}, u32[]{:S(2)}) %collective-permute-start.15) | collective-permute-done | bytes 786464 | tf_op jit(solution)/shard_map/ppermute | solution.py:41
  59.4 2.2 %collective-permute-done.16.refs_2_ = bf16[768,512]{1,0:T(8,128)(2,1)S(1)} collective-permute-done((bf16[768,512]{1,0:T(8,128)(2,1)S(1)}, bf16[768,512]{1,0:T(8,128)(2,1)S(1)}, u32[]{:S(2)}, u32[]{:S(2)}) %collective-permute-start.16) | collective-permute-done | bytes 786464 | tf_op jit(solution)/shard_map/ppermute | solution.py:41
  61.6 3.4 %collective-permute-done.17.refs_3_ = bf16[4,768,256]{2,1,0:T(8,128)(2,1)S(1)} collective-permute-done((bf16[4,768,256]{2,1,0:T(8,128)(2,1)S(1)}, bf16[4,768,256]{2,1,0:T(8,128)(2,1)S(1)}, u32[]{:S(2)}, u32[]{:S(2)}) %collective-permute-start.17) | collective-permute-done | bytes 1572896 | tf_op jit(solution)/shard_map/ppermute | solution.py:41
  65.0 2.6 %collective-permute-start.18 = (bf16[4,768,256]{2,1,0:T(8,128)(2,1)S(1)}, bf16[4,768,256]{2,1,0:T(8,128)(2,1)S(1)}, u32[]{:S(2)}, u32[]{:S(2)}) collective-permute-start(bf16[4,768,256]{2,1,0:T(8,128)(2,1)S(1)} %get-tuple-element.64.refs_2_), channel_id=1, source_target_pairs={{0,2},{1,7},{2,4},{3,1},{4,6},{5,3},{6,0},{7,5},{8,10},{9,15},{10,... | collective-permute-start | bytes 4718600 | tf_op jit(solution)/shard_map/ppermute | solution.py:41
  67.5 3.4 %collective-permute-start.21 = (bf16[768,512]{1,0:T(8,128)(2,1)S(1)}, bf16[768,512]{1,0:T(8,128)(2,1)S(1)}, u32[]{:S(2)}, u32[]{:S(2)}) collective-permute-start(bf16[768,512]{1,0:T(8,128)(2,1)S(1)} %get-tuple-element.69.refs_7_), channel_id=1, source_target_pairs={{0,32},{1,97},{2,34},{3,99},{4,36},{5,101},{6,38},{7,103},{8,40},{... | collective-permute-start | bytes 2359304 | tf_op jit(solution)/shard_map/ppermute | solution.py:41
  71.1 0.5 collective-permute-start.24
  71.5 0.3 shard_map.54.refs_1_.k
  71.9 10.4 %shard_map.60 = (f32[768,1024]{1,0:T(8,128)S(1)}, f32[768,1024]{1,0:T(8,128)S(1)}) custom-call(bf16[16,768,256]{2,1,0:T(8,128)(2,1)S(1)} %shard_map.54.refs_1_.k, bf16[256,1024]{1,0:T(8,128)(2,1)S(1)} %collective-permute-done.refs_0_, bf16[256,1024]{1,0:T(8,128)(2,1)S(1)} %get-tuple-element.49.refs_1_, bf16[256,1024]{1,0:T(8,128)(2,1)S(1)} %get-tuple-element.55.refs_2_, ...), custom_call_target="tpu_custom_call" | custom-call | flops 1000000 | tf_op jit(solution)/shard_map/pallas_call | solution.py:233
  82.3 1.0 collective-permute-start.27
  83.3 1.1 %collective-permute-start.28 = (bf16[768,512]{1,0:T(8,128)(2,1)S(1)}, bf16[768,512]{1,0:T(8,128)(2,1)S(1)}, u32[]{:S(2)}, u32[]{:S(2)}) collective-permute-start(bf16[768,512]{1,0:T(8,128)(2,1)S(1)} %get-tuple-element.79.refs_1_), channel_id=1, source_target_pairs={{0,8},{1,25},{2,10},{3,27},{4,12},{5,29},{6,14},{7,31},{8,16},{9,1... | collective-permute-start | bytes 2359304 | tf_op jit(solution)/shard_map/ppermute | solution.py:41
  84.4 3.9 %collective-permute-done.23.refs_1_ = bf16[768,512]{1,0:T(8,128)(2,1)S(1)} collective-permute-done((bf16[768,512]{1,0:T(8,128)(2,1)S(1)}, bf16[768,512]{1,0:T(8,128)(2,1)S(1)}, u32[]{:S(2)}, u32[]{:S(2)}) %collective-permute-start.23) | collective-permute-done | bytes 786464 | tf_op jit(solution)/shard_map/ppermute | solution.py:41
  88.3 2.2 %collective-permute-done.24.refs_2_ = bf16[768,512]{1,0:T(8,128)(2,1)S(1)} collective-permute-done((bf16[768,512]{1,0:T(8,128)(2,1)S(1)}, bf16[768,512]{1,0:T(8,128)(2,1)S(1)}, u32[]{:S(2)}, u32[]{:S(2)}) %collective-permute-start.24) | collective-permute-done | bytes 786464 | tf_op jit(solution)/shard_map/ppermute | solution.py:41
  90.5 1.2 %collective-permute-start.25 = (bf16[768,512]{1,0:T(8,128)(2,1)S(1)}, bf16[768,512]{1,0:T(8,128)(2,1)S(1)}, u32[]{:S(2)}, u32[]{:S(2)}) collective-permute-start(bf16[768,512]{1,0:T(8,128)(2,1)S(1)} %get-tuple-element.74.refs_2_), channel_id=1, source_target_pairs={{0,32},{1,97},{2,34},{3,99},{4,36},{5,101},{6,38},{7,103},{8,40},{... | collective-permute-start | bytes 2359304 | tf_op jit(solution)/shard_map/ppermute | solution.py:41
  91.8 2.4 %shard_map.61 = (f32[768,1024]{1,0:T(8,128)S(1)}, f32[768,1024]{1,0:T(8,128)S(1)}) custom-call(bf16[16,768,256]{2,1,0:T(8,128)(2,1)S(1)} %shard_map.55.k, bf16[256,1024]{1,0:T(8,128)(2,1)S(1)} %collective-permute-done.refs_0_, bf16[256,1024]{1,0:T(8,128)(2,1)S(1)} %get-tuple-element.49.refs_1_, ...), custom_call_target="tpu_custom_call", output_to_operand_aliasing={{0}: (19, {}), {1}: (20, {})} | custom-call | flops 1000000 | tf_op jit(solution)/shard_map/pallas_call | solution.py:233
  94.3 3.0 %shard_map.62 = (f32[768,1024]{1,0:T(8,128)S(1)}, f32[768,1024]{1,0:T(8,128)S(1)}) custom-call(bf16[16,768,256]{2,1,0:T(8,128)(2,1)S(1)} %shard_map.55.k, bf16[768,512]{1,0:T(8,128)(2,1)S(1)} %get-tuple-element.78.refs_0_, bf16[768,512]{1,0:T(8,128)(2,1)S(1)} %get-tuple-element.79.refs_1_, ...), custom_call_target="tpu_custom_call", output_to_operand_aliasing={{0}: (5, {}), {1}: (6, {})} | custom-call | flops 1000000 | tf_op jit(solution)/shard_map/pallas_call | solution.py:233
  97.3 1.6 %collective-permute-done.28.refs_2_ = bf16[768,512]{1,0:T(8,128)(2,1)S(1)} collective-permute-done((bf16[768,512]{1,0:T(8,128)(2,1)S(1)}, bf16[768,512]{1,0:T(8,128)(2,1)S(1)}, u32[]{:S(2)}, u32[]{:S(2)}) %collective-permute-start.28) | collective-permute-done | bytes 786464 | tf_op jit(solution)/shard_map/ppermute | solution.py:41
  98.9 1.8 %shard_map.64 = f32[768,1024]{1,0:T(8,128)S(1)} custom-call(bf16[16,768,256]{2,1,0:T(8,128)(2,1)S(1)} %shard_map.55.k, bf16[768,512]{1,0:T(8,128)(2,1)S(1)} %get-tuple-element.86.refs_0_, bf16[768,512]{1,0:T(8,128)(2,1)S(1)} %get-tuple-element.87.refs_1_, f32[768,1024]{1,0:T(8,128)S(1)} %get-tuple-element.88.refs_2_), custom_call_target="tpu_custom_call", output_to_operand_aliasing={{}: (3, {})} | custom-call | flops 1000000 | tf_op jit(solution)/shard_map/pallas_call | solution.py:233
  100.7 0.7 collective-permute-start.29
  101.4 3.8 %collective-permute-done.25.refs_0_ = bf16[768,512]{1,0:T(8,128)(2,1)S(1)} collective-permute-done((bf16[768,512]{1,0:T(8,128)(2,1)S(1)}, bf16[768,512]{1,0:T(8,128)(2,1)S(1)}, u32[]{:S(2)}, u32[]{:S(2)}) %collective-permute-start.25) | collective-permute-done | bytes 786464 | tf_op jit(solution)/shard_map/ppermute | solution.py:41
  105.2 2.2 %collective-permute-done.26.refs_1_ = bf16[768,512]{1,0:T(8,128)(2,1)S(1)} collective-permute-done((bf16[768,512]{1,0:T(8,128)(2,1)S(1)}, bf16[768,512]{1,0:T(8,128)(2,1)S(1)}, u32[]{:S(2)}, u32[]{:S(2)}) %collective-permute-start.26) | collective-permute-done | bytes 786464 | tf_op jit(solution)/shard_map/ppermute | solution.py:41
  107.4 2.4 %shard_map.65 = f32[768,1024]{1,0:T(8,128)} custom-call(bf16[16,768,256]{2,1,0:T(8,128)(2,1)S(1)} %shard_map.55.k, bf16[768,512]{1,0:T(8,128)(2,1)S(1)} %get-tuple-element.76.refs_0_, bf16[768,512]{1,0:T(8,128)(2,1)S(1)} %get-tuple-element.77.refs_1_, f32[768,1024]{1,0:T(8,128)S(1)} %get-tuple-element.84.refs_2_, f32[768,1024]{1,0:T(8,128)S(1)} %collective-permute-done.29.refs_3_), custom_call_target="tpu_custom_call" | custom-call | flops 1000000 | tf_op jit(solution)/shard_map/pallas_call | solution.py:271
  (57 shorter events, 1.1 us)
Async XLA Ops:
  0.0 4.7 %copy-start = (bf16[512,1024]{1,0:T(8,128)(2,1)S(1)}, bf16[512,1024]{1,0:T(8,128)(2,1)}, u32[]{:S(2)}) copy-start(bf16[512,1024]{1,0:T(8,128)(2,1)} %param.8) | copy-start | bytes 3145732
  3.3 8.2 %copy-start.1 = (s32[768]{0:T(1024)S(1)}, s32[768]{0:T(1024)}, u32[]{:S(2)}) copy-start(s32[768]{0:T(1024)} %param.6) | copy-start | bytes 9220
  3.3 12.4 %collective-permute-start.11 = (bf16[512,2048]{1,0:T(8,128)(2,1)}, bf16[512,2048]{1,0:T(8,128)(2,1)S(1)}, u32[]{:S(2)}, u32[]{:S(2)}) collective-permute-start(bf16[512,2048]{1,0:T(8,128)(2,1)} %bitcast.1), channel_id=1, source_target_pairs={{0,1},{1,0},{2,3},{3,2},{4,5},{5,4},{6,7},{7,6},{8,9},{9,8},{10,11... | collective-permute-start | bytes 6291464 | tf_op jit(solution)/shard_map/ppermute | solution.py:41
  4.8 6.9 %collective-permute-start = (bf16[256,1024]{1,0:T(8,128)(2,1)S(1)}, bf16[256,1024]{1,0:T(8,128)(2,1)S(1)}, u32[]{:S(2)}, u32[]{:S(2)}) collective-permute-start(bf16[256,1024]{1,0:T(8,128)(2,1)S(1)} %get-tuple-element.90), channel_id=1, source_target_pairs={{0,1},{1,0},{2,3},{3,2},{4,5},{5,4},{6,7},{7,6},{8,9},{9,8},{10,11... | collective-permute-start | bytes 1572872 | tf_op jit(solution)/shard_map/ppermute | solution.py:41
  4.8 22.0 %collective-permute-start.3 = (bf16[256,1024]{1,0:T(8,128)(2,1)S(1)}, bf16[256,1024]{1,0:T(8,128)(2,1)S(1)}, u32[]{:S(2)}, u32[]{:S(2)}) collective-permute-start(bf16[256,1024]{1,0:T(8,128)(2,1)S(1)} %get-tuple-element.89.refs_9_), channel_id=1, source_target_pairs={{0,8},{1,25},{2,10},{3,27},{4,12},{5,29},{6,14},{7,31},{8,16},{9,1... | collective-permute-start | bytes 1572872 | tf_op jit(solution)/shard_map/ppermute | solution.py:41
  7.7 19.1 %collective-permute-start.4 = (bf16[256,1024]{1,0:T(8,128)(2,1)S(1)}, bf16[256,1024]{1,0:T(8,128)(2,1)S(1)}, u32[]{:S(2)}, u32[]{:S(2)}) collective-permute-start(bf16[256,1024]{1,0:T(8,128)(2,1)S(1)} %get-tuple-element.89.refs_9_), channel_id=1, source_target_pairs={{0,32},{1,97},{2,34},{3,99},{4,36},{5,101},{6,38},{7,103},{8,40},{... | collective-permute-start | bytes 1572872 | tf_op jit(solution)/shard_map/ppermute | solution.py:41
  11.7 13.5 %collective-permute-start.1 = (bf16[256,1024]{1,0:T(8,128)(2,1)S(1)}, bf16[256,1024]{1,0:T(8,128)(2,1)S(1)}, u32[]{:S(2)}, u32[]{:S(2)}) collective-permute-start(bf16[256,1024]{1,0:T(8,128)(2,1)S(1)} %collective-permute-done.refs_0_), channel_id=1, source_target_pairs={{0,8},{1,25},{2,10},{3,27},{4,12},{5,29},{6,14},{7,31},{8,16},{9,1... | collective-permute-start | bytes 1572872 | tf_op jit(solution)/shard_map/ppermute | solution.py:41
  12.2 13.0 %collective-permute-start.2 = (bf16[256,1024]{1,0:T(8,128)(2,1)S(1)}, bf16[256,1024]{1,0:T(8,128)(2,1)S(1)}, u32[]{:S(2)}, u32[]{:S(2)}) collective-permute-start(bf16[256,1024]{1,0:T(8,128)(2,1)S(1)} %collective-permute-done.refs_0_), channel_id=1, source_target_pairs={{0,32},{1,97},{2,34},{3,99},{4,36},{5,101},{6,38},{7,103},{8,40},{... | collective-permute-start | bytes 1572872 | tf_op jit(solution)/shard_map/ppermute | solution.py:41
  22.6 22.7 %collective-permute-start.12 = (bf16[4,768,256]{2,1,0:T(8,128)(2,1)S(1)}, bf16[4,768,256]{2,1,0:T(8,128)(2,1)S(1)}, u32[]{:S(2)}, u32[]{:S(2)}) collective-permute-start(bf16[4,768,256]{2,1,0:T(8,128)(2,1)S(1)} %shard_map.50.refs_0_), channel_id=1, source_target_pairs={{0,2},{1,7},{2,4},{3,1},{4,6},{5,3},{6,0},{7,5},{8,10},{9,15},{10,... | collective-permute-start | bytes 4718600 | tf_op jit(solution)/shard_map/ppermute | solution.py:41
  25.2 8.4 %collective-permute-start.5 = (bf16[256,1024]{1,0:T(8,128)(2,1)S(1)}, bf16[256,1024]{1,0:T(8,128)(2,1)S(1)}, u32[]{:S(2)}, u32[]{:S(2)}) collective-permute-start(bf16[256,1024]{1,0:T(8,128)(2,1)S(1)} %get-tuple-element.49.refs_1_), channel_id=1, source_target_pairs={{0,8},{1,25},{2,10},{3,27},{4,12},{5,29},{6,14},{7,31},{8,16},{9,1... | collective-permute-start | bytes 1572872 | tf_op jit(solution)/shard_map/ppermute | solution.py:41
  25.7 8.3 %collective-permute-start.6 = (bf16[256,1024]{1,0:T(8,128)(2,1)S(1)}, bf16[256,1024]{1,0:T(8,128)(2,1)S(1)}, u32[]{:S(2)}, u32[]{:S(2)}) collective-permute-start(bf16[256,1024]{1,0:T(8,128)(2,1)S(1)} %get-tuple-element.50.refs_4_), channel_id=1, source_target_pairs={{0,32},{1,97},{2,34},{3,99},{4,36},{5,101},{6,38},{7,103},{8,40},{... | collective-permute-start | bytes 1572872 | tf_op jit(solution)/shard_map/ppermute | solution.py:41
  26.8 12.4 %collective-permute-start.7 = (bf16[256,1024]{1,0:T(8,128)(2,1)S(1)}, bf16[256,1024]{1,0:T(8,128)(2,1)S(1)}, u32[]{:S(2)}, u32[]{:S(2)}) collective-permute-start(bf16[256,1024]{1,0:T(8,128)(2,1)S(1)} %get-tuple-element.52.refs_10_), channel_id=1, source_target_pairs={{0,8},{1,25},{2,10},{3,27},{4,12},{5,29},{6,14},{7,31},{8,16},{9,1... | collective-permute-start | bytes 1572872 | tf_op jit(solution)/shard_map/ppermute | solution.py:41
  27.0 12.7 %collective-permute-start.8 = (bf16[256,1024]{1,0:T(8,128)(2,1)S(1)}, bf16[256,1024]{1,0:T(8,128)(2,1)S(1)}, u32[]{:S(2)}, u32[]{:S(2)}) collective-permute-start(bf16[256,1024]{1,0:T(8,128)(2,1)S(1)} %get-tuple-element.53.refs_13_), channel_id=1, source_target_pairs={{0,32},{1,97},{2,34},{3,99},{4,36},{5,101},{6,38},{7,103},{8,40},{... | collective-permute-start | bytes 1572872 | tf_op jit(solution)/shard_map/ppermute | solution.py:41
  34.1 10.8 %collective-permute-start.9 = (bf16[256,1024]{1,0:T(8,128)(2,1)S(1)}, bf16[256,1024]{1,0:T(8,128)(2,1)S(1)}, u32[]{:S(2)}, u32[]{:S(2)}) collective-permute-start(bf16[256,1024]{1,0:T(8,128)(2,1)S(1)} %get-tuple-element.55.refs_2_), channel_id=1, source_target_pairs={{0,8},{1,25},{2,10},{3,27},{4,12},{5,29},{6,14},{7,31},{8,16},{9,1... | collective-permute-start | bytes 1572872 | tf_op jit(solution)/shard_map/ppermute | solution.py:41
  35.3 10.0 %collective-permute-start.10 = (bf16[256,1024]{1,0:T(8,128)(2,1)S(1)}, bf16[256,1024]{1,0:T(8,128)(2,1)S(1)}, u32[]{:S(2)}, u32[]{:S(2)}) collective-permute-start(bf16[256,1024]{1,0:T(8,128)(2,1)S(1)} %get-tuple-element.56.refs_5_), channel_id=1, source_target_pairs={{0,32},{1,97},{2,34},{3,99},{4,36},{5,101},{6,38},{7,103},{8,40},{... | collective-permute-start | bytes 1572872 | tf_op jit(solution)/shard_map/ppermute | solution.py:41
  39.7 10.8 %collective-permute-start.13 = (bf16[256,1024]{1,0:T(8,128)(2,1)S(1)}, bf16[256,1024]{1,0:T(8,128)(2,1)S(1)}, u32[]{:S(2)}, u32[]{:S(2)}) collective-permute-start(bf16[256,1024]{1,0:T(8,128)(2,1)S(1)} %get-tuple-element.58.refs_11_), channel_id=1, source_target_pairs={{0,8},{1,25},{2,10},{3,27},{4,12},{5,29},{6,14},{7,31},{8,16},{9,1... | collective-permute-start | bytes 1572872 | tf_op jit(solution)/shard_map/ppermute | solution.py:41
  40.9 10.0 %collective-permute-start.14 = (bf16[256,1024]{1,0:T(8,128)(2,1)S(1)}, bf16[256,1024]{1,0:T(8,128)(2,1)S(1)}, u32[]{:S(2)}, u32[]{:S(2)}) collective-permute-start(bf16[256,1024]{1,0:T(8,128)(2,1)S(1)} %get-tuple-element.59.refs_14_), channel_id=1, source_target_pairs={{0,32},{1,97},{2,34},{3,99},{4,36},{5,101},{6,38},{7,103},{8,40},{... | collective-permute-start | bytes 1572872 | tf_op jit(solution)/shard_map/ppermute | solution.py:41
  45.3 19.6 %collective-permute-start.17 = (bf16[4,768,256]{2,1,0:T(8,128)(2,1)S(1)}, bf16[4,768,256]{2,1,0:T(8,128)(2,1)S(1)}, u32[]{:S(2)}, u32[]{:S(2)}) collective-permute-start(bf16[4,768,256]{2,1,0:T(8,128)(2,1)S(1)} %get-tuple-element.63.refs_1_), channel_id=1, source_target_pairs={{0,2},{1,7},{2,4},{3,1},{4,6},{5,3},{6,0},{7,5},{8,10},{9,15},{10,... | collective-permute-start | bytes 4718600 | tf_op jit(solution)/shard_map/ppermute | solution.py:41
  46.8 12.5 %collective-permute-start.15 = (bf16[768,512]{1,0:T(8,128)(2,1)S(1)}, bf16[768,512]{1,0:T(8,128)(2,1)S(1)}, u32[]{:S(2)}, u32[]{:S(2)}) collective-permute-start(bf16[768,512]{1,0:T(8,128)(2,1)S(1)} %pad_maximum_fusion), channel_id=1, source_target_pairs={{0,32},{1,97},{2,34},{3,99},{4,36},{5,101},{6,38},{7,103},{8,40},{... | collective-permute-start | bytes 2359304 | tf_op jit(solution)/shard_map/ppermute | solution.py:41
  50.4 11.2 %collective-permute-start.16 = (bf16[768,512]{1,0:T(8,128)(2,1)S(1)}, bf16[768,512]{1,0:T(8,128)(2,1)S(1)}, u32[]{:S(2)}, u32[]{:S(2)}) collective-permute-start(bf16[768,512]{1,0:T(8,128)(2,1)S(1)} %pad_maximum_fusion.1), channel_id=1, source_target_pairs={{0,8},{1,25},{2,10},{3,27},{4,12},{5,29},{6,14},{7,31},{8,16},{9,1... | collective-permute-start | bytes 2359304 | tf_op jit(solution)/shard_map/ppermute | solution.py:41
  51.0 19.9 %collective-permute-start.19 = (bf16[768,512]{1,0:T(8,128)(2,1)S(1)}, bf16[768,512]{1,0:T(8,128)(2,1)S(1)}, u32[]{:S(2)}, u32[]{:S(2)}) collective-permute-start(bf16[768,512]{1,0:T(8,128)(2,1)S(1)} %pad_maximum_fusion.2), channel_id=1, source_target_pairs={{0,32},{1,97},{2,34},{3,99},{4,36},{5,101},{6,38},{7,103},{8,40},{... | collective-permute-start | bytes 2359304 | tf_op jit(solution)/shard_map/ppermute | solution.py:41
  53.4 17.5 %collective-permute-start.20 = (bf16[768,512]{1,0:T(8,128)(2,1)S(1)}, bf16[768,512]{1,0:T(8,128)(2,1)S(1)}, u32[]{:S(2)}, u32[]{:S(2)}) collective-permute-start(bf16[768,512]{1,0:T(8,128)(2,1)S(1)} %pad_maximum_fusion.3), channel_id=1, source_target_pairs={{0,8},{1,25},{2,10},{3,27},{4,12},{5,29},{6,14},{7,31},{8,16},{9,1... | collective-permute-start | bytes 2359304 | tf_op jit(solution)/shard_map/ppermute | solution.py:41
  65.0 26.8 %collective-permute-start.18 = (bf16[4,768,256]{2,1,0:T(8,128)(2,1)S(1)}, bf16[4,768,256]{2,1,0:T(8,128)(2,1)S(1)}, u32[]{:S(2)}, u32[]{:S(2)}) collective-permute-start(bf16[4,768,256]{2,1,0:T(8,128)(2,1)S(1)} %get-tuple-element.64.refs_2_), channel_id=1, source_target_pairs={{0,2},{1,7},{2,4},{3,1},{4,6},{5,3},{6,0},{7,5},{8,10},{9,15},{10,... | collective-permute-start | bytes 4718600 | tf_op jit(solution)/shard_map/ppermute | solution.py:41
  67.5 14.7 %collective-permute-start.21 = (bf16[768,512]{1,0:T(8,128)(2,1)S(1)}, bf16[768,512]{1,0:T(8,128)(2,1)S(1)}, u32[]{:S(2)}, u32[]{:S(2)}) collective-permute-start(bf16[768,512]{1,0:T(8,128)(2,1)S(1)} %get-tuple-element.69.refs_7_), channel_id=1, source_target_pairs={{0,32},{1,97},{2,34},{3,99},{4,36},{5,101},{6,38},{7,103},{8,40},{... | collective-permute-start | bytes 2359304 | tf_op jit(solution)/shard_map/ppermute | solution.py:41
  70.9 11.3 %collective-permute-start.22 = (bf16[768,512]{1,0:T(8,128)(2,1)S(1)}, bf16[768,512]{1,0:T(8,128)(2,1)S(1)}, u32[]{:S(2)}, u32[]{:S(2)}) collective-permute-start(bf16[768,512]{1,0:T(8,128)(2,1)S(1)} %get-tuple-element.70.refs_8_), channel_id=1, source_target_pairs={{0,8},{1,25},{2,10},{3,27},{4,12},{5,29},{6,14},{7,31},{8,16},{9,1... | collective-permute-start | bytes 2359304 | tf_op jit(solution)/shard_map/ppermute | solution.py:41
  71.0 17.3 %collective-permute-start.23 = (bf16[768,512]{1,0:T(8,128)(2,1)S(1)}, bf16[768,512]{1,0:T(8,128)(2,1)S(1)}, u32[]{:S(2)}, u32[]{:S(2)}) collective-permute-start(bf16[768,512]{1,0:T(8,128)(2,1)S(1)} %get-tuple-element.72.refs_16_), channel_id=1, source_target_pairs={{0,32},{1,97},{2,34},{3,99},{4,36},{5,101},{6,38},{7,103},{8,40},{... | collective-permute-start | bytes 2359304 | tf_op jit(solution)/shard_map/ppermute | solution.py:41
  71.1 19.4 %collective-permute-start.24 = (bf16[768,512]{1,0:T(8,128)(2,1)S(1)}, bf16[768,512]{1,0:T(8,128)(2,1)S(1)}, u32[]{:S(2)}, u32[]{:S(2)}) collective-permute-start(bf16[768,512]{1,0:T(8,128)(2,1)S(1)} %get-tuple-element.73.refs_17_), channel_id=1, source_target_pairs={{0,8},{1,25},{2,10},{3,27},{4,12},{5,29},{6,14},{7,31},{8,16},{9,1... | collective-permute-start | bytes 2359304 | tf_op jit(solution)/shard_map/ppermute | solution.py:41
  82.3 15.1 %collective-permute-start.27 = (bf16[768,512]{1,0:T(8,128)(2,1)S(1)}, bf16[768,512]{1,0:T(8,128)(2,1)S(1)}, u32[]{:S(2)}, u32[]{:S(2)}) collective-permute-start(bf16[768,512]{1,0:T(8,128)(2,1)S(1)} %get-tuple-element.78.refs_0_), channel_id=1, source_target_pairs={{0,32},{1,97},{2,34},{3,99},{4,36},{5,101},{6,38},{7,103},{8,40},{... | collective-permute-start | bytes 2359304 | tf_op jit(solution)/shard_map/ppermute | solution.py:41
  83.3 15.6 %collective-permute-start.28 = (bf16[768,512]{1,0:T(8,128)(2,1)S(1)}, bf16[768,512]{1,0:T(8,128)(2,1)S(1)}, u32[]{:S(2)}, u32[]{:S(2)}) collective-permute-start(bf16[768,512]{1,0:T(8,128)(2,1)S(1)} %get-tuple-element.79.refs_1_), channel_id=1, source_target_pairs={{0,8},{1,25},{2,10},{3,27},{4,12},{5,29},{6,14},{7,31},{8,16},{9,1... | collective-permute-start | bytes 2359304 | tf_op jit(solution)/shard_map/ppermute | solution.py:41
  90.5 14.7 %collective-permute-start.25 = (bf16[768,512]{1,0:T(8,128)(2,1)S(1)}, bf16[768,512]{1,0:T(8,128)(2,1)S(1)}, u32[]{:S(2)}, u32[]{:S(2)}) collective-permute-start(bf16[768,512]{1,0:T(8,128)(2,1)S(1)} %get-tuple-element.74.refs_2_), channel_id=1, source_target_pairs={{0,32},{1,97},{2,34},{3,99},{4,36},{5,101},{6,38},{7,103},{8,40},{... | collective-permute-start | bytes 2359304 | tf_op jit(solution)/shard_map/ppermute | solution.py:41
  91.7 15.6 %collective-permute-start.26 = (bf16[768,512]{1,0:T(8,128)(2,1)S(1)}, bf16[768,512]{1,0:T(8,128)(2,1)S(1)}, u32[]{:S(2)}, u32[]{:S(2)}) collective-permute-start(bf16[768,512]{1,0:T(8,128)(2,1)S(1)} %get-tuple-element.75.refs_3_), channel_id=1, source_target_pairs={{0,8},{1,25},{2,10},{3,27},{4,12},{5,29},{6,14},{7,31},{8,16},{9,1... | collective-permute-start | bytes 2359304 | tf_op jit(solution)/shard_map/ppermute | solution.py:41
  100.7 6.7 %collective-permute-start.29 = (f32[768,1024]{1,0:T(8,128)S(1)}, f32[768,1024]{1,0:T(8,128)S(1)}, u32[]{:S(2)}, u32[]{:S(2)}) collective-permute-start(f32[768,1024]{1,0:T(8,128)S(1)} %shard_map.64), channel_id=1, source_target_pairs={{0,1},{1,0},{2,3},{3,2},{4,5},{5,4},{6,7},{7,6},{8,9},{9,8},{10,11... | collective-permute-start | bytes 9437192 | tf_op jit(solution)/shard_map/ppermute | solution.py:41

commit v3 on v2

v3 whole, which is shorter than its diff:
```python
import functools

import jax
import jax.numpy as jnp
from jax import lax
from jax.experimental import pallas as pl
from jax.experimental.pallas import tpu as pltpu
from jax.sharding import PartitionSpec as P

AXES = ("lib", "lmk")
NZ, NY, NX, NC = 4, 4, 4, 2
TILE = 256
TIES = [5, 7, 7, 7, 7, 7, 9, 9, 9, 9, 9]
TAIL = 5 * 10**10
X1 = 3
X2 = 6
TV = 8 * 10**9


def pairs_of(move):
    pairs = []
    for z in range(NZ):
        for y in range(NY):
            for x in range(NX):
                for c in range(NC):
                    tz, ty, tx, tc = move(z, y, x, c, 1 if c == 0 else -1)
                    to = ((tz % NZ * NY + ty % NY) * NX + tx % NX) * NC + tc
                    pairs.append((((z * NY + y) * NX + x) * NC + c, to))
    return pairs


PAIRS = {
    "z": pairs_of(lambda z, y, x, c, s: (z + s, y, x, c)),
    "y": pairs_of(lambda z, y, x, c, s: (z, y + s, x, c)),
    "x": pairs_of(lambda z, y, x, c, s: (z, y, x + s, c)),
    "core": pairs_of(lambda z, y, x, c, s: (z, y, x, 1 - c)),
}


def send(block, axis):
    return lax.ppermute(block, AXES, PAIRS[axis])


def vmem(x):
    return pltpu.with_memory_space_constraint(x, pltpu.VMEM)


def hbm(x):
    return pltpu.with_memory_space_constraint(x, pltpu.HBM)


def position():
    lib, lmk = lax.axis_index("lib"), lax.axis_index("lmk")
    return lib // NY, lib % NY, lmk // NC, lmk % NC


def root_index(i, j):
    z, y, _, c = position()
    back = 3 + 2 * c
    return (z + i * back) % NZ * NY + (y + j * back) % NY


def kernel_index(i):
    _, _, x, c = position()
    return (x + i * (3 + 2 * c)) % NX * 4


VM = pl.BlockSpec(memory_space=pltpu.VMEM)
ANY = pl.BlockSpec(memory_space=pl.ANY)


def params(mib):
    return pltpu.CompilerParams(vmem_limit_bytes=mib * 2**20)


def cost(flops, bytes_accessed=0):
    return pl.CostEstimate(flops=flops, bytes_accessed=bytes_accessed, transcendentals=0)


def load_kernel(row_bits, col_bits, rbuf, cbuf, token, sems):
    core = position()[3]
    copies = [pltpu.make_async_copy(row_bits, rbuf, sems.at[0])] + [
        pltpu.make_async_copy(
            col_bits.at[pl.ds(pl.multiple_of(h * 512 + core * 256, 256), 256), :],
            cbuf.at[pl.ds(h * 256, 256), :],
            sems.at[1 + h],
        )
        for h in range(2)
    ]
    for cp in copies:
        cp.start()
    token[...] = jnp.zeros(token.shape, token.dtype)
    for cp in copies:
        cp.wait()


def load(row_bits, col_bits):
    rows, depth = row_bits.shape
    return pl.pallas_call(
        load_kernel,
        out_shape=(
            pltpu.VMEM((rows, depth), jnp.bfloat16),
            pltpu.VMEM((512, depth), jnp.bfloat16),
            pltpu.VMEM((16, 128), jnp.bfloat16),
        ),
        in_specs=[ANY, ANY],
        out_specs=(VM,) * 3,
        scratch_shapes=[pltpu.SemaphoreType.DMA((3,))],
        compiler_params=params(1),
        cost_estimate=cost(10**6),
    )(hbm(row_bits), hbm(col_bits))


def tversky_kernel(row_bits, row_scale, col_bits, col_scale, got_bits, out, gbuf, ones, sems):
    core = position()[3]
    nt = (((1,), (1,)), ((), ()))
    cols = [pl.multiple_of(h * 512 + core * 256, 256) for h in range(2)]
    copies = [
        pltpu.make_async_copy(got_bits.at[pl.ds(cols[h], 256), :], gbuf.at[pl.ds(h * 256, 256), :], sems.at[h])
        for h in range(2)
    ]
    for cp in copies:
        cp.start()
    ones[...] = jnp.ones(ones.shape, ones.dtype)
    for part, bits_ref in enumerate((col_bits, gbuf)):
        for h in range(2):
            if part == 1:
                copies[h].wait()
            bits = bits_ref[h * 256 : (h + 1) * 256, :]
            if part == 0:
                scale, to = col_scale[:, pl.ds(cols[h], 256)], 2 * core + h
            else:
                count = lax.dot_general(ones[...], bits, nt, preferred_element_type=jnp.float32)[:1, :]
                scale, to = 0.1 * count, 2 * (1 - core) + h
            for t in range(row_bits.shape[0] // TILE):
                rows = slice(t * TILE, (t + 1) * TILE)
                common = lax.dot_general(row_bits[rows, :], bits, nt, preferred_element_type=jnp.float32)
                out[to, rows, :] = (common / (row_scale[rows, :] + scale)).astype(jnp.bfloat16)


def tversky(row_bits, row_scale, col_bits, col_scale, got_bits):
    rows, depth = row_bits.shape
    return pl.pallas_call(
        tversky_kernel,
        out_shape=pltpu.VMEM((4, rows, 256), jnp.bfloat16),
        in_specs=[VM, VM, VM, VM, ANY],
        out_specs=VM,
        scratch_shapes=[
            pltpu.VMEM((512, depth), jnp.bfloat16),
            pltpu.VMEM((TILE, depth), jnp.bfloat16),
            pltpu.SemaphoreType.DMA((2,)),
        ],
        compiler_params=params(8),
        cost_estimate=cost(TV),
    )(*map(vmem, (row_bits, row_scale, col_bits, col_scale, got_bits)))


def tie_kernel(*refs):
    pass


def tie(*arrays, flops):
    return pl.pallas_call(
        tie_kernel,
        out_shape=tuple(pltpu.VMEM(a.shape, a.dtype) for a in arrays),
        in_specs=[VM] * len(arrays),
        out_specs=(VM,) * len(arrays),
        input_output_aliases={i: i for i in range(len(arrays))},
        compiler_params=params(1),
        cost_estimate=cost(flops),
    )(*map(vmem, arrays))


def place_kernel(hops, has_full, *refs):
    n = len(hops)
    blocks, full, sems = refs[:n], refs[n + has_full], refs[n + has_full + 1]
    copies = [
        pltpu.make_async_copy(b, full.at[pl.ds(kernel_index(i), 4)], sems.at[at])
        for at, (i, b) in enumerate(zip(hops, blocks))
    ]
    for cp in copies:
        cp.start()
    for cp in copies:
        cp.wait()


def place(hops, blocks, full=None):
    args = [*map(vmem, blocks)] + ([] if full is None else [vmem(full)])
    return pl.pallas_call(
        functools.partial(place_kernel, hops, full is not None),
        out_shape=pltpu.VMEM((16, *blocks[0].shape[1:]), blocks[0].dtype),
        in_specs=[VM] * len(args),
        out_specs=VM,
        scratch_shapes=[pltpu.SemaphoreType.DMA((len(hops),))],
        input_output_aliases={} if full is None else {len(hops): 0},
        compiler_params=params(1),
        cost_estimate=cost(10**6),
    )(*args)


def sum_kernel(jobs, n_r, n_acc, k, *refs):
    rs, accs, outs = refs[:n_r], refs[n_r : n_r + n_acc], refs[n_r + n_acc :]
    z, _, x, c = position()
    ahead = (x - z) * (1 - 2 * c) + 4

    def tile(t, carry):
        rows = pl.ds(t * TILE, TILE)

        def add(out, half, pieces, start):
            cols = slice(half * 512, (half + 1) * 512)
            total = start[rows, cols]
            for r, row0, col0, at in pieces:
                total += jnp.dot(
                    k[root_index(*at), rows, :],
                    rs[r][row0 : row0 + 256, col0 : col0 + 512],
                    preferred_element_type=jnp.float32,
                )
            out[rows, cols] = total

        for out, (acc, hops, terms) in zip(outs, jobs):
            if hops is None:
                for half, pieces in enumerate(terms):
                    add(out, half, pieces, accs[acc])
                continue
            if acc is None:
                out[rows, :] = jnp.zeros((TILE, 1024), jnp.float32)
            for i in range(4):
                hop = (ahead + i) % 4

                @pl.when((hop >= hops[0]) & (hop <= hops[1]))
                def _():
                    for half, pieces in enumerate(terms):
                        here = [p for p in pieces if p[3][0] == i]
                        if here:
                            add(out, half, here, out)

        return carry

    lax.fori_loop(0, outs[0].shape[0] // TILE, tile, 0)


def sums(jobs, rs, k, accs):
    rows = k.shape[1]
    args = [*map(vmem, (k, *rs, *accs))]
    first = 1 + len(rs)
    return pl.pallas_call(
        functools.partial(sum_kernel, jobs, len(rs), len(accs)),
        out_shape=tuple(pltpu.VMEM((rows, 1024), jnp.float32) for _ in jobs),
        in_specs=[VM] * len(args),
        out_specs=tuple(VM for _ in jobs),
        input_output_aliases={first + acc: o for o, (acc, _, _) in enumerate(jobs) if acc is not None},
        compiler_params=params(8),
        cost_estimate=cost(10**6),
    )(*args)


def last_kernel(halves, n_r, k, *refs):
    rs, (acc, other, out, buf, sems) = refs[:n_r], refs[n_r:]
    copies = []
    for t in range(acc.shape[0] // TILE):
        rows = slice(t * TILE, (t + 1) * TILE)
        for half, pieces in enumerate(halves):
            cols = slice(half * 512, (half + 1) * 512)
            total = acc[rows, cols] + other[rows, cols]
            for r, row0, col0, at in pieces:
                total += jnp.dot(
                    k[root_index(*at), rows, :],
                    rs[r][row0 : row0 + 256, col0 : col0 + 512],
                    preferred_element_type=jnp.float32,
                )
            buf[rows, cols] = total
        cp = pltpu.make_async_copy(buf.at[pl.ds(t * TILE, TILE), :], out.at[pl.ds(t * TILE, TILE), :], sems.at[t])
        cp.start()
        copies.append(cp)
    for cp in copies:
        cp.wait()


def last(halves, rs, k, acc, other):
    rows = k.shape[1]
    args = [*map(vmem, (k, *rs, acc, other))]
    return pl.pallas_call(
        functools.partial(last_kernel, halves, len(rs)),
        out_shape=jax.ShapeDtypeStruct((rows, 1024), jnp.float32),
        in_specs=[VM] * len(args),
        out_specs=ANY,
        scratch_shapes=[pltpu.VMEM((rows, 1024), jnp.float32), pltpu.SemaphoreType.DMA((rows // TILE,))],
        compiler_params=params(8),
        cost_estimate=cost(10**6),
    )(*args)


def shards(library_bits, library_count, landmark_bits, landmark_count, inverse_root):
    core = lax.axis_index("lmk") % NC
    mine = lax.dynamic_slice_in_dim(inverse_root, core * 256, 256, 0)
    theirs = send(lax.dynamic_slice_in_dim(inverse_root, (1 - core) * 256, 256, 0), "core")
    row_scale = 0.9 * library_count.astype(jnp.float32)[:, None]
    col_scale = 0.1 * landmark_count.astype(jnp.float32)[None, :]
    row_bits, col_bits, token = load(library_bits, landmark_bits)
    theirs, token = tie(theirs, token, flops=10**6)
    own = [theirs, mine]
    first = [[[], []] for _ in range(2)]
    second = [[[], []] for _ in range(2)]
    for s in range(2):
        first[s][0].append(send(own[s], "y"))
        first[s][1].append(send(own[s], "z"))
    ks = [tversky(row_bits, row_scale, col_bits, col_scale, send(landmark_bits, "core"))]

    def second_terms(hop, p):
        return [[(p, 256 * m, 0, (hop, m + 1)) for m in range(3)], [(p + 1, 256 * m, 0, (m + 1, hop)) for m in range(3)]]

    def first_terms(s, p):
        rs = [own[s], *first[s][0], *first[s][1], second[s][0][0], second[s][1][0]]
        where = [(0, 0), (0, 1), (0, 2), (0, 3), (1, 0), (2, 0), (3, 0)]
        more = second_terms(1, p + 7)
        return [[(p + n, 0, 512 * h, at) for n, at in enumerate(where)] + more[h] for h in range(2)], rs

    for step in range(10):
        s, hop = step % 2, step // 2
        rings = (first if hop < 3 else second)[s]
        ready = [rings[0][hop % 3], rings[1][hop % 3]]
        if step == 8:
            k = place([0, 1, 2], ks[:3])
            terms, rs = first_terms(0, 0)
            (acc,) = sums([(None, (0, 2), terms)], rs, k, [])
            ready.append(acc)
        if step == 9:
            terms, rs = first_terms(1, 0)
            jobs = [(None, (0, 2), terms), (0, (0, 2), second_terms(2, len(rs)))]
            other, acc = sums(jobs, [*rs, second[0][0][1], second[0][1][1]], k, [acc])
            ready.append(other)
        if step in (X1, X2):
            ready.append(ks[-1])
        token, *done = tie(token, *ready, flops=TIES[step] * 10**9)
        rings[0][hop % 3], rings[1][hop % 3] = done[:2]
        if step == 8:
            acc = done[2]
        if step == 9:
            other = done[2]
        if step in (X1, X2):
            ks[-1] = done[2]
        if hop < 2:
            rings[0].append(send(done[0], "y"))
            rings[1].append(send(done[1], "z"))
        elif hop == 2:
            left = jnp.concatenate([q[:, :512] for q in rings[0]])
            right = jnp.concatenate([q[:, 512:] for q in rings[1]])
            second[s][0].append(send(left, "z"))
            second[s][1].append(send(right, "y"))
        elif hop < 5:
            rings[0].append(send(done[0], "z"))
            rings[1].append(send(done[1], "y"))
        if step in (0, X1, X2):
            ks.append(send(ks[-1], "x"))

    k = place([3], ks[3:], k)
    terms, rs = first_terms(0, 0)
    more = second_terms(2, len(rs))
    terms = [terms[h] + more[h] for h in range(2)]
    (acc,) = sums([(0, (3, 3), terms)], [*rs, second[0][0][1], second[0][1][1]], k, [acc])
    (acc,) = sums([(0, None, second_terms(3, 0))], [second[0][0][2], second[0][1][2]], k, [acc])
    theirs = send(acc, "core")
    terms, rs = first_terms(1, 0)
    (other,) = sums([(0, (3, 3), terms)], rs, k, [other])
    (other,) = sums([(0, None, second_terms(2, 0))], [second[1][0][1], second[1][1][1]], k, [other])
    tail = tie(second[1][0][2], second[1][1][2], flops=TAIL)
    return last(second_terms(3, 0), tail, k, other, theirs)


def solution(mesh):
    placed = (P("lib", None), P("lib"), P("lmk", None), P("lmk"), P("lib", "lmk"))
    return jax.shard_map(
        shards, mesh=mesh, in_specs=placed, out_specs=P("lib", "lmk"), check_vma=False
    )
```

time: 110 us -> 106 us (0.964)
  local copies, waits for them, and re-layouts: 3.7 us -> 1.65 us
  starting transfers between devices: 39.6 us -> 37.8 us
  waiting for transfers between devices: 38.5 us -> 36.7 us
  Pallas kernels: 27.5 us -> 28.6 us
    pallas_call x4 -> x7, Pallas kernels: 17.6 us -> 21.3 us  [the longest x6 18.8 us: sums(): pl.pallas_call(functools.partial(sum_kernel, jobs, len(rs), len(accs)), o...]
    dynamic_slice x1 -> x0, local copies, waits for them, and re-layouts: 3.25 us -> none  [shards(): lax.dynamic_slice_in_dim(blocks, (1 - core) * 256, 256, 1).reshape(512, -1)]
    pallas_call x1, Pallas kernels: 6.98 us -> 4.44 us  [tversky(): pl.pallas_call(tversky_kernel, out_shape=pltpu.VMEM((4, rows, 256), jnp.b...]
    ppermute x30, starting transfers between devices: 39.6 us -> 37.8 us  [send(): return lax.ppermute(block, AXES, PAIRS[axis])]
    ppermute x30, waiting for transfers between devices: 38.5 us -> 36.7 us  [send(): return lax.ppermute(block, AXES, PAIRS[axis])]
    dynamic_slice x1, local copies, waits for them, and re-layouts: 0.07 us -> 1.27 us  [shards(): mine = lax.dynamic_slice_in_dim(inverse_root, core * 256, 256, 0)]
  transfers between devices with their start and end apart: 30 -> 30, of which waited for: 15 -> 14; matrix products, arithmetic and copies ran while one was open for 1% -> 2% of each run, Pallas kernels for 23% -> 25%
where the time goes in v3:
time: 106 us
  starting transfers between devices  37.8 us (36%)
  waiting for transfers between devices  36.7 us (35%)
  Pallas kernels  28.6 us (27%)
  local copies, waits for them, and re-layouts  1.65 us (2%)
    ppermute x30, starting transfers between devices, send(): return lax.ppermute(block, AXES, PAIRS[axis])  37.8 us
    ppermute x30, waiting for transfers between devices, send(): return lax.ppermute(block, AXES, PAIRS[axis])  36.7 us
    pallas_call x6, Pallas kernels, sums(): pl.pallas_call(functools.partial(sum_kernel, jobs, len(rs), len(accs)), o...  18.8 us
    pallas_call x1, Pallas kernels, tversky(): pl.pallas_call(tversky_kernel, out_shape=pltpu.VMEM((4, rows, 256), jnp.b...  4.44 us
    pallas_call x1, Pallas kernels, load(): pl.pallas_call(load_kernel, out_shape=(pltpu.VMEM((rows, depth), jnp.bflo...  2.52 us
    pallas_call x1, Pallas kernels, last(): pl.pallas_call(functools.partial(last_kernel, halves, len(rs)), out_shape...  2.42 us
  transfers between devices with their start and end apart: 30, of which 14 were waited for; matrix products, arithmetic and copies ran while one was open for 2% of the time, Pallas kernels for 25%

profile of v3, /device:TPU:1, one launch (start us, length us, event | category | flops | bytes accessed | tf_op | source)
XLA Modules:
  0.0 105.6 jit_solution(5625642306697121331)
XLA Ops:
  0.0 1.4 %collective-permute-start.9 = (bf16[1024,2048]{1,0:T(8,128)(2,1)}, bf16[1024,2048]{1,0:T(8,128)(2,1)}, u32[]{:S(2)}, u32[]{:S(2)}) collective-permute-start(bf16[1024,2048]{1,0:T(8,128)(2,1)} %col_bits.1), channel_id=1, source_target_pairs={{0,1},{1,0},{2,3},{3,2},{4,5},{5,4},{6,7},{7,6},{8,9},{9,8},{10,11... | collective-permute-start | bytes 12582920 | tf_op jit(solution)/shard_map/ppermute | solution.py:41
  1.4 1.3 %constant_dynamic-slice_fusion = (bf16[256,1024]{1,0:T(8,128)(2,1)S(1)}, bf16[256,1024]{1,0:T(8,128)(2,1)S(1)}) fusion(bf16[512,1024]{1,0:T(8,128)(2,1)} %param.9, s32[]{:T(128)S(6)} %select_n.15, s32[]{:T(128)S(6)} %select_n.14), kind=kLoop, calls=%fused_computation.6 | loop fusion | bytes 2097160 | tf_op jit(solution)/shard_map/dynamic_slice | solution.py:295
  2.8 2.9 %collective-permute-start.3 = (bf16[256,1024]{1,0:T(8,128)(2,1)S(1)}, bf16[256,1024]{1,0:T(8,128)(2,1)S(1)}, u32[]{:S(2)}, u32[]{:S(2)}) collective-permute-start(bf16[256,1024]{1,0:T(8,128)(2,1)S(1)} %get-tuple-element.89.refs_0_), channel_id=1, source_target_pairs={{0,8},{1,25},{2,10},{3,27},{4,12},{5,29},{6,14},{7,31},{8,16},{9,1... | collective-permute-start | bytes 1572872 | tf_op jit(solution)/shard_map/ppermute | solution.py:41
  5.7 3.8 %collective-permute-start.4 = (bf16[256,1024]{1,0:T(8,128)(2,1)S(1)}, bf16[256,1024]{1,0:T(8,128)(2,1)S(1)}, u32[]{:S(2)}, u32[]{:S(2)}) collective-permute-start(bf16[256,1024]{1,0:T(8,128)(2,1)S(1)} %get-tuple-element.89.refs_0_), channel_id=1, source_target_pairs={{0,32},{1,97},{2,34},{3,99},{4,36},{5,101},{6,38},{7,103},{8,40},{... | collective-permute-start | bytes 1572872 | tf_op jit(solution)/shard_map/ppermute | solution.py:41
  9.6 2.5 %shard_map.55 = (bf16[768,2048]{1,0:T(8,128)(2,1)S(1)}, bf16[512,2048]{1,0:T(8,128)(2,1)S(1)}, bf16[16,128]{1,0:T(8,128)(2,1)S(1)}) custom-call(bf16[768,2048]{1,0:T(8,128)(2,1)} %row_bits.1, bf16[1024,2048]{1,0:T(8,128)(2,1)} %col_bits.1), custom_call_target="tpu_custom_call" | custom-call | flops 1000000 | tf_op jit(solution)/shard_map/pallas_call | solution.py:99
  12.2 0.5 collective-permute-start.1
  12.7 2.8 %collective-permute-start.2 = (bf16[256,1024]{1,0:T(8,128)(2,1)S(1)}, bf16[256,1024]{1,0:T(8,128)(2,1)S(1)}, u32[]{:S(2)}, u32[]{:S(2)}) collective-permute-start(bf16[256,1024]{1,0:T(8,128)(2,1)S(1)} %get-tuple-element.49.refs_0_), channel_id=1, source_target_pairs={{0,32},{1,97},{2,34},{3,99},{4,36},{5,101},{6,38},{7,103},{8,40},{... | collective-permute-start | bytes 1572872 | tf_op jit(solution)/shard_map/ppermute | solution.py:41
  15.5 4.4 %shard_map.60.refs_0_ = bf16[4,768,256]{2,1,0:T(8,128)(2,1)S(1)} custom-call(bf16[768,2048]{1,0:T(8,128)(2,1)S(1)} %get-tuple-element.57.row_bits, f32[768,1]{1,0:T(8,128)S(1)} %mul.30.row_scale, bf16[512,2048]{1,0:T(8,128)(2,1)S(1)} %get-tuple-element.58.col_bits, f32[1,1024]{1,0:T(1,128)S(1)} %bitcast.1, bf16[1024,2048]{1,0:T(8,128)(2,1)} %collective-permute-done.9.got_bits), custom_call_target="tpu_custom_call" | custom-call | flops 8000000000 | tf_op jit(solution)/shard_map/pallas_call | solution.py:143
  20.0 2.5 %collective-permute-start.10 = (bf16[4,768,256]{2,1,0:T(8,128)(2,1)S(1)}, bf16[4,768,256]{2,1,0:T(8,128)(2,1)S(1)}, u32[]{:S(2)}, u32[]{:S(2)}) collective-permute-start(bf16[4,768,256]{2,1,0:T(8,128)(2,1)S(1)} %shard_map.60.refs_0_), channel_id=1, source_target_pairs={{0,2},{1,7},{2,4},{3,1},{4,6},{5,3},{6,0},{7,5},{8,10},{9,15},{10,... | collective-permute-start | bytes 4718600 | tf_op jit(solution)/shard_map/ppermute | solution.py:41
  22.5 2.5 %collective-permute-start.6 = (bf16[256,1024]{1,0:T(8,128)(2,1)S(1)}, bf16[256,1024]{1,0:T(8,128)(2,1)S(1)}, u32[]{:S(2)}, u32[]{:S(2)}) collective-permute-start(bf16[256,1024]{1,0:T(8,128)(2,1)S(1)} %get-tuple-element.53.refs_4_), channel_id=1, source_target_pairs={{0,32},{1,97},{2,34},{3,99},{4,36},{5,101},{6,38},{7,103},{8,40},{... | collective-permute-start | bytes 1572872 | tf_op jit(solution)/shard_map/ppermute | solution.py:41
  25.1 0.5 collective-permute-start.5
  25.9 7.6 %collective-permute-done.5.refs_1_ = bf16[256,1024]{1,0:T(8,128)(2,1)S(1)} collective-permute-done((bf16[256,1024]{1,0:T(8,128)(2,1)S(1)}, bf16[256,1024]{1,0:T(8,128)(2,1)S(1)}, u32[]{:S(2)}, u32[]{:S(2)}) %collective-permute-start.5) | collective-permute-done | bytes 524320 | tf_op jit(solution)/shard_map/ppermute | solution.py:41
  33.5 1.1 %collective-permute-start.12 = (bf16[256,1024]{1,0:T(8,128)(2,1)S(1)}, bf16[256,1024]{1,0:T(8,128)(2,1)S(1)}, u32[]{:S(2)}, u32[]{:S(2)}) collective-permute-start(bf16[256,1024]{1,0:T(8,128)(2,1)S(1)} %get-tuple-element.61.refs_5_), channel_id=1, source_target_pairs={{0,32},{1,97},{2,34},{3,99},{4,36},{5,101},{6,38},{7,103},{8,40},{... | collective-permute-start | bytes 1572872 | tf_op jit(solution)/shard_map/ppermute | solution.py:41
  34.6 0.6 collective-permute-start.11
  35.3 3.8 %collective-permute-done.7.refs_1_ = bf16[256,1024]{1,0:T(8,128)(2,1)S(1)} collective-permute-done((bf16[256,1024]{1,0:T(8,128)(2,1)S(1)}, bf16[256,1024]{1,0:T(8,128)(2,1)S(1)}, u32[]{:S(2)}, u32[]{:S(2)}) %collective-permute-start.7) | collective-permute-done | bytes 524320 | tf_op jit(solution)/shard_map/ppermute | solution.py:41
  39.1 0.8 collective-permute-done.10.refs_3_
  39.9 1.0 collective-permute-start.13
  40.9 2.9 %collective-permute-start.17 = (bf16[4,768,256]{2,1,0:T(8,128)(2,1)S(1)}, bf16[4,768,256]{2,1,0:T(8,128)(2,1)S(1)}, u32[]{:S(2)}, u32[]{:S(2)}) collective-permute-start(bf16[4,768,256]{2,1,0:T(8,128)(2,1)S(1)} %get-tuple-element.68.refs_1_), channel_id=1, source_target_pairs={{0,2},{1,7},{2,4},{3,1},{4,6},{5,3},{6,0},{7,5},{8,10},{9,15},{10,... | collective-permute-start | bytes 4718600 | tf_op jit(solution)/shard_map/ppermute | solution.py:41
  43.8 0.9 collective-permute-done.11.refs_1_
  44.9 1.4 %collective-permute-start.16 = (bf16[768,512]{1,0:T(8,128)(2,1)S(1)}, bf16[768,512]{1,0:T(8,128)(2,1)S(1)}, u32[]{:S(2)}, u32[]{:S(2)}) collective-permute-start(bf16[768,512]{1,0:T(8,128)(2,1)S(1)} %pad_maximum_fusion.1), channel_id=1, source_target_pairs={{0,8},{1,25},{2,10},{3,27},{4,12},{5,29},{6,14},{7,31},{8,16},{9,1... | collective-permute-start | bytes 2359304 | tf_op jit(solution)/shard_map/ppermute | solution.py:41
  46.5 3.9 %collective-permute-done.13.refs_1_ = bf16[256,1024]{1,0:T(8,128)(2,1)S(1)} collective-permute-done((bf16[256,1024]{1,0:T(8,128)(2,1)S(1)}, bf16[256,1024]{1,0:T(8,128)(2,1)S(1)}, u32[]{:S(2)}, u32[]{:S(2)}) %collective-permute-start.13) | collective-permute-done | bytes 524320 | tf_op jit(solution)/shard_map/ppermute | solution.py:41
  50.4 1.7 %collective-permute-start.20 = (bf16[768,512]{1,0:T(8,128)(2,1)S(1)}, bf16[768,512]{1,0:T(8,128)(2,1)S(1)}, u32[]{:S(2)}, u32[]{:S(2)}) collective-permute-start(bf16[768,512]{1,0:T(8,128)(2,1)S(1)} %pad_maximum_fusion.3), channel_id=1, source_target_pairs={{0,8},{1,25},{2,10},{3,27},{4,12},{5,29},{6,14},{7,31},{8,16},{9,1... | collective-permute-start | bytes 2359304 | tf_op jit(solution)/shard_map/ppermute | solution.py:41
  52.3 6.4 %collective-permute-done.16.refs_2_ = bf16[768,512]{1,0:T(8,128)(2,1)S(1)} collective-permute-done((bf16[768,512]{1,0:T(8,128)(2,1)S(1)}, bf16[768,512]{1,0:T(8,128)(2,1)S(1)}, u32[]{:S(2)}, u32[]{:S(2)}) %collective-permute-start.16) | collective-permute-done | bytes 786464 | tf_op jit(solution)/shard_map/ppermute | solution.py:41
  58.8 2.4 %collective-permute-done.17.refs_3_ = bf16[4,768,256]{2,1,0:T(8,128)(2,1)S(1)} collective-permute-done((bf16[4,768,256]{2,1,0:T(8,128)(2,1)S(1)}, bf16[4,768,256]{2,1,0:T(8,128)(2,1)S(1)}, u32[]{:S(2)}, u32[]{:S(2)}) %collective-permute-start.17) | collective-permute-done | bytes 1572896 | tf_op jit(solution)/shard_map/ppermute | solution.py:41
  61.1 0.2 collective-permute-start.22
  61.3 3.4 %collective-permute-start.18 = (bf16[4,768,256]{2,1,0:T(8,128)(2,1)S(1)}, bf16[4,768,256]{2,1,0:T(8,128)(2,1)S(1)}, u32[]{:S(2)}, u32[]{:S(2)}) collective-permute-start(bf16[4,768,256]{2,1,0:T(8,128)(2,1)S(1)} %get-tuple-element.69.refs_2_), channel_id=1, source_target_pairs={{0,2},{1,7},{2,4},{3,1},{4,6},{5,3},{6,0},{7,5},{8,10},{9,15},{10,... | collective-permute-start | bytes 4718600 | tf_op jit(solution)/shard_map/ppermute | solution.py:41
  64.7 2.5 %collective-permute-done.20.refs_2_ = bf16[768,512]{1,0:T(8,128)(2,1)S(1)} collective-permute-done((bf16[768,512]{1,0:T(8,128)(2,1)S(1)}, bf16[768,512]{1,0:T(8,128)(2,1)S(1)}, u32[]{:S(2)}, u32[]{:S(2)}) %collective-permute-start.20) | collective-permute-done | bytes 786464 | tf_op jit(solution)/shard_map/ppermute | solution.py:41
  67.2 1.1 %collective-permute-start.23 = (bf16[768,512]{1,0:T(8,128)(2,1)S(1)}, bf16[768,512]{1,0:T(8,128)(2,1)S(1)}, u32[]{:S(2)}, u32[]{:S(2)}) collective-permute-start(bf16[768,512]{1,0:T(8,128)(2,1)S(1)} %get-tuple-element.77.refs_7_), channel_id=1, source_target_pairs={{0,32},{1,97},{2,34},{3,99},{4,36},{5,101},{6,38},{7,103},{8,40},{... | collective-permute-start | bytes 2359304 | tf_op jit(solution)/shard_map/ppermute | solution.py:41
  68.3 0.6 collective-permute-start.24
  68.9 0.3 shard_map.65.refs_1_.k
  69.3 5.2 %shard_map.68.refs_3_ = f32[768,1024]{1,0:T(8,128)S(1)} custom-call(bf16[16,768,256]{2,1,0:T(8,128)(2,1)S(1)} %shard_map.65.refs_1_.k, bf16[256,1024]{1,0:T(8,128)(2,1)S(1)} %get-tuple-element.49.refs_0_, bf16[256,1024]{1,0:T(8,128)(2,1)S(1)} %get-tuple-element.52.refs_1_, bf16[256,1024]{1,0:T(8,128)(2,1)S(1)} %get-tuple-element.60.refs_2_, ...), custom_call_target="tpu_custom_call" | custom-call | flops 1000000 | tf_op jit(solution)/shard_map/pallas_call | solution.py:246
  74.6 1.1 %collective-permute-done.22.refs_2_ = bf16[768,512]{1,0:T(8,128)(2,1)S(1)} collective-permute-done((bf16[768,512]{1,0:T(8,128)(2,1)S(1)}, bf16[768,512]{1,0:T(8,128)(2,1)S(1)}, u32[]{:S(2)}, u32[]{:S(2)}) %collective-permute-start.22) | collective-permute-done | bytes 786464 | tf_op jit(solution)/shard_map/ppermute | solution.py:41
  75.6 1.1 %collective-permute-start.27 = (bf16[768,512]{1,0:T(8,128)(2,1)S(1)}, bf16[768,512]{1,0:T(8,128)(2,1)S(1)}, u32[]{:S(2)}, u32[]{:S(2)}) collective-permute-start(bf16[768,512]{1,0:T(8,128)(2,1)S(1)} %get-tuple-element.79.refs_9_), channel_id=1, source_target_pairs={{0,32},{1,97},{2,34},{3,99},{4,36},{5,101},{6,38},{7,103},{8,40},{... | collective-permute-start | bytes 2359304 | tf_op jit(solution)/shard_map/ppermute | solution.py:41
  76.8 0.6 collective-permute-start.28
  77.3 7.2 %shard_map.70 = (f32[768,1024]{1,0:T(8,128)S(1)}, f32[768,1024]{1,0:T(8,128)S(1)}) custom-call(bf16[16,768,256]{2,1,0:T(8,128)(2,1)S(1)} %shard_map.65.refs_1_.k, bf16[256,1024]{1,0:T(8,128)(2,1)S(1)} %get-tuple-element.89.refs_0_, bf16[256,1024]{1,0:T(8,128)(2,1)S(1)} %get-tuple-element.55.refs_1_, ...), custom_call_target="tpu_custom_call", output_to_operand_aliasing={{1}: (12, {})} | custom-call | flops 1000000 | tf_op jit(solution)/shard_map/pallas_call | solution.py:246
  84.6 0.6 collective-permute-start.25
  85.2 0.6 collective-permute-start.26
  85.9 1.5 %shard_map.75.refs_2_ = f32[768,1024]{1,0:T(8,128)S(1)} custom-call(bf16[16,768,256]{2,1,0:T(8,128)(2,1)S(1)} %shard_map.66.k, bf16[256,1024]{1,0:T(8,128)(2,1)S(1)} %get-tuple-element.49.refs_0_, bf16[256,1024]{1,0:T(8,128)(2,1)S(1)} %get-tuple-element.52.refs_1_, bf16[256,1024]{1,0:T(8,128)(2,1)S(1)} %get-tuple-element.60.refs_2_, ...), custom_call_target="tpu_custom_call", output_to_operand_aliasing={{}: (12, {})} | custom-call | flops 1000000 | tf_op jit(solution)/shard_map/pallas_call | solution.py:246
  87.4 1.3 %shard_map.73.refs_2_ = f32[768,1024]{1,0:T(8,128)S(1)} custom-call(bf16[16,768,256]{2,1,0:T(8,128)(2,1)S(1)} %shard_map.66.k, bf16[256,1024]{1,0:T(8,128)(2,1)S(1)} %get-tuple-element.89.refs_0_, bf16[256,1024]{1,0:T(8,128)(2,1)S(1)} %get-tuple-element.55.refs_1_, bf16[256,1024]{1,0:T(8,128)(2,1)S(1)} %get-tuple-element.63.refs_2_, ...), custom_call_target="tpu_custom_call", output_to_operand_aliasing={{}: (10, {})} | custom-call | flops 1000000 | tf_op jit(solution)/shard_map/pallas_call | solution.py:246
  88.6 1.8 %shard_map.74.refs_2_ = f32[768,1024]{1,0:T(8,128)S(1)} custom-call(bf16[16,768,256]{2,1,0:T(8,128)(2,1)S(1)} %shard_map.66.k, bf16[768,512]{1,0:T(8,128)(2,1)S(1)} %get-tuple-element.83.refs_0_, bf16[768,512]{1,0:T(8,128)(2,1)S(1)} %get-tuple-element.84.refs_1_, f32[768,1024]{1,0:T(8,128)S(1)} %shard_map.73.refs_2_), custom_call_target="tpu_custom_call", output_to_operand_aliasing={{}: (3, {})} | custom-call | flops 1000000 | tf_op jit(solution)/shard_map/pallas_call | solution.py:246
  90.4 0.9 collective-permute-done.27.refs_0_
  91.3 1.2 %collective-permute-done.28.refs_1_ = bf16[768,512]{1,0:T(8,128)(2,1)S(1)} collective-permute-done((bf16[768,512]{1,0:T(8,128)(2,1)S(1)}, bf16[768,512]{1,0:T(8,128)(2,1)S(1)}, u32[]{:S(2)}, u32[]{:S(2)}) %collective-permute-start.28) | collective-permute-done | bytes 786464 | tf_op jit(solution)/shard_map/ppermute | solution.py:41
  92.5 1.8 %shard_map.76 = f32[768,1024]{1,0:T(8,128)S(1)} custom-call(bf16[16,768,256]{2,1,0:T(8,128)(2,1)S(1)} %shard_map.66.k, bf16[768,512]{1,0:T(8,128)(2,1)S(1)} %collective-permute-done.27.refs_0_, bf16[768,512]{1,0:T(8,128)(2,1)S(1)} %collective-permute-done.28.refs_1_, f32[768,1024]{1,0:T(8,128)S(1)} %shard_map.75.refs_2_), custom_call_target="tpu_custom_call", output_to_operand_aliasing={{}: (3, {})} | custom-call | flops 1000000 | tf_op jit(solution)/shard_map/pallas_call | solution.py:246
  94.3 3.5 %collective-permute-start.29 = (f32[768,1024]{1,0:T(8,128)S(1)}, f32[768,1024]{1,0:T(8,128)S(1)}, u32[]{:S(2)}, u32[]{:S(2)}) collective-permute-start(f32[768,1024]{1,0:T(8,128)S(1)} %shard_map.76), channel_id=1, source_target_pairs={{0,1},{1,0},{2,3},{3,2},{4,5},{5,4},{6,7},{7,6},{8,9},{9,8},{10,11... | collective-permute-start | bytes 9437192 | tf_op jit(solution)/shard_map/ppermute | solution.py:41
  97.7 2.0 %collective-permute-done.25.refs_0_ = bf16[768,512]{1,0:T(8,128)(2,1)S(1)} collective-permute-done((bf16[768,512]{1,0:T(8,128)(2,1)S(1)}, bf16[768,512]{1,0:T(8,128)(2,1)S(1)}, u32[]{:S(2)}, u32[]{:S(2)}) %collective-permute-start.25) | collective-permute-done | bytes 786464 | tf_op jit(solution)/shard_map/ppermute | solution.py:41
  99.7 1.2 %collective-permute-done.26.refs_1_ = bf16[768,512]{1,0:T(8,128)(2,1)S(1)} collective-permute-done((bf16[768,512]{1,0:T(8,128)(2,1)S(1)}, bf16[768,512]{1,0:T(8,128)(2,1)S(1)}, u32[]{:S(2)}, u32[]{:S(2)}) %collective-permute-start.26) | collective-permute-done | bytes 786464 | tf_op jit(solution)/shard_map/ppermute | solution.py:41
  100.9 2.1 %collective-permute-done.29.refs_3_ = f32[768,1024]{1,0:T(8,128)S(1)} collective-permute-done((f32[768,1024]{1,0:T(8,128)S(1)}, f32[768,1024]{1,0:T(8,128)S(1)}, u32[]{:S(2)}, u32[]{:S(2)}) %collective-permute-start.29) | collective-permute-done | bytes 3145760 | tf_op jit(solution)/shard_map/ppermute | solution.py:41
  103.0 2.4 %shard_map.77 = f32[768,1024]{1,0:T(8,128)} custom-call(bf16[16,768,256]{2,1,0:T(8,128)(2,1)S(1)} %shard_map.66.k, bf16[768,512]{1,0:T(8,128)(2,1)S(1)} %get-tuple-element.85.refs_0_, bf16[768,512]{1,0:T(8,128)(2,1)S(1)} %get-tuple-element.86.refs_1_, f32[768,1024]{1,0:T(8,128)S(1)} %shard_map.74.refs_2_, f32[768,1024]{1,0:T(8,128)S(1)} %collective-permute-done.29.refs_3_), custom_call_target="tpu_custom_call" | custom-call | flops 1000000 | tf_op jit(solution)/shard_map/pallas_call | solution.py:282
  (59 shorter events, 1.2 us)
Async XLA Ops:
  0.0 9.4 %copy-start = (s32[768]{0:T(1024)S(1)}, s32[768]{0:T(1024)}, u32[]{:S(2)}) copy-start(s32[768]{0:T(1024)} %param.6) | copy-start | bytes 9220
  0.0 15.5 %collective-permute-start.9 = (bf16[1024,2048]{1,0:T(8,128)(2,1)}, bf16[1024,2048]{1,0:T(8,128)(2,1)}, u32[]{:S(2)}, u32[]{:S(2)}) collective-permute-start(bf16[1024,2048]{1,0:T(8,128)(2,1)} %col_bits.1), channel_id=1, source_target_pairs={{0,1},{1,0},{2,3},{3,2},{4,5},{5,4},{6,7},{7,6},{8,9},{9,8},{10,11... | collective-permute-start | bytes 12582920 | tf_op jit(solution)/shard_map/ppermute | solution.py:41
  2.7 9.5 %collective-permute-start = (bf16[256,1024]{1,0:T(8,128)(2,1)S(1)}, bf16[256,1024]{1,0:T(8,128)(2,1)S(1)}, u32[]{:S(2)}, u32[]{:S(2)}) collective-permute-start(bf16[256,1024]{1,0:T(8,128)(2,1)S(1)} %get-tuple-element.90), channel_id=1, source_target_pairs={{0,1},{1,0},{2,3},{3,2},{4,5},{5,4},{6,7},{7,6},{8,9},{9,8},{10,11... | collective-permute-start | bytes 1572872 | tf_op jit(solution)/shard_map/ppermute | solution.py:41
  2.8 22.9 %collective-permute-start.3 = (bf16[256,1024]{1,0:T(8,128)(2,1)S(1)}, bf16[256,1024]{1,0:T(8,128)(2,1)S(1)}, u32[]{:S(2)}, u32[]{:S(2)}) collective-permute-start(bf16[256,1024]{1,0:T(8,128)(2,1)S(1)} %get-tuple-element.89.refs_0_), channel_id=1, source_target_pairs={{0,8},{1,25},{2,10},{3,27},{4,12},{5,29},{6,14},{7,31},{8,16},{9,1... | collective-permute-start | bytes 1572872 | tf_op jit(solution)/shard_map/ppermute | solution.py:41
  5.7 20.0 %collective-permute-start.4 = (bf16[256,1024]{1,0:T(8,128)(2,1)S(1)}, bf16[256,1024]{1,0:T(8,128)(2,1)S(1)}, u32[]{:S(2)}, u32[]{:S(2)}) collective-permute-start(bf16[256,1024]{1,0:T(8,128)(2,1)S(1)} %get-tuple-element.89.refs_0_), channel_id=1, source_target_pairs={{0,32},{1,97},{2,34},{3,99},{4,36},{5,101},{6,38},{7,103},{8,40},{... | collective-permute-start | bytes 1572872 | tf_op jit(solution)/shard_map/ppermute | solution.py:41
  9.6 2.5 %copy-start.1 = (s32[1024]{0:T(1024)S(1)}, s32[1024]{0:T(1024)}, u32[]{:S(2)}) copy-start(s32[1024]{0:T(1024)} %param.8) | copy-start | bytes 12292
  12.2 10.3 %collective-permute-start.1 = (bf16[256,1024]{1,0:T(8,128)(2,1)S(1)}, bf16[256,1024]{1,0:T(8,128)(2,1)S(1)}, u32[]{:S(2)}, u32[]{:S(2)}) collective-permute-start(bf16[256,1024]{1,0:T(8,128)(2,1)S(1)} %get-tuple-element.49.refs_0_), channel_id=1, source_target_pairs={{0,8},{1,25},{2,10},{3,27},{4,12},{5,29},{6,14},{7,31},{8,16},{9,1... | collective-permute-start | bytes 1572872 | tf_op jit(solution)/shard_map/ppermute | solution.py:41
  12.7 9.8 %collective-permute-start.2 = (bf16[256,1024]{1,0:T(8,128)(2,1)S(1)}, bf16[256,1024]{1,0:T(8,128)(2,1)S(1)}, u32[]{:S(2)}, u32[]{:S(2)}) collective-permute-start(bf16[256,1024]{1,0:T(8,128)(2,1)S(1)} %get-tuple-element.49.refs_0_), channel_id=1, source_target_pairs={{0,32},{1,97},{2,34},{3,99},{4,36},{5,101},{6,38},{7,103},{8,40},{... | collective-permute-start | bytes 1572872 | tf_op jit(solution)/shard_map/ppermute | solution.py:41
  20.0 19.9 %collective-permute-start.10 = (bf16[4,768,256]{2,1,0:T(8,128)(2,1)S(1)}, bf16[4,768,256]{2,1,0:T(8,128)(2,1)S(1)}, u32[]{:S(2)}, u32[]{:S(2)}) collective-permute-start(bf16[4,768,256]{2,1,0:T(8,128)(2,1)S(1)} %shard_map.60.refs_0_), channel_id=1, source_target_pairs={{0,2},{1,7},{2,4},{3,1},{4,6},{5,3},{6,0},{7,5},{8,10},{9,15},{10,... | collective-permute-start | bytes 4718600 | tf_op jit(solution)/shard_map/ppermute | solution.py:41
  22.5 11.0 %collective-permute-start.6 = (bf16[256,1024]{1,0:T(8,128)(2,1)S(1)}, bf16[256,1024]{1,0:T(8,128)(2,1)S(1)}, u32[]{:S(2)}, u32[]{:S(2)}) collective-permute-start(bf16[256,1024]{1,0:T(8,128)(2,1)S(1)} %get-tuple-element.53.refs_4_), channel_id=1, source_target_pairs={{0,32},{1,97},{2,34},{3,99},{4,36},{5,101},{6,38},{7,103},{8,40},{... | collective-permute-start | bytes 1572872 | tf_op jit(solution)/shard_map/ppermute | solution.py:41
  25.1 8.4 %collective-permute-start.5 = (bf16[256,1024]{1,0:T(8,128)(2,1)S(1)}, bf16[256,1024]{1,0:T(8,128)(2,1)S(1)}, u32[]{:S(2)}, u32[]{:S(2)}) collective-permute-start(bf16[256,1024]{1,0:T(8,128)(2,1)S(1)} %get-tuple-element.52.refs_1_), channel_id=1, source_target_pairs={{0,8},{1,25},{2,10},{3,27},{4,12},{5,29},{6,14},{7,31},{8,16},{9,1... | collective-permute-start | bytes 1572872 | tf_op jit(solution)/shard_map/ppermute | solution.py:41
  25.7 13.4 %collective-permute-start.8 = (bf16[256,1024]{1,0:T(8,128)(2,1)S(1)}, bf16[256,1024]{1,0:T(8,128)(2,1)S(1)}, u32[]{:S(2)}, u32[]{:S(2)}) collective-permute-start(bf16[256,1024]{1,0:T(8,128)(2,1)S(1)} %get-tuple-element.56.refs_4_), channel_id=1, source_target_pairs={{0,32},{1,97},{2,34},{3,99},{4,36},{5,101},{6,38},{7,103},{8,40},{... | collective-permute-start | bytes 1572872 | tf_op jit(solution)/shard_map/ppermute | solution.py:41
  25.8 13.3 %collective-permute-start.7 = (bf16[256,1024]{1,0:T(8,128)(2,1)S(1)}, bf16[256,1024]{1,0:T(8,128)(2,1)S(1)}, u32[]{:S(2)}, u32[]{:S(2)}) collective-permute-start(bf16[256,1024]{1,0:T(8,128)(2,1)S(1)} %get-tuple-element.55.refs_1_), channel_id=1, source_target_pairs={{0,8},{1,25},{2,10},{3,27},{4,12},{5,29},{6,14},{7,31},{8,16},{9,1... | collective-permute-start | bytes 1572872 | tf_op jit(solution)/shard_map/ppermute | solution.py:41
  33.5 11.2 %collective-permute-start.12 = (bf16[256,1024]{1,0:T(8,128)(2,1)S(1)}, bf16[256,1024]{1,0:T(8,128)(2,1)S(1)}, u32[]{:S(2)}, u32[]{:S(2)}) collective-permute-start(bf16[256,1024]{1,0:T(8,128)(2,1)S(1)} %get-tuple-element.61.refs_5_), channel_id=1, source_target_pairs={{0,32},{1,97},{2,34},{3,99},{4,36},{5,101},{6,38},{7,103},{8,40},{... | collective-permute-start | bytes 1572872 | tf_op jit(solution)/shard_map/ppermute | solution.py:41
  34.6 10.1 %collective-permute-start.11 = (bf16[256,1024]{1,0:T(8,128)(2,1)S(1)}, bf16[256,1024]{1,0:T(8,128)(2,1)S(1)}, u32[]{:S(2)}, u32[]{:S(2)}) collective-permute-start(bf16[256,1024]{1,0:T(8,128)(2,1)S(1)} %get-tuple-element.60.refs_2_), channel_id=1, source_target_pairs={{0,8},{1,25},{2,10},{3,27},{4,12},{5,29},{6,14},{7,31},{8,16},{9,1... | collective-permute-start | bytes 1572872 | tf_op jit(solution)/shard_map/ppermute | solution.py:41
  39.9 10.5 %collective-permute-start.13 = (bf16[256,1024]{1,0:T(8,128)(2,1)S(1)}, bf16[256,1024]{1,0:T(8,128)(2,1)S(1)}, u32[]{:S(2)}, u32[]{:S(2)}) collective-permute-start(bf16[256,1024]{1,0:T(8,128)(2,1)S(1)} %get-tuple-element.63.refs_2_), channel_id=1, source_target_pairs={{0,8},{1,25},{2,10},{3,27},{4,12},{5,29},{6,14},{7,31},{8,16},{9,1... | collective-permute-start | bytes 1572872 | tf_op jit(solution)/shard_map/ppermute | solution.py:41
  40.9 9.5 %collective-permute-start.14 = (bf16[256,1024]{1,0:T(8,128)(2,1)S(1)}, bf16[256,1024]{1,0:T(8,128)(2,1)S(1)}, u32[]{:S(2)}, u32[]{:S(2)}) collective-permute-start(bf16[256,1024]{1,0:T(8,128)(2,1)S(1)} %get-tuple-element.64.refs_5_), channel_id=1, source_target_pairs={{0,32},{1,97},{2,34},{3,99},{4,36},{5,101},{6,38},{7,103},{8,40},{... | collective-permute-start | bytes 1572872 | tf_op jit(solution)/shard_map/ppermute | solution.py:41
  40.9 20.3 %collective-permute-start.17 = (bf16[4,768,256]{2,1,0:T(8,128)(2,1)S(1)}, bf16[4,768,256]{2,1,0:T(8,128)(2,1)S(1)}, u32[]{:S(2)}, u32[]{:S(2)}) collective-permute-start(bf16[4,768,256]{2,1,0:T(8,128)(2,1)S(1)} %get-tuple-element.68.refs_1_), channel_id=1, source_target_pairs={{0,2},{1,7},{2,4},{3,1},{4,6},{5,3},{6,0},{7,5},{8,10},{9,15},{10,... | collective-permute-start | bytes 4718600 | tf_op jit(solution)/shard_map/ppermute | solution.py:41
  44.9 13.9 %collective-permute-start.16 = (bf16[768,512]{1,0:T(8,128)(2,1)S(1)}, bf16[768,512]{1,0:T(8,128)(2,1)S(1)}, u32[]{:S(2)}, u32[]{:S(2)}) collective-permute-start(bf16[768,512]{1,0:T(8,128)(2,1)S(1)} %pad_maximum_fusion.1), channel_id=1, source_target_pairs={{0,8},{1,25},{2,10},{3,27},{4,12},{5,29},{6,14},{7,31},{8,16},{9,1... | collective-permute-start | bytes 2359304 | tf_op jit(solution)/shard_map/ppermute | solution.py:41
  46.4 12.4 %collective-permute-start.15 = (bf16[768,512]{1,0:T(8,128)(2,1)S(1)}, bf16[768,512]{1,0:T(8,128)(2,1)S(1)}, u32[]{:S(2)}, u32[]{:S(2)}) collective-permute-start(bf16[768,512]{1,0:T(8,128)(2,1)S(1)} %pad_maximum_fusion), channel_id=1, source_target_pairs={{0,32},{1,97},{2,34},{3,99},{4,36},{5,101},{6,38},{7,103},{8,40},{... | collective-permute-start | bytes 2359304 | tf_op jit(solution)/shard_map/ppermute | solution.py:41
  50.4 16.8 %collective-permute-start.20 = (bf16[768,512]{1,0:T(8,128)(2,1)S(1)}, bf16[768,512]{1,0:T(8,128)(2,1)S(1)}, u32[]{:S(2)}, u32[]{:S(2)}) collective-permute-start(bf16[768,512]{1,0:T(8,128)(2,1)S(1)} %pad_maximum_fusion.3), channel_id=1, source_target_pairs={{0,8},{1,25},{2,10},{3,27},{4,12},{5,29},{6,14},{7,31},{8,16},{9,1... | collective-permute-start | bytes 2359304 | tf_op jit(solution)/shard_map/ppermute | solution.py:41
  52.3 14.9 %collective-permute-start.19 = (bf16[768,512]{1,0:T(8,128)(2,1)S(1)}, bf16[768,512]{1,0:T(8,128)(2,1)S(1)}, u32[]{:S(2)}, u32[]{:S(2)}) collective-permute-start(bf16[768,512]{1,0:T(8,128)(2,1)S(1)} %pad_maximum_fusion.2), channel_id=1, source_target_pairs={{0,32},{1,97},{2,34},{3,99},{4,36},{5,101},{6,38},{7,103},{8,40},{... | collective-permute-start | bytes 2359304 | tf_op jit(solution)/shard_map/ppermute | solution.py:41
  61.1 13.4 %collective-permute-start.21 = (bf16[768,512]{1,0:T(8,128)(2,1)S(1)}, bf16[768,512]{1,0:T(8,128)(2,1)S(1)}, u32[]{:S(2)}, u32[]{:S(2)}) collective-permute-start(bf16[768,512]{1,0:T(8,128)(2,1)S(1)} %get-tuple-element.74.refs_7_), channel_id=1, source_target_pairs={{0,32},{1,97},{2,34},{3,99},{4,36},{5,101},{6,38},{7,103},{8,40},{... | collective-permute-start | bytes 2359304 | tf_op jit(solution)/shard_map/ppermute | solution.py:41
  61.1 14.5 %collective-permute-start.22 = (bf16[768,512]{1,0:T(8,128)(2,1)S(1)}, bf16[768,512]{1,0:T(8,128)(2,1)S(1)}, u32[]{:S(2)}, u32[]{:S(2)}) collective-permute-start(bf16[768,512]{1,0:T(8,128)(2,1)S(1)} %get-tuple-element.75.refs_8_), channel_id=1, source_target_pairs={{0,8},{1,25},{2,10},{3,27},{4,12},{5,29},{6,14},{7,31},{8,16},{9,1... | collective-permute-start | bytes 2359304 | tf_op jit(solution)/shard_map/ppermute | solution.py:41
  61.3 24.4 %collective-permute-start.18 = (bf16[4,768,256]{2,1,0:T(8,128)(2,1)S(1)}, bf16[4,768,256]{2,1,0:T(8,128)(2,1)S(1)}, u32[]{:S(2)}, u32[]{:S(2)}) collective-permute-start(bf16[4,768,256]{2,1,0:T(8,128)(2,1)S(1)} %get-tuple-element.69.refs_2_), channel_id=1, source_target_pairs={{0,2},{1,7},{2,4},{3,1},{4,6},{5,3},{6,0},{7,5},{8,10},{9,15},{10,... | collective-permute-start | bytes 4718600 | tf_op jit(solution)/shard_map/ppermute | solution.py:41
  67.2 17.4 %collective-permute-start.23 = (bf16[768,512]{1,0:T(8,128)(2,1)S(1)}, bf16[768,512]{1,0:T(8,128)(2,1)S(1)}, u32[]{:S(2)}, u32[]{:S(2)}) collective-permute-start(bf16[768,512]{1,0:T(8,128)(2,1)S(1)} %get-tuple-element.77.refs_7_), channel_id=1, source_target_pairs={{0,32},{1,97},{2,34},{3,99},{4,36},{5,101},{6,38},{7,103},{8,40},{... | collective-permute-start | bytes 2359304 | tf_op jit(solution)/shard_map/ppermute | solution.py:41
  68.3 16.2 %collective-permute-start.24 = (bf16[768,512]{1,0:T(8,128)(2,1)S(1)}, bf16[768,512]{1,0:T(8,128)(2,1)S(1)}, u32[]{:S(2)}, u32[]{:S(2)}) collective-permute-start(bf16[768,512]{1,0:T(8,128)(2,1)S(1)} %get-tuple-element.78.refs_8_), channel_id=1, source_target_pairs={{0,8},{1,25},{2,10},{3,27},{4,12},{5,29},{6,14},{7,31},{8,16},{9,1... | collective-permute-start | bytes 2359304 | tf_op jit(solution)/shard_map/ppermute | solution.py:41
  75.6 15.7 %collective-permute-start.27 = (bf16[768,512]{1,0:T(8,128)(2,1)S(1)}, bf16[768,512]{1,0:T(8,128)(2,1)S(1)}, u32[]{:S(2)}, u32[]{:S(2)}) collective-permute-start(bf16[768,512]{1,0:T(8,128)(2,1)S(1)} %get-tuple-element.79.refs_9_), channel_id=1, source_target_pairs={{0,32},{1,97},{2,34},{3,99},{4,36},{5,101},{6,38},{7,103},{8,40},{... | collective-permute-start | bytes 2359304 | tf_op jit(solution)/shard_map/ppermute | solution.py:41
  76.8 15.7 %collective-permute-start.28 = (bf16[768,512]{1,0:T(8,128)(2,1)S(1)}, bf16[768,512]{1,0:T(8,128)(2,1)S(1)}, u32[]{:S(2)}, u32[]{:S(2)}) collective-permute-start(bf16[768,512]{1,0:T(8,128)(2,1)S(1)} %get-tuple-element.80.refs_10_), channel_id=1, source_target_pairs={{0,8},{1,25},{2,10},{3,27},{4,12},{5,29},{6,14},{7,31},{8,16},{9,1... | collective-permute-start | bytes 2359304 | tf_op jit(solution)/shard_map/ppermute | solution.py:41
  84.6 15.2 %collective-permute-start.25 = (bf16[768,512]{1,0:T(8,128)(2,1)S(1)}, bf16[768,512]{1,0:T(8,128)(2,1)S(1)}, u32[]{:S(2)}, u32[]{:S(2)}) collective-permute-start(bf16[768,512]{1,0:T(8,128)(2,1)S(1)} %get-tuple-element.83.refs_0_), channel_id=1, source_target_pairs={{0,32},{1,97},{2,34},{3,99},{4,36},{5,101},{6,38},{7,103},{8,40},{... | collective-permute-start | bytes 2359304 | tf_op jit(solution)/shard_map/ppermute | solution.py:41
  85.2 15.7 %collective-permute-start.26 = (bf16[768,512]{1,0:T(8,128)(2,1)S(1)}, bf16[768,512]{1,0:T(8,128)(2,1)S(1)}, u32[]{:S(2)}, u32[]{:S(2)}) collective-permute-start(bf16[768,512]{1,0:T(8,128)(2,1)S(1)} %get-tuple-element.84.refs_1_), channel_id=1, source_target_pairs={{0,8},{1,25},{2,10},{3,27},{4,12},{5,29},{6,14},{7,31},{8,16},{9,1... | collective-permute-start | bytes 2359304 | tf_op jit(solution)/shard_map/ppermute | solution.py:41
  94.3 8.7 %collective-permute-start.29 = (f32[768,1024]{1,0:T(8,128)S(1)}, f32[768,1024]{1,0:T(8,128)S(1)}, u32[]{:S(2)}, u32[]{:S(2)}) collective-permute-start(f32[768,1024]{1,0:T(8,128)S(1)} %shard_map.76), channel_id=1, source_target_pairs={{0,1},{1,0},{2,3},{3,2},{4,5},{5,4},{6,7},{7,6},{8,9},{9,8},{10,11... | collective-permute-start | bytes 9437192 | tf_op jit(solution)/shard_map/ppermute | solution.py:41

commit v4 on v3

--- a/solution.py
+++ b/solution.py
@@ -10,10 +10,10 @@
 AXES = ("lib", "lmk")
 NZ, NY, NX, NC = 4, 4, 4, 2
 TILE = 256
-TIES = [5, 7, 7, 7, 7, 7, 9, 9, 9, 9, 9]
+TIES = [5, 7, 7, 7, 7, 5, 5, 5, 9, 9, 9]
 TAIL = 5 * 10**10
 X1 = 3
-X2 = 6
+X2 = 7
 TV = 8 * 10**9
 
 

time: 106 us -> 105 us (level)
  starting transfers between devices: 37.8 us -> 32.4 us
  waiting for transfers between devices: 36.7 us -> 41.4 us
    ppermute x30, starting transfers between devices: 37.8 us -> 32.4 us  [send(): return lax.ppermute(block, AXES, PAIRS[axis])]
    ppermute x30, waiting for transfers between devices: 36.7 us -> 41.4 us  [send(): return lax.ppermute(block, AXES, PAIRS[axis])]
  transfers between devices with their start and end apart: 30 -> 30, of which waited for: 14 -> 13; matrix products, arithmetic and copies ran while one was open for 2% -> 2% of each run, Pallas kernels for 25% -> 25%
where the time goes in v4:
time: 105 us
  waiting for transfers between devices  41.4 us (39%)
  starting transfers between devices  32.4 us (31%)
  Pallas kernels  28.6 us (27%)
  local copies, waits for them, and re-layouts  1.65 us (2%)
    ppermute x30, waiting for transfers between devices, send(): return lax.ppermute(block, AXES, PAIRS[axis])  41.4 us
    ppermute x30, starting transfers between devices, send(): return lax.ppermute(block, AXES, PAIRS[axis])  32.4 us
    pallas_call x6, Pallas kernels, sums(): pl.pallas_call(functools.partial(sum_kernel, jobs, len(rs), len(accs)), o...  18.7 us
    pallas_call x1, Pallas kernels, tversky(): pl.pallas_call(tversky_kernel, out_shape=pltpu.VMEM((4, rows, 256), jnp.b...  4.5 us
    pallas_call x1, Pallas kernels, load(): pl.pallas_call(load_kernel, out_shape=(pltpu.VMEM((rows, depth), jnp.bflo...  2.52 us
    pallas_call x1, Pallas kernels, last(): pl.pallas_call(functools.partial(last_kernel, halves, len(rs)), out_shape...  2.42 us
  transfers between devices with their start and end apart: 30, of which 13 were waited for; matrix products, arithmetic and copies ran while one was open for 2% of the time, Pallas kernels for 25%

profile of v4, /device:TPU:1, one launch (start us, length us, event | category | flops | bytes accessed | tf_op | source)
XLA Modules:
  0.0 104.8 jit_solution(17641122726484738396)
XLA Ops:
  0.0 1.4 %collective-permute-start.9 = (bf16[1024,2048]{1,0:T(8,128)(2,1)}, bf16[1024,2048]{1,0:T(8,128)(2,1)}, u32[]{:S(2)}, u32[]{:S(2)}) collective-permute-start(bf16[1024,2048]{1,0:T(8,128)(2,1)} %col_bits.1), channel_id=1, source_target_pairs={{0,1},{1,0},{2,3},{3,2},{4,5},{5,4},{6,7},{7,6},{8,9},{9,8},{10,11... | collective-permute-start | bytes 12582920 | tf_op jit(solution)/shard_map/ppermute | solution.py:41
  1.4 1.3 %constant_dynamic-slice_fusion = (bf16[256,1024]{1,0:T(8,128)(2,1)S(1)}, bf16[256,1024]{1,0:T(8,128)(2,1)S(1)}) fusion(bf16[512,1024]{1,0:T(8,128)(2,1)} %param.9, s32[]{:T(128)S(6)} %select_n.15, s32[]{:T(128)S(6)} %select_n.14), kind=kLoop, calls=%fused_computation.6 | loop fusion | bytes 2097160 | tf_op jit(solution)/shard_map/dynamic_slice | solution.py:295
  2.7 0.1 collective-permute-start
  2.8 2.9 %collective-permute-start.3 = (bf16[256,1024]{1,0:T(8,128)(2,1)S(1)}, bf16[256,1024]{1,0:T(8,128)(2,1)S(1)}, u32[]{:S(2)}, u32[]{:S(2)}) collective-permute-start(bf16[256,1024]{1,0:T(8,128)(2,1)S(1)} %get-tuple-element.89.refs_0_), channel_id=1, source_target_pairs={{0,8},{1,25},{2,10},{3,27},{4,12},{5,29},{6,14},{7,31},{8,16},{9,1... | collective-permute-start | bytes 1572872 | tf_op jit(solution)/shard_map/ppermute | solution.py:41
  5.7 3.8 %collective-permute-start.4 = (bf16[256,1024]{1,0:T(8,128)(2,1)S(1)}, bf16[256,1024]{1,0:T(8,128)(2,1)S(1)}, u32[]{:S(2)}, u32[]{:S(2)}) collective-permute-start(bf16[256,1024]{1,0:T(8,128)(2,1)S(1)} %get-tuple-element.89.refs_0_), channel_id=1, source_target_pairs={{0,32},{1,97},{2,34},{3,99},{4,36},{5,101},{6,38},{7,103},{8,40},{... | collective-permute-start | bytes 1572872 | tf_op jit(solution)/shard_map/ppermute | solution.py:41
  9.4 0.2 mul.30.row_scale
  9.6 2.5 %shard_map.55 = (bf16[768,2048]{1,0:T(8,128)(2,1)S(1)}, bf16[512,2048]{1,0:T(8,128)(2,1)S(1)}, bf16[16,128]{1,0:T(8,128)(2,1)S(1)}) custom-call(bf16[768,2048]{1,0:T(8,128)(2,1)} %row_bits.1, bf16[1024,2048]{1,0:T(8,128)(2,1)} %col_bits.1), custom_call_target="tpu_custom_call" | custom-call | flops 1000000 | tf_op jit(solution)/shard_map/pallas_call | solution.py:99
  12.2 0.5 collective-permute-start.1
  12.7 2.8 %collective-permute-start.2 = (bf16[256,1024]{1,0:T(8,128)(2,1)S(1)}, bf16[256,1024]{1,0:T(8,128)(2,1)S(1)}, u32[]{:S(2)}, u32[]{:S(2)}) collective-permute-start(bf16[256,1024]{1,0:T(8,128)(2,1)S(1)} %get-tuple-element.49.refs_0_), channel_id=1, source_target_pairs={{0,32},{1,97},{2,34},{3,99},{4,36},{5,101},{6,38},{7,103},{8,40},{... | collective-permute-start | bytes 1572872 | tf_op jit(solution)/shard_map/ppermute | solution.py:41
  15.5 4.5 %shard_map.60.refs_0_ = bf16[4,768,256]{2,1,0:T(8,128)(2,1)S(1)} custom-call(bf16[768,2048]{1,0:T(8,128)(2,1)S(1)} %get-tuple-element.57.row_bits, f32[768,1]{1,0:T(8,128)S(1)} %mul.30.row_scale, bf16[512,2048]{1,0:T(8,128)(2,1)S(1)} %get-tuple-element.58.col_bits, f32[1,1024]{1,0:T(1,128)S(1)} %bitcast.1, bf16[1024,2048]{1,0:T(8,128)(2,1)} %collective-permute-done.9.got_bits), custom_call_target="tpu_custom_call" | custom-call | flops 8000000000 | tf_op jit(solution)/shard_map/pallas_call | solution.py:143
  20.1 2.6 %collective-permute-start.10 = (bf16[4,768,256]{2,1,0:T(8,128)(2,1)S(1)}, bf16[4,768,256]{2,1,0:T(8,128)(2,1)S(1)}, u32[]{:S(2)}, u32[]{:S(2)}) collective-permute-start(bf16[4,768,256]{2,1,0:T(8,128)(2,1)S(1)} %shard_map.60.refs_0_), channel_id=1, source_target_pairs={{0,2},{1,7},{2,4},{3,1},{4,6},{5,3},{6,0},{7,5},{8,10},{9,15},{10,... | collective-permute-start | bytes 4718600 | tf_op jit(solution)/shard_map/ppermute | solution.py:41
  22.6 2.5 %collective-permute-start.6 = (bf16[256,1024]{1,0:T(8,128)(2,1)S(1)}, bf16[256,1024]{1,0:T(8,128)(2,1)S(1)}, u32[]{:S(2)}, u32[]{:S(2)}) collective-permute-start(bf16[256,1024]{1,0:T(8,128)(2,1)S(1)} %get-tuple-element.53.refs_4_), channel_id=1, source_target_pairs={{0,32},{1,97},{2,34},{3,99},{4,36},{5,101},{6,38},{7,103},{8,40},{... | collective-permute-start | bytes 1572872 | tf_op jit(solution)/shard_map/ppermute | solution.py:41
  25.1 0.5 collective-permute-start.5
  25.8 7.6 %collective-permute-done.5.refs_1_ = bf16[256,1024]{1,0:T(8,128)(2,1)S(1)} collective-permute-done((bf16[256,1024]{1,0:T(8,128)(2,1)S(1)}, bf16[256,1024]{1,0:T(8,128)(2,1)S(1)}, u32[]{:S(2)}, u32[]{:S(2)}) %collective-permute-start.5) | collective-permute-done | bytes 524320 | tf_op jit(solution)/shard_map/ppermute | solution.py:41
  33.5 1.1 %collective-permute-start.12 = (bf16[256,1024]{1,0:T(8,128)(2,1)S(1)}, bf16[256,1024]{1,0:T(8,128)(2,1)S(1)}, u32[]{:S(2)}, u32[]{:S(2)}) collective-permute-start(bf16[256,1024]{1,0:T(8,128)(2,1)S(1)} %get-tuple-element.61.refs_5_), channel_id=1, source_target_pairs={{0,32},{1,97},{2,34},{3,99},{4,36},{5,101},{6,38},{7,103},{8,40},{... | collective-permute-start | bytes 1572872 | tf_op jit(solution)/shard_map/ppermute | solution.py:41
  34.6 0.6 collective-permute-start.11
  35.3 3.8 %collective-permute-done.7.refs_1_ = bf16[256,1024]{1,0:T(8,128)(2,1)S(1)} collective-permute-done((bf16[256,1024]{1,0:T(8,128)(2,1)S(1)}, bf16[256,1024]{1,0:T(8,128)(2,1)S(1)}, u32[]{:S(2)}, u32[]{:S(2)}) %collective-permute-start.7) | collective-permute-done | bytes 524320 | tf_op jit(solution)/shard_map/ppermute | solution.py:41
  39.1 0.9 collective-permute-done.10.refs_3_
  40.0 0.9 collective-permute-start.13
  40.9 3.9 %collective-permute-done.11.refs_1_ = bf16[256,1024]{1,0:T(8,128)(2,1)S(1)} collective-permute-done((bf16[256,1024]{1,0:T(8,128)(2,1)S(1)}, bf16[256,1024]{1,0:T(8,128)(2,1)S(1)}, u32[]{:S(2)}, u32[]{:S(2)}) %collective-permute-start.11) | collective-permute-done | bytes 524320 | tf_op jit(solution)/shard_map/ppermute | solution.py:41
  44.8 1.4 %collective-permute-start.16 = (bf16[768,512]{1,0:T(8,128)(2,1)S(1)}, bf16[768,512]{1,0:T(8,128)(2,1)S(1)}, u32[]{:S(2)}, u32[]{:S(2)}) collective-permute-start(bf16[768,512]{1,0:T(8,128)(2,1)S(1)} %pad_maximum_fusion.1), channel_id=1, source_target_pairs={{0,8},{1,25},{2,10},{3,27},{4,12},{5,29},{6,14},{7,31},{8,16},{9,1... | collective-permute-start | bytes 2359304 | tf_op jit(solution)/shard_map/ppermute | solution.py:41
  46.3 2.5 %collective-permute-start.19 = (bf16[4,768,256]{2,1,0:T(8,128)(2,1)S(1)}, bf16[4,768,256]{2,1,0:T(8,128)(2,1)S(1)}, u32[]{:S(2)}, u32[]{:S(2)}) collective-permute-start(bf16[4,768,256]{2,1,0:T(8,128)(2,1)S(1)} %get-tuple-element.71.refs_1_), channel_id=1, source_target_pairs={{0,2},{1,7},{2,4},{3,1},{4,6},{5,3},{6,0},{7,5},{8,10},{9,15},{10,... | collective-permute-start | bytes 4718600 | tf_op jit(solution)/shard_map/ppermute | solution.py:41
  49.1 1.3 %collective-permute-done.13.refs_1_ = bf16[256,1024]{1,0:T(8,128)(2,1)S(1)} collective-permute-done((bf16[256,1024]{1,0:T(8,128)(2,1)S(1)}, bf16[256,1024]{1,0:T(8,128)(2,1)S(1)}, u32[]{:S(2)}, u32[]{:S(2)}) %collective-permute-start.13) | collective-permute-done | bytes 524320 | tf_op jit(solution)/shard_map/ppermute | solution.py:41
  50.4 1.7 %collective-permute-start.18 = (bf16[768,512]{1,0:T(8,128)(2,1)S(1)}, bf16[768,512]{1,0:T(8,128)(2,1)S(1)}, u32[]{:S(2)}, u32[]{:S(2)}) collective-permute-start(bf16[768,512]{1,0:T(8,128)(2,1)S(1)} %pad_maximum_fusion.3), channel_id=1, source_target_pairs={{0,8},{1,25},{2,10},{3,27},{4,12},{5,29},{6,14},{7,31},{8,16},{9,1... | collective-permute-start | bytes 2359304 | tf_op jit(solution)/shard_map/ppermute | solution.py:41
  52.3 6.4 %collective-permute-done.16.refs_2_ = bf16[768,512]{1,0:T(8,128)(2,1)S(1)} collective-permute-done((bf16[768,512]{1,0:T(8,128)(2,1)S(1)}, bf16[768,512]{1,0:T(8,128)(2,1)S(1)}, u32[]{:S(2)}, u32[]{:S(2)}) %collective-permute-start.16) | collective-permute-done | bytes 786464 | tf_op jit(solution)/shard_map/ppermute | solution.py:41
  58.8 1.3 %collective-permute-done.15.refs_1_ = bf16[768,512]{1,0:T(8,128)(2,1)S(1)} collective-permute-done((bf16[768,512]{1,0:T(8,128)(2,1)S(1)}, bf16[768,512]{1,0:T(8,128)(2,1)S(1)}, u32[]{:S(2)}, u32[]{:S(2)}) %collective-permute-start.15) | collective-permute-done | bytes 786464 | tf_op jit(solution)/shard_map/ppermute | solution.py:41
  60.1 1.2 %collective-permute-start.21 = (bf16[768,512]{1,0:T(8,128)(2,1)S(1)}, bf16[768,512]{1,0:T(8,128)(2,1)S(1)}, u32[]{:S(2)}, u32[]{:S(2)}) collective-permute-start(bf16[768,512]{1,0:T(8,128)(2,1)S(1)} %get-tuple-element.74.refs_7_), channel_id=1, source_target_pairs={{0,32},{1,97},{2,34},{3,99},{4,36},{5,101},{6,38},{7,103},{8,40},{... | collective-permute-start | bytes 2359304 | tf_op jit(solution)/shard_map/ppermute | solution.py:41
  61.3 5.9 %collective-permute-done.18.refs_2_ = bf16[768,512]{1,0:T(8,128)(2,1)S(1)} collective-permute-done((bf16[768,512]{1,0:T(8,128)(2,1)S(1)}, bf16[768,512]{1,0:T(8,128)(2,1)S(1)}, u32[]{:S(2)}, u32[]{:S(2)}) %collective-permute-start.18) | collective-permute-done | bytes 786464 | tf_op jit(solution)/shard_map/ppermute | solution.py:41
  67.2 1.3 %collective-permute-done.17.refs_1_ = bf16[768,512]{1,0:T(8,128)(2,1)S(1)} collective-permute-done((bf16[768,512]{1,0:T(8,128)(2,1)S(1)}, bf16[768,512]{1,0:T(8,128)(2,1)S(1)}, u32[]{:S(2)}, u32[]{:S(2)}) %collective-permute-start.17) | collective-permute-done | bytes 786464 | tf_op jit(solution)/shard_map/ppermute | solution.py:41
  68.5 1.1 %collective-permute-start.20 = (bf16[4,768,256]{2,1,0:T(8,128)(2,1)S(1)}, bf16[4,768,256]{2,1,0:T(8,128)(2,1)S(1)}, u32[]{:S(2)}, u32[]{:S(2)}) collective-permute-start(bf16[4,768,256]{2,1,0:T(8,128)(2,1)S(1)} %get-tuple-element.72.refs_2_), channel_id=1, source_target_pairs={{0,2},{1,7},{2,4},{3,1},{4,6},{5,3},{6,0},{7,5},{8,10},{9,15},{10,... | collective-permute-start | bytes 4718600 | tf_op jit(solution)/shard_map/ppermute | solution.py:41
  69.6 0.9 collective-permute-start.23
  70.5 0.6 collective-permute-start.24
  71.1 0.3 shard_map.66.refs_1_.k
  71.5 5.2 %shard_map.68.refs_3_ = f32[768,1024]{1,0:T(8,128)S(1)} custom-call(bf16[16,768,256]{2,1,0:T(8,128)(2,1)S(1)} %shard_map.66.refs_1_.k, bf16[256,1024]{1,0:T(8,128)(2,1)S(1)} %get-tuple-element.49.refs_0_, bf16[256,1024]{1,0:T(8,128)(2,1)S(1)} %get-tuple-element.52.refs_1_, bf16[256,1024]{1,0:T(8,128)(2,1)S(1)} %get-tuple-element.60.refs_2_, ...), custom_call_target="tpu_custom_call" | custom-call | flops 1000000 | tf_op jit(solution)/shard_map/pallas_call | solution.py:246
  76.7 0.2 collective-permute-done.21.refs_1_
  77.0 1.2 %collective-permute-start.27 = (bf16[768,512]{1,0:T(8,128)(2,1)S(1)}, bf16[768,512]{1,0:T(8,128)(2,1)S(1)}, u32[]{:S(2)}, u32[]{:S(2)}) collective-permute-start(bf16[768,512]{1,0:T(8,128)(2,1)S(1)} %get-tuple-element.79.refs_9_), channel_id=1, source_target_pairs={{0,32},{1,97},{2,34},{3,99},{4,36},{5,101},{6,38},{7,103},{8,40},{... | collective-permute-start | bytes 2359304 | tf_op jit(solution)/shard_map/ppermute | solution.py:41
  78.2 7.2 %shard_map.70 = (f32[768,1024]{1,0:T(8,128)S(1)}, f32[768,1024]{1,0:T(8,128)S(1)}) custom-call(bf16[16,768,256]{2,1,0:T(8,128)(2,1)S(1)} %shard_map.66.refs_1_.k, bf16[256,1024]{1,0:T(8,128)(2,1)S(1)} %get-tuple-element.89.refs_0_, bf16[256,1024]{1,0:T(8,128)(2,1)S(1)} %get-tuple-element.55.refs_1_, ...), custom_call_target="tpu_custom_call", output_to_operand_aliasing={{1}: (12, {})} | custom-call | flops 1000000 | tf_op jit(solution)/shard_map/pallas_call | solution.py:246
  85.5 1.1 %collective-permute-start.25 = (bf16[768,512]{1,0:T(8,128)(2,1)S(1)}, bf16[768,512]{1,0:T(8,128)(2,1)S(1)}, u32[]{:S(2)}, u32[]{:S(2)}) collective-permute-start(bf16[768,512]{1,0:T(8,128)(2,1)S(1)} %get-tuple-element.83.refs_0_), channel_id=1, source_target_pairs={{0,32},{1,97},{2,34},{3,99},{4,36},{5,101},{6,38},{7,103},{8,40},{... | collective-permute-start | bytes 2359304 | tf_op jit(solution)/shard_map/ppermute | solution.py:41
  86.6 1.5 %collective-permute-done.20.refs_0_ = bf16[4,768,256]{2,1,0:T(8,128)(2,1)S(1)} collective-permute-done((bf16[4,768,256]{2,1,0:T(8,128)(2,1)S(1)}, bf16[4,768,256]{2,1,0:T(8,128)(2,1)S(1)}, u32[]{:S(2)}, u32[]{:S(2)}) %collective-permute-start.20) | collective-permute-done | bytes 1572896 | tf_op jit(solution)/shard_map/ppermute | solution.py:41
  88.1 0.1 shard_map.67.k
  88.2 1.5 %shard_map.75.refs_2_ = f32[768,1024]{1,0:T(8,128)S(1)} custom-call(bf16[16,768,256]{2,1,0:T(8,128)(2,1)S(1)} %shard_map.67.k, bf16[256,1024]{1,0:T(8,128)(2,1)S(1)} %get-tuple-element.49.refs_0_, bf16[256,1024]{1,0:T(8,128)(2,1)S(1)} %get-tuple-element.52.refs_1_, bf16[256,1024]{1,0:T(8,128)(2,1)S(1)} %get-tuple-element.60.refs_2_, ...), custom_call_target="tpu_custom_call", output_to_operand_aliasing={{}: (12, {})} | custom-call | flops 1000000 | tf_op jit(solution)/shard_map/pallas_call | solution.py:246
  89.7 4.1 %collective-permute-done.27.refs_0_ = bf16[768,512]{1,0:T(8,128)(2,1)S(1)} collective-permute-done((bf16[768,512]{1,0:T(8,128)(2,1)S(1)}, bf16[768,512]{1,0:T(8,128)(2,1)S(1)}, u32[]{:S(2)}, u32[]{:S(2)}) %collective-permute-start.27) | collective-permute-done | bytes 786464 | tf_op jit(solution)/shard_map/ppermute | solution.py:41
  93.8 1.8 %shard_map.76 = f32[768,1024]{1,0:T(8,128)S(1)} custom-call(bf16[16,768,256]{2,1,0:T(8,128)(2,1)S(1)} %shard_map.67.k, bf16[768,512]{1,0:T(8,128)(2,1)S(1)} %collective-permute-done.27.refs_0_, bf16[768,512]{1,0:T(8,128)(2,1)S(1)} %collective-permute-done.28.refs_1_, f32[768,1024]{1,0:T(8,128)S(1)} %shard_map.75.refs_2_), custom_call_target="tpu_custom_call", output_to_operand_aliasing={{}: (3, {})} | custom-call | flops 1000000 | tf_op jit(solution)/shard_map/pallas_call | solution.py:246
  95.6 0.4 collective-permute-start.29
  96.0 1.2 %shard_map.73.refs_2_ = f32[768,1024]{1,0:T(8,128)S(1)} custom-call(bf16[16,768,256]{2,1,0:T(8,128)(2,1)S(1)} %shard_map.67.k, bf16[256,1024]{1,0:T(8,128)(2,1)S(1)} %get-tuple-element.89.refs_0_, bf16[256,1024]{1,0:T(8,128)(2,1)S(1)} %get-tuple-element.55.refs_1_, bf16[256,1024]{1,0:T(8,128)(2,1)S(1)} %get-tuple-element.63.refs_2_, ...), custom_call_target="tpu_custom_call", output_to_operand_aliasing={{}: (10, {})} | custom-call | flops 1000000 | tf_op jit(solution)/shard_map/pallas_call | solution.py:246
  97.2 1.8 %shard_map.74.refs_2_ = f32[768,1024]{1,0:T(8,128)S(1)} custom-call(bf16[16,768,256]{2,1,0:T(8,128)(2,1)S(1)} %shard_map.67.k, bf16[768,512]{1,0:T(8,128)(2,1)S(1)} %get-tuple-element.83.refs_0_, bf16[768,512]{1,0:T(8,128)(2,1)S(1)} %get-tuple-element.84.refs_1_, f32[768,1024]{1,0:T(8,128)S(1)} %shard_map.73.refs_2_), custom_call_target="tpu_custom_call", output_to_operand_aliasing={{}: (3, {})} | custom-call | flops 1000000 | tf_op jit(solution)/shard_map/pallas_call | solution.py:246
  99.0 3.2 %collective-permute-done.25.refs_0_ = bf16[768,512]{1,0:T(8,128)(2,1)S(1)} collective-permute-done((bf16[768,512]{1,0:T(8,128)(2,1)S(1)}, bf16[768,512]{1,0:T(8,128)(2,1)S(1)}, u32[]{:S(2)}, u32[]{:S(2)}) %collective-permute-start.25) | collective-permute-done | bytes 786464 | tf_op jit(solution)/shard_map/ppermute | solution.py:41
  102.2 2.4 %shard_map.77 = f32[768,1024]{1,0:T(8,128)} custom-call(bf16[16,768,256]{2,1,0:T(8,128)(2,1)S(1)} %shard_map.67.k, bf16[768,512]{1,0:T(8,128)(2,1)S(1)} %get-tuple-element.85.refs_0_, bf16[768,512]{1,0:T(8,128)(2,1)S(1)} %get-tuple-element.86.refs_1_, f32[768,1024]{1,0:T(8,128)S(1)} %shard_map.74.refs_2_, f32[768,1024]{1,0:T(8,128)S(1)} %collective-permute-done.29.refs_3_), custom_call_target="tpu_custom_call" | custom-call | flops 1000000 | tf_op jit(solution)/shard_map/pallas_call | solution.py:282
  (59 shorter events, 0.9 us)
Async XLA Ops:
  0.0 9.4 %copy-start = (s32[768]{0:T(1024)S(1)}, s32[768]{0:T(1024)}, u32[]{:S(2)}) copy-start(s32[768]{0:T(1024)} %param.6) | copy-start | bytes 9220
  0.0 15.5 %collective-permute-start.9 = (bf16[1024,2048]{1,0:T(8,128)(2,1)}, bf16[1024,2048]{1,0:T(8,128)(2,1)}, u32[]{:S(2)}, u32[]{:S(2)}) collective-permute-start(bf16[1024,2048]{1,0:T(8,128)(2,1)} %col_bits.1), channel_id=1, source_target_pairs={{0,1},{1,0},{2,3},{3,2},{4,5},{5,4},{6,7},{7,6},{8,9},{9,8},{10,11... | collective-permute-start | bytes 12582920 | tf_op jit(solution)/shard_map/ppermute | solution.py:41
  2.7 9.5 %collective-permute-start = (bf16[256,1024]{1,0:T(8,128)(2,1)S(1)}, bf16[256,1024]{1,0:T(8,128)(2,1)S(1)}, u32[]{:S(2)}, u32[]{:S(2)}) collective-permute-start(bf16[256,1024]{1,0:T(8,128)(2,1)S(1)} %get-tuple-element.90), channel_id=1, source_target_pairs={{0,1},{1,0},{2,3},{3,2},{4,5},{5,4},{6,7},{7,6},{8,9},{9,8},{10,11... | collective-permute-start | bytes 1572872 | tf_op jit(solution)/shard_map/ppermute | solution.py:41
  2.8 22.9 %collective-permute-start.3 = (bf16[256,1024]{1,0:T(8,128)(2,1)S(1)}, bf16[256,1024]{1,0:T(8,128)(2,1)S(1)}, u32[]{:S(2)}, u32[]{:S(2)}) collective-permute-start(bf16[256,1024]{1,0:T(8,128)(2,1)S(1)} %get-tuple-element.89.refs_0_), channel_id=1, source_target_pairs={{0,8},{1,25},{2,10},{3,27},{4,12},{5,29},{6,14},{7,31},{8,16},{9,1... | collective-permute-start | bytes 1572872 | tf_op jit(solution)/shard_map/ppermute | solution.py:41
  5.7 20.0 %collective-permute-start.4 = (bf16[256,1024]{1,0:T(8,128)(2,1)S(1)}, bf16[256,1024]{1,0:T(8,128)(2,1)S(1)}, u32[]{:S(2)}, u32[]{:S(2)}) collective-permute-start(bf16[256,1024]{1,0:T(8,128)(2,1)S(1)} %get-tuple-element.89.refs_0_), channel_id=1, source_target_pairs={{0,32},{1,97},{2,34},{3,99},{4,36},{5,101},{6,38},{7,103},{8,40},{... | collective-permute-start | bytes 1572872 | tf_op jit(solution)/shard_map/ppermute | solution.py:41
  9.6 2.5 %copy-start.1 = (s32[1024]{0:T(1024)S(1)}, s32[1024]{0:T(1024)}, u32[]{:S(2)}) copy-start(s32[1024]{0:T(1024)} %param.8) | copy-start | bytes 12292
  12.2 10.4 %collective-permute-start.1 = (bf16[256,1024]{1,0:T(8,128)(2,1)S(1)}, bf16[256,1024]{1,0:T(8,128)(2,1)S(1)}, u32[]{:S(2)}, u32[]{:S(2)}) collective-permute-start(bf16[256,1024]{1,0:T(8,128)(2,1)S(1)} %get-tuple-element.49.refs_0_), channel_id=1, source_target_pairs={{0,8},{1,25},{2,10},{3,27},{4,12},{5,29},{6,14},{7,31},{8,16},{9,1... | collective-permute-start | bytes 1572872 | tf_op jit(solution)/shard_map/ppermute | solution.py:41
  12.7 9.9 %collective-permute-start.2 = (bf16[256,1024]{1,0:T(8,128)(2,1)S(1)}, bf16[256,1024]{1,0:T(8,128)(2,1)S(1)}, u32[]{:S(2)}, u32[]{:S(2)}) collective-permute-start(bf16[256,1024]{1,0:T(8,128)(2,1)S(1)} %get-tuple-element.49.refs_0_), channel_id=1, source_target_pairs={{0,32},{1,97},{2,34},{3,99},{4,36},{5,101},{6,38},{7,103},{8,40},{... | collective-permute-start | bytes 1572872 | tf_op jit(solution)/shard_map/ppermute | solution.py:41
  20.1 19.9 %collective-permute-start.10 = (bf16[4,768,256]{2,1,0:T(8,128)(2,1)S(1)}, bf16[4,768,256]{2,1,0:T(8,128)(2,1)S(1)}, u32[]{:S(2)}, u32[]{:S(2)}) collective-permute-start(bf16[4,768,256]{2,1,0:T(8,128)(2,1)S(1)} %shard_map.60.refs_0_), channel_id=1, source_target_pairs={{0,2},{1,7},{2,4},{3,1},{4,6},{5,3},{6,0},{7,5},{8,10},{9,15},{10,... | collective-permute-start | bytes 4718600 | tf_op jit(solution)/shard_map/ppermute | solution.py:41
  22.6 10.9 %collective-permute-start.6 = (bf16[256,1024]{1,0:T(8,128)(2,1)S(1)}, bf16[256,1024]{1,0:T(8,128)(2,1)S(1)}, u32[]{:S(2)}, u32[]{:S(2)}) collective-permute-start(bf16[256,1024]{1,0:T(8,128)(2,1)S(1)} %get-tuple-element.53.refs_4_), channel_id=1, source_target_pairs={{0,32},{1,97},{2,34},{3,99},{4,36},{5,101},{6,38},{7,103},{8,40},{... | collective-permute-start | bytes 1572872 | tf_op jit(solution)/shard_map/ppermute | solution.py:41
  25.1 8.4 %collective-permute-start.5 = (bf16[256,1024]{1,0:T(8,128)(2,1)S(1)}, bf16[256,1024]{1,0:T(8,128)(2,1)S(1)}, u32[]{:S(2)}, u32[]{:S(2)}) collective-permute-start(bf16[256,1024]{1,0:T(8,128)(2,1)S(1)} %get-tuple-element.52.refs_1_), channel_id=1, source_target_pairs={{0,8},{1,25},{2,10},{3,27},{4,12},{5,29},{6,14},{7,31},{8,16},{9,1... | collective-permute-start | bytes 1572872 | tf_op jit(solution)/shard_map/ppermute | solution.py:41
  25.7 13.4 %collective-permute-start.7 = (bf16[256,1024]{1,0:T(8,128)(2,1)S(1)}, bf16[256,1024]{1,0:T(8,128)(2,1)S(1)}, u32[]{:S(2)}, u32[]{:S(2)}) collective-permute-start(bf16[256,1024]{1,0:T(8,128)(2,1)S(1)} %get-tuple-element.55.refs_1_), channel_id=1, source_target_pairs={{0,8},{1,25},{2,10},{3,27},{4,12},{5,29},{6,14},{7,31},{8,16},{9,1... | collective-permute-start | bytes 1572872 | tf_op jit(solution)/shard_map/ppermute | solution.py:41
  25.8 13.3 %collective-permute-start.8 = (bf16[256,1024]{1,0:T(8,128)(2,1)S(1)}, bf16[256,1024]{1,0:T(8,128)(2,1)S(1)}, u32[]{:S(2)}, u32[]{:S(2)}) collective-permute-start(bf16[256,1024]{1,0:T(8,128)(2,1)S(1)} %get-tuple-element.56.refs_4_), channel_id=1, source_target_pairs={{0,32},{1,97},{2,34},{3,99},{4,36},{5,101},{6,38},{7,103},{8,40},{... | collective-permute-start | bytes 1572872 | tf_op jit(solution)/shard_map/ppermute | solution.py:41
  33.5 11.2 %collective-permute-start.12 = (bf16[256,1024]{1,0:T(8,128)(2,1)S(1)}, bf16[256,1024]{1,0:T(8,128)(2,1)S(1)}, u32[]{:S(2)}, u32[]{:S(2)}) collective-permute-start(bf16[256,1024]{1,0:T(8,128)(2,1)S(1)} %get-tuple-element.61.refs_5_), channel_id=1, source_target_pairs={{0,32},{1,97},{2,34},{3,99},{4,36},{5,101},{6,38},{7,103},{8,40},{... | collective-permute-start | bytes 1572872 | tf_op jit(solution)/shard_map/ppermute | solution.py:41
  34.6 10.1 %collective-permute-start.11 = (bf16[256,1024]{1,0:T(8,128)(2,1)S(1)}, bf16[256,1024]{1,0:T(8,128)(2,1)S(1)}, u32[]{:S(2)}, u32[]{:S(2)}) collective-permute-start(bf16[256,1024]{1,0:T(8,128)(2,1)S(1)} %get-tuple-element.60.refs_2_), channel_id=1, source_target_pairs={{0,8},{1,25},{2,10},{3,27},{4,12},{5,29},{6,14},{7,31},{8,16},{9,1... | collective-permute-start | bytes 1572872 | tf_op jit(solution)/shard_map/ppermute | solution.py:41
  40.0 10.4 %collective-permute-start.13 = (bf16[256,1024]{1,0:T(8,128)(2,1)S(1)}, bf16[256,1024]{1,0:T(8,128)(2,1)S(1)}, u32[]{:S(2)}, u32[]{:S(2)}) collective-permute-start(bf16[256,1024]{1,0:T(8,128)(2,1)S(1)} %get-tuple-element.63.refs_2_), channel_id=1, source_target_pairs={{0,8},{1,25},{2,10},{3,27},{4,12},{5,29},{6,14},{7,31},{8,16},{9,1... | collective-permute-start | bytes 1572872 | tf_op jit(solution)/shard_map/ppermute | solution.py:41
  40.9 9.5 %collective-permute-start.14 = (bf16[256,1024]{1,0:T(8,128)(2,1)S(1)}, bf16[256,1024]{1,0:T(8,128)(2,1)S(1)}, u32[]{:S(2)}, u32[]{:S(2)}) collective-permute-start(bf16[256,1024]{1,0:T(8,128)(2,1)S(1)} %get-tuple-element.64.refs_5_), channel_id=1, source_target_pairs={{0,32},{1,97},{2,34},{3,99},{4,36},{5,101},{6,38},{7,103},{8,40},{... | collective-permute-start | bytes 1572872 | tf_op jit(solution)/shard_map/ppermute | solution.py:41
  44.8 14.0 %collective-permute-start.16 = (bf16[768,512]{1,0:T(8,128)(2,1)S(1)}, bf16[768,512]{1,0:T(8,128)(2,1)S(1)}, u32[]{:S(2)}, u32[]{:S(2)}) collective-permute-start(bf16[768,512]{1,0:T(8,128)(2,1)S(1)} %pad_maximum_fusion.1), channel_id=1, source_target_pairs={{0,8},{1,25},{2,10},{3,27},{4,12},{5,29},{6,14},{7,31},{8,16},{9,1... | collective-permute-start | bytes 2359304 | tf_op jit(solution)/shard_map/ppermute | solution.py:41
  46.3 22.2 %collective-permute-start.19 = (bf16[4,768,256]{2,1,0:T(8,128)(2,1)S(1)}, bf16[4,768,256]{2,1,0:T(8,128)(2,1)S(1)}, u32[]{:S(2)}, u32[]{:S(2)}) collective-permute-start(bf16[4,768,256]{2,1,0:T(8,128)(2,1)S(1)} %get-tuple-element.71.refs_1_), channel_id=1, source_target_pairs={{0,2},{1,7},{2,4},{3,1},{4,6},{5,3},{6,0},{7,5},{8,10},{9,15},{10,... | collective-permute-start | bytes 4718600 | tf_op jit(solution)/shard_map/ppermute | solution.py:41
  48.9 11.2 %collective-permute-start.15 = (bf16[768,512]{1,0:T(8,128)(2,1)S(1)}, bf16[768,512]{1,0:T(8,128)(2,1)S(1)}, u32[]{:S(2)}, u32[]{:S(2)}) collective-permute-start(bf16[768,512]{1,0:T(8,128)(2,1)S(1)} %pad_maximum_fusion), channel_id=1, source_target_pairs={{0,32},{1,97},{2,34},{3,99},{4,36},{5,101},{6,38},{7,103},{8,40},{... | collective-permute-start | bytes 2359304 | tf_op jit(solution)/shard_map/ppermute | solution.py:41
  50.4 16.8 %collective-permute-start.18 = (bf16[768,512]{1,0:T(8,128)(2,1)S(1)}, bf16[768,512]{1,0:T(8,128)(2,1)S(1)}, u32[]{:S(2)}, u32[]{:S(2)}) collective-permute-start(bf16[768,512]{1,0:T(8,128)(2,1)S(1)} %pad_maximum_fusion.3), channel_id=1, source_target_pairs={{0,8},{1,25},{2,10},{3,27},{4,12},{5,29},{6,14},{7,31},{8,16},{9,1... | collective-permute-start | bytes 2359304 | tf_op jit(solution)/shard_map/ppermute | solution.py:41
  52.3 16.3 %collective-permute-start.17 = (bf16[768,512]{1,0:T(8,128)(2,1)S(1)}, bf16[768,512]{1,0:T(8,128)(2,1)S(1)}, u32[]{:S(2)}, u32[]{:S(2)}) collective-permute-start(bf16[768,512]{1,0:T(8,128)(2,1)S(1)} %pad_maximum_fusion.2), channel_id=1, source_target_pairs={{0,32},{1,97},{2,34},{3,99},{4,36},{5,101},{6,38},{7,103},{8,40},{... | collective-permute-start | bytes 2359304 | tf_op jit(solution)/shard_map/ppermute | solution.py:41
  60.1 16.9 %collective-permute-start.21 = (bf16[768,512]{1,0:T(8,128)(2,1)S(1)}, bf16[768,512]{1,0:T(8,128)(2,1)S(1)}, u32[]{:S(2)}, u32[]{:S(2)}) collective-permute-start(bf16[768,512]{1,0:T(8,128)(2,1)S(1)} %get-tuple-element.74.refs_7_), channel_id=1, source_target_pairs={{0,32},{1,97},{2,34},{3,99},{4,36},{5,101},{6,38},{7,103},{8,40},{... | collective-permute-start | bytes 2359304 | tf_op jit(solution)/shard_map/ppermute | solution.py:41
  61.3 15.6 %collective-permute-start.22 = (bf16[768,512]{1,0:T(8,128)(2,1)S(1)}, bf16[768,512]{1,0:T(8,128)(2,1)S(1)}, u32[]{:S(2)}, u32[]{:S(2)}) collective-permute-start(bf16[768,512]{1,0:T(8,128)(2,1)S(1)} %get-tuple-element.75.refs_8_), channel_id=1, source_target_pairs={{0,8},{1,25},{2,10},{3,27},{4,12},{5,29},{6,14},{7,31},{8,16},{9,1... | collective-permute-start | bytes 2359304 | tf_op jit(solution)/shard_map/ppermute | solution.py:41
  68.5 19.6 %collective-permute-start.20 = (bf16[4,768,256]{2,1,0:T(8,128)(2,1)S(1)}, bf16[4,768,256]{2,1,0:T(8,128)(2,1)S(1)}, u32[]{:S(2)}, u32[]{:S(2)}) collective-permute-start(bf16[4,768,256]{2,1,0:T(8,128)(2,1)S(1)} %get-tuple-element.72.refs_2_), channel_id=1, source_target_pairs={{0,2},{1,7},{2,4},{3,1},{4,6},{5,3},{6,0},{7,5},{8,10},{9,15},{10,... | collective-permute-start | bytes 4718600 | tf_op jit(solution)/shard_map/ppermute | solution.py:41
  69.6 15.8 %collective-permute-start.23 = (bf16[768,512]{1,0:T(8,128)(2,1)S(1)}, bf16[768,512]{1,0:T(8,128)(2,1)S(1)}, u32[]{:S(2)}, u32[]{:S(2)}) collective-permute-start(bf16[768,512]{1,0:T(8,128)(2,1)S(1)} %get-tuple-element.77.refs_7_), channel_id=1, source_target_pairs={{0,32},{1,97},{2,34},{3,99},{4,36},{5,101},{6,38},{7,103},{8,40},{... | collective-permute-start | bytes 2359304 | tf_op jit(solution)/shard_map/ppermute | solution.py:41
  70.5 14.9 %collective-permute-start.24 = (bf16[768,512]{1,0:T(8,128)(2,1)S(1)}, bf16[768,512]{1,0:T(8,128)(2,1)S(1)}, u32[]{:S(2)}, u32[]{:S(2)}) collective-permute-start(bf16[768,512]{1,0:T(8,128)(2,1)S(1)} %get-tuple-element.78.refs_8_), channel_id=1, source_target_pairs={{0,8},{1,25},{2,10},{3,27},{4,12},{5,29},{6,14},{7,31},{8,16},{9,1... | collective-permute-start | bytes 2359304 | tf_op jit(solution)/shard_map/ppermute | solution.py:41
  77.0 16.8 %collective-permute-start.27 = (bf16[768,512]{1,0:T(8,128)(2,1)S(1)}, bf16[768,512]{1,0:T(8,128)(2,1)S(1)}, u32[]{:S(2)}, u32[]{:S(2)}) collective-permute-start(bf16[768,512]{1,0:T(8,128)(2,1)S(1)} %get-tuple-element.79.refs_9_), channel_id=1, source_target_pairs={{0,32},{1,97},{2,34},{3,99},{4,36},{5,101},{6,38},{7,103},{8,40},{... | collective-permute-start | bytes 2359304 | tf_op jit(solution)/shard_map/ppermute | solution.py:41
  78.2 15.6 %collective-permute-start.28 = (bf16[768,512]{1,0:T(8,128)(2,1)S(1)}, bf16[768,512]{1,0:T(8,128)(2,1)S(1)}, u32[]{:S(2)}, u32[]{:S(2)}) collective-permute-start(bf16[768,512]{1,0:T(8,128)(2,1)S(1)} %get-tuple-element.80.refs_10_), channel_id=1, source_target_pairs={{0,8},{1,25},{2,10},{3,27},{4,12},{5,29},{6,14},{7,31},{8,16},{9,1... | collective-permute-start | bytes 2359304 | tf_op jit(solution)/shard_map/ppermute | solution.py:41
  85.5 16.7 %collective-permute-start.25 = (bf16[768,512]{1,0:T(8,128)(2,1)S(1)}, bf16[768,512]{1,0:T(8,128)(2,1)S(1)}, u32[]{:S(2)}, u32[]{:S(2)}) collective-permute-start(bf16[768,512]{1,0:T(8,128)(2,1)S(1)} %get-tuple-element.83.refs_0_), channel_id=1, source_target_pairs={{0,32},{1,97},{2,34},{3,99},{4,36},{5,101},{6,38},{7,103},{8,40},{... | collective-permute-start | bytes 2359304 | tf_op jit(solution)/shard_map/ppermute | solution.py:41
  86.6 15.6 %collective-permute-start.26 = (bf16[768,512]{1,0:T(8,128)(2,1)S(1)}, bf16[768,512]{1,0:T(8,128)(2,1)S(1)}, u32[]{:S(2)}, u32[]{:S(2)}) collective-permute-start(bf16[768,512]{1,0:T(8,128)(2,1)S(1)} %get-tuple-element.84.refs_1_), channel_id=1, source_target_pairs={{0,8},{1,25},{2,10},{3,27},{4,12},{5,29},{6,14},{7,31},{8,16},{9,1... | collective-permute-start | bytes 2359304 | tf_op jit(solution)/shard_map/ppermute | solution.py:41
  95.6 6.6 %collective-permute-start.29 = (f32[768,1024]{1,0:T(8,128)S(1)}, f32[768,1024]{1,0:T(8,128)S(1)}, u32[]{:S(2)}, u32[]{:S(2)}) collective-permute-start(f32[768,1024]{1,0:T(8,128)S(1)} %shard_map.76), channel_id=1, source_target_pairs={{0,1},{1,0},{2,3},{3,2},{4,5},{5,4},{6,7},{7,6},{8,9},{9,8},{10,11... | collective-permute-start | bytes 9437192 | tf_op jit(solution)/shard_map/ppermute | solution.py:41

commit v5 on v4

--- a/solution.py
+++ b/solution.py
@@ -10,11 +10,12 @@
 AXES = ("lib", "lmk")
 NZ, NY, NX, NC = 4, 4, 4, 2
 TILE = 256
-TIES = [5, 7, 7, 7, 7, 5, 5, 5, 9, 9, 9]
+TIES = [5, 5, 5, 5, 5, 5, 5, 5, 9, 9, 9]
 TAIL = 5 * 10**10
-X1 = 3
+X1 = 4
 X2 = 7
-TV = 8 * 10**9
+TV = 10**6
+LD = 10**6
 
 
 def pairs_of(move):
@@ -107,28 +108,47 @@
         out_specs=(VM,) * 3,
         scratch_shapes=[pltpu.SemaphoreType.DMA((3,))],
         compiler_params=params(1),
+        cost_estimate=cost(LD),
+    )(hbm(row_bits), hbm(col_bits))
+
+
+def pick_kernel(col_bits, out, sems):
+    core = position()[3]
+    copies = [
+        pltpu.make_async_copy(
+            col_bits.at[pl.ds(pl.multiple_of(h * 512 + (1 - core) * 256, 256), 256), :],
+            out.at[pl.ds(h * 256, 256), :],
+            sems.at[h],
+        )
+        for h in range(2)
+    ]
+    for cp in copies:
+        cp.start()
+    for cp in copies:
+        cp.wait()
+
+
+def pick(col_bits):
+    return pl.pallas_call(
+        pick_kernel,
+        out_shape=pltpu.VMEM((512, col_bits.shape[1]), col_bits.dtype),
+        in_specs=[ANY],
+        out_specs=VM,
+        scratch_shapes=[pltpu.SemaphoreType.DMA((2,))],
+        compiler_params=params(1),
         cost_estimate=cost(10**6),
-    )(hbm(row_bits), hbm(col_bits))
-
-
-def tversky_kernel(row_bits, row_scale, col_bits, col_scale, got_bits, out, gbuf, ones, sems):
+    )(hbm(col_bits))
+
+
+def tversky_kernel(row_bits, row_scale, col_bits, col_scale, got_bits, out, ones):
     core = position()[3]
     nt = (((1,), (1,)), ((), ()))
-    cols = [pl.multiple_of(h * 512 + core * 256, 256) for h in range(2)]
-    copies = [
-        pltpu.make_async_copy(got_bits.at[pl.ds(cols[h], 256), :], gbuf.at[pl.ds(h * 256, 256), :], sems.at[h])
-        for h in range(2)
-    ]
-    for cp in copies:
-        cp.start()
     ones[...] = jnp.ones(ones.shape, ones.dtype)
-    for part, bits_ref in enumerate((col_bits, gbuf)):
+    for part, bits_ref in enumerate((col_bits, got_bits)):
         for h in range(2):
-            if part == 1:
-                copies[h].wait()
             bits = bits_ref[h * 256 : (h + 1) * 256, :]
             if part == 0:
-                scale, to = col_scale[:, pl.ds(cols[h], 256)], 2 * core + h
+                scale, to = col_scale[:, pl.ds(pl.multiple_of(h * 512 + core * 256, 256), 256)], 2 * core + h
             else:
                 count = lax.dot_general(ones[...], bits, nt, preferred_element_type=jnp.float32)[:1, :]
                 scale, to = 0.1 * count, 2 * (1 - core) + h
@@ -143,13 +163,9 @@
     return pl.pallas_call(
         tversky_kernel,
         out_shape=pltpu.VMEM((4, rows, 256), jnp.bfloat16),
-        in_specs=[VM, VM, VM, VM, ANY],
+        in_specs=[VM] * 5,
         out_specs=VM,
-        scratch_shapes=[
-            pltpu.VMEM((512, depth), jnp.bfloat16),
-            pltpu.VMEM((TILE, depth), jnp.bfloat16),
-            pltpu.SemaphoreType.DMA((2,)),
-        ],
+        scratch_shapes=[pltpu.VMEM((TILE, depth), jnp.bfloat16)],
         compiler_params=params(8),
         cost_estimate=cost(TV),
     )(*map(vmem, (row_bits, row_scale, col_bits, col_scale, got_bits)))
@@ -297,14 +313,14 @@
     row_scale = 0.9 * library_count.astype(jnp.float32)[:, None]
     col_scale = 0.1 * landmark_count.astype(jnp.float32)[None, :]
     row_bits, col_bits, token = load(library_bits, landmark_bits)
-    theirs, token = tie(theirs, token, flops=10**6)
+    theirs, swapped = lax.optimization_barrier((theirs, pick(landmark_bits)))
     own = [theirs, mine]
     first = [[[], []] for _ in range(2)]
     second = [[[], []] for _ in range(2)]
     for s in range(2):
         first[s][0].append(send(own[s], "y"))
         first[s][1].append(send(own[s], "z"))
-    ks = [tversky(row_bits, row_scale, col_bits, col_scale, send(landmark_bits, "core"))]
+    ks = [tversky(row_bits, row_scale, col_bits, col_scale, send(swapped, "core"))]
 
     def second_terms(hop, p):
         return [[(p, 256 * m, 0, (hop, m + 1)) for m in range(3)], [(p + 1, 256 * m, 0, (m + 1, hop)) for m in range(3)]]

time: 105 us -> 102 us (0.971)
  waiting for transfers between devices: 41.4 us -> 27.2 us
  starting transfers between devices: 32.4 us -> 42.7 us
    ppermute x30, waiting for transfers between devices: 41.4 us -> 27.2 us  [send(): return lax.ppermute(block, AXES, PAIRS[axis])]
    ppermute x30, starting transfers between devices: 32.4 us -> 42.7 us  [send(): return lax.ppermute(block, AXES, PAIRS[axis])]
    pallas_call x0 -> x1, Pallas kernels: none -> 1.56 us  [pick(): pl.pallas_call(pick_kernel, out_shape=pltpu.VMEM((512, col_bits.shape[1])...]
  transfers between devices with their start and end apart: 30 -> 30, of which waited for: 13 -> 14; matrix products, arithmetic and copies ran while one was open for 2% -> 1% of each run, Pallas kernels for 25% -> 27%
where the time goes in v5:
time: 102 us
  starting transfers between devices  42.7 us (42%)
  Pallas kernels  29.6 us (29%)
  waiting for transfers between devices  27.2 us (27%)
  local copies, waits for them, and re-layouts  1.66 us (2%)
    ppermute x30, starting transfers between devices, send(): return lax.ppermute(block, AXES, PAIRS[axis])  42.7 us
    ppermute x30, waiting for transfers between devices, send(): return lax.ppermute(block, AXES, PAIRS[axis])  27.2 us
    pallas_call x6, Pallas kernels, sums(): pl.pallas_call(functools.partial(sum_kernel, jobs, len(rs), len(accs)), o...  18.7 us
    pallas_call x1, Pallas kernels, tversky(): pl.pallas_call(tversky_kernel, out_shape=pltpu.VMEM((4, rows, 256), jnp.b...  4.01 us
    pallas_call x1, Pallas kernels, load(): pl.pallas_call(load_kernel, out_shape=(pltpu.VMEM((rows, depth), jnp.bflo...  2.52 us
    pallas_call x1, Pallas kernels, last(): pl.pallas_call(functools.partial(last_kernel, halves, len(rs)), out_shape...  2.39 us
  transfers between devices with their start and end apart: 30, of which 14 were waited for; matrix products, arithmetic and copies ran while one was open for 1% of the time, Pallas kernels for 27%

profile of v5, /device:TPU:1, one launch (start us, length us, event | category | flops | bytes accessed | tf_op | source)
XLA Modules:
  0.0 102.0 jit_solution(10864534151451214205)
XLA Ops:
  0.0 1.3 %constant_dynamic-slice_fusion = (bf16[256,1024]{1,0:T(8,128)(2,1)S(1)}, bf16[256,1024]{1,0:T(8,128)(2,1)S(1)}) fusion(bf16[512,1024]{1,0:T(8,128)(2,1)} %param.9, s32[]{:T(128)S(6)} %select_n.15, s32[]{:T(128)S(6)} %select_n.14), kind=kLoop, calls=%fused_computation.6 | loop fusion | bytes 2097160 | tf_op jit(solution)/shard_map/dynamic_slice | solution.py:311
  1.3 1.5 %collective-permute-start = (bf16[256,1024]{1,0:T(8,128)(2,1)S(1)}, bf16[256,1024]{1,0:T(8,128)(2,1)S(1)}, u32[]{:S(2)}, u32[]{:S(2)}) collective-permute-start(bf16[256,1024]{1,0:T(8,128)(2,1)S(1)} %get-tuple-element.90), channel_id=1, source_target_pairs={{0,1},{1,0},{2,3},{3,2},{4,5},{5,4},{6,7},{7,6},{8,9},{9,8},{10,11... | collective-permute-start | bytes 1572872 | tf_op jit(solution)/shard_map/ppermute | solution.py:42
  2.8 1.6 %shard_map.56 = bf16[512,2048]{1,0:T(8,128)(2,1)S(1)} custom-call(bf16[1024,2048]{1,0:T(8,128)(2,1)} %col_bits.3), custom_call_target="tpu_custom_call" | custom-call | flops 1000000 | tf_op jit(solution)/shard_map/pallas_call | solution.py:132
  4.4 0.3 collective-permute-start.11
  4.7 2.8 %collective-permute-start.1 = (bf16[256,1024]{1,0:T(8,128)(2,1)S(1)}, bf16[256,1024]{1,0:T(8,128)(2,1)S(1)}, u32[]{:S(2)}, u32[]{:S(2)}) collective-permute-start(bf16[256,1024]{1,0:T(8,128)(2,1)S(1)} %collective-permute-done.refs_0_), channel_id=1, source_target_pairs={{0,8},{1,25},{2,10},{3,27},{4,12},{5,29},{6,14},{7,31},{8,16},{9,1... | collective-permute-start | bytes 1572872 | tf_op jit(solution)/shard_map/ppermute | solution.py:42
  7.5 3.8 %collective-permute-start.2 = (bf16[256,1024]{1,0:T(8,128)(2,1)S(1)}, bf16[256,1024]{1,0:T(8,128)(2,1)S(1)}, u32[]{:S(2)}, u32[]{:S(2)}) collective-permute-start(bf16[256,1024]{1,0:T(8,128)(2,1)S(1)} %collective-permute-done.refs_0_), channel_id=1, source_target_pairs={{0,32},{1,97},{2,34},{3,99},{4,36},{5,101},{6,38},{7,103},{8,40},{... | collective-permute-start | bytes 1572872 | tf_op jit(solution)/shard_map/ppermute | solution.py:42
  11.3 0.5 collective-permute-start.3
  12.0 2.5 %shard_map.55 = (bf16[768,2048]{1,0:T(8,128)(2,1)S(1)}, bf16[512,2048]{1,0:T(8,128)(2,1)S(1)}, bf16[16,128]{1,0:T(8,128)(2,1)S(1)}) custom-call(bf16[768,2048]{1,0:T(8,128)(2,1)} %row_bits.1, bf16[1024,2048]{1,0:T(8,128)(2,1)} %col_bits.3), custom_call_target="tpu_custom_call" | custom-call | flops 1000000 | tf_op jit(solution)/shard_map/pallas_call | solution.py:100
  14.6 4.0 %shard_map.61.refs_0_ = bf16[4,768,256]{2,1,0:T(8,128)(2,1)S(1)} custom-call(bf16[768,2048]{1,0:T(8,128)(2,1)S(1)} %get-tuple-element.59.row_bits, f32[768,1]{1,0:T(8,128)S(1)} %mul.30.row_scale, bf16[512,2048]{1,0:T(8,128)(2,1)S(1)} %get-tuple-element.60.col_bits, f32[1,1024]{1,0:T(1,128)S(1)} %bitcast.1, bf16[512,2048]{1,0:T(8,128)(2,1)S(1)} %collective-permute-done.11.got_bits), custom_call_target="tpu_custom_call" | custom-call | flops 1000000 | tf_op jit(solution)/shard_map/pallas_call | solution.py:163
  18.6 2.5 %collective-permute-start.12 = (bf16[4,768,256]{2,1,0:T(8,128)(2,1)S(1)}, bf16[4,768,256]{2,1,0:T(8,128)(2,1)S(1)}, u32[]{:S(2)}, u32[]{:S(2)}) collective-permute-start(bf16[4,768,256]{2,1,0:T(8,128)(2,1)S(1)} %shard_map.61.refs_0_), channel_id=1, source_target_pairs={{0,2},{1,7},{2,4},{3,1},{4,6},{5,3},{6,0},{7,5},{8,10},{9,15},{10,... | collective-permute-start | bytes 4718600 | tf_op jit(solution)/shard_map/ppermute | solution.py:42
  21.4 0.4 collective-permute-start.6
  21.8 1.3 %collective-permute-done.4.refs_2_ = bf16[256,1024]{1,0:T(8,128)(2,1)S(1)} collective-permute-done((bf16[256,1024]{1,0:T(8,128)(2,1)S(1)}, bf16[256,1024]{1,0:T(8,128)(2,1)S(1)}, u32[]{:S(2)}, u32[]{:S(2)}) %collective-permute-start.4) | collective-permute-done | bytes 524320 | tf_op jit(solution)/shard_map/ppermute | solution.py:42
  23.0 0.5 collective-permute-start.7
  23.5 3.4 %collective-permute-start.8 = (bf16[256,1024]{1,0:T(8,128)(2,1)S(1)}, bf16[256,1024]{1,0:T(8,128)(2,1)S(1)}, u32[]{:S(2)}, u32[]{:S(2)}) collective-permute-start(bf16[256,1024]{1,0:T(8,128)(2,1)S(1)} %get-tuple-element.55.refs_4_), channel_id=1, source_target_pairs={{0,32},{1,97},{2,34},{3,99},{4,36},{5,101},{6,38},{7,103},{8,40},{... | collective-permute-start | bytes 1572872 | tf_op jit(solution)/shard_map/ppermute | solution.py:42
  26.9 2.6 %collective-permute-done.5.refs_1_ = bf16[256,1024]{1,0:T(8,128)(2,1)S(1)} collective-permute-done((bf16[256,1024]{1,0:T(8,128)(2,1)S(1)}, bf16[256,1024]{1,0:T(8,128)(2,1)S(1)}, u32[]{:S(2)}, u32[]{:S(2)}) %collective-permute-start.5) | collective-permute-done | bytes 524320 | tf_op jit(solution)/shard_map/ppermute | solution.py:42
  29.7 2.4 %collective-permute-start.10 = (bf16[256,1024]{1,0:T(8,128)(2,1)S(1)}, bf16[256,1024]{1,0:T(8,128)(2,1)S(1)}, u32[]{:S(2)}, u32[]{:S(2)}) collective-permute-start(bf16[256,1024]{1,0:T(8,128)(2,1)S(1)} %get-tuple-element.58.refs_5_), channel_id=1, source_target_pairs={{0,32},{1,97},{2,34},{3,99},{4,36},{5,101},{6,38},{7,103},{8,40},{... | collective-permute-start | bytes 1572872 | tf_op jit(solution)/shard_map/ppermute | solution.py:42
  32.0 0.5 collective-permute-start.9
  32.6 2.5 %collective-permute-done.7.refs_1_ = bf16[256,1024]{1,0:T(8,128)(2,1)S(1)} collective-permute-done((bf16[256,1024]{1,0:T(8,128)(2,1)S(1)}, bf16[256,1024]{1,0:T(8,128)(2,1)S(1)}, u32[]{:S(2)}, u32[]{:S(2)}) %collective-permute-start.7) | collective-permute-done | bytes 524320 | tf_op jit(solution)/shard_map/ppermute | solution.py:42
  35.3 1.2 %collective-permute-start.13 = (bf16[256,1024]{1,0:T(8,128)(2,1)S(1)}, bf16[256,1024]{1,0:T(8,128)(2,1)S(1)}, u32[]{:S(2)}, u32[]{:S(2)}) collective-permute-start(bf16[256,1024]{1,0:T(8,128)(2,1)S(1)} %get-tuple-element.63.refs_2_), channel_id=1, source_target_pairs={{0,8},{1,25},{2,10},{3,27},{4,12},{5,29},{6,14},{7,31},{8,16},{9,1... | collective-permute-start | bytes 1572872 | tf_op jit(solution)/shard_map/ppermute | solution.py:42
  36.5 1.6 %collective-permute-start.14 = (bf16[256,1024]{1,0:T(8,128)(2,1)S(1)}, bf16[256,1024]{1,0:T(8,128)(2,1)S(1)}, u32[]{:S(2)}, u32[]{:S(2)}) collective-permute-start(bf16[256,1024]{1,0:T(8,128)(2,1)S(1)} %get-tuple-element.64.refs_5_), channel_id=1, source_target_pairs={{0,32},{1,97},{2,34},{3,99},{4,36},{5,101},{6,38},{7,103},{8,40},{... | collective-permute-start | bytes 1572872 | tf_op jit(solution)/shard_map/ppermute | solution.py:42
  38.1 2.8 %collective-permute-done.10.refs_2_ = bf16[256,1024]{1,0:T(8,128)(2,1)S(1)} collective-permute-done((bf16[256,1024]{1,0:T(8,128)(2,1)S(1)}, bf16[256,1024]{1,0:T(8,128)(2,1)S(1)}, u32[]{:S(2)}, u32[]{:S(2)}) %collective-permute-start.10) | collective-permute-done | bytes 524320 | tf_op jit(solution)/shard_map/ppermute | solution.py:42
  41.0 1.3 %collective-permute-start.16 = (bf16[768,512]{1,0:T(8,128)(2,1)S(1)}, bf16[768,512]{1,0:T(8,128)(2,1)S(1)}, u32[]{:S(2)}, u32[]{:S(2)}) collective-permute-start(bf16[768,512]{1,0:T(8,128)(2,1)S(1)} %pad_maximum_fusion.1), channel_id=1, source_target_pairs={{0,8},{1,25},{2,10},{3,27},{4,12},{5,29},{6,14},{7,31},{8,16},{9,1... | collective-permute-start | bytes 2359304 | tf_op jit(solution)/shard_map/ppermute | solution.py:42
  42.3 2.2 %collective-permute-start.19 = (bf16[4,768,256]{2,1,0:T(8,128)(2,1)S(1)}, bf16[4,768,256]{2,1,0:T(8,128)(2,1)S(1)}, u32[]{:S(2)}, u32[]{:S(2)}) collective-permute-start(bf16[4,768,256]{2,1,0:T(8,128)(2,1)S(1)} %get-tuple-element.71.refs_1_), channel_id=1, source_target_pairs={{0,2},{1,7},{2,4},{3,1},{4,6},{5,3},{6,0},{7,5},{8,10},{9,15},{10,... | collective-permute-start | bytes 4718600 | tf_op jit(solution)/shard_map/ppermute | solution.py:42
  44.5 1.8 %collective-permute-start.15 = (bf16[768,512]{1,0:T(8,128)(2,1)S(1)}, bf16[768,512]{1,0:T(8,128)(2,1)S(1)}, u32[]{:S(2)}, u32[]{:S(2)}) collective-permute-start(bf16[768,512]{1,0:T(8,128)(2,1)S(1)} %pad_maximum_fusion), channel_id=1, source_target_pairs={{0,32},{1,97},{2,34},{3,99},{4,36},{5,101},{6,38},{7,103},{8,40},{... | collective-permute-start | bytes 2359304 | tf_op jit(solution)/shard_map/ppermute | solution.py:42
  46.6 1.3 %collective-permute-start.18 = (bf16[768,512]{1,0:T(8,128)(2,1)S(1)}, bf16[768,512]{1,0:T(8,128)(2,1)S(1)}, u32[]{:S(2)}, u32[]{:S(2)}) collective-permute-start(bf16[768,512]{1,0:T(8,128)(2,1)S(1)} %pad_maximum_fusion.3), channel_id=1, source_target_pairs={{0,8},{1,25},{2,10},{3,27},{4,12},{5,29},{6,14},{7,31},{8,16},{9,1... | collective-permute-start | bytes 2359304 | tf_op jit(solution)/shard_map/ppermute | solution.py:42
  48.0 1.4 %collective-permute-start.17 = (bf16[768,512]{1,0:T(8,128)(2,1)S(1)}, bf16[768,512]{1,0:T(8,128)(2,1)S(1)}, u32[]{:S(2)}, u32[]{:S(2)}) collective-permute-start(bf16[768,512]{1,0:T(8,128)(2,1)S(1)} %pad_maximum_fusion.2), channel_id=1, source_target_pairs={{0,32},{1,97},{2,34},{3,99},{4,36},{5,101},{6,38},{7,103},{8,40},{... | collective-permute-start | bytes 2359304 | tf_op jit(solution)/shard_map/ppermute | solution.py:42
  49.4 5.4 %collective-permute-done.16.refs_2_ = bf16[768,512]{1,0:T(8,128)(2,1)S(1)} collective-permute-done((bf16[768,512]{1,0:T(8,128)(2,1)S(1)}, bf16[768,512]{1,0:T(8,128)(2,1)S(1)}, u32[]{:S(2)}, u32[]{:S(2)}) %collective-permute-start.16) | collective-permute-done | bytes 786464 | tf_op jit(solution)/shard_map/ppermute | solution.py:42
  54.8 0.9 collective-permute-done.15.refs_1_
  55.7 2.9 %collective-permute-start.21 = (bf16[768,512]{1,0:T(8,128)(2,1)S(1)}, bf16[768,512]{1,0:T(8,128)(2,1)S(1)}, u32[]{:S(2)}, u32[]{:S(2)}) collective-permute-start(bf16[768,512]{1,0:T(8,128)(2,1)S(1)} %get-tuple-element.74.refs_7_), channel_id=1, source_target_pairs={{0,32},{1,97},{2,34},{3,99},{4,36},{5,101},{6,38},{7,103},{8,40},{... | collective-permute-start | bytes 2359304 | tf_op jit(solution)/shard_map/ppermute | solution.py:42
  58.8 4.4 %collective-permute-done.18.refs_2_ = bf16[768,512]{1,0:T(8,128)(2,1)S(1)} collective-permute-done((bf16[768,512]{1,0:T(8,128)(2,1)S(1)}, bf16[768,512]{1,0:T(8,128)(2,1)S(1)}, u32[]{:S(2)}, u32[]{:S(2)}) %collective-permute-start.18) | collective-permute-done | bytes 786464 | tf_op jit(solution)/shard_map/ppermute | solution.py:42
  63.2 0.9 collective-permute-done.17.refs_1_
  64.2 1.2 %collective-permute-start.20 = (bf16[4,768,256]{2,1,0:T(8,128)(2,1)S(1)}, bf16[4,768,256]{2,1,0:T(8,128)(2,1)S(1)}, u32[]{:S(2)}, u32[]{:S(2)}) collective-permute-start(bf16[4,768,256]{2,1,0:T(8,128)(2,1)S(1)} %get-tuple-element.72.refs_2_), channel_id=1, source_target_pairs={{0,2},{1,7},{2,4},{3,1},{4,6},{5,3},{6,0},{7,5},{8,10},{9,15},{10,... | collective-permute-start | bytes 4718600 | tf_op jit(solution)/shard_map/ppermute | solution.py:42
  65.4 2.8 %collective-permute-start.23 = (bf16[768,512]{1,0:T(8,128)(2,1)S(1)}, bf16[768,512]{1,0:T(8,128)(2,1)S(1)}, u32[]{:S(2)}, u32[]{:S(2)}) collective-permute-start(bf16[768,512]{1,0:T(8,128)(2,1)S(1)} %get-tuple-element.77.refs_7_), channel_id=1, source_target_pairs={{0,32},{1,97},{2,34},{3,99},{4,36},{5,101},{6,38},{7,103},{8,40},{... | collective-permute-start | bytes 2359304 | tf_op jit(solution)/shard_map/ppermute | solution.py:42
  68.4 0.3 shard_map.66.refs_1_.k
  68.8 5.2 %shard_map.68.refs_3_ = f32[768,1024]{1,0:T(8,128)S(1)} custom-call(bf16[16,768,256]{2,1,0:T(8,128)(2,1)S(1)} %shard_map.66.refs_1_.k, bf16[256,1024]{1,0:T(8,128)(2,1)S(1)} %collective-permute-done.refs_0_, bf16[256,1024]{1,0:T(8,128)(2,1)S(1)} %get-tuple-element.51.refs_1_, bf16[256,1024]{1,0:T(8,128)(2,1)S(1)} %get-tuple-element.57.refs_2_, ...), custom_call_target="tpu_custom_call" | custom-call | flops 1000000 | tf_op jit(solution)/shard_map/pallas_call | solution.py:262
  74.0 1.5 %collective-permute-start.27 = (bf16[768,512]{1,0:T(8,128)(2,1)S(1)}, bf16[768,512]{1,0:T(8,128)(2,1)S(1)}, u32[]{:S(2)}, u32[]{:S(2)}) collective-permute-start(bf16[768,512]{1,0:T(8,128)(2,1)S(1)} %get-tuple-element.79.refs_9_), channel_id=1, source_target_pairs={{0,32},{1,97},{2,34},{3,99},{4,36},{5,101},{6,38},{7,103},{8,40},{... | collective-permute-start | bytes 2359304 | tf_op jit(solution)/shard_map/ppermute | solution.py:42
  75.7 7.2 %shard_map.70 = (f32[768,1024]{1,0:T(8,128)S(1)}, f32[768,1024]{1,0:T(8,128)S(1)}) custom-call(bf16[16,768,256]{2,1,0:T(8,128)(2,1)S(1)} %shard_map.66.refs_1_.k, bf16[256,1024]{1,0:T(8,128)(2,1)S(1)} %get-tuple-element.89.refs_0_, bf16[256,1024]{1,0:T(8,128)(2,1)S(1)} %get-tuple-element.54.refs_1_, ...), custom_call_target="tpu_custom_call", output_to_operand_aliasing={{1}: (12, {})} | custom-call | flops 1000000 | tf_op jit(solution)/shard_map/pallas_call | solution.py:262
  82.9 1.0 collective-permute-start.25
  83.9 0.4 collective-permute-start.26
  84.4 1.5 %shard_map.75.refs_2_ = f32[768,1024]{1,0:T(8,128)S(1)} custom-call(bf16[16,768,256]{2,1,0:T(8,128)(2,1)S(1)} %shard_map.67.k, bf16[256,1024]{1,0:T(8,128)(2,1)S(1)} %collective-permute-done.refs_0_, bf16[256,1024]{1,0:T(8,128)(2,1)S(1)} %get-tuple-element.51.refs_1_, ...), custom_call_target="tpu_custom_call", output_to_operand_aliasing={{}: (12, {})} | custom-call | flops 1000000 | tf_op jit(solution)/shard_map/pallas_call | solution.py:262
  85.9 3.5 %collective-permute-done.27.refs_0_ = bf16[768,512]{1,0:T(8,128)(2,1)S(1)} collective-permute-done((bf16[768,512]{1,0:T(8,128)(2,1)S(1)}, bf16[768,512]{1,0:T(8,128)(2,1)S(1)}, u32[]{:S(2)}, u32[]{:S(2)}) %collective-permute-start.27) | collective-permute-done | bytes 786464 | tf_op jit(solution)/shard_map/ppermute | solution.py:42
  89.4 1.8 %shard_map.76 = f32[768,1024]{1,0:T(8,128)S(1)} custom-call(bf16[16,768,256]{2,1,0:T(8,128)(2,1)S(1)} %shard_map.67.k, bf16[768,512]{1,0:T(8,128)(2,1)S(1)} %collective-permute-done.27.refs_0_, bf16[768,512]{1,0:T(8,128)(2,1)S(1)} %collective-permute-done.28.refs_1_, f32[768,1024]{1,0:T(8,128)S(1)} %shard_map.75.refs_2_), custom_call_target="tpu_custom_call", output_to_operand_aliasing={{}: (3, {})} | custom-call | flops 1000000 | tf_op jit(solution)/shard_map/pallas_call | solution.py:262
  91.2 2.9 %collective-permute-start.29 = (f32[768,1024]{1,0:T(8,128)S(1)}, f32[768,1024]{1,0:T(8,128)S(1)}, u32[]{:S(2)}, u32[]{:S(2)}) collective-permute-start(f32[768,1024]{1,0:T(8,128)S(1)} %shard_map.76), channel_id=1, source_target_pairs={{0,1},{1,0},{2,3},{3,2},{4,5},{5,4},{6,7},{7,6},{8,9},{9,8},{10,11... | collective-permute-start | bytes 9437192 | tf_op jit(solution)/shard_map/ppermute | solution.py:42
  94.1 1.2 %shard_map.73.refs_2_ = f32[768,1024]{1,0:T(8,128)S(1)} custom-call(bf16[16,768,256]{2,1,0:T(8,128)(2,1)S(1)} %shard_map.67.k, bf16[256,1024]{1,0:T(8,128)(2,1)S(1)} %get-tuple-element.89.refs_0_, bf16[256,1024]{1,0:T(8,128)(2,1)S(1)} %get-tuple-element.54.refs_1_, bf16[256,1024]{1,0:T(8,128)(2,1)S(1)} %get-tuple-element.63.refs_2_, ...), custom_call_target="tpu_custom_call", output_to_operand_aliasing={{}: (10, {})} | custom-call | flops 1000000 | tf_op jit(solution)/shard_map/pallas_call | solution.py:262
  95.3 1.8 %shard_map.74.refs_2_ = f32[768,1024]{1,0:T(8,128)S(1)} custom-call(bf16[16,768,256]{2,1,0:T(8,128)(2,1)S(1)} %shard_map.67.k, bf16[768,512]{1,0:T(8,128)(2,1)S(1)} %get-tuple-element.83.refs_0_, bf16[768,512]{1,0:T(8,128)(2,1)S(1)} %get-tuple-element.84.refs_1_, f32[768,1024]{1,0:T(8,128)S(1)} %shard_map.73.refs_2_), custom_call_target="tpu_custom_call", output_to_operand_aliasing={{}: (3, {})} | custom-call | flops 1000000 | tf_op jit(solution)/shard_map/pallas_call | solution.py:262
  97.1 0.7 collective-permute-done.25.refs_0_
  97.9 1.5 %collective-permute-done.29.refs_3_ = f32[768,1024]{1,0:T(8,128)S(1)} collective-permute-done((f32[768,1024]{1,0:T(8,128)S(1)}, f32[768,1024]{1,0:T(8,128)S(1)}, u32[]{:S(2)}, u32[]{:S(2)}) %collective-permute-start.29) | collective-permute-done | bytes 3145760 | tf_op jit(solution)/shard_map/ppermute | solution.py:42
  99.4 2.4 %shard_map.77 = f32[768,1024]{1,0:T(8,128)} custom-call(bf16[16,768,256]{2,1,0:T(8,128)(2,1)S(1)} %shard_map.67.k, bf16[768,512]{1,0:T(8,128)(2,1)S(1)} %get-tuple-element.85.refs_0_, bf16[768,512]{1,0:T(8,128)(2,1)S(1)} %get-tuple-element.86.refs_1_, f32[768,1024]{1,0:T(8,128)S(1)} %shard_map.74.refs_2_, f32[768,1024]{1,0:T(8,128)S(1)} %collective-permute-done.29.refs_3_), custom_call_target="tpu_custom_call" | custom-call | flops 1000000 | tf_op jit(solution)/shard_map/pallas_call | solution.py:298
  (59 shorter events, 2.0 us)
Async XLA Ops:
  1.3 10.6 %copy-start = (s32[768]{0:T(1024)S(1)}, s32[768]{0:T(1024)}, u32[]{:S(2)}) copy-start(s32[768]{0:T(1024)} %param.6) | copy-start | bytes 9220
  1.3 3.1 %collective-permute-start = (bf16[256,1024]{1,0:T(8,128)(2,1)S(1)}, bf16[256,1024]{1,0:T(8,128)(2,1)S(1)}, u32[]{:S(2)}, u32[]{:S(2)}) collective-permute-start(bf16[256,1024]{1,0:T(8,128)(2,1)S(1)} %get-tuple-element.90), channel_id=1, source_target_pairs={{0,1},{1,0},{2,3},{3,2},{4,5},{5,4},{6,7},{7,6},{8,9},{9,8},{10,11... | collective-permute-start | bytes 1572872 | tf_op jit(solution)/shard_map/ppermute | solution.py:42
  4.4 10.2 %collective-permute-start.11 = (bf16[512,2048]{1,0:T(8,128)(2,1)S(1)}, bf16[512,2048]{1,0:T(8,128)(2,1)S(1)}, u32[]{:S(2)}, u32[]{:S(2)}) collective-permute-start(bf16[512,2048]{1,0:T(8,128)(2,1)S(1)} %shard_map.56), channel_id=1, source_target_pairs={{0,1},{1,0},{2,3},{3,2},{4,5},{5,4},{6,7},{7,6},{8,9},{9,8},{10,11... | collective-permute-start | bytes 6291464 | tf_op jit(solution)/shard_map/ppermute | solution.py:42
  4.7 16.5 %collective-permute-start.1 = (bf16[256,1024]{1,0:T(8,128)(2,1)S(1)}, bf16[256,1024]{1,0:T(8,128)(2,1)S(1)}, u32[]{:S(2)}, u32[]{:S(2)}) collective-permute-start(bf16[256,1024]{1,0:T(8,128)(2,1)S(1)} %collective-permute-done.refs_0_), channel_id=1, source_target_pairs={{0,8},{1,25},{2,10},{3,27},{4,12},{5,29},{6,14},{7,31},{8,16},{9,1... | collective-permute-start | bytes 1572872 | tf_op jit(solution)/shard_map/ppermute | solution.py:42
  7.5 13.7 %collective-permute-start.2 = (bf16[256,1024]{1,0:T(8,128)(2,1)S(1)}, bf16[256,1024]{1,0:T(8,128)(2,1)S(1)}, u32[]{:S(2)}, u32[]{:S(2)}) collective-permute-start(bf16[256,1024]{1,0:T(8,128)(2,1)S(1)} %collective-permute-done.refs_0_), channel_id=1, source_target_pairs={{0,32},{1,97},{2,34},{3,99},{4,36},{5,101},{6,38},{7,103},{8,40},{... | collective-permute-start | bytes 1572872 | tf_op jit(solution)/shard_map/ppermute | solution.py:42
  11.3 10.5 %collective-permute-start.3 = (bf16[256,1024]{1,0:T(8,128)(2,1)S(1)}, bf16[256,1024]{1,0:T(8,128)(2,1)S(1)}, u32[]{:S(2)}, u32[]{:S(2)}) collective-permute-start(bf16[256,1024]{1,0:T(8,128)(2,1)S(1)} %get-tuple-element.89.refs_0_), channel_id=1, source_target_pairs={{0,8},{1,25},{2,10},{3,27},{4,12},{5,29},{6,14},{7,31},{8,16},{9,1... | collective-permute-start | bytes 1572872 | tf_op jit(solution)/shard_map/ppermute | solution.py:42
  11.7 11.3 %collective-permute-start.4 = (bf16[256,1024]{1,0:T(8,128)(2,1)S(1)}, bf16[256,1024]{1,0:T(8,128)(2,1)S(1)}, u32[]{:S(2)}, u32[]{:S(2)}) collective-permute-start(bf16[256,1024]{1,0:T(8,128)(2,1)S(1)} %get-tuple-element.89.refs_0_), channel_id=1, source_target_pairs={{0,32},{1,97},{2,34},{3,99},{4,36},{5,101},{6,38},{7,103},{8,40},{... | collective-permute-start | bytes 1572872 | tf_op jit(solution)/shard_map/ppermute | solution.py:42
  12.0 2.5 %copy-start.1 = (s32[1024]{0:T(1024)S(1)}, s32[1024]{0:T(1024)}, u32[]{:S(2)}) copy-start(s32[1024]{0:T(1024)} %param.8) | copy-start | bytes 12292
  18.6 22.3 %collective-permute-start.12 = (bf16[4,768,256]{2,1,0:T(8,128)(2,1)S(1)}, bf16[4,768,256]{2,1,0:T(8,128)(2,1)S(1)}, u32[]{:S(2)}, u32[]{:S(2)}) collective-permute-start(bf16[4,768,256]{2,1,0:T(8,128)(2,1)S(1)} %shard_map.61.refs_0_), channel_id=1, source_target_pairs={{0,2},{1,7},{2,4},{3,1},{4,6},{5,3},{6,0},{7,5},{8,10},{9,15},{10,... | collective-permute-start | bytes 4718600 | tf_op jit(solution)/shard_map/ppermute | solution.py:42
  21.2 8.3 %collective-permute-start.5 = (bf16[256,1024]{1,0:T(8,128)(2,1)S(1)}, bf16[256,1024]{1,0:T(8,128)(2,1)S(1)}, u32[]{:S(2)}, u32[]{:S(2)}) collective-permute-start(bf16[256,1024]{1,0:T(8,128)(2,1)S(1)} %get-tuple-element.51.refs_1_), channel_id=1, source_target_pairs={{0,8},{1,25},{2,10},{3,27},{4,12},{5,29},{6,14},{7,31},{8,16},{9,1... | collective-permute-start | bytes 1572872 | tf_op jit(solution)/shard_map/ppermute | solution.py:42
  21.4 8.3 %collective-permute-start.6 = (bf16[256,1024]{1,0:T(8,128)(2,1)S(1)}, bf16[256,1024]{1,0:T(8,128)(2,1)S(1)}, u32[]{:S(2)}, u32[]{:S(2)}) collective-permute-start(bf16[256,1024]{1,0:T(8,128)(2,1)S(1)} %get-tuple-element.52.refs_4_), channel_id=1, source_target_pairs={{0,32},{1,97},{2,34},{3,99},{4,36},{5,101},{6,38},{7,103},{8,40},{... | collective-permute-start | bytes 1572872 | tf_op jit(solution)/shard_map/ppermute | solution.py:42
  23.0 12.1 %collective-permute-start.7 = (bf16[256,1024]{1,0:T(8,128)(2,1)S(1)}, bf16[256,1024]{1,0:T(8,128)(2,1)S(1)}, u32[]{:S(2)}, u32[]{:S(2)}) collective-permute-start(bf16[256,1024]{1,0:T(8,128)(2,1)S(1)} %get-tuple-element.54.refs_1_), channel_id=1, source_target_pairs={{0,8},{1,25},{2,10},{3,27},{4,12},{5,29},{6,14},{7,31},{8,16},{9,1... | collective-permute-start | bytes 1572872 | tf_op jit(solution)/shard_map/ppermute | solution.py:42
  23.5 11.8 %collective-permute-start.8 = (bf16[256,1024]{1,0:T(8,128)(2,1)S(1)}, bf16[256,1024]{1,0:T(8,128)(2,1)S(1)}, u32[]{:S(2)}, u32[]{:S(2)}) collective-permute-start(bf16[256,1024]{1,0:T(8,128)(2,1)S(1)} %get-tuple-element.55.refs_4_), channel_id=1, source_target_pairs={{0,32},{1,97},{2,34},{3,99},{4,36},{5,101},{6,38},{7,103},{8,40},{... | collective-permute-start | bytes 1572872 | tf_op jit(solution)/shard_map/ppermute | solution.py:42
  29.7 11.2 %collective-permute-start.10 = (bf16[256,1024]{1,0:T(8,128)(2,1)S(1)}, bf16[256,1024]{1,0:T(8,128)(2,1)S(1)}, u32[]{:S(2)}, u32[]{:S(2)}) collective-permute-start(bf16[256,1024]{1,0:T(8,128)(2,1)S(1)} %get-tuple-element.58.refs_5_), channel_id=1, source_target_pairs={{0,32},{1,97},{2,34},{3,99},{4,36},{5,101},{6,38},{7,103},{8,40},{... | collective-permute-start | bytes 1572872 | tf_op jit(solution)/shard_map/ppermute | solution.py:42
  32.0 8.9 %collective-permute-start.9 = (bf16[256,1024]{1,0:T(8,128)(2,1)S(1)}, bf16[256,1024]{1,0:T(8,128)(2,1)S(1)}, u32[]{:S(2)}, u32[]{:S(2)}) collective-permute-start(bf16[256,1024]{1,0:T(8,128)(2,1)S(1)} %get-tuple-element.57.refs_2_), channel_id=1, source_target_pairs={{0,8},{1,25},{2,10},{3,27},{4,12},{5,29},{6,14},{7,31},{8,16},{9,1... | collective-permute-start | bytes 1572872 | tf_op jit(solution)/shard_map/ppermute | solution.py:42
  35.3 11.1 %collective-permute-start.13 = (bf16[256,1024]{1,0:T(8,128)(2,1)S(1)}, bf16[256,1024]{1,0:T(8,128)(2,1)S(1)}, u32[]{:S(2)}, u32[]{:S(2)}) collective-permute-start(bf16[256,1024]{1,0:T(8,128)(2,1)S(1)} %get-tuple-element.63.refs_2_), channel_id=1, source_target_pairs={{0,8},{1,25},{2,10},{3,27},{4,12},{5,29},{6,14},{7,31},{8,16},{9,1... | collective-permute-start | bytes 1572872 | tf_op jit(solution)/shard_map/ppermute | solution.py:42
  36.5 10.0 %collective-permute-start.14 = (bf16[256,1024]{1,0:T(8,128)(2,1)S(1)}, bf16[256,1024]{1,0:T(8,128)(2,1)S(1)}, u32[]{:S(2)}, u32[]{:S(2)}) collective-permute-start(bf16[256,1024]{1,0:T(8,128)(2,1)S(1)} %get-tuple-element.64.refs_5_), channel_id=1, source_target_pairs={{0,32},{1,97},{2,34},{3,99},{4,36},{5,101},{6,38},{7,103},{8,40},{... | collective-permute-start | bytes 1572872 | tf_op jit(solution)/shard_map/ppermute | solution.py:42
  41.0 13.8 %collective-permute-start.16 = (bf16[768,512]{1,0:T(8,128)(2,1)S(1)}, bf16[768,512]{1,0:T(8,128)(2,1)S(1)}, u32[]{:S(2)}, u32[]{:S(2)}) collective-permute-start(bf16[768,512]{1,0:T(8,128)(2,1)S(1)} %pad_maximum_fusion.1), channel_id=1, source_target_pairs={{0,8},{1,25},{2,10},{3,27},{4,12},{5,29},{6,14},{7,31},{8,16},{9,1... | collective-permute-start | bytes 2359304 | tf_op jit(solution)/shard_map/ppermute | solution.py:42
  42.3 21.9 %collective-permute-start.19 = (bf16[4,768,256]{2,1,0:T(8,128)(2,1)S(1)}, bf16[4,768,256]{2,1,0:T(8,128)(2,1)S(1)}, u32[]{:S(2)}, u32[]{:S(2)}) collective-permute-start(bf16[4,768,256]{2,1,0:T(8,128)(2,1)S(1)} %get-tuple-element.71.refs_1_), channel_id=1, source_target_pairs={{0,2},{1,7},{2,4},{3,1},{4,6},{5,3},{6,0},{7,5},{8,10},{9,15},{10,... | collective-permute-start | bytes 4718600 | tf_op jit(solution)/shard_map/ppermute | solution.py:42
  44.5 11.2 %collective-permute-start.15 = (bf16[768,512]{1,0:T(8,128)(2,1)S(1)}, bf16[768,512]{1,0:T(8,128)(2,1)S(1)}, u32[]{:S(2)}, u32[]{:S(2)}) collective-permute-start(bf16[768,512]{1,0:T(8,128)(2,1)S(1)} %pad_maximum_fusion), channel_id=1, source_target_pairs={{0,32},{1,97},{2,34},{3,99},{4,36},{5,101},{6,38},{7,103},{8,40},{... | collective-permute-start | bytes 2359304 | tf_op jit(solution)/shard_map/ppermute | solution.py:42
  46.6 16.6 %collective-permute-start.18 = (bf16[768,512]{1,0:T(8,128)(2,1)S(1)}, bf16[768,512]{1,0:T(8,128)(2,1)S(1)}, u32[]{:S(2)}, u32[]{:S(2)}) collective-permute-start(bf16[768,512]{1,0:T(8,128)(2,1)S(1)} %pad_maximum_fusion.3), channel_id=1, source_target_pairs={{0,8},{1,25},{2,10},{3,27},{4,12},{5,29},{6,14},{7,31},{8,16},{9,1... | collective-permute-start | bytes 2359304 | tf_op jit(solution)/shard_map/ppermute | solution.py:42
  48.0 16.2 %collective-permute-start.17 = (bf16[768,512]{1,0:T(8,128)(2,1)S(1)}, bf16[768,512]{1,0:T(8,128)(2,1)S(1)}, u32[]{:S(2)}, u32[]{:S(2)}) collective-permute-start(bf16[768,512]{1,0:T(8,128)(2,1)S(1)} %pad_maximum_fusion.2), channel_id=1, source_target_pairs={{0,32},{1,97},{2,34},{3,99},{4,36},{5,101},{6,38},{7,103},{8,40},{... | collective-permute-start | bytes 2359304 | tf_op jit(solution)/shard_map/ppermute | solution.py:42
  55.7 18.3 %collective-permute-start.21 = (bf16[768,512]{1,0:T(8,128)(2,1)S(1)}, bf16[768,512]{1,0:T(8,128)(2,1)S(1)}, u32[]{:S(2)}, u32[]{:S(2)}) collective-permute-start(bf16[768,512]{1,0:T(8,128)(2,1)S(1)} %get-tuple-element.74.refs_7_), channel_id=1, source_target_pairs={{0,32},{1,97},{2,34},{3,99},{4,36},{5,101},{6,38},{7,103},{8,40},{... | collective-permute-start | bytes 2359304 | tf_op jit(solution)/shard_map/ppermute | solution.py:42
  58.6 15.4 %collective-permute-start.22 = (bf16[768,512]{1,0:T(8,128)(2,1)S(1)}, bf16[768,512]{1,0:T(8,128)(2,1)S(1)}, u32[]{:S(2)}, u32[]{:S(2)}) collective-permute-start(bf16[768,512]{1,0:T(8,128)(2,1)S(1)} %get-tuple-element.75.refs_8_), channel_id=1, source_target_pairs={{0,8},{1,25},{2,10},{3,27},{4,12},{5,29},{6,14},{7,31},{8,16},{9,1... | collective-permute-start | bytes 2359304 | tf_op jit(solution)/shard_map/ppermute | solution.py:42
  64.2 20.1 %collective-permute-start.20 = (bf16[4,768,256]{2,1,0:T(8,128)(2,1)S(1)}, bf16[4,768,256]{2,1,0:T(8,128)(2,1)S(1)}, u32[]{:S(2)}, u32[]{:S(2)}) collective-permute-start(bf16[4,768,256]{2,1,0:T(8,128)(2,1)S(1)} %get-tuple-element.72.refs_2_), channel_id=1, source_target_pairs={{0,2},{1,7},{2,4},{3,1},{4,6},{5,3},{6,0},{7,5},{8,10},{9,15},{10,... | collective-permute-start | bytes 4718600 | tf_op jit(solution)/shard_map/ppermute | solution.py:42
  65.4 17.5 %collective-permute-start.23 = (bf16[768,512]{1,0:T(8,128)(2,1)S(1)}, bf16[768,512]{1,0:T(8,128)(2,1)S(1)}, u32[]{:S(2)}, u32[]{:S(2)}) collective-permute-start(bf16[768,512]{1,0:T(8,128)(2,1)S(1)} %get-tuple-element.77.refs_7_), channel_id=1, source_target_pairs={{0,32},{1,97},{2,34},{3,99},{4,36},{5,101},{6,38},{7,103},{8,40},{... | collective-permute-start | bytes 2359304 | tf_op jit(solution)/shard_map/ppermute | solution.py:42
  68.2 14.7 %collective-permute-start.24 = (bf16[768,512]{1,0:T(8,128)(2,1)S(1)}, bf16[768,512]{1,0:T(8,128)(2,1)S(1)}, u32[]{:S(2)}, u32[]{:S(2)}) collective-permute-start(bf16[768,512]{1,0:T(8,128)(2,1)S(1)} %get-tuple-element.78.refs_8_), channel_id=1, source_target_pairs={{0,8},{1,25},{2,10},{3,27},{4,12},{5,29},{6,14},{7,31},{8,16},{9,1... | collective-permute-start | bytes 2359304 | tf_op jit(solution)/shard_map/ppermute | solution.py:42
  74.0 15.4 %collective-permute-start.27 = (bf16[768,512]{1,0:T(8,128)(2,1)S(1)}, bf16[768,512]{1,0:T(8,128)(2,1)S(1)}, u32[]{:S(2)}, u32[]{:S(2)}) collective-permute-start(bf16[768,512]{1,0:T(8,128)(2,1)S(1)} %get-tuple-element.79.refs_9_), channel_id=1, source_target_pairs={{0,32},{1,97},{2,34},{3,99},{4,36},{5,101},{6,38},{7,103},{8,40},{... | collective-permute-start | bytes 2359304 | tf_op jit(solution)/shard_map/ppermute | solution.py:42
  75.5 13.9 %collective-permute-start.28 = (bf16[768,512]{1,0:T(8,128)(2,1)S(1)}, bf16[768,512]{1,0:T(8,128)(2,1)S(1)}, u32[]{:S(2)}, u32[]{:S(2)}) collective-permute-start(bf16[768,512]{1,0:T(8,128)(2,1)S(1)} %get-tuple-element.80.refs_10_), channel_id=1, source_target_pairs={{0,8},{1,25},{2,10},{3,27},{4,12},{5,29},{6,14},{7,31},{8,16},{9,1... | collective-permute-start | bytes 2359304 | tf_op jit(solution)/shard_map/ppermute | solution.py:42
  82.9 14.9 %collective-permute-start.25 = (bf16[768,512]{1,0:T(8,128)(2,1)S(1)}, bf16[768,512]{1,0:T(8,128)(2,1)S(1)}, u32[]{:S(2)}, u32[]{:S(2)}) collective-permute-start(bf16[768,512]{1,0:T(8,128)(2,1)S(1)} %get-tuple-element.83.refs_0_), channel_id=1, source_target_pairs={{0,32},{1,97},{2,34},{3,99},{4,36},{5,101},{6,38},{7,103},{8,40},{... | collective-permute-start | bytes 2359304 | tf_op jit(solution)/shard_map/ppermute | solution.py:42
  83.9 13.9 %collective-permute-start.26 = (bf16[768,512]{1,0:T(8,128)(2,1)S(1)}, bf16[768,512]{1,0:T(8,128)(2,1)S(1)}, u32[]{:S(2)}, u32[]{:S(2)}) collective-permute-start(bf16[768,512]{1,0:T(8,128)(2,1)S(1)} %get-tuple-element.84.refs_1_), channel_id=1, source_target_pairs={{0,8},{1,25},{2,10},{3,27},{4,12},{5,29},{6,14},{7,31},{8,16},{9,1... | collective-permute-start | bytes 2359304 | tf_op jit(solution)/shard_map/ppermute | solution.py:42
  91.2 8.2 %collective-permute-start.29 = (f32[768,1024]{1,0:T(8,128)S(1)}, f32[768,1024]{1,0:T(8,128)S(1)}, u32[]{:S(2)}, u32[]{:S(2)}) collective-permute-start(f32[768,1024]{1,0:T(8,128)S(1)} %shard_map.76), channel_id=1, source_target_pairs={{0,1},{1,0},{2,3},{3,2},{4,5},{5,4},{6,7},{7,6},{8,9},{9,8},{10,11... | collective-permute-start | bytes 9437192 | tf_op jit(solution)/shard_map/ppermute | solution.py:42

commit v6 on v5

--- a/solution.py
+++ b/solution.py
@@ -10,7 +10,7 @@
 AXES = ("lib", "lmk")
 NZ, NY, NX, NC = 4, 4, 4, 2
 TILE = 256
-TIES = [5, 5, 5, 5, 5, 5, 5, 5, 9, 9, 9]
+TIES = [5, 5, 5, 5, 5, 6, 6, 6, 9, 9, 9]
 TAIL = 5 * 10**10
 X1 = 4
 X2 = 7
@@ -285,9 +285,10 @@
                     preferred_element_type=jnp.float32,
                 )
             buf[rows, cols] = total
-        cp = pltpu.make_async_copy(buf.at[pl.ds(t * TILE, TILE), :], out.at[pl.ds(t * TILE, TILE), :], sems.at[t])
-        cp.start()
-        copies.append(cp)
+            at = (pl.ds(t * TILE, TILE), pl.ds(half * 512, 512))
+            cp = pltpu.make_async_copy(buf.at[at], out.at[at], sems.at[2 * t + half])
+            cp.start()
+            copies.append(cp)
     for cp in copies:
         cp.wait()
 
@@ -300,7 +301,7 @@
         out_shape=jax.ShapeDtypeStruct((rows, 1024), jnp.float32),
         in_specs=[VM] * len(args),
         out_specs=ANY,
-        scratch_shapes=[pltpu.VMEM((rows, 1024), jnp.float32), pltpu.SemaphoreType.DMA((rows // TILE,))],
+        scratch_shapes=[pltpu.VMEM((rows, 1024), jnp.float32), pltpu.SemaphoreType.DMA((2 * (rows // TILE),))],
         compiler_params=params(8),
         cost_estimate=cost(10**6),
     )(*args)

time: 102 us -> 101 us (level)
  transfers between devices with their start and end apart: 30 -> 30, of which waited for: 14 -> 17; matrix products, arithmetic and copies ran while one was open for 1% -> 1% of each run, Pallas kernels for 27% -> 27%
where the time goes in v6:
time: 101 us
  starting transfers between devices  41.9 us (41%)
  Pallas kernels  29.5 us (29%)
  waiting for transfers between devices  26.8 us (27%)
  local copies, waits for them, and re-layouts  1.66 us (2%)
    ppermute x30, starting transfers between devices, send(): return lax.ppermute(block, AXES, PAIRS[axis])  41.9 us
    ppermute x30, waiting for transfers between devices, send(): return lax.ppermute(block, AXES, PAIRS[axis])  26.8 us
    pallas_call x6, Pallas kernels, sums(): pl.pallas_call(functools.partial(sum_kernel, jobs, len(rs), len(accs)), o...  18.7 us
    pallas_call x1, Pallas kernels, tversky(): pl.pallas_call(tversky_kernel, out_shape=pltpu.VMEM((4, rows, 256), jnp.b...  4.01 us
    pallas_call x1, Pallas kernels, load(): pl.pallas_call(load_kernel, out_shape=(pltpu.VMEM((rows, depth), jnp.bflo...  2.52 us
    pallas_call x1, Pallas kernels, last(): pl.pallas_call(functools.partial(last_kernel, halves, len(rs)), out_shape...  2.24 us
  transfers between devices with their start and end apart: 30, of which 17 were waited for; matrix products, arithmetic and copies ran while one was open for 1% of the time, Pallas kernels for 27%

profile of v6, /device:TPU:1, one launch (start us, length us, event | category | flops | bytes accessed | tf_op | source)
XLA Modules:
  0.0 100.6 jit_solution(4892575335444170614)
XLA Ops:
  0.0 1.3 %constant_dynamic-slice_fusion = (bf16[256,1024]{1,0:T(8,128)(2,1)S(1)}, bf16[256,1024]{1,0:T(8,128)(2,1)S(1)}) fusion(bf16[512,1024]{1,0:T(8,128)(2,1)} %param.9, s32[]{:T(128)S(6)} %select_n.15, s32[]{:T(128)S(6)} %select_n.14), kind=kLoop, calls=%fused_computation.6 | loop fusion | bytes 2097160 | tf_op jit(solution)/shard_map/dynamic_slice | solution.py:312
  1.3 1.5 %collective-permute-start = (bf16[256,1024]{1,0:T(8,128)(2,1)S(1)}, bf16[256,1024]{1,0:T(8,128)(2,1)S(1)}, u32[]{:S(2)}, u32[]{:S(2)}) collective-permute-start(bf16[256,1024]{1,0:T(8,128)(2,1)S(1)} %get-tuple-element.90), channel_id=1, source_target_pairs={{0,1},{1,0},{2,3},{3,2},{4,5},{5,4},{6,7},{7,6},{8,9},{9,8},{10,11... | collective-permute-start | bytes 1572872 | tf_op jit(solution)/shard_map/ppermute | solution.py:42
  2.8 1.6 %shard_map.56 = bf16[512,2048]{1,0:T(8,128)(2,1)S(1)} custom-call(bf16[1024,2048]{1,0:T(8,128)(2,1)} %col_bits.3), custom_call_target="tpu_custom_call" | custom-call | flops 1000000 | tf_op jit(solution)/shard_map/pallas_call | solution.py:132
  4.4 0.3 collective-permute-start.11
  4.7 2.8 %collective-permute-start.1 = (bf16[256,1024]{1,0:T(8,128)(2,1)S(1)}, bf16[256,1024]{1,0:T(8,128)(2,1)S(1)}, u32[]{:S(2)}, u32[]{:S(2)}) collective-permute-start(bf16[256,1024]{1,0:T(8,128)(2,1)S(1)} %collective-permute-done.refs_0_), channel_id=1, source_target_pairs={{0,8},{1,25},{2,10},{3,27},{4,12},{5,29},{6,14},{7,31},{8,16},{9,1... | collective-permute-start | bytes 1572872 | tf_op jit(solution)/shard_map/ppermute | solution.py:42
  7.5 3.8 %collective-permute-start.2 = (bf16[256,1024]{1,0:T(8,128)(2,1)S(1)}, bf16[256,1024]{1,0:T(8,128)(2,1)S(1)}, u32[]{:S(2)}, u32[]{:S(2)}) collective-permute-start(bf16[256,1024]{1,0:T(8,128)(2,1)S(1)} %collective-permute-done.refs_0_), channel_id=1, source_target_pairs={{0,32},{1,97},{2,34},{3,99},{4,36},{5,101},{6,38},{7,103},{8,40},{... | collective-permute-start | bytes 1572872 | tf_op jit(solution)/shard_map/ppermute | solution.py:42
  11.3 0.5 collective-permute-start.3
  12.0 2.5 %shard_map.55 = (bf16[768,2048]{1,0:T(8,128)(2,1)S(1)}, bf16[512,2048]{1,0:T(8,128)(2,1)S(1)}, bf16[16,128]{1,0:T(8,128)(2,1)S(1)}) custom-call(bf16[768,2048]{1,0:T(8,128)(2,1)} %row_bits.1, bf16[1024,2048]{1,0:T(8,128)(2,1)} %col_bits.3), custom_call_target="tpu_custom_call" | custom-call | flops 1000000 | tf_op jit(solution)/shard_map/pallas_call | solution.py:100
  14.6 4.0 %shard_map.61.refs_0_ = bf16[4,768,256]{2,1,0:T(8,128)(2,1)S(1)} custom-call(bf16[768,2048]{1,0:T(8,128)(2,1)S(1)} %get-tuple-element.59.row_bits, f32[768,1]{1,0:T(8,128)S(1)} %mul.30.row_scale, bf16[512,2048]{1,0:T(8,128)(2,1)S(1)} %get-tuple-element.60.col_bits, f32[1,1024]{1,0:T(1,128)S(1)} %bitcast.1, bf16[512,2048]{1,0:T(8,128)(2,1)S(1)} %collective-permute-done.11.got_bits), custom_call_target="tpu_custom_call" | custom-call | flops 1000000 | tf_op jit(solution)/shard_map/pallas_call | solution.py:163
  18.6 2.5 %collective-permute-start.12 = (bf16[4,768,256]{2,1,0:T(8,128)(2,1)S(1)}, bf16[4,768,256]{2,1,0:T(8,128)(2,1)S(1)}, u32[]{:S(2)}, u32[]{:S(2)}) collective-permute-start(bf16[4,768,256]{2,1,0:T(8,128)(2,1)S(1)} %shard_map.61.refs_0_), channel_id=1, source_target_pairs={{0,2},{1,7},{2,4},{3,1},{4,6},{5,3},{6,0},{7,5},{8,10},{9,15},{10,... | collective-permute-start | bytes 4718600 | tf_op jit(solution)/shard_map/ppermute | solution.py:42
  21.3 0.4 collective-permute-start.6
  21.7 1.3 %collective-permute-done.4.refs_2_ = bf16[256,1024]{1,0:T(8,128)(2,1)S(1)} collective-permute-done((bf16[256,1024]{1,0:T(8,128)(2,1)S(1)}, bf16[256,1024]{1,0:T(8,128)(2,1)S(1)}, u32[]{:S(2)}, u32[]{:S(2)}) %collective-permute-start.4) | collective-permute-done | bytes 524320 | tf_op jit(solution)/shard_map/ppermute | solution.py:42
  23.0 0.5 collective-permute-start.7
  23.5 3.4 %collective-permute-start.8 = (bf16[256,1024]{1,0:T(8,128)(2,1)S(1)}, bf16[256,1024]{1,0:T(8,128)(2,1)S(1)}, u32[]{:S(2)}, u32[]{:S(2)}) collective-permute-start(bf16[256,1024]{1,0:T(8,128)(2,1)S(1)} %get-tuple-element.55.refs_4_), channel_id=1, source_target_pairs={{0,32},{1,97},{2,34},{3,99},{4,36},{5,101},{6,38},{7,103},{8,40},{... | collective-permute-start | bytes 1572872 | tf_op jit(solution)/shard_map/ppermute | solution.py:42
  26.9 2.6 %collective-permute-done.5.refs_1_ = bf16[256,1024]{1,0:T(8,128)(2,1)S(1)} collective-permute-done((bf16[256,1024]{1,0:T(8,128)(2,1)S(1)}, bf16[256,1024]{1,0:T(8,128)(2,1)S(1)}, u32[]{:S(2)}, u32[]{:S(2)}) %collective-permute-start.5) | collective-permute-done | bytes 524320 | tf_op jit(solution)/shard_map/ppermute | solution.py:42
  29.7 2.4 %collective-permute-start.10 = (bf16[256,1024]{1,0:T(8,128)(2,1)S(1)}, bf16[256,1024]{1,0:T(8,128)(2,1)S(1)}, u32[]{:S(2)}, u32[]{:S(2)}) collective-permute-start(bf16[256,1024]{1,0:T(8,128)(2,1)S(1)} %get-tuple-element.58.refs_5_), channel_id=1, source_target_pairs={{0,32},{1,97},{2,34},{3,99},{4,36},{5,101},{6,38},{7,103},{8,40},{... | collective-permute-start | bytes 1572872 | tf_op jit(solution)/shard_map/ppermute | solution.py:42
  32.0 0.5 collective-permute-start.9
  32.6 2.5 %collective-permute-done.7.refs_1_ = bf16[256,1024]{1,0:T(8,128)(2,1)S(1)} collective-permute-done((bf16[256,1024]{1,0:T(8,128)(2,1)S(1)}, bf16[256,1024]{1,0:T(8,128)(2,1)S(1)}, u32[]{:S(2)}, u32[]{:S(2)}) %collective-permute-start.7) | collective-permute-done | bytes 524320 | tf_op jit(solution)/shard_map/ppermute | solution.py:42
  35.3 2.4 %collective-permute-start.14 = (bf16[256,1024]{1,0:T(8,128)(2,1)S(1)}, bf16[256,1024]{1,0:T(8,128)(2,1)S(1)}, u32[]{:S(2)}, u32[]{:S(2)}) collective-permute-start(bf16[256,1024]{1,0:T(8,128)(2,1)S(1)} %get-tuple-element.64.refs_5_), channel_id=1, source_target_pairs={{0,32},{1,97},{2,34},{3,99},{4,36},{5,101},{6,38},{7,103},{8,40},{... | collective-permute-start | bytes 1572872 | tf_op jit(solution)/shard_map/ppermute | solution.py:42
  37.7 0.5 collective-permute-start.13
  38.3 2.6 %collective-permute-done.10.refs_2_ = bf16[256,1024]{1,0:T(8,128)(2,1)S(1)} collective-permute-done((bf16[256,1024]{1,0:T(8,128)(2,1)S(1)}, bf16[256,1024]{1,0:T(8,128)(2,1)S(1)}, u32[]{:S(2)}, u32[]{:S(2)}) %collective-permute-start.10) | collective-permute-done | bytes 524320 | tf_op jit(solution)/shard_map/ppermute | solution.py:42
  41.0 1.3 %collective-permute-start.16 = (bf16[768,512]{1,0:T(8,128)(2,1)S(1)}, bf16[768,512]{1,0:T(8,128)(2,1)S(1)}, u32[]{:S(2)}, u32[]{:S(2)}) collective-permute-start(bf16[768,512]{1,0:T(8,128)(2,1)S(1)} %pad_maximum_fusion.1), channel_id=1, source_target_pairs={{0,8},{1,25},{2,10},{3,27},{4,12},{5,29},{6,14},{7,31},{8,16},{9,1... | collective-permute-start | bytes 2359304 | tf_op jit(solution)/shard_map/ppermute | solution.py:42
  42.4 1.4 %collective-permute-start.15 = (bf16[768,512]{1,0:T(8,128)(2,1)S(1)}, bf16[768,512]{1,0:T(8,128)(2,1)S(1)}, u32[]{:S(2)}, u32[]{:S(2)}) collective-permute-start(bf16[768,512]{1,0:T(8,128)(2,1)S(1)} %pad_maximum_fusion), channel_id=1, source_target_pairs={{0,32},{1,97},{2,34},{3,99},{4,36},{5,101},{6,38},{7,103},{8,40},{... | collective-permute-start | bytes 2359304 | tf_op jit(solution)/shard_map/ppermute | solution.py:42
  43.8 2.5 %collective-permute-start.19 = (bf16[4,768,256]{2,1,0:T(8,128)(2,1)S(1)}, bf16[4,768,256]{2,1,0:T(8,128)(2,1)S(1)}, u32[]{:S(2)}, u32[]{:S(2)}) collective-permute-start(bf16[4,768,256]{2,1,0:T(8,128)(2,1)S(1)} %get-tuple-element.71.refs_1_), channel_id=1, source_target_pairs={{0,2},{1,7},{2,4},{3,1},{4,6},{5,3},{6,0},{7,5},{8,10},{9,15},{10,... | collective-permute-start | bytes 4718600 | tf_op jit(solution)/shard_map/ppermute | solution.py:42
  46.6 1.3 %collective-permute-start.18 = (bf16[768,512]{1,0:T(8,128)(2,1)S(1)}, bf16[768,512]{1,0:T(8,128)(2,1)S(1)}, u32[]{:S(2)}, u32[]{:S(2)}) collective-permute-start(bf16[768,512]{1,0:T(8,128)(2,1)S(1)} %pad_maximum_fusion.3), channel_id=1, source_target_pairs={{0,8},{1,25},{2,10},{3,27},{4,12},{5,29},{6,14},{7,31},{8,16},{9,1... | collective-permute-start | bytes 2359304 | tf_op jit(solution)/shard_map/ppermute | solution.py:42
  48.0 1.4 %collective-permute-start.17 = (bf16[768,512]{1,0:T(8,128)(2,1)S(1)}, bf16[768,512]{1,0:T(8,128)(2,1)S(1)}, u32[]{:S(2)}, u32[]{:S(2)}) collective-permute-start(bf16[768,512]{1,0:T(8,128)(2,1)S(1)} %pad_maximum_fusion.2), channel_id=1, source_target_pairs={{0,32},{1,97},{2,34},{3,99},{4,36},{5,101},{6,38},{7,103},{8,40},{... | collective-permute-start | bytes 2359304 | tf_op jit(solution)/shard_map/ppermute | solution.py:42
  49.4 5.4 %collective-permute-done.16.refs_2_ = bf16[768,512]{1,0:T(8,128)(2,1)S(1)} collective-permute-done((bf16[768,512]{1,0:T(8,128)(2,1)S(1)}, bf16[768,512]{1,0:T(8,128)(2,1)S(1)}, u32[]{:S(2)}, u32[]{:S(2)}) %collective-permute-start.16) | collective-permute-done | bytes 786464 | tf_op jit(solution)/shard_map/ppermute | solution.py:42
  55.0 2.4 %collective-permute-start.21 = (bf16[768,512]{1,0:T(8,128)(2,1)S(1)}, bf16[768,512]{1,0:T(8,128)(2,1)S(1)}, u32[]{:S(2)}, u32[]{:S(2)}) collective-permute-start(bf16[768,512]{1,0:T(8,128)(2,1)S(1)} %get-tuple-element.74.refs_7_), channel_id=1, source_target_pairs={{0,32},{1,97},{2,34},{3,99},{4,36},{5,101},{6,38},{7,103},{8,40},{... | collective-permute-start | bytes 2359304 | tf_op jit(solution)/shard_map/ppermute | solution.py:42
  57.3 0.5 collective-permute-start.22
  57.8 5.4 %collective-permute-done.18.refs_2_ = bf16[768,512]{1,0:T(8,128)(2,1)S(1)} collective-permute-done((bf16[768,512]{1,0:T(8,128)(2,1)S(1)}, bf16[768,512]{1,0:T(8,128)(2,1)S(1)}, u32[]{:S(2)}, u32[]{:S(2)}) %collective-permute-start.18) | collective-permute-done | bytes 786464 | tf_op jit(solution)/shard_map/ppermute | solution.py:42
  63.4 0.2 collective-permute-done.19.refs_3_
  63.6 3.4 %collective-permute-start.20 = (bf16[4,768,256]{2,1,0:T(8,128)(2,1)S(1)}, bf16[4,768,256]{2,1,0:T(8,128)(2,1)S(1)}, u32[]{:S(2)}, u32[]{:S(2)}) collective-permute-start(bf16[4,768,256]{2,1,0:T(8,128)(2,1)S(1)} %get-tuple-element.72.refs_2_), channel_id=1, source_target_pairs={{0,2},{1,7},{2,4},{3,1},{4,6},{5,3},{6,0},{7,5},{8,10},{9,15},{10,... | collective-permute-start | bytes 4718600 | tf_op jit(solution)/shard_map/ppermute | solution.py:42
  67.0 1.2 %collective-permute-start.23 = (bf16[768,512]{1,0:T(8,128)(2,1)S(1)}, bf16[768,512]{1,0:T(8,128)(2,1)S(1)}, u32[]{:S(2)}, u32[]{:S(2)}) collective-permute-start(bf16[768,512]{1,0:T(8,128)(2,1)S(1)} %get-tuple-element.77.refs_7_), channel_id=1, source_target_pairs={{0,32},{1,97},{2,34},{3,99},{4,36},{5,101},{6,38},{7,103},{8,40},{... | collective-permute-start | bytes 2359304 | tf_op jit(solution)/shard_map/ppermute | solution.py:42
  68.4 0.3 shard_map.66.refs_1_.k
  68.8 5.2 %shard_map.68.refs_3_ = f32[768,1024]{1,0:T(8,128)S(1)} custom-call(bf16[16,768,256]{2,1,0:T(8,128)(2,1)S(1)} %shard_map.66.refs_1_.k, bf16[256,1024]{1,0:T(8,128)(2,1)S(1)} %collective-permute-done.refs_0_, bf16[256,1024]{1,0:T(8,128)(2,1)S(1)} %get-tuple-element.51.refs_1_, bf16[256,1024]{1,0:T(8,128)(2,1)S(1)} %get-tuple-element.57.refs_2_, ...), custom_call_target="tpu_custom_call" | custom-call | flops 1000000 | tf_op jit(solution)/shard_map/pallas_call | solution.py:262
  74.4 7.2 %shard_map.70 = (f32[768,1024]{1,0:T(8,128)S(1)}, f32[768,1024]{1,0:T(8,128)S(1)}) custom-call(bf16[16,768,256]{2,1,0:T(8,128)(2,1)S(1)} %shard_map.66.refs_1_.k, bf16[256,1024]{1,0:T(8,128)(2,1)S(1)} %get-tuple-element.89.refs_0_, bf16[256,1024]{1,0:T(8,128)(2,1)S(1)} %get-tuple-element.54.refs_1_, ...), custom_call_target="tpu_custom_call", output_to_operand_aliasing={{1}: (12, {})} | custom-call | flops 1000000 | tf_op jit(solution)/shard_map/pallas_call | solution.py:262
  81.6 1.0 collective-permute-start.25
  82.6 1.0 collective-permute-start.26
  83.6 0.8 collective-permute-done.20.refs_0_
  84.5 1.5 %shard_map.75.refs_2_ = f32[768,1024]{1,0:T(8,128)S(1)} custom-call(bf16[16,768,256]{2,1,0:T(8,128)(2,1)S(1)} %shard_map.67.k, bf16[256,1024]{1,0:T(8,128)(2,1)S(1)} %collective-permute-done.refs_0_, bf16[256,1024]{1,0:T(8,128)(2,1)S(1)} %get-tuple-element.51.refs_1_, ...), custom_call_target="tpu_custom_call", output_to_operand_aliasing={{}: (12, {})} | custom-call | flops 1000000 | tf_op jit(solution)/shard_map/pallas_call | solution.py:262
  86.0 2.7 %collective-permute-done.27.refs_0_ = bf16[768,512]{1,0:T(8,128)(2,1)S(1)} collective-permute-done((bf16[768,512]{1,0:T(8,128)(2,1)S(1)}, bf16[768,512]{1,0:T(8,128)(2,1)S(1)}, u32[]{:S(2)}, u32[]{:S(2)}) %collective-permute-start.27) | collective-permute-done | bytes 786464 | tf_op jit(solution)/shard_map/ppermute | solution.py:42
  88.7 1.8 %shard_map.76 = f32[768,1024]{1,0:T(8,128)S(1)} custom-call(bf16[16,768,256]{2,1,0:T(8,128)(2,1)S(1)} %shard_map.67.k, bf16[768,512]{1,0:T(8,128)(2,1)S(1)} %collective-permute-done.27.refs_0_, bf16[768,512]{1,0:T(8,128)(2,1)S(1)} %collective-permute-done.28.refs_1_, f32[768,1024]{1,0:T(8,128)S(1)} %shard_map.75.refs_2_), custom_call_target="tpu_custom_call", output_to_operand_aliasing={{}: (3, {})} | custom-call | flops 1000000 | tf_op jit(solution)/shard_map/pallas_call | solution.py:262
  90.4 2.4 %collective-permute-start.29 = (f32[768,1024]{1,0:T(8,128)S(1)}, f32[768,1024]{1,0:T(8,128)S(1)}, u32[]{:S(2)}, u32[]{:S(2)}) collective-permute-start(f32[768,1024]{1,0:T(8,128)S(1)} %shard_map.76), channel_id=1, source_target_pairs={{0,1},{1,0},{2,3},{3,2},{4,5},{5,4},{6,7},{7,6},{8,9},{9,8},{10,11... | collective-permute-start | bytes 9437192 | tf_op jit(solution)/shard_map/ppermute | solution.py:42
  92.9 1.2 %shard_map.73.refs_2_ = f32[768,1024]{1,0:T(8,128)S(1)} custom-call(bf16[16,768,256]{2,1,0:T(8,128)(2,1)S(1)} %shard_map.67.k, bf16[256,1024]{1,0:T(8,128)(2,1)S(1)} %get-tuple-element.89.refs_0_, bf16[256,1024]{1,0:T(8,128)(2,1)S(1)} %get-tuple-element.54.refs_1_, bf16[256,1024]{1,0:T(8,128)(2,1)S(1)} %get-tuple-element.63.refs_2_, ...), custom_call_target="tpu_custom_call", output_to_operand_aliasing={{}: (10, {})} | custom-call | flops 1000000 | tf_op jit(solution)/shard_map/pallas_call | solution.py:262
  94.1 1.8 %shard_map.74.refs_2_ = f32[768,1024]{1,0:T(8,128)S(1)} custom-call(bf16[16,768,256]{2,1,0:T(8,128)(2,1)S(1)} %shard_map.67.k, bf16[768,512]{1,0:T(8,128)(2,1)S(1)} %get-tuple-element.83.refs_0_, bf16[768,512]{1,0:T(8,128)(2,1)S(1)} %get-tuple-element.84.refs_1_, f32[768,1024]{1,0:T(8,128)S(1)} %shard_map.73.refs_2_), custom_call_target="tpu_custom_call", output_to_operand_aliasing={{}: (3, {})} | custom-call | flops 1000000 | tf_op jit(solution)/shard_map/pallas_call | solution.py:262
  95.9 1.2 %collective-permute-done.25.refs_0_ = bf16[768,512]{1,0:T(8,128)(2,1)S(1)} collective-permute-done((bf16[768,512]{1,0:T(8,128)(2,1)S(1)}, bf16[768,512]{1,0:T(8,128)(2,1)S(1)}, u32[]{:S(2)}, u32[]{:S(2)}) %collective-permute-start.25) | collective-permute-done | bytes 786464 | tf_op jit(solution)/shard_map/ppermute | solution.py:42
  97.1 1.1 %collective-permute-done.29.refs_3_ = f32[768,1024]{1,0:T(8,128)S(1)} collective-permute-done((f32[768,1024]{1,0:T(8,128)S(1)}, f32[768,1024]{1,0:T(8,128)S(1)}, u32[]{:S(2)}, u32[]{:S(2)}) %collective-permute-start.29) | collective-permute-done | bytes 3145760 | tf_op jit(solution)/shard_map/ppermute | solution.py:42
  98.2 2.2 %shard_map.77 = f32[768,1024]{1,0:T(8,128)} custom-call(bf16[16,768,256]{2,1,0:T(8,128)(2,1)S(1)} %shard_map.67.k, bf16[768,512]{1,0:T(8,128)(2,1)S(1)} %get-tuple-element.85.refs_0_, bf16[768,512]{1,0:T(8,128)(2,1)S(1)} %get-tuple-element.86.refs_1_, f32[768,1024]{1,0:T(8,128)S(1)} %shard_map.74.refs_2_, f32[768,1024]{1,0:T(8,128)S(1)} %collective-permute-done.29.refs_3_), custom_call_target="tpu_custom_call" | custom-call | flops 1000000 | tf_op jit(solution)/shard_map/pallas_call | solution.py:299
  (59 shorter events, 2.5 us)
Async XLA Ops:
  1.3 10.6 %copy-start = (s32[768]{0:T(1024)S(1)}, s32[768]{0:T(1024)}, u32[]{:S(2)}) copy-start(s32[768]{0:T(1024)} %param.6) | copy-start | bytes 9220
  1.3 3.1 %collective-permute-start = (bf16[256,1024]{1,0:T(8,128)(2,1)S(1)}, bf16[256,1024]{1,0:T(8,128)(2,1)S(1)}, u32[]{:S(2)}, u32[]{:S(2)}) collective-permute-start(bf16[256,1024]{1,0:T(8,128)(2,1)S(1)} %get-tuple-element.90), channel_id=1, source_target_pairs={{0,1},{1,0},{2,3},{3,2},{4,5},{5,4},{6,7},{7,6},{8,9},{9,8},{10,11... | collective-permute-start | bytes 1572872 | tf_op jit(solution)/shard_map/ppermute | solution.py:42
  4.4 10.2 %collective-permute-start.11 = (bf16[512,2048]{1,0:T(8,128)(2,1)S(1)}, bf16[512,2048]{1,0:T(8,128)(2,1)S(1)}, u32[]{:S(2)}, u32[]{:S(2)}) collective-permute-start(bf16[512,2048]{1,0:T(8,128)(2,1)S(1)} %shard_map.56), channel_id=1, source_target_pairs={{0,1},{1,0},{2,3},{3,2},{4,5},{5,4},{6,7},{7,6},{8,9},{9,8},{10,11... | collective-permute-start | bytes 6291464 | tf_op jit(solution)/shard_map/ppermute | solution.py:42
  4.7 16.5 %collective-permute-start.1 = (bf16[256,1024]{1,0:T(8,128)(2,1)S(1)}, bf16[256,1024]{1,0:T(8,128)(2,1)S(1)}, u32[]{:S(2)}, u32[]{:S(2)}) collective-permute-start(bf16[256,1024]{1,0:T(8,128)(2,1)S(1)} %collective-permute-done.refs_0_), channel_id=1, source_target_pairs={{0,8},{1,25},{2,10},{3,27},{4,12},{5,29},{6,14},{7,31},{8,16},{9,1... | collective-permute-start | bytes 1572872 | tf_op jit(solution)/shard_map/ppermute | solution.py:42
  7.5 13.7 %collective-permute-start.2 = (bf16[256,1024]{1,0:T(8,128)(2,1)S(1)}, bf16[256,1024]{1,0:T(8,128)(2,1)S(1)}, u32[]{:S(2)}, u32[]{:S(2)}) collective-permute-start(bf16[256,1024]{1,0:T(8,128)(2,1)S(1)} %collective-permute-done.refs_0_), channel_id=1, source_target_pairs={{0,32},{1,97},{2,34},{3,99},{4,36},{5,101},{6,38},{7,103},{8,40},{... | collective-permute-start | bytes 1572872 | tf_op jit(solution)/shard_map/ppermute | solution.py:42
  11.3 10.5 %collective-permute-start.3 = (bf16[256,1024]{1,0:T(8,128)(2,1)S(1)}, bf16[256,1024]{1,0:T(8,128)(2,1)S(1)}, u32[]{:S(2)}, u32[]{:S(2)}) collective-permute-start(bf16[256,1024]{1,0:T(8,128)(2,1)S(1)} %get-tuple-element.89.refs_0_), channel_id=1, source_target_pairs={{0,8},{1,25},{2,10},{3,27},{4,12},{5,29},{6,14},{7,31},{8,16},{9,1... | collective-permute-start | bytes 1572872 | tf_op jit(solution)/shard_map/ppermute | solution.py:42
  11.7 11.3 %collective-permute-start.4 = (bf16[256,1024]{1,0:T(8,128)(2,1)S(1)}, bf16[256,1024]{1,0:T(8,128)(2,1)S(1)}, u32[]{:S(2)}, u32[]{:S(2)}) collective-permute-start(bf16[256,1024]{1,0:T(8,128)(2,1)S(1)} %get-tuple-element.89.refs_0_), channel_id=1, source_target_pairs={{0,32},{1,97},{2,34},{3,99},{4,36},{5,101},{6,38},{7,103},{8,40},{... | collective-permute-start | bytes 1572872 | tf_op jit(solution)/shard_map/ppermute | solution.py:42
  12.0 2.5 %copy-start.1 = (s32[1024]{0:T(1024)S(1)}, s32[1024]{0:T(1024)}, u32[]{:S(2)}) copy-start(s32[1024]{0:T(1024)} %param.8) | copy-start | bytes 12292
  18.6 22.3 %collective-permute-start.12 = (bf16[4,768,256]{2,1,0:T(8,128)(2,1)S(1)}, bf16[4,768,256]{2,1,0:T(8,128)(2,1)S(1)}, u32[]{:S(2)}, u32[]{:S(2)}) collective-permute-start(bf16[4,768,256]{2,1,0:T(8,128)(2,1)S(1)} %shard_map.61.refs_0_), channel_id=1, source_target_pairs={{0,2},{1,7},{2,4},{3,1},{4,6},{5,3},{6,0},{7,5},{8,10},{9,15},{10,... | collective-permute-start | bytes 4718600 | tf_op jit(solution)/shard_map/ppermute | solution.py:42
  21.2 8.3 %collective-permute-start.5 = (bf16[256,1024]{1,0:T(8,128)(2,1)S(1)}, bf16[256,1024]{1,0:T(8,128)(2,1)S(1)}, u32[]{:S(2)}, u32[]{:S(2)}) collective-permute-start(bf16[256,1024]{1,0:T(8,128)(2,1)S(1)} %get-tuple-element.51.refs_1_), channel_id=1, source_target_pairs={{0,8},{1,25},{2,10},{3,27},{4,12},{5,29},{6,14},{7,31},{8,16},{9,1... | collective-permute-start | bytes 1572872 | tf_op jit(solution)/shard_map/ppermute | solution.py:42
  21.3 8.3 %collective-permute-start.6 = (bf16[256,1024]{1,0:T(8,128)(2,1)S(1)}, bf16[256,1024]{1,0:T(8,128)(2,1)S(1)}, u32[]{:S(2)}, u32[]{:S(2)}) collective-permute-start(bf16[256,1024]{1,0:T(8,128)(2,1)S(1)} %get-tuple-element.52.refs_4_), channel_id=1, source_target_pairs={{0,32},{1,97},{2,34},{3,99},{4,36},{5,101},{6,38},{7,103},{8,40},{... | collective-permute-start | bytes 1572872 | tf_op jit(solution)/shard_map/ppermute | solution.py:42
  23.0 12.1 %collective-permute-start.7 = (bf16[256,1024]{1,0:T(8,128)(2,1)S(1)}, bf16[256,1024]{1,0:T(8,128)(2,1)S(1)}, u32[]{:S(2)}, u32[]{:S(2)}) collective-permute-start(bf16[256,1024]{1,0:T(8,128)(2,1)S(1)} %get-tuple-element.54.refs_1_), channel_id=1, source_target_pairs={{0,8},{1,25},{2,10},{3,27},{4,12},{5,29},{6,14},{7,31},{8,16},{9,1... | collective-permute-start | bytes 1572872 | tf_op jit(solution)/shard_map/ppermute | solution.py:42
  23.5 11.8 %collective-permute-start.8 = (bf16[256,1024]{1,0:T(8,128)(2,1)S(1)}, bf16[256,1024]{1,0:T(8,128)(2,1)S(1)}, u32[]{:S(2)}, u32[]{:S(2)}) collective-permute-start(bf16[256,1024]{1,0:T(8,128)(2,1)S(1)} %get-tuple-element.55.refs_4_), channel_id=1, source_target_pairs={{0,32},{1,97},{2,34},{3,99},{4,36},{5,101},{6,38},{7,103},{8,40},{... | collective-permute-start | bytes 1572872 | tf_op jit(solution)/shard_map/ppermute | solution.py:42
  29.7 11.2 %collective-permute-start.10 = (bf16[256,1024]{1,0:T(8,128)(2,1)S(1)}, bf16[256,1024]{1,0:T(8,128)(2,1)S(1)}, u32[]{:S(2)}, u32[]{:S(2)}) collective-permute-start(bf16[256,1024]{1,0:T(8,128)(2,1)S(1)} %get-tuple-element.58.refs_5_), channel_id=1, source_target_pairs={{0,32},{1,97},{2,34},{3,99},{4,36},{5,101},{6,38},{7,103},{8,40},{... | collective-permute-start | bytes 1572872 | tf_op jit(solution)/shard_map/ppermute | solution.py:42
  32.0 8.9 %collective-permute-start.9 = (bf16[256,1024]{1,0:T(8,128)(2,1)S(1)}, bf16[256,1024]{1,0:T(8,128)(2,1)S(1)}, u32[]{:S(2)}, u32[]{:S(2)}) collective-permute-start(bf16[256,1024]{1,0:T(8,128)(2,1)S(1)} %get-tuple-element.57.refs_2_), channel_id=1, source_target_pairs={{0,8},{1,25},{2,10},{3,27},{4,12},{5,29},{6,14},{7,31},{8,16},{9,1... | collective-permute-start | bytes 1572872 | tf_op jit(solution)/shard_map/ppermute | solution.py:42
  35.3 11.2 %collective-permute-start.14 = (bf16[256,1024]{1,0:T(8,128)(2,1)S(1)}, bf16[256,1024]{1,0:T(8,128)(2,1)S(1)}, u32[]{:S(2)}, u32[]{:S(2)}) collective-permute-start(bf16[256,1024]{1,0:T(8,128)(2,1)S(1)} %get-tuple-element.64.refs_5_), channel_id=1, source_target_pairs={{0,32},{1,97},{2,34},{3,99},{4,36},{5,101},{6,38},{7,103},{8,40},{... | collective-permute-start | bytes 1572872 | tf_op jit(solution)/shard_map/ppermute | solution.py:42
  37.7 8.7 %collective-permute-start.13 = (bf16[256,1024]{1,0:T(8,128)(2,1)S(1)}, bf16[256,1024]{1,0:T(8,128)(2,1)S(1)}, u32[]{:S(2)}, u32[]{:S(2)}) collective-permute-start(bf16[256,1024]{1,0:T(8,128)(2,1)S(1)} %get-tuple-element.63.refs_2_), channel_id=1, source_target_pairs={{0,8},{1,25},{2,10},{3,27},{4,12},{5,29},{6,14},{7,31},{8,16},{9,1... | collective-permute-start | bytes 1572872 | tf_op jit(solution)/shard_map/ppermute | solution.py:42
  41.0 13.8 %collective-permute-start.16 = (bf16[768,512]{1,0:T(8,128)(2,1)S(1)}, bf16[768,512]{1,0:T(8,128)(2,1)S(1)}, u32[]{:S(2)}, u32[]{:S(2)}) collective-permute-start(bf16[768,512]{1,0:T(8,128)(2,1)S(1)} %pad_maximum_fusion.1), channel_id=1, source_target_pairs={{0,8},{1,25},{2,10},{3,27},{4,12},{5,29},{6,14},{7,31},{8,16},{9,1... | collective-permute-start | bytes 2359304 | tf_op jit(solution)/shard_map/ppermute | solution.py:42
  42.4 12.6 %collective-permute-start.15 = (bf16[768,512]{1,0:T(8,128)(2,1)S(1)}, bf16[768,512]{1,0:T(8,128)(2,1)S(1)}, u32[]{:S(2)}, u32[]{:S(2)}) collective-permute-start(bf16[768,512]{1,0:T(8,128)(2,1)S(1)} %pad_maximum_fusion), channel_id=1, source_target_pairs={{0,32},{1,97},{2,34},{3,99},{4,36},{5,101},{6,38},{7,103},{8,40},{... | collective-permute-start | bytes 2359304 | tf_op jit(solution)/shard_map/ppermute | solution.py:42
  43.8 19.8 %collective-permute-start.19 = (bf16[4,768,256]{2,1,0:T(8,128)(2,1)S(1)}, bf16[4,768,256]{2,1,0:T(8,128)(2,1)S(1)}, u32[]{:S(2)}, u32[]{:S(2)}) collective-permute-start(bf16[4,768,256]{2,1,0:T(8,128)(2,1)S(1)} %get-tuple-element.71.refs_1_), channel_id=1, source_target_pairs={{0,2},{1,7},{2,4},{3,1},{4,6},{5,3},{6,0},{7,5},{8,10},{9,15},{10,... | collective-permute-start | bytes 4718600 | tf_op jit(solution)/shard_map/ppermute | solution.py:42
  46.6 16.6 %collective-permute-start.18 = (bf16[768,512]{1,0:T(8,128)(2,1)S(1)}, bf16[768,512]{1,0:T(8,128)(2,1)S(1)}, u32[]{:S(2)}, u32[]{:S(2)}) collective-permute-start(bf16[768,512]{1,0:T(8,128)(2,1)S(1)} %pad_maximum_fusion.3), channel_id=1, source_target_pairs={{0,8},{1,25},{2,10},{3,27},{4,12},{5,29},{6,14},{7,31},{8,16},{9,1... | collective-permute-start | bytes 2359304 | tf_op jit(solution)/shard_map/ppermute | solution.py:42
  48.0 15.4 %collective-permute-start.17 = (bf16[768,512]{1,0:T(8,128)(2,1)S(1)}, bf16[768,512]{1,0:T(8,128)(2,1)S(1)}, u32[]{:S(2)}, u32[]{:S(2)}) collective-permute-start(bf16[768,512]{1,0:T(8,128)(2,1)S(1)} %pad_maximum_fusion.2), channel_id=1, source_target_pairs={{0,32},{1,97},{2,34},{3,99},{4,36},{5,101},{6,38},{7,103},{8,40},{... | collective-permute-start | bytes 2359304 | tf_op jit(solution)/shard_map/ppermute | solution.py:42
  55.0 19.1 %collective-permute-start.21 = (bf16[768,512]{1,0:T(8,128)(2,1)S(1)}, bf16[768,512]{1,0:T(8,128)(2,1)S(1)}, u32[]{:S(2)}, u32[]{:S(2)}) collective-permute-start(bf16[768,512]{1,0:T(8,128)(2,1)S(1)} %get-tuple-element.74.refs_7_), channel_id=1, source_target_pairs={{0,32},{1,97},{2,34},{3,99},{4,36},{5,101},{6,38},{7,103},{8,40},{... | collective-permute-start | bytes 2359304 | tf_op jit(solution)/shard_map/ppermute | solution.py:42
  57.3 16.7 %collective-permute-start.22 = (bf16[768,512]{1,0:T(8,128)(2,1)S(1)}, bf16[768,512]{1,0:T(8,128)(2,1)S(1)}, u32[]{:S(2)}, u32[]{:S(2)}) collective-permute-start(bf16[768,512]{1,0:T(8,128)(2,1)S(1)} %get-tuple-element.75.refs_8_), channel_id=1, source_target_pairs={{0,8},{1,25},{2,10},{3,27},{4,12},{5,29},{6,14},{7,31},{8,16},{9,1... | collective-permute-start | bytes 2359304 | tf_op jit(solution)/shard_map/ppermute | solution.py:42
  63.6 20.8 %collective-permute-start.20 = (bf16[4,768,256]{2,1,0:T(8,128)(2,1)S(1)}, bf16[4,768,256]{2,1,0:T(8,128)(2,1)S(1)}, u32[]{:S(2)}, u32[]{:S(2)}) collective-permute-start(bf16[4,768,256]{2,1,0:T(8,128)(2,1)S(1)} %get-tuple-element.72.refs_2_), channel_id=1, source_target_pairs={{0,2},{1,7},{2,4},{3,1},{4,6},{5,3},{6,0},{7,5},{8,10},{9,15},{10,... | collective-permute-start | bytes 4718600 | tf_op jit(solution)/shard_map/ppermute | solution.py:42
  67.0 14.6 %collective-permute-start.23 = (bf16[768,512]{1,0:T(8,128)(2,1)S(1)}, bf16[768,512]{1,0:T(8,128)(2,1)S(1)}, u32[]{:S(2)}, u32[]{:S(2)}) collective-permute-start(bf16[768,512]{1,0:T(8,128)(2,1)S(1)} %get-tuple-element.77.refs_7_), channel_id=1, source_target_pairs={{0,32},{1,97},{2,34},{3,99},{4,36},{5,101},{6,38},{7,103},{8,40},{... | collective-permute-start | bytes 2359304 | tf_op jit(solution)/shard_map/ppermute | solution.py:42
  68.2 13.4 %collective-permute-start.24 = (bf16[768,512]{1,0:T(8,128)(2,1)S(1)}, bf16[768,512]{1,0:T(8,128)(2,1)S(1)}, u32[]{:S(2)}, u32[]{:S(2)}) collective-permute-start(bf16[768,512]{1,0:T(8,128)(2,1)S(1)} %get-tuple-element.78.refs_8_), channel_id=1, source_target_pairs={{0,8},{1,25},{2,10},{3,27},{4,12},{5,29},{6,14},{7,31},{8,16},{9,1... | collective-permute-start | bytes 2359304 | tf_op jit(solution)/shard_map/ppermute | solution.py:42
  74.0 14.6 %collective-permute-start.27 = (bf16[768,512]{1,0:T(8,128)(2,1)S(1)}, bf16[768,512]{1,0:T(8,128)(2,1)S(1)}, u32[]{:S(2)}, u32[]{:S(2)}) collective-permute-start(bf16[768,512]{1,0:T(8,128)(2,1)S(1)} %get-tuple-element.79.refs_9_), channel_id=1, source_target_pairs={{0,32},{1,97},{2,34},{3,99},{4,36},{5,101},{6,38},{7,103},{8,40},{... | collective-permute-start | bytes 2359304 | tf_op jit(solution)/shard_map/ppermute | solution.py:42
  74.2 14.5 %collective-permute-start.28 = (bf16[768,512]{1,0:T(8,128)(2,1)S(1)}, bf16[768,512]{1,0:T(8,128)(2,1)S(1)}, u32[]{:S(2)}, u32[]{:S(2)}) collective-permute-start(bf16[768,512]{1,0:T(8,128)(2,1)S(1)} %get-tuple-element.80.refs_10_), channel_id=1, source_target_pairs={{0,8},{1,25},{2,10},{3,27},{4,12},{5,29},{6,14},{7,31},{8,16},{9,1... | collective-permute-start | bytes 2359304 | tf_op jit(solution)/shard_map/ppermute | solution.py:42
  81.6 15.5 %collective-permute-start.25 = (bf16[768,512]{1,0:T(8,128)(2,1)S(1)}, bf16[768,512]{1,0:T(8,128)(2,1)S(1)}, u32[]{:S(2)}, u32[]{:S(2)}) collective-permute-start(bf16[768,512]{1,0:T(8,128)(2,1)S(1)} %get-tuple-element.83.refs_0_), channel_id=1, source_target_pairs={{0,32},{1,97},{2,34},{3,99},{4,36},{5,101},{6,38},{7,103},{8,40},{... | collective-permute-start | bytes 2359304 | tf_op jit(solution)/shard_map/ppermute | solution.py:42
  82.6 14.5 %collective-permute-start.26 = (bf16[768,512]{1,0:T(8,128)(2,1)S(1)}, bf16[768,512]{1,0:T(8,128)(2,1)S(1)}, u32[]{:S(2)}, u32[]{:S(2)}) collective-permute-start(bf16[768,512]{1,0:T(8,128)(2,1)S(1)} %get-tuple-element.84.refs_1_), channel_id=1, source_target_pairs={{0,8},{1,25},{2,10},{3,27},{4,12},{5,29},{6,14},{7,31},{8,16},{9,1... | collective-permute-start | bytes 2359304 | tf_op jit(solution)/shard_map/ppermute | solution.py:42
  90.4 7.7 %collective-permute-start.29 = (f32[768,1024]{1,0:T(8,128)S(1)}, f32[768,1024]{1,0:T(8,128)S(1)}, u32[]{:S(2)}, u32[]{:S(2)}) collective-permute-start(f32[768,1024]{1,0:T(8,128)S(1)} %shard_map.76), channel_id=1, source_target_pairs={{0,1},{1,0},{2,3},{3,2},{4,5},{5,4},{6,7},{7,6},{8,9},{9,8},{10,11... | collective-permute-start | bytes 9437192 | tf_op jit(solution)/shard_map/ppermute | solution.py:42

commit v7 on v6

--- a/solution.py
+++ b/solution.py
@@ -138,6 +138,25 @@
         compiler_params=params(1),
         cost_estimate=cost(10**6),
     )(hbm(col_bits))
+
+
+def other_rows_kernel(block, out, sems):
+    at = pl.multiple_of((1 - position()[3]) * 256, 256)
+    copy = pltpu.make_async_copy(block.at[pl.ds(at, 256), :], out, sems.at[0])
+    copy.start()
+    copy.wait()
+
+
+def other_rows(block):
+    return pl.pallas_call(
+        other_rows_kernel,
+        out_shape=pltpu.VMEM((256, block.shape[1]), block.dtype),
+        in_specs=[ANY],
+        out_specs=VM,
+        scratch_shapes=[pltpu.SemaphoreType.DMA((1,))],
+        compiler_params=params(1),
+        cost_estimate=cost(10**6),
+    )(hbm(block))
 
 
 def tversky_kernel(row_bits, row_scale, col_bits, col_scale, got_bits, out, ones):
@@ -310,7 +329,7 @@
 def shards(library_bits, library_count, landmark_bits, landmark_count, inverse_root):
     core = lax.axis_index("lmk") % NC
     mine = lax.dynamic_slice_in_dim(inverse_root, core * 256, 256, 0)
-    theirs = send(lax.dynamic_slice_in_dim(inverse_root, (1 - core) * 256, 256, 0), "core")
+    theirs = send(other_rows(inverse_root), "core")
     row_scale = 0.9 * library_count.astype(jnp.float32)[:, None]
     col_scale = 0.1 * landmark_count.astype(jnp.float32)[None, :]
     row_bits, col_bits, token = load(library_bits, landmark_bits)

time: 101 us -> 103 us (1.020)
  waiting for transfers between devices: 26.8 us -> 36.2 us
  starting transfers between devices: 41.9 us -> 32.6 us
  Pallas kernels: 29.5 us -> 32.1 us
    ppermute x30, waiting for transfers between devices: 26.8 us -> 36.2 us  [send(): return lax.ppermute(block, AXES, PAIRS[axis])]
    ppermute x30, starting transfers between devices: 41.9 us -> 32.6 us  [send(): return lax.ppermute(block, AXES, PAIRS[axis])]
    pallas_call x1, Pallas kernels: 4.01 us -> 5.61 us  [tversky(): pl.pallas_call(tversky_kernel, out_shape=pltpu.VMEM((4, rows, 256), jnp.b...]
    pallas_call x0 -> x1, Pallas kernels: none -> 1.05 us  [other_rows(): pl.pallas_call(other_rows_kernel, out_shape=pltpu.VMEM((256, block.shape[...]
  transfers between devices with their start and end apart: 30 -> 30, of which waited for: 17 -> 14; matrix products, arithmetic and copies ran while one was open for 1% -> 2% of each run, Pallas kernels for 27% -> 28%
where the time goes in v7:
time: 103 us
  waiting for transfers between devices  36.2 us (35%)
  starting transfers between devices  32.6 us (32%)
  Pallas kernels  32.1 us (31%)
  local copies, waits for them, and re-layouts  1.47 us (1%)
    ppermute x30, waiting for transfers between devices, send(): return lax.ppermute(block, AXES, PAIRS[axis])  36.2 us
    ppermute x30, starting transfers between devices, send(): return lax.ppermute(block, AXES, PAIRS[axis])  32.6 us
    pallas_call x6, Pallas kernels, sums(): pl.pallas_call(functools.partial(sum_kernel, jobs, len(rs), len(accs)), o...  18.7 us
    pallas_call x1, Pallas kernels, tversky(): pl.pallas_call(tversky_kernel, out_shape=pltpu.VMEM((4, rows, 256), jnp.b...  5.61 us
    pallas_call x1, Pallas kernels, load(): pl.pallas_call(load_kernel, out_shape=(pltpu.VMEM((rows, depth), jnp.bflo...  2.52 us
    pallas_call x1, Pallas kernels, last(): pl.pallas_call(functools.partial(last_kernel, halves, len(rs)), out_shape...  2.24 us
  transfers between devices with their start and end apart: 30, of which 14 were waited for; matrix products, arithmetic and copies ran while one was open for 2% of the time, Pallas kernels for 28%

profile of v7, /device:TPU:1, one launch (start us, length us, event | category | flops | bytes accessed | tf_op | source)
XLA Modules:
  0.0 103.1 jit_solution(14860466884175084677)
XLA Ops:
  0.0 1.0 %shard_map.56 = bf16[256,1024]{1,0:T(8,128)(2,1)S(1)} custom-call(bf16[512,1024]{1,0:T(8,128)(2,1)} %block.1), custom_call_target="tpu_custom_call" | custom-call | flops 1000000 | tf_op jit(solution)/shard_map/pallas_call | solution.py:151
  1.1 1.5 %collective-permute-start = (bf16[256,1024]{1,0:T(8,128)(2,1)S(1)}, bf16[256,1024]{1,0:T(8,128)(2,1)S(1)}, u32[]{:S(2)}, u32[]{:S(2)}) collective-permute-start(bf16[256,1024]{1,0:T(8,128)(2,1)S(1)} %shard_map.56), channel_id=1, source_target_pairs={{0,1},{1,0},{2,3},{3,2},{4,5},{5,4},{6,7},{7,6},{8,9},{9,8},{10,11... | collective-permute-start | bytes 1572872 | tf_op jit(solution)/shard_map/ppermute | solution.py:42
  2.6 1.6 %shard_map.57 = bf16[512,2048]{1,0:T(8,128)(2,1)S(1)} custom-call(bf16[1024,2048]{1,0:T(8,128)(2,1)} %col_bits.3), custom_call_target="tpu_custom_call" | custom-call | flops 1000000 | tf_op jit(solution)/shard_map/pallas_call | solution.py:132
  4.1 0.3 collective-permute-start.11
  4.5 2.8 %collective-permute-start.1 = (bf16[256,1024]{1,0:T(8,128)(2,1)S(1)}, bf16[256,1024]{1,0:T(8,128)(2,1)S(1)}, u32[]{:S(2)}, u32[]{:S(2)}) collective-permute-start(bf16[256,1024]{1,0:T(8,128)(2,1)S(1)} %collective-permute-done.refs_0_), channel_id=1, source_target_pairs={{0,8},{1,25},{2,10},{3,27},{4,12},{5,29},{6,14},{7,31},{8,16},{9,1... | collective-permute-start | bytes 1572872 | tf_op jit(solution)/shard_map/ppermute | solution.py:42
  7.3 3.8 %collective-permute-start.2 = (bf16[256,1024]{1,0:T(8,128)(2,1)S(1)}, bf16[256,1024]{1,0:T(8,128)(2,1)S(1)}, u32[]{:S(2)}, u32[]{:S(2)}) collective-permute-start(bf16[256,1024]{1,0:T(8,128)(2,1)S(1)} %collective-permute-done.refs_0_), channel_id=1, source_target_pairs={{0,32},{1,97},{2,34},{3,99},{4,36},{5,101},{6,38},{7,103},{8,40},{... | collective-permute-start | bytes 1572872 | tf_op jit(solution)/shard_map/ppermute | solution.py:42
  11.1 1.1 %constant_dynamic-slice_fusion.refs_0_ = bf16[256,1024]{1,0:T(8,128)(2,1)S(1)} fusion(bf16[512,1024]{1,0:T(8,128)(2,1)} %block.1, s32[]{:T(128)S(6)} %select_n.11), kind=kLoop, calls=%fused_computation.6 | loop fusion | bytes 1048580 | tf_op jit(solution)/shard_map/dynamic_slice | solution.py:331
  12.1 0.5 collective-permute-start.3
  13.0 2.5 %shard_map.55 = (bf16[768,2048]{1,0:T(8,128)(2,1)S(1)}, bf16[512,2048]{1,0:T(8,128)(2,1)S(1)}, bf16[16,128]{1,0:T(8,128)(2,1)S(1)}) custom-call(bf16[768,2048]{1,0:T(8,128)(2,1)} %row_bits.1, bf16[1024,2048]{1,0:T(8,128)(2,1)} %col_bits.3), custom_call_target="tpu_custom_call" | custom-call | flops 1000000 | tf_op jit(solution)/shard_map/pallas_call | solution.py:100
  15.5 5.6 %shard_map.62.refs_0_ = bf16[4,768,256]{2,1,0:T(8,128)(2,1)S(1)} custom-call(bf16[768,2048]{1,0:T(8,128)(2,1)S(1)} %get-tuple-element.59.row_bits, f32[768,1]{1,0:T(8,128)S(1)} %mul.26.row_scale, bf16[512,2048]{1,0:T(8,128)(2,1)S(1)} %get-tuple-element.60.col_bits, f32[1,1024]{1,0:T(1,128)S(1)} %bitcast.1, bf16[512,2048]{1,0:T(8,128)(2,1)} %collective-permute-done.11.got_bits), custom_call_target="tpu_custom_call" | custom-call | flops 1000000 | tf_op jit(solution)/shard_map/pallas_call | solution.py:182
  21.2 2.5 %collective-permute-start.12 = (bf16[4,768,256]{2,1,0:T(8,128)(2,1)S(1)}, bf16[4,768,256]{2,1,0:T(8,128)(2,1)S(1)}, u32[]{:S(2)}, u32[]{:S(2)}) collective-permute-start(bf16[4,768,256]{2,1,0:T(8,128)(2,1)S(1)} %shard_map.62.refs_0_), channel_id=1, source_target_pairs={{0,2},{1,7},{2,4},{3,1},{4,6},{5,3},{6,0},{7,5},{8,10},{9,15},{10,... | collective-permute-start | bytes 4718600 | tf_op jit(solution)/shard_map/ppermute | solution.py:42
  23.9 0.2 collective-permute-start.7
  24.1 2.3 %collective-permute-start.8 = (bf16[256,1024]{1,0:T(8,128)(2,1)S(1)}, bf16[256,1024]{1,0:T(8,128)(2,1)S(1)}, u32[]{:S(2)}, u32[]{:S(2)}) collective-permute-start(bf16[256,1024]{1,0:T(8,128)(2,1)S(1)} %get-tuple-element.55.refs_4_), channel_id=1, source_target_pairs={{0,32},{1,97},{2,34},{3,99},{4,36},{5,101},{6,38},{7,103},{8,40},{... | collective-permute-start | bytes 1572872 | tf_op jit(solution)/shard_map/ppermute | solution.py:42
  26.4 5.7 %collective-permute-done.5.refs_1_ = bf16[256,1024]{1,0:T(8,128)(2,1)S(1)} collective-permute-done((bf16[256,1024]{1,0:T(8,128)(2,1)S(1)}, bf16[256,1024]{1,0:T(8,128)(2,1)S(1)}, u32[]{:S(2)}, u32[]{:S(2)}) %collective-permute-start.5) | collective-permute-done | bytes 524320 | tf_op jit(solution)/shard_map/ppermute | solution.py:42
  32.2 1.2 %collective-permute-start.10 = (bf16[256,1024]{1,0:T(8,128)(2,1)S(1)}, bf16[256,1024]{1,0:T(8,128)(2,1)S(1)}, u32[]{:S(2)}, u32[]{:S(2)}) collective-permute-start(bf16[256,1024]{1,0:T(8,128)(2,1)S(1)} %get-tuple-element.58.refs_5_), channel_id=1, source_target_pairs={{0,32},{1,97},{2,34},{3,99},{4,36},{5,101},{6,38},{7,103},{8,40},{... | collective-permute-start | bytes 1572872 | tf_op jit(solution)/shard_map/ppermute | solution.py:42
  33.4 0.2 collective-permute-start.9
  33.7 4.0 %collective-permute-done.7.refs_1_ = bf16[256,1024]{1,0:T(8,128)(2,1)S(1)} collective-permute-done((bf16[256,1024]{1,0:T(8,128)(2,1)S(1)}, bf16[256,1024]{1,0:T(8,128)(2,1)S(1)}, u32[]{:S(2)}, u32[]{:S(2)}) %collective-permute-start.7) | collective-permute-done | bytes 524320 | tf_op jit(solution)/shard_map/ppermute | solution.py:42
  37.8 1.2 %collective-permute-start.14 = (bf16[256,1024]{1,0:T(8,128)(2,1)S(1)}, bf16[256,1024]{1,0:T(8,128)(2,1)S(1)}, u32[]{:S(2)}, u32[]{:S(2)}) collective-permute-start(bf16[256,1024]{1,0:T(8,128)(2,1)S(1)} %get-tuple-element.64.refs_5_), channel_id=1, source_target_pairs={{0,32},{1,97},{2,34},{3,99},{4,36},{5,101},{6,38},{7,103},{8,40},{... | collective-permute-start | bytes 1572872 | tf_op jit(solution)/shard_map/ppermute | solution.py:42
  39.1 0.2 collective-permute-start.13
  39.4 4.1 %collective-permute-done.10.refs_2_ = bf16[256,1024]{1,0:T(8,128)(2,1)S(1)} collective-permute-done((bf16[256,1024]{1,0:T(8,128)(2,1)S(1)}, bf16[256,1024]{1,0:T(8,128)(2,1)S(1)}, u32[]{:S(2)}, u32[]{:S(2)}) %collective-permute-start.10) | collective-permute-done | bytes 524320 | tf_op jit(solution)/shard_map/ppermute | solution.py:42
  43.5 1.3 %collective-permute-start.16 = (bf16[768,512]{1,0:T(8,128)(2,1)S(1)}, bf16[768,512]{1,0:T(8,128)(2,1)S(1)}, u32[]{:S(2)}, u32[]{:S(2)}) collective-permute-start(bf16[768,512]{1,0:T(8,128)(2,1)S(1)} %pad_maximum_fusion.1), channel_id=1, source_target_pairs={{0,8},{1,25},{2,10},{3,27},{4,12},{5,29},{6,14},{7,31},{8,16},{9,1... | collective-permute-start | bytes 2359304 | tf_op jit(solution)/shard_map/ppermute | solution.py:42
  44.9 0.3 collective-permute-start.15
  45.1 0.9 collective-permute-start.19
  46.0 2.9 %collective-permute-done.13.refs_1_ = bf16[256,1024]{1,0:T(8,128)(2,1)S(1)} collective-permute-done((bf16[256,1024]{1,0:T(8,128)(2,1)S(1)}, bf16[256,1024]{1,0:T(8,128)(2,1)S(1)}, u32[]{:S(2)}, u32[]{:S(2)}) %collective-permute-start.13) | collective-permute-done | bytes 524320 | tf_op jit(solution)/shard_map/ppermute | solution.py:42
  49.1 1.3 %collective-permute-start.18 = (bf16[768,512]{1,0:T(8,128)(2,1)S(1)}, bf16[768,512]{1,0:T(8,128)(2,1)S(1)}, u32[]{:S(2)}, u32[]{:S(2)}) collective-permute-start(bf16[768,512]{1,0:T(8,128)(2,1)S(1)} %pad_maximum_fusion.3), channel_id=1, source_target_pairs={{0,8},{1,25},{2,10},{3,27},{4,12},{5,29},{6,14},{7,31},{8,16},{9,1... | collective-permute-start | bytes 2359304 | tf_op jit(solution)/shard_map/ppermute | solution.py:42
  50.6 6.7 %collective-permute-done.16.refs_2_ = bf16[768,512]{1,0:T(8,128)(2,1)S(1)} collective-permute-done((bf16[768,512]{1,0:T(8,128)(2,1)S(1)}, bf16[768,512]{1,0:T(8,128)(2,1)S(1)}, u32[]{:S(2)}, u32[]{:S(2)}) %collective-permute-start.16) | collective-permute-done | bytes 786464 | tf_op jit(solution)/shard_map/ppermute | solution.py:42
  57.5 1.2 %collective-permute-start.21 = (bf16[768,512]{1,0:T(8,128)(2,1)S(1)}, bf16[768,512]{1,0:T(8,128)(2,1)S(1)}, u32[]{:S(2)}, u32[]{:S(2)}) collective-permute-start(bf16[768,512]{1,0:T(8,128)(2,1)S(1)} %get-tuple-element.74.refs_7_), channel_id=1, source_target_pairs={{0,32},{1,97},{2,34},{3,99},{4,36},{5,101},{6,38},{7,103},{8,40},{... | collective-permute-start | bytes 2359304 | tf_op jit(solution)/shard_map/ppermute | solution.py:42
  58.7 1.2 %collective-permute-start.22 = (bf16[768,512]{1,0:T(8,128)(2,1)S(1)}, bf16[768,512]{1,0:T(8,128)(2,1)S(1)}, u32[]{:S(2)}, u32[]{:S(2)}) collective-permute-start(bf16[768,512]{1,0:T(8,128)(2,1)S(1)} %get-tuple-element.75.refs_8_), channel_id=1, source_target_pairs={{0,8},{1,25},{2,10},{3,27},{4,12},{5,29},{6,14},{7,31},{8,16},{9,1... | collective-permute-start | bytes 2359304 | tf_op jit(solution)/shard_map/ppermute | solution.py:42
  59.9 5.8 %collective-permute-done.18.refs_2_ = bf16[768,512]{1,0:T(8,128)(2,1)S(1)} collective-permute-done((bf16[768,512]{1,0:T(8,128)(2,1)S(1)}, bf16[768,512]{1,0:T(8,128)(2,1)S(1)}, u32[]{:S(2)}, u32[]{:S(2)}) %collective-permute-start.18) | collective-permute-done | bytes 786464 | tf_op jit(solution)/shard_map/ppermute | solution.py:42
  65.9 0.9 collective-permute-start.20
  66.8 1.2 %collective-permute-start.23 = (bf16[768,512]{1,0:T(8,128)(2,1)S(1)}, bf16[768,512]{1,0:T(8,128)(2,1)S(1)}, u32[]{:S(2)}, u32[]{:S(2)}) collective-permute-start(bf16[768,512]{1,0:T(8,128)(2,1)S(1)} %get-tuple-element.77.refs_7_), channel_id=1, source_target_pairs={{0,32},{1,97},{2,34},{3,99},{4,36},{5,101},{6,38},{7,103},{8,40},{... | collective-permute-start | bytes 2359304 | tf_op jit(solution)/shard_map/ppermute | solution.py:42
  68.0 0.9 collective-permute-start.24
  68.9 0.3 shard_map.67.refs_1_.k
  69.3 5.2 %shard_map.69.refs_3_ = f32[768,1024]{1,0:T(8,128)S(1)} custom-call(bf16[16,768,256]{2,1,0:T(8,128)(2,1)S(1)} %shard_map.67.refs_1_.k, bf16[256,1024]{1,0:T(8,128)(2,1)S(1)} %collective-permute-done.refs_0_, bf16[256,1024]{1,0:T(8,128)(2,1)S(1)} %get-tuple-element.51.refs_1_, bf16[256,1024]{1,0:T(8,128)(2,1)S(1)} %get-tuple-element.57.refs_2_, ...), custom_call_target="tpu_custom_call" | custom-call | flops 1000000 | tf_op jit(solution)/shard_map/pallas_call | solution.py:281
  74.5 1.3 %collective-permute-start.27 = (bf16[768,512]{1,0:T(8,128)(2,1)S(1)}, bf16[768,512]{1,0:T(8,128)(2,1)S(1)}, u32[]{:S(2)}, u32[]{:S(2)}) collective-permute-start(bf16[768,512]{1,0:T(8,128)(2,1)S(1)} %get-tuple-element.79.refs_9_), channel_id=1, source_target_pairs={{0,32},{1,97},{2,34},{3,99},{4,36},{5,101},{6,38},{7,103},{8,40},{... | collective-permute-start | bytes 2359304 | tf_op jit(solution)/shard_map/ppermute | solution.py:42
  75.8 0.7 collective-permute-start.28
  76.5 7.2 %shard_map.71 = (f32[768,1024]{1,0:T(8,128)S(1)}, f32[768,1024]{1,0:T(8,128)S(1)}) custom-call(bf16[16,768,256]{2,1,0:T(8,128)(2,1)S(1)} %shard_map.67.refs_1_.k, bf16[256,1024]{1,0:T(8,128)(2,1)S(1)} %constant_dynamic-slice_fusion.refs_0_, bf16[256,1024]{1,0:T(8,128)(2,1)S(1)} %get-tuple-element.54.refs_1_, ...), custom_call_target="tpu_custom_call", output_to_operand_aliasing={{1}: (12, {})} | custom-call | flops 1000000 | tf_op jit(solution)/shard_map/pallas_call | solution.py:281
  83.7 1.2 %collective-permute-start.25 = (bf16[768,512]{1,0:T(8,128)(2,1)S(1)}, bf16[768,512]{1,0:T(8,128)(2,1)S(1)}, u32[]{:S(2)}, u32[]{:S(2)}) collective-permute-start(bf16[768,512]{1,0:T(8,128)(2,1)S(1)} %get-tuple-element.83.refs_0_), channel_id=1, source_target_pairs={{0,32},{1,97},{2,34},{3,99},{4,36},{5,101},{6,38},{7,103},{8,40},{... | collective-permute-start | bytes 2359304 | tf_op jit(solution)/shard_map/ppermute | solution.py:42
  84.9 0.6 collective-permute-start.26
  85.7 1.5 %shard_map.76.refs_2_ = f32[768,1024]{1,0:T(8,128)S(1)} custom-call(bf16[16,768,256]{2,1,0:T(8,128)(2,1)S(1)} %shard_map.68.k, bf16[256,1024]{1,0:T(8,128)(2,1)S(1)} %collective-permute-done.refs_0_, bf16[256,1024]{1,0:T(8,128)(2,1)S(1)} %get-tuple-element.51.refs_1_, ...), custom_call_target="tpu_custom_call", output_to_operand_aliasing={{}: (12, {})} | custom-call | flops 1000000 | tf_op jit(solution)/shard_map/pallas_call | solution.py:281
  87.2 4.0 %collective-permute-done.27.refs_0_ = bf16[768,512]{1,0:T(8,128)(2,1)S(1)} collective-permute-done((bf16[768,512]{1,0:T(8,128)(2,1)S(1)}, bf16[768,512]{1,0:T(8,128)(2,1)S(1)}, u32[]{:S(2)}, u32[]{:S(2)}) %collective-permute-start.27) | collective-permute-done | bytes 786464 | tf_op jit(solution)/shard_map/ppermute | solution.py:42
  91.2 1.8 %shard_map.77 = f32[768,1024]{1,0:T(8,128)S(1)} custom-call(bf16[16,768,256]{2,1,0:T(8,128)(2,1)S(1)} %shard_map.68.k, bf16[768,512]{1,0:T(8,128)(2,1)S(1)} %collective-permute-done.27.refs_0_, bf16[768,512]{1,0:T(8,128)(2,1)S(1)} %collective-permute-done.28.refs_1_, f32[768,1024]{1,0:T(8,128)S(1)} %shard_map.76.refs_2_), custom_call_target="tpu_custom_call", output_to_operand_aliasing={{}: (3, {})} | custom-call | flops 1000000 | tf_op jit(solution)/shard_map/pallas_call | solution.py:281
  93.0 2.4 %collective-permute-start.29 = (f32[768,1024]{1,0:T(8,128)S(1)}, f32[768,1024]{1,0:T(8,128)S(1)}, u32[]{:S(2)}, u32[]{:S(2)}) collective-permute-start(f32[768,1024]{1,0:T(8,128)S(1)} %shard_map.77), channel_id=1, source_target_pairs={{0,1},{1,0},{2,3},{3,2},{4,5},{5,4},{6,7},{7,6},{8,9},{9,8},{10,11... | collective-permute-start | bytes 9437192 | tf_op jit(solution)/shard_map/ppermute | solution.py:42
  95.4 1.2 %shard_map.74.refs_2_ = f32[768,1024]{1,0:T(8,128)S(1)} custom-call(bf16[16,768,256]{2,1,0:T(8,128)(2,1)S(1)} %shard_map.68.k, bf16[256,1024]{1,0:T(8,128)(2,1)S(1)} %constant_dynamic-slice_fusion.refs_0_, bf16[256,1024]{1,0:T(8,128)(2,1)S(1)} %get-tuple-element.54.refs_1_, ...), custom_call_target="tpu_custom_call", output_to_operand_aliasing={{}: (10, {})} | custom-call | flops 1000000 | tf_op jit(solution)/shard_map/pallas_call | solution.py:281
  96.6 1.8 %shard_map.75.refs_2_ = f32[768,1024]{1,0:T(8,128)S(1)} custom-call(bf16[16,768,256]{2,1,0:T(8,128)(2,1)S(1)} %shard_map.68.k, bf16[768,512]{1,0:T(8,128)(2,1)S(1)} %get-tuple-element.83.refs_0_, bf16[768,512]{1,0:T(8,128)(2,1)S(1)} %get-tuple-element.84.refs_1_, f32[768,1024]{1,0:T(8,128)S(1)} %shard_map.74.refs_2_), custom_call_target="tpu_custom_call", output_to_operand_aliasing={{}: (3, {})} | custom-call | flops 1000000 | tf_op jit(solution)/shard_map/pallas_call | solution.py:281
  98.4 1.2 %collective-permute-done.25.refs_0_ = bf16[768,512]{1,0:T(8,128)(2,1)S(1)} collective-permute-done((bf16[768,512]{1,0:T(8,128)(2,1)S(1)}, bf16[768,512]{1,0:T(8,128)(2,1)S(1)}, u32[]{:S(2)}, u32[]{:S(2)}) %collective-permute-start.25) | collective-permute-done | bytes 786464 | tf_op jit(solution)/shard_map/ppermute | solution.py:42
  99.6 1.1 %collective-permute-done.29.refs_3_ = f32[768,1024]{1,0:T(8,128)S(1)} collective-permute-done((f32[768,1024]{1,0:T(8,128)S(1)}, f32[768,1024]{1,0:T(8,128)S(1)}, u32[]{:S(2)}, u32[]{:S(2)}) %collective-permute-start.29) | collective-permute-done | bytes 3145760 | tf_op jit(solution)/shard_map/ppermute | solution.py:42
  100.7 2.2 %shard_map.78 = f32[768,1024]{1,0:T(8,128)} custom-call(bf16[16,768,256]{2,1,0:T(8,128)(2,1)S(1)} %shard_map.68.k, bf16[768,512]{1,0:T(8,128)(2,1)S(1)} %get-tuple-element.85.refs_0_, bf16[768,512]{1,0:T(8,128)(2,1)S(1)} %get-tuple-element.86.refs_1_, f32[768,1024]{1,0:T(8,128)S(1)} %shard_map.75.refs_2_, f32[768,1024]{1,0:T(8,128)S(1)} %collective-permute-done.29.refs_3_), custom_call_target="tpu_custom_call" | custom-call | flops 1000000 | tf_op jit(solution)/shard_map/pallas_call | solution.py:318
  (60 shorter events, 2.0 us)
Async XLA Ops:
  1.1 11.7 %copy-start = (s32[768]{0:T(1024)S(1)}, s32[768]{0:T(1024)}, u32[]{:S(2)}) copy-start(s32[768]{0:T(1024)} %param.6) | copy-start | bytes 9220
  1.1 3.1 %collective-permute-start = (bf16[256,1024]{1,0:T(8,128)(2,1)S(1)}, bf16[256,1024]{1,0:T(8,128)(2,1)S(1)}, u32[]{:S(2)}, u32[]{:S(2)}) collective-permute-start(bf16[256,1024]{1,0:T(8,128)(2,1)S(1)} %shard_map.56), channel_id=1, source_target_pairs={{0,1},{1,0},{2,3},{3,2},{4,5},{5,4},{6,7},{7,6},{8,9},{9,8},{10,11... | collective-permute-start | bytes 1572872 | tf_op jit(solution)/shard_map/ppermute | solution.py:42
  4.1 11.4 %collective-permute-start.11 = (bf16[512,2048]{1,0:T(8,128)(2,1)S(1)}, bf16[512,2048]{1,0:T(8,128)(2,1)}, u32[]{:S(2)}, u32[]{:S(2)}) collective-permute-start(bf16[512,2048]{1,0:T(8,128)(2,1)S(1)} %shard_map.57), channel_id=1, source_target_pairs={{0,1},{1,0},{2,3},{3,2},{4,5},{5,4},{6,7},{7,6},{8,9},{9,8},{10,11... | collective-permute-start | bytes 6291464 | tf_op jit(solution)/shard_map/ppermute | solution.py:42
  4.5 19.2 %collective-permute-start.1 = (bf16[256,1024]{1,0:T(8,128)(2,1)S(1)}, bf16[256,1024]{1,0:T(8,128)(2,1)S(1)}, u32[]{:S(2)}, u32[]{:S(2)}) collective-permute-start(bf16[256,1024]{1,0:T(8,128)(2,1)S(1)} %collective-permute-done.refs_0_), channel_id=1, source_target_pairs={{0,8},{1,25},{2,10},{3,27},{4,12},{5,29},{6,14},{7,31},{8,16},{9,1... | collective-permute-start | bytes 1572872 | tf_op jit(solution)/shard_map/ppermute | solution.py:42
  7.3 16.4 %collective-permute-start.2 = (bf16[256,1024]{1,0:T(8,128)(2,1)S(1)}, bf16[256,1024]{1,0:T(8,128)(2,1)S(1)}, u32[]{:S(2)}, u32[]{:S(2)}) collective-permute-start(bf16[256,1024]{1,0:T(8,128)(2,1)S(1)} %collective-permute-done.refs_0_), channel_id=1, source_target_pairs={{0,32},{1,97},{2,34},{3,99},{4,36},{5,101},{6,38},{7,103},{8,40},{... | collective-permute-start | bytes 1572872 | tf_op jit(solution)/shard_map/ppermute | solution.py:42
  12.1 11.7 %collective-permute-start.3 = (bf16[256,1024]{1,0:T(8,128)(2,1)S(1)}, bf16[256,1024]{1,0:T(8,128)(2,1)S(1)}, u32[]{:S(2)}, u32[]{:S(2)}) collective-permute-start(bf16[256,1024]{1,0:T(8,128)(2,1)S(1)} %constant_dynamic-slice_fusion.refs_0_), channel_id=1, source_target_pairs={{0,8},{1,25},{2,10},{3,27},{4,12},{5,29},{6,14},{7,31},{8,16},{9,1... | collective-permute-start | bytes 1572872 | tf_op jit(solution)/shard_map/ppermute | solution.py:42
  12.7 11.2 %collective-permute-start.4 = (bf16[256,1024]{1,0:T(8,128)(2,1)S(1)}, bf16[256,1024]{1,0:T(8,128)(2,1)S(1)}, u32[]{:S(2)}, u32[]{:S(2)}) collective-permute-start(bf16[256,1024]{1,0:T(8,128)(2,1)S(1)} %constant_dynamic-slice_fusion.refs_0_), channel_id=1, source_target_pairs={{0,32},{1,97},{2,34},{3,99},{4,36},{5,101},{6,38},{7,103},{8,40},{... | collective-permute-start | bytes 1572872 | tf_op jit(solution)/shard_map/ppermute | solution.py:42
  13.0 2.5 %copy-start.1 = (s32[1024]{0:T(1024)S(1)}, s32[1024]{0:T(1024)}, u32[]{:S(2)}) copy-start(s32[1024]{0:T(1024)} %param.8) | copy-start | bytes 12292
  21.2 22.3 %collective-permute-start.12 = (bf16[4,768,256]{2,1,0:T(8,128)(2,1)S(1)}, bf16[4,768,256]{2,1,0:T(8,128)(2,1)S(1)}, u32[]{:S(2)}, u32[]{:S(2)}) collective-permute-start(bf16[4,768,256]{2,1,0:T(8,128)(2,1)S(1)} %shard_map.62.refs_0_), channel_id=1, source_target_pairs={{0,2},{1,7},{2,4},{3,1},{4,6},{5,3},{6,0},{7,5},{8,10},{9,15},{10,... | collective-permute-start | bytes 4718600 | tf_op jit(solution)/shard_map/ppermute | solution.py:42
  23.7 8.3 %collective-permute-start.5 = (bf16[256,1024]{1,0:T(8,128)(2,1)S(1)}, bf16[256,1024]{1,0:T(8,128)(2,1)S(1)}, u32[]{:S(2)}, u32[]{:S(2)}) collective-permute-start(bf16[256,1024]{1,0:T(8,128)(2,1)S(1)} %get-tuple-element.51.refs_1_), channel_id=1, source_target_pairs={{0,8},{1,25},{2,10},{3,27},{4,12},{5,29},{6,14},{7,31},{8,16},{9,1... | collective-permute-start | bytes 1572872 | tf_op jit(solution)/shard_map/ppermute | solution.py:42
  23.9 8.3 %collective-permute-start.6 = (bf16[256,1024]{1,0:T(8,128)(2,1)S(1)}, bf16[256,1024]{1,0:T(8,128)(2,1)S(1)}, u32[]{:S(2)}, u32[]{:S(2)}) collective-permute-start(bf16[256,1024]{1,0:T(8,128)(2,1)S(1)} %get-tuple-element.52.refs_4_), channel_id=1, source_target_pairs={{0,32},{1,97},{2,34},{3,99},{4,36},{5,101},{6,38},{7,103},{8,40},{... | collective-permute-start | bytes 1572872 | tf_op jit(solution)/shard_map/ppermute | solution.py:42
  23.9 13.8 %collective-permute-start.7 = (bf16[256,1024]{1,0:T(8,128)(2,1)S(1)}, bf16[256,1024]{1,0:T(8,128)(2,1)S(1)}, u32[]{:S(2)}, u32[]{:S(2)}) collective-permute-start(bf16[256,1024]{1,0:T(8,128)(2,1)S(1)} %get-tuple-element.54.refs_1_), channel_id=1, source_target_pairs={{0,8},{1,25},{2,10},{3,27},{4,12},{5,29},{6,14},{7,31},{8,16},{9,1... | collective-permute-start | bytes 1572872 | tf_op jit(solution)/shard_map/ppermute | solution.py:42
  24.1 13.7 %collective-permute-start.8 = (bf16[256,1024]{1,0:T(8,128)(2,1)S(1)}, bf16[256,1024]{1,0:T(8,128)(2,1)S(1)}, u32[]{:S(2)}, u32[]{:S(2)}) collective-permute-start(bf16[256,1024]{1,0:T(8,128)(2,1)S(1)} %get-tuple-element.55.refs_4_), channel_id=1, source_target_pairs={{0,32},{1,97},{2,34},{3,99},{4,36},{5,101},{6,38},{7,103},{8,40},{... | collective-permute-start | bytes 1572872 | tf_op jit(solution)/shard_map/ppermute | solution.py:42
  32.2 11.2 %collective-permute-start.10 = (bf16[256,1024]{1,0:T(8,128)(2,1)S(1)}, bf16[256,1024]{1,0:T(8,128)(2,1)S(1)}, u32[]{:S(2)}, u32[]{:S(2)}) collective-permute-start(bf16[256,1024]{1,0:T(8,128)(2,1)S(1)} %get-tuple-element.58.refs_5_), channel_id=1, source_target_pairs={{0,32},{1,97},{2,34},{3,99},{4,36},{5,101},{6,38},{7,103},{8,40},{... | collective-permute-start | bytes 1572872 | tf_op jit(solution)/shard_map/ppermute | solution.py:42
  33.4 10.0 %collective-permute-start.9 = (bf16[256,1024]{1,0:T(8,128)(2,1)S(1)}, bf16[256,1024]{1,0:T(8,128)(2,1)S(1)}, u32[]{:S(2)}, u32[]{:S(2)}) collective-permute-start(bf16[256,1024]{1,0:T(8,128)(2,1)S(1)} %get-tuple-element.57.refs_2_), channel_id=1, source_target_pairs={{0,8},{1,25},{2,10},{3,27},{4,12},{5,29},{6,14},{7,31},{8,16},{9,1... | collective-permute-start | bytes 1572872 | tf_op jit(solution)/shard_map/ppermute | solution.py:42
  37.8 11.2 %collective-permute-start.14 = (bf16[256,1024]{1,0:T(8,128)(2,1)S(1)}, bf16[256,1024]{1,0:T(8,128)(2,1)S(1)}, u32[]{:S(2)}, u32[]{:S(2)}) collective-permute-start(bf16[256,1024]{1,0:T(8,128)(2,1)S(1)} %get-tuple-element.64.refs_5_), channel_id=1, source_target_pairs={{0,32},{1,97},{2,34},{3,99},{4,36},{5,101},{6,38},{7,103},{8,40},{... | collective-permute-start | bytes 1572872 | tf_op jit(solution)/shard_map/ppermute | solution.py:42
  39.1 9.8 %collective-permute-start.13 = (bf16[256,1024]{1,0:T(8,128)(2,1)S(1)}, bf16[256,1024]{1,0:T(8,128)(2,1)S(1)}, u32[]{:S(2)}, u32[]{:S(2)}) collective-permute-start(bf16[256,1024]{1,0:T(8,128)(2,1)S(1)} %get-tuple-element.63.refs_2_), channel_id=1, source_target_pairs={{0,8},{1,25},{2,10},{3,27},{4,12},{5,29},{6,14},{7,31},{8,16},{9,1... | collective-permute-start | bytes 1572872 | tf_op jit(solution)/shard_map/ppermute | solution.py:42
  43.5 13.8 %collective-permute-start.16 = (bf16[768,512]{1,0:T(8,128)(2,1)S(1)}, bf16[768,512]{1,0:T(8,128)(2,1)S(1)}, u32[]{:S(2)}, u32[]{:S(2)}) collective-permute-start(bf16[768,512]{1,0:T(8,128)(2,1)S(1)} %pad_maximum_fusion.1), channel_id=1, source_target_pairs={{0,8},{1,25},{2,10},{3,27},{4,12},{5,29},{6,14},{7,31},{8,16},{9,1... | collective-permute-start | bytes 2359304 | tf_op jit(solution)/shard_map/ppermute | solution.py:42
  44.9 12.6 %collective-permute-start.15 = (bf16[768,512]{1,0:T(8,128)(2,1)S(1)}, bf16[768,512]{1,0:T(8,128)(2,1)S(1)}, u32[]{:S(2)}, u32[]{:S(2)}) collective-permute-start(bf16[768,512]{1,0:T(8,128)(2,1)S(1)} %pad_maximum_fusion), channel_id=1, source_target_pairs={{0,32},{1,97},{2,34},{3,99},{4,36},{5,101},{6,38},{7,103},{8,40},{... | collective-permute-start | bytes 2359304 | tf_op jit(solution)/shard_map/ppermute | solution.py:42
  45.1 20.8 %collective-permute-start.19 = (bf16[4,768,256]{2,1,0:T(8,128)(2,1)S(1)}, bf16[4,768,256]{2,1,0:T(8,128)(2,1)S(1)}, u32[]{:S(2)}, u32[]{:S(2)}) collective-permute-start(bf16[4,768,256]{2,1,0:T(8,128)(2,1)S(1)} %get-tuple-element.71.refs_1_), channel_id=1, source_target_pairs={{0,2},{1,7},{2,4},{3,1},{4,6},{5,3},{6,0},{7,5},{8,10},{9,15},{10,... | collective-permute-start | bytes 4718600 | tf_op jit(solution)/shard_map/ppermute | solution.py:42
  49.1 16.6 %collective-permute-start.18 = (bf16[768,512]{1,0:T(8,128)(2,1)S(1)}, bf16[768,512]{1,0:T(8,128)(2,1)S(1)}, u32[]{:S(2)}, u32[]{:S(2)}) collective-permute-start(bf16[768,512]{1,0:T(8,128)(2,1)S(1)} %pad_maximum_fusion.3), channel_id=1, source_target_pairs={{0,8},{1,25},{2,10},{3,27},{4,12},{5,29},{6,14},{7,31},{8,16},{9,1... | collective-permute-start | bytes 2359304 | tf_op jit(solution)/shard_map/ppermute | solution.py:42
  50.5 15.4 %collective-permute-start.17 = (bf16[768,512]{1,0:T(8,128)(2,1)S(1)}, bf16[768,512]{1,0:T(8,128)(2,1)S(1)}, u32[]{:S(2)}, u32[]{:S(2)}) collective-permute-start(bf16[768,512]{1,0:T(8,128)(2,1)S(1)} %pad_maximum_fusion.2), channel_id=1, source_target_pairs={{0,32},{1,97},{2,34},{3,99},{4,36},{5,101},{6,38},{7,103},{8,40},{... | collective-permute-start | bytes 2359304 | tf_op jit(solution)/shard_map/ppermute | solution.py:42
  57.5 17.0 %collective-permute-start.21 = (bf16[768,512]{1,0:T(8,128)(2,1)S(1)}, bf16[768,512]{1,0:T(8,128)(2,1)S(1)}, u32[]{:S(2)}, u32[]{:S(2)}) collective-permute-start(bf16[768,512]{1,0:T(8,128)(2,1)S(1)} %get-tuple-element.74.refs_7_), channel_id=1, source_target_pairs={{0,32},{1,97},{2,34},{3,99},{4,36},{5,101},{6,38},{7,103},{8,40},{... | collective-permute-start | bytes 2359304 | tf_op jit(solution)/shard_map/ppermute | solution.py:42
  58.7 15.8 %collective-permute-start.22 = (bf16[768,512]{1,0:T(8,128)(2,1)S(1)}, bf16[768,512]{1,0:T(8,128)(2,1)S(1)}, u32[]{:S(2)}, u32[]{:S(2)}) collective-permute-start(bf16[768,512]{1,0:T(8,128)(2,1)S(1)} %get-tuple-element.75.refs_8_), channel_id=1, source_target_pairs={{0,8},{1,25},{2,10},{3,27},{4,12},{5,29},{6,14},{7,31},{8,16},{9,1... | collective-permute-start | bytes 2359304 | tf_op jit(solution)/shard_map/ppermute | solution.py:42
  65.9 19.7 %collective-permute-start.20 = (bf16[4,768,256]{2,1,0:T(8,128)(2,1)S(1)}, bf16[4,768,256]{2,1,0:T(8,128)(2,1)S(1)}, u32[]{:S(2)}, u32[]{:S(2)}) collective-permute-start(bf16[4,768,256]{2,1,0:T(8,128)(2,1)S(1)} %get-tuple-element.72.refs_2_), channel_id=1, source_target_pairs={{0,2},{1,7},{2,4},{3,1},{4,6},{5,3},{6,0},{7,5},{8,10},{9,15},{10,... | collective-permute-start | bytes 4718600 | tf_op jit(solution)/shard_map/ppermute | solution.py:42
  66.8 16.9 %collective-permute-start.23 = (bf16[768,512]{1,0:T(8,128)(2,1)S(1)}, bf16[768,512]{1,0:T(8,128)(2,1)S(1)}, u32[]{:S(2)}, u32[]{:S(2)}) collective-permute-start(bf16[768,512]{1,0:T(8,128)(2,1)S(1)} %get-tuple-element.77.refs_7_), channel_id=1, source_target_pairs={{0,32},{1,97},{2,34},{3,99},{4,36},{5,101},{6,38},{7,103},{8,40},{... | collective-permute-start | bytes 2359304 | tf_op jit(solution)/shard_map/ppermute | solution.py:42
  68.0 15.7 %collective-permute-start.24 = (bf16[768,512]{1,0:T(8,128)(2,1)S(1)}, bf16[768,512]{1,0:T(8,128)(2,1)S(1)}, u32[]{:S(2)}, u32[]{:S(2)}) collective-permute-start(bf16[768,512]{1,0:T(8,128)(2,1)S(1)} %get-tuple-element.78.refs_8_), channel_id=1, source_target_pairs={{0,8},{1,25},{2,10},{3,27},{4,12},{5,29},{6,14},{7,31},{8,16},{9,1... | collective-permute-start | bytes 2359304 | tf_op jit(solution)/shard_map/ppermute | solution.py:42
  74.5 16.6 %collective-permute-start.27 = (bf16[768,512]{1,0:T(8,128)(2,1)S(1)}, bf16[768,512]{1,0:T(8,128)(2,1)S(1)}, u32[]{:S(2)}, u32[]{:S(2)}) collective-permute-start(bf16[768,512]{1,0:T(8,128)(2,1)S(1)} %get-tuple-element.79.refs_9_), channel_id=1, source_target_pairs={{0,32},{1,97},{2,34},{3,99},{4,36},{5,101},{6,38},{7,103},{8,40},{... | collective-permute-start | bytes 2359304 | tf_op jit(solution)/shard_map/ppermute | solution.py:42
  75.8 15.4 %collective-permute-start.28 = (bf16[768,512]{1,0:T(8,128)(2,1)S(1)}, bf16[768,512]{1,0:T(8,128)(2,1)S(1)}, u32[]{:S(2)}, u32[]{:S(2)}) collective-permute-start(bf16[768,512]{1,0:T(8,128)(2,1)S(1)} %get-tuple-element.80.refs_10_), channel_id=1, source_target_pairs={{0,8},{1,25},{2,10},{3,27},{4,12},{5,29},{6,14},{7,31},{8,16},{9,1... | collective-permute-start | bytes 2359304 | tf_op jit(solution)/shard_map/ppermute | solution.py:42
  83.7 15.9 %collective-permute-start.25 = (bf16[768,512]{1,0:T(8,128)(2,1)S(1)}, bf16[768,512]{1,0:T(8,128)(2,1)S(1)}, u32[]{:S(2)}, u32[]{:S(2)}) collective-permute-start(bf16[768,512]{1,0:T(8,128)(2,1)S(1)} %get-tuple-element.83.refs_0_), channel_id=1, source_target_pairs={{0,32},{1,97},{2,34},{3,99},{4,36},{5,101},{6,38},{7,103},{8,40},{... | collective-permute-start | bytes 2359304 | tf_op jit(solution)/shard_map/ppermute | solution.py:42
  84.9 14.7 %collective-permute-start.26 = (bf16[768,512]{1,0:T(8,128)(2,1)S(1)}, bf16[768,512]{1,0:T(8,128)(2,1)S(1)}, u32[]{:S(2)}, u32[]{:S(2)}) collective-permute-start(bf16[768,512]{1,0:T(8,128)(2,1)S(1)} %get-tuple-element.84.refs_1_), channel_id=1, source_target_pairs={{0,8},{1,25},{2,10},{3,27},{4,12},{5,29},{6,14},{7,31},{8,16},{9,1... | collective-permute-start | bytes 2359304 | tf_op jit(solution)/shard_map/ppermute | solution.py:42
  93.0 7.7 %collective-permute-start.29 = (f32[768,1024]{1,0:T(8,128)S(1)}, f32[768,1024]{1,0:T(8,128)S(1)}, u32[]{:S(2)}, u32[]{:S(2)}) collective-permute-start(f32[768,1024]{1,0:T(8,128)S(1)} %shard_map.77), channel_id=1, source_target_pairs={{0,1},{1,0},{2,3},{3,2},{4,5},{5,4},{6,7},{7,6},{8,9},{9,8},{10,11... | collective-permute-start | bytes 9437192 | tf_op jit(solution)/shard_map/ppermute | solution.py:42

commit v8 on v6

--- a/solution.py
+++ b/solution.py
@@ -252,7 +252,7 @@
 
         return carry
 
-    lax.fori_loop(0, outs[0].shape[0] // TILE, tile, 0)
+    lax.fori_loop(0, outs[0].shape[0] // TILE, tile, 0, unroll=all(job[1] is None for job in jobs))
 
 
 def sums(jobs, rs, k, accs):

time: 101 us -> 101 us (level)
  no operation moved by 1% of the time
where the time goes in v8:
time: 101 us
  starting transfers between devices  42.1 us (42%)
  Pallas kernels  29 us (29%)
  waiting for transfers between devices  27.1 us (27%)
  local copies, waits for them, and re-layouts  1.66 us (2%)
    ppermute x30, starting transfers between devices, send(): return lax.ppermute(block, AXES, PAIRS[axis])  42.1 us
    ppermute x30, waiting for transfers between devices, send(): return lax.ppermute(block, AXES, PAIRS[axis])  27.1 us
    pallas_call x6, Pallas kernels, sums(): pl.pallas_call(functools.partial(sum_kernel, jobs, len(rs), len(accs)), o...  18.2 us
    pallas_call x1, Pallas kernels, tversky(): pl.pallas_call(tversky_kernel, out_shape=pltpu.VMEM((4, rows, 256), jnp.b...  4.01 us
    pallas_call x1, Pallas kernels, load(): pl.pallas_call(load_kernel, out_shape=(pltpu.VMEM((rows, depth), jnp.bflo...  2.52 us
    pallas_call x1, Pallas kernels, last(): pl.pallas_call(functools.partial(last_kernel, halves, len(rs)), out_shape...  2.24 us
  transfers between devices with their start and end apart: 30, of which 17 were waited for; matrix products, arithmetic and copies ran while one was open for 1% of the time, Pallas kernels for 27%

profile of v8, /device:TPU:1, one launch (start us, length us, event | category | flops | bytes accessed | tf_op | source)
XLA Modules:
  0.0 100.5 jit_solution(11518801867779995416)
XLA Ops:
  0.0 1.3 %constant_dynamic-slice_fusion = (bf16[256,1024]{1,0:T(8,128)(2,1)S(1)}, bf16[256,1024]{1,0:T(8,128)(2,1)S(1)}) fusion(bf16[512,1024]{1,0:T(8,128)(2,1)} %param.9, s32[]{:T(128)S(6)} %select_n.15, s32[]{:T(128)S(6)} %select_n.14), kind=kLoop, calls=%fused_computation.6 | loop fusion | bytes 2097160 | tf_op jit(solution)/shard_map/dynamic_slice | solution.py:312
  1.3 1.5 %collective-permute-start = (bf16[256,1024]{1,0:T(8,128)(2,1)S(1)}, bf16[256,1024]{1,0:T(8,128)(2,1)S(1)}, u32[]{:S(2)}, u32[]{:S(2)}) collective-permute-start(bf16[256,1024]{1,0:T(8,128)(2,1)S(1)} %get-tuple-element.90), channel_id=1, source_target_pairs={{0,1},{1,0},{2,3},{3,2},{4,5},{5,4},{6,7},{7,6},{8,9},{9,8},{10,11... | collective-permute-start | bytes 1572872 | tf_op jit(solution)/shard_map/ppermute | solution.py:42
  2.8 1.6 %shard_map.56 = bf16[512,2048]{1,0:T(8,128)(2,1)S(1)} custom-call(bf16[1024,2048]{1,0:T(8,128)(2,1)} %col_bits.3), custom_call_target="tpu_custom_call" | custom-call | flops 1000000 | tf_op jit(solution)/shard_map/pallas_call | solution.py:132
  4.4 0.3 collective-permute-start.11
  4.7 2.8 %collective-permute-start.1 = (bf16[256,1024]{1,0:T(8,128)(2,1)S(1)}, bf16[256,1024]{1,0:T(8,128)(2,1)S(1)}, u32[]{:S(2)}, u32[]{:S(2)}) collective-permute-start(bf16[256,1024]{1,0:T(8,128)(2,1)S(1)} %collective-permute-done.refs_0_), channel_id=1, source_target_pairs={{0,8},{1,25},{2,10},{3,27},{4,12},{5,29},{6,14},{7,31},{8,16},{9,1... | collective-permute-start | bytes 1572872 | tf_op jit(solution)/shard_map/ppermute | solution.py:42
  7.5 3.8 %collective-permute-start.2 = (bf16[256,1024]{1,0:T(8,128)(2,1)S(1)}, bf16[256,1024]{1,0:T(8,128)(2,1)S(1)}, u32[]{:S(2)}, u32[]{:S(2)}) collective-permute-start(bf16[256,1024]{1,0:T(8,128)(2,1)S(1)} %collective-permute-done.refs_0_), channel_id=1, source_target_pairs={{0,32},{1,97},{2,34},{3,99},{4,36},{5,101},{6,38},{7,103},{8,40},{... | collective-permute-start | bytes 1572872 | tf_op jit(solution)/shard_map/ppermute | solution.py:42
  11.3 0.5 collective-permute-start.3
  12.0 2.5 %shard_map.55 = (bf16[768,2048]{1,0:T(8,128)(2,1)S(1)}, bf16[512,2048]{1,0:T(8,128)(2,1)S(1)}, bf16[16,128]{1,0:T(8,128)(2,1)S(1)}) custom-call(bf16[768,2048]{1,0:T(8,128)(2,1)} %row_bits.1, bf16[1024,2048]{1,0:T(8,128)(2,1)} %col_bits.3), custom_call_target="tpu_custom_call" | custom-call | flops 1000000 | tf_op jit(solution)/shard_map/pallas_call | solution.py:100
  14.6 4.0 %shard_map.61.refs_0_ = bf16[4,768,256]{2,1,0:T(8,128)(2,1)S(1)} custom-call(bf16[768,2048]{1,0:T(8,128)(2,1)S(1)} %get-tuple-element.59.row_bits, f32[768,1]{1,0:T(8,128)S(1)} %mul.30.row_scale, bf16[512,2048]{1,0:T(8,128)(2,1)S(1)} %get-tuple-element.60.col_bits, f32[1,1024]{1,0:T(1,128)S(1)} %bitcast.1, bf16[512,2048]{1,0:T(8,128)(2,1)S(1)} %collective-permute-done.11.got_bits), custom_call_target="tpu_custom_call" | custom-call | flops 1000000 | tf_op jit(solution)/shard_map/pallas_call | solution.py:163
  18.6 2.5 %collective-permute-start.12 = (bf16[4,768,256]{2,1,0:T(8,128)(2,1)S(1)}, bf16[4,768,256]{2,1,0:T(8,128)(2,1)S(1)}, u32[]{:S(2)}, u32[]{:S(2)}) collective-permute-start(bf16[4,768,256]{2,1,0:T(8,128)(2,1)S(1)} %shard_map.61.refs_0_), channel_id=1, source_target_pairs={{0,2},{1,7},{2,4},{3,1},{4,6},{5,3},{6,0},{7,5},{8,10},{9,15},{10,... | collective-permute-start | bytes 4718600 | tf_op jit(solution)/shard_map/ppermute | solution.py:42
  21.3 0.4 collective-permute-start.6
  21.7 1.3 %collective-permute-done.4.refs_2_ = bf16[256,1024]{1,0:T(8,128)(2,1)S(1)} collective-permute-done((bf16[256,1024]{1,0:T(8,128)(2,1)S(1)}, bf16[256,1024]{1,0:T(8,128)(2,1)S(1)}, u32[]{:S(2)}, u32[]{:S(2)}) %collective-permute-start.4) | collective-permute-done | bytes 524320 | tf_op jit(solution)/shard_map/ppermute | solution.py:42
  23.0 0.5 collective-permute-start.7
  23.5 3.4 %collective-permute-start.8 = (bf16[256,1024]{1,0:T(8,128)(2,1)S(1)}, bf16[256,1024]{1,0:T(8,128)(2,1)S(1)}, u32[]{:S(2)}, u32[]{:S(2)}) collective-permute-start(bf16[256,1024]{1,0:T(8,128)(2,1)S(1)} %get-tuple-element.55.refs_4_), channel_id=1, source_target_pairs={{0,32},{1,97},{2,34},{3,99},{4,36},{5,101},{6,38},{7,103},{8,40},{... | collective-permute-start | bytes 1572872 | tf_op jit(solution)/shard_map/ppermute | solution.py:42
  26.9 2.6 %collective-permute-done.5.refs_1_ = bf16[256,1024]{1,0:T(8,128)(2,1)S(1)} collective-permute-done((bf16[256,1024]{1,0:T(8,128)(2,1)S(1)}, bf16[256,1024]{1,0:T(8,128)(2,1)S(1)}, u32[]{:S(2)}, u32[]{:S(2)}) %collective-permute-start.5) | collective-permute-done | bytes 524320 | tf_op jit(solution)/shard_map/ppermute | solution.py:42
  29.7 2.4 %collective-permute-start.10 = (bf16[256,1024]{1,0:T(8,128)(2,1)S(1)}, bf16[256,1024]{1,0:T(8,128)(2,1)S(1)}, u32[]{:S(2)}, u32[]{:S(2)}) collective-permute-start(bf16[256,1024]{1,0:T(8,128)(2,1)S(1)} %get-tuple-element.58.refs_5_), channel_id=1, source_target_pairs={{0,32},{1,97},{2,34},{3,99},{4,36},{5,101},{6,38},{7,103},{8,40},{... | collective-permute-start | bytes 1572872 | tf_op jit(solution)/shard_map/ppermute | solution.py:42
  32.0 0.5 collective-permute-start.9
  32.6 2.5 %collective-permute-done.7.refs_1_ = bf16[256,1024]{1,0:T(8,128)(2,1)S(1)} collective-permute-done((bf16[256,1024]{1,0:T(8,128)(2,1)S(1)}, bf16[256,1024]{1,0:T(8,128)(2,1)S(1)}, u32[]{:S(2)}, u32[]{:S(2)}) %collective-permute-start.7) | collective-permute-done | bytes 524320 | tf_op jit(solution)/shard_map/ppermute | solution.py:42
  35.3 2.4 %collective-permute-start.14 = (bf16[256,1024]{1,0:T(8,128)(2,1)S(1)}, bf16[256,1024]{1,0:T(8,128)(2,1)S(1)}, u32[]{:S(2)}, u32[]{:S(2)}) collective-permute-start(bf16[256,1024]{1,0:T(8,128)(2,1)S(1)} %get-tuple-element.64.refs_5_), channel_id=1, source_target_pairs={{0,32},{1,97},{2,34},{3,99},{4,36},{5,101},{6,38},{7,103},{8,40},{... | collective-permute-start | bytes 1572872 | tf_op jit(solution)/shard_map/ppermute | solution.py:42
  37.7 0.5 collective-permute-start.13
  38.3 2.6 %collective-permute-done.10.refs_2_ = bf16[256,1024]{1,0:T(8,128)(2,1)S(1)} collective-permute-done((bf16[256,1024]{1,0:T(8,128)(2,1)S(1)}, bf16[256,1024]{1,0:T(8,128)(2,1)S(1)}, u32[]{:S(2)}, u32[]{:S(2)}) %collective-permute-start.10) | collective-permute-done | bytes 524320 | tf_op jit(solution)/shard_map/ppermute | solution.py:42
  41.0 1.3 %collective-permute-start.16 = (bf16[768,512]{1,0:T(8,128)(2,1)S(1)}, bf16[768,512]{1,0:T(8,128)(2,1)S(1)}, u32[]{:S(2)}, u32[]{:S(2)}) collective-permute-start(bf16[768,512]{1,0:T(8,128)(2,1)S(1)} %pad_maximum_fusion.1), channel_id=1, source_target_pairs={{0,8},{1,25},{2,10},{3,27},{4,12},{5,29},{6,14},{7,31},{8,16},{9,1... | collective-permute-start | bytes 2359304 | tf_op jit(solution)/shard_map/ppermute | solution.py:42
  42.4 1.4 %collective-permute-start.15 = (bf16[768,512]{1,0:T(8,128)(2,1)S(1)}, bf16[768,512]{1,0:T(8,128)(2,1)S(1)}, u32[]{:S(2)}, u32[]{:S(2)}) collective-permute-start(bf16[768,512]{1,0:T(8,128)(2,1)S(1)} %pad_maximum_fusion), channel_id=1, source_target_pairs={{0,32},{1,97},{2,34},{3,99},{4,36},{5,101},{6,38},{7,103},{8,40},{... | collective-permute-start | bytes 2359304 | tf_op jit(solution)/shard_map/ppermute | solution.py:42
  43.8 2.5 %collective-permute-start.19 = (bf16[4,768,256]{2,1,0:T(8,128)(2,1)S(1)}, bf16[4,768,256]{2,1,0:T(8,128)(2,1)S(1)}, u32[]{:S(2)}, u32[]{:S(2)}) collective-permute-start(bf16[4,768,256]{2,1,0:T(8,128)(2,1)S(1)} %get-tuple-element.71.refs_1_), channel_id=1, source_target_pairs={{0,2},{1,7},{2,4},{3,1},{4,6},{5,3},{6,0},{7,5},{8,10},{9,15},{10,... | collective-permute-start | bytes 4718600 | tf_op jit(solution)/shard_map/ppermute | solution.py:42
  46.6 1.3 %collective-permute-start.18 = (bf16[768,512]{1,0:T(8,128)(2,1)S(1)}, bf16[768,512]{1,0:T(8,128)(2,1)S(1)}, u32[]{:S(2)}, u32[]{:S(2)}) collective-permute-start(bf16[768,512]{1,0:T(8,128)(2,1)S(1)} %pad_maximum_fusion.3), channel_id=1, source_target_pairs={{0,8},{1,25},{2,10},{3,27},{4,12},{5,29},{6,14},{7,31},{8,16},{9,1... | collective-permute-start | bytes 2359304 | tf_op jit(solution)/shard_map/ppermute | solution.py:42
  48.0 1.4 %collective-permute-start.17 = (bf16[768,512]{1,0:T(8,128)(2,1)S(1)}, bf16[768,512]{1,0:T(8,128)(2,1)S(1)}, u32[]{:S(2)}, u32[]{:S(2)}) collective-permute-start(bf16[768,512]{1,0:T(8,128)(2,1)S(1)} %pad_maximum_fusion.2), channel_id=1, source_target_pairs={{0,32},{1,97},{2,34},{3,99},{4,36},{5,101},{6,38},{7,103},{8,40},{... | collective-permute-start | bytes 2359304 | tf_op jit(solution)/shard_map/ppermute | solution.py:42
  49.4 5.4 %collective-permute-done.16.refs_2_ = bf16[768,512]{1,0:T(8,128)(2,1)S(1)} collective-permute-done((bf16[768,512]{1,0:T(8,128)(2,1)S(1)}, bf16[768,512]{1,0:T(8,128)(2,1)S(1)}, u32[]{:S(2)}, u32[]{:S(2)}) %collective-permute-start.16) | collective-permute-done | bytes 786464 | tf_op jit(solution)/shard_map/ppermute | solution.py:42
  55.0 2.4 %collective-permute-start.21 = (bf16[768,512]{1,0:T(8,128)(2,1)S(1)}, bf16[768,512]{1,0:T(8,128)(2,1)S(1)}, u32[]{:S(2)}, u32[]{:S(2)}) collective-permute-start(bf16[768,512]{1,0:T(8,128)(2,1)S(1)} %get-tuple-element.74.refs_7_), channel_id=1, source_target_pairs={{0,32},{1,97},{2,34},{3,99},{4,36},{5,101},{6,38},{7,103},{8,40},{... | collective-permute-start | bytes 2359304 | tf_op jit(solution)/shard_map/ppermute | solution.py:42
  57.3 0.5 collective-permute-start.22
  57.8 5.4 %collective-permute-done.18.refs_2_ = bf16[768,512]{1,0:T(8,128)(2,1)S(1)} collective-permute-done((bf16[768,512]{1,0:T(8,128)(2,1)S(1)}, bf16[768,512]{1,0:T(8,128)(2,1)S(1)}, u32[]{:S(2)}, u32[]{:S(2)}) %collective-permute-start.18) | collective-permute-done | bytes 786464 | tf_op jit(solution)/shard_map/ppermute | solution.py:42
  63.4 0.2 collective-permute-done.19.refs_3_
  63.6 3.4 %collective-permute-start.20 = (bf16[4,768,256]{2,1,0:T(8,128)(2,1)S(1)}, bf16[4,768,256]{2,1,0:T(8,128)(2,1)S(1)}, u32[]{:S(2)}, u32[]{:S(2)}) collective-permute-start(bf16[4,768,256]{2,1,0:T(8,128)(2,1)S(1)} %get-tuple-element.72.refs_2_), channel_id=1, source_target_pairs={{0,2},{1,7},{2,4},{3,1},{4,6},{5,3},{6,0},{7,5},{8,10},{9,15},{10,... | collective-permute-start | bytes 4718600 | tf_op jit(solution)/shard_map/ppermute | solution.py:42
  67.0 1.2 %collective-permute-start.23 = (bf16[768,512]{1,0:T(8,128)(2,1)S(1)}, bf16[768,512]{1,0:T(8,128)(2,1)S(1)}, u32[]{:S(2)}, u32[]{:S(2)}) collective-permute-start(bf16[768,512]{1,0:T(8,128)(2,1)S(1)} %get-tuple-element.77.refs_7_), channel_id=1, source_target_pairs={{0,32},{1,97},{2,34},{3,99},{4,36},{5,101},{6,38},{7,103},{8,40},{... | collective-permute-start | bytes 2359304 | tf_op jit(solution)/shard_map/ppermute | solution.py:42
  68.4 0.3 shard_map.66.refs_1_.k
  68.8 5.2 %shard_map.68.refs_3_ = f32[768,1024]{1,0:T(8,128)S(1)} custom-call(bf16[16,768,256]{2,1,0:T(8,128)(2,1)S(1)} %shard_map.66.refs_1_.k, bf16[256,1024]{1,0:T(8,128)(2,1)S(1)} %collective-permute-done.refs_0_, bf16[256,1024]{1,0:T(8,128)(2,1)S(1)} %get-tuple-element.51.refs_1_, bf16[256,1024]{1,0:T(8,128)(2,1)S(1)} %get-tuple-element.57.refs_2_, ...), custom_call_target="tpu_custom_call" | custom-call | flops 1000000 | tf_op jit(solution)/shard_map/pallas_call | solution.py:262
  74.4 7.2 %shard_map.70 = (f32[768,1024]{1,0:T(8,128)S(1)}, f32[768,1024]{1,0:T(8,128)S(1)}) custom-call(bf16[16,768,256]{2,1,0:T(8,128)(2,1)S(1)} %shard_map.66.refs_1_.k, bf16[256,1024]{1,0:T(8,128)(2,1)S(1)} %get-tuple-element.89.refs_0_, bf16[256,1024]{1,0:T(8,128)(2,1)S(1)} %get-tuple-element.54.refs_1_, ...), custom_call_target="tpu_custom_call", output_to_operand_aliasing={{1}: (12, {})} | custom-call | flops 1000000 | tf_op jit(solution)/shard_map/pallas_call | solution.py:262
  81.6 1.0 collective-permute-start.25
  82.6 1.0 collective-permute-start.26
  83.6 0.8 collective-permute-done.20.refs_0_
  84.5 1.5 %shard_map.75.refs_2_ = f32[768,1024]{1,0:T(8,128)S(1)} custom-call(bf16[16,768,256]{2,1,0:T(8,128)(2,1)S(1)} %shard_map.67.k, bf16[256,1024]{1,0:T(8,128)(2,1)S(1)} %collective-permute-done.refs_0_, bf16[256,1024]{1,0:T(8,128)(2,1)S(1)} %get-tuple-element.51.refs_1_, ...), custom_call_target="tpu_custom_call", output_to_operand_aliasing={{}: (12, {})} | custom-call | flops 1000000 | tf_op jit(solution)/shard_map/pallas_call | solution.py:262
  86.0 2.7 %collective-permute-done.27.refs_0_ = bf16[768,512]{1,0:T(8,128)(2,1)S(1)} collective-permute-done((bf16[768,512]{1,0:T(8,128)(2,1)S(1)}, bf16[768,512]{1,0:T(8,128)(2,1)S(1)}, u32[]{:S(2)}, u32[]{:S(2)}) %collective-permute-start.27) | collective-permute-done | bytes 786464 | tf_op jit(solution)/shard_map/ppermute | solution.py:42
  88.7 1.5 %shard_map.76 = f32[768,1024]{1,0:T(8,128)S(1)} custom-call(bf16[16,768,256]{2,1,0:T(8,128)(2,1)S(1)} %shard_map.67.k, bf16[768,512]{1,0:T(8,128)(2,1)S(1)} %collective-permute-done.27.refs_0_, bf16[768,512]{1,0:T(8,128)(2,1)S(1)} %collective-permute-done.28.refs_1_, f32[768,1024]{1,0:T(8,128)S(1)} %shard_map.75.refs_2_), custom_call_target="tpu_custom_call", output_to_operand_aliasing={{}: (3, {})} | custom-call | flops 1000000 | tf_op jit(solution)/shard_map/pallas_call | solution.py:262
  90.2 2.7 %collective-permute-start.29 = (f32[768,1024]{1,0:T(8,128)S(1)}, f32[768,1024]{1,0:T(8,128)S(1)}, u32[]{:S(2)}, u32[]{:S(2)}) collective-permute-start(f32[768,1024]{1,0:T(8,128)S(1)} %shard_map.76), channel_id=1, source_target_pairs={{0,1},{1,0},{2,3},{3,2},{4,5},{5,4},{6,7},{7,6},{8,9},{9,8},{10,11... | collective-permute-start | bytes 9437192 | tf_op jit(solution)/shard_map/ppermute | solution.py:42
  92.8 1.2 %shard_map.73.refs_2_ = f32[768,1024]{1,0:T(8,128)S(1)} custom-call(bf16[16,768,256]{2,1,0:T(8,128)(2,1)S(1)} %shard_map.67.k, bf16[256,1024]{1,0:T(8,128)(2,1)S(1)} %get-tuple-element.89.refs_0_, bf16[256,1024]{1,0:T(8,128)(2,1)S(1)} %get-tuple-element.54.refs_1_, bf16[256,1024]{1,0:T(8,128)(2,1)S(1)} %get-tuple-element.63.refs_2_, ...), custom_call_target="tpu_custom_call", output_to_operand_aliasing={{}: (10, {})} | custom-call | flops 1000000 | tf_op jit(solution)/shard_map/pallas_call | solution.py:262
  94.1 1.5 %shard_map.74.refs_2_ = f32[768,1024]{1,0:T(8,128)S(1)} custom-call(bf16[16,768,256]{2,1,0:T(8,128)(2,1)S(1)} %shard_map.67.k, bf16[768,512]{1,0:T(8,128)(2,1)S(1)} %get-tuple-element.83.refs_0_, bf16[768,512]{1,0:T(8,128)(2,1)S(1)} %get-tuple-element.84.refs_1_, f32[768,1024]{1,0:T(8,128)S(1)} %shard_map.73.refs_2_), custom_call_target="tpu_custom_call", output_to_operand_aliasing={{}: (3, {})} | custom-call | flops 1000000 | tf_op jit(solution)/shard_map/pallas_call | solution.py:262
  95.6 1.5 %collective-permute-done.25.refs_0_ = bf16[768,512]{1,0:T(8,128)(2,1)S(1)} collective-permute-done((bf16[768,512]{1,0:T(8,128)(2,1)S(1)}, bf16[768,512]{1,0:T(8,128)(2,1)S(1)}, u32[]{:S(2)}, u32[]{:S(2)}) %collective-permute-start.25) | collective-permute-done | bytes 786464 | tf_op jit(solution)/shard_map/ppermute | solution.py:42
  97.1 1.0 %collective-permute-done.29.refs_3_ = f32[768,1024]{1,0:T(8,128)S(1)} collective-permute-done((f32[768,1024]{1,0:T(8,128)S(1)}, f32[768,1024]{1,0:T(8,128)S(1)}, u32[]{:S(2)}, u32[]{:S(2)}) %collective-permute-start.29) | collective-permute-done | bytes 3145760 | tf_op jit(solution)/shard_map/ppermute | solution.py:42
  98.1 2.2 %shard_map.77 = f32[768,1024]{1,0:T(8,128)} custom-call(bf16[16,768,256]{2,1,0:T(8,128)(2,1)S(1)} %shard_map.67.k, bf16[768,512]{1,0:T(8,128)(2,1)S(1)} %get-tuple-element.85.refs_0_, bf16[768,512]{1,0:T(8,128)(2,1)S(1)} %get-tuple-element.86.refs_1_, f32[768,1024]{1,0:T(8,128)S(1)} %shard_map.74.refs_2_, f32[768,1024]{1,0:T(8,128)S(1)} %collective-permute-done.29.refs_3_), custom_call_target="tpu_custom_call" | custom-call | flops 1000000 | tf_op jit(solution)/shard_map/pallas_call | solution.py:299
  (59 shorter events, 2.5 us)
Async XLA Ops:
  1.3 10.6 %copy-start = (s32[768]{0:T(1024)S(1)}, s32[768]{0:T(1024)}, u32[]{:S(2)}) copy-start(s32[768]{0:T(1024)} %param.6) | copy-start | bytes 9220
  1.3 3.1 %collective-permute-start = (bf16[256,1024]{1,0:T(8,128)(2,1)S(1)}, bf16[256,1024]{1,0:T(8,128)(2,1)S(1)}, u32[]{:S(2)}, u32[]{:S(2)}) collective-permute-start(bf16[256,1024]{1,0:T(8,128)(2,1)S(1)} %get-tuple-element.90), channel_id=1, source_target_pairs={{0,1},{1,0},{2,3},{3,2},{4,5},{5,4},{6,7},{7,6},{8,9},{9,8},{10,11... | collective-permute-start | bytes 1572872 | tf_op jit(solution)/shard_map/ppermute | solution.py:42
  4.4 10.2 %collective-permute-start.11 = (bf16[512,2048]{1,0:T(8,128)(2,1)S(1)}, bf16[512,2048]{1,0:T(8,128)(2,1)S(1)}, u32[]{:S(2)}, u32[]{:S(2)}) collective-permute-start(bf16[512,2048]{1,0:T(8,128)(2,1)S(1)} %shard_map.56), channel_id=1, source_target_pairs={{0,1},{1,0},{2,3},{3,2},{4,5},{5,4},{6,7},{7,6},{8,9},{9,8},{10,11... | collective-permute-start | bytes 6291464 | tf_op jit(solution)/shard_map/ppermute | solution.py:42
  4.7 16.5 %collective-permute-start.1 = (bf16[256,1024]{1,0:T(8,128)(2,1)S(1)}, bf16[256,1024]{1,0:T(8,128)(2,1)S(1)}, u32[]{:S(2)}, u32[]{:S(2)}) collective-permute-start(bf16[256,1024]{1,0:T(8,128)(2,1)S(1)} %collective-permute-done.refs_0_), channel_id=1, source_target_pairs={{0,8},{1,25},{2,10},{3,27},{4,12},{5,29},{6,14},{7,31},{8,16},{9,1... | collective-permute-start | bytes 1572872 | tf_op jit(solution)/shard_map/ppermute | solution.py:42
  7.5 13.7 %collective-permute-start.2 = (bf16[256,1024]{1,0:T(8,128)(2,1)S(1)}, bf16[256,1024]{1,0:T(8,128)(2,1)S(1)}, u32[]{:S(2)}, u32[]{:S(2)}) collective-permute-start(bf16[256,1024]{1,0:T(8,128)(2,1)S(1)} %collective-permute-done.refs_0_), channel_id=1, source_target_pairs={{0,32},{1,97},{2,34},{3,99},{4,36},{5,101},{6,38},{7,103},{8,40},{... | collective-permute-start | bytes 1572872 | tf_op jit(solution)/shard_map/ppermute | solution.py:42
  11.3 10.5 %collective-permute-start.3 = (bf16[256,1024]{1,0:T(8,128)(2,1)S(1)}, bf16[256,1024]{1,0:T(8,128)(2,1)S(1)}, u32[]{:S(2)}, u32[]{:S(2)}) collective-permute-start(bf16[256,1024]{1,0:T(8,128)(2,1)S(1)} %get-tuple-element.89.refs_0_), channel_id=1, source_target_pairs={{0,8},{1,25},{2,10},{3,27},{4,12},{5,29},{6,14},{7,31},{8,16},{9,1... | collective-permute-start | bytes 1572872 | tf_op jit(solution)/shard_map/ppermute | solution.py:42
  11.7 11.3 %collective-permute-start.4 = (bf16[256,1024]{1,0:T(8,128)(2,1)S(1)}, bf16[256,1024]{1,0:T(8,128)(2,1)S(1)}, u32[]{:S(2)}, u32[]{:S(2)}) collective-permute-start(bf16[256,1024]{1,0:T(8,128)(2,1)S(1)} %get-tuple-element.89.refs_0_), channel_id=1, source_target_pairs={{0,32},{1,97},{2,34},{3,99},{4,36},{5,101},{6,38},{7,103},{8,40},{... | collective-permute-start | bytes 1572872 | tf_op jit(solution)/shard_map/ppermute | solution.py:42
  12.0 2.5 %copy-start.1 = (s32[1024]{0:T(1024)S(1)}, s32[1024]{0:T(1024)}, u32[]{:S(2)}) copy-start(s32[1024]{0:T(1024)} %param.8) | copy-start | bytes 12292
  18.6 22.3 %collective-permute-start.12 = (bf16[4,768,256]{2,1,0:T(8,128)(2,1)S(1)}, bf16[4,768,256]{2,1,0:T(8,128)(2,1)S(1)}, u32[]{:S(2)}, u32[]{:S(2)}) collective-permute-start(bf16[4,768,256]{2,1,0:T(8,128)(2,1)S(1)} %shard_map.61.refs_0_), channel_id=1, source_target_pairs={{0,2},{1,7},{2,4},{3,1},{4,6},{5,3},{6,0},{7,5},{8,10},{9,15},{10,... | collective-permute-start | bytes 4718600 | tf_op jit(solution)/shard_map/ppermute | solution.py:42
  21.2 8.3 %collective-permute-start.5 = (bf16[256,1024]{1,0:T(8,128)(2,1)S(1)}, bf16[256,1024]{1,0:T(8,128)(2,1)S(1)}, u32[]{:S(2)}, u32[]{:S(2)}) collective-permute-start(bf16[256,1024]{1,0:T(8,128)(2,1)S(1)} %get-tuple-element.51.refs_1_), channel_id=1, source_target_pairs={{0,8},{1,25},{2,10},{3,27},{4,12},{5,29},{6,14},{7,31},{8,16},{9,1... | collective-permute-start | bytes 1572872 | tf_op jit(solution)/shard_map/ppermute | solution.py:42
  21.3 8.3 %collective-permute-start.6 = (bf16[256,1024]{1,0:T(8,128)(2,1)S(1)}, bf16[256,1024]{1,0:T(8,128)(2,1)S(1)}, u32[]{:S(2)}, u32[]{:S(2)}) collective-permute-start(bf16[256,1024]{1,0:T(8,128)(2,1)S(1)} %get-tuple-element.52.refs_4_), channel_id=1, source_target_pairs={{0,32},{1,97},{2,34},{3,99},{4,36},{5,101},{6,38},{7,103},{8,40},{... | collective-permute-start | bytes 1572872 | tf_op jit(solution)/shard_map/ppermute | solution.py:42
  23.0 12.1 %collective-permute-start.7 = (bf16[256,1024]{1,0:T(8,128)(2,1)S(1)}, bf16[256,1024]{1,0:T(8,128)(2,1)S(1)}, u32[]{:S(2)}, u32[]{:S(2)}) collective-permute-start(bf16[256,1024]{1,0:T(8,128)(2,1)S(1)} %get-tuple-element.54.refs_1_), channel_id=1, source_target_pairs={{0,8},{1,25},{2,10},{3,27},{4,12},{5,29},{6,14},{7,31},{8,16},{9,1... | collective-permute-start | bytes 1572872 | tf_op jit(solution)/shard_map/ppermute | solution.py:42
  23.5 11.8 %collective-permute-start.8 = (bf16[256,1024]{1,0:T(8,128)(2,1)S(1)}, bf16[256,1024]{1,0:T(8,128)(2,1)S(1)}, u32[]{:S(2)}, u32[]{:S(2)}) collective-permute-start(bf16[256,1024]{1,0:T(8,128)(2,1)S(1)} %get-tuple-element.55.refs_4_), channel_id=1, source_target_pairs={{0,32},{1,97},{2,34},{3,99},{4,36},{5,101},{6,38},{7,103},{8,40},{... | collective-permute-start | bytes 1572872 | tf_op jit(solution)/shard_map/ppermute | solution.py:42
  29.7 11.2 %collective-permute-start.10 = (bf16[256,1024]{1,0:T(8,128)(2,1)S(1)}, bf16[256,1024]{1,0:T(8,128)(2,1)S(1)}, u32[]{:S(2)}, u32[]{:S(2)}) collective-permute-start(bf16[256,1024]{1,0:T(8,128)(2,1)S(1)} %get-tuple-element.58.refs_5_), channel_id=1, source_target_pairs={{0,32},{1,97},{2,34},{3,99},{4,36},{5,101},{6,38},{7,103},{8,40},{... | collective-permute-start | bytes 1572872 | tf_op jit(solution)/shard_map/ppermute | solution.py:42
  32.0 8.9 %collective-permute-start.9 = (bf16[256,1024]{1,0:T(8,128)(2,1)S(1)}, bf16[256,1024]{1,0:T(8,128)(2,1)S(1)}, u32[]{:S(2)}, u32[]{:S(2)}) collective-permute-start(bf16[256,1024]{1,0:T(8,128)(2,1)S(1)} %get-tuple-element.57.refs_2_), channel_id=1, source_target_pairs={{0,8},{1,25},{2,10},{3,27},{4,12},{5,29},{6,14},{7,31},{8,16},{9,1... | collective-permute-start | bytes 1572872 | tf_op jit(solution)/shard_map/ppermute | solution.py:42
  35.3 11.2 %collective-permute-start.14 = (bf16[256,1024]{1,0:T(8,128)(2,1)S(1)}, bf16[256,1024]{1,0:T(8,128)(2,1)S(1)}, u32[]{:S(2)}, u32[]{:S(2)}) collective-permute-start(bf16[256,1024]{1,0:T(8,128)(2,1)S(1)} %get-tuple-element.64.refs_5_), channel_id=1, source_target_pairs={{0,32},{1,97},{2,34},{3,99},{4,36},{5,101},{6,38},{7,103},{8,40},{... | collective-permute-start | bytes 1572872 | tf_op jit(solution)/shard_map/ppermute | solution.py:42
  37.7 8.7 %collective-permute-start.13 = (bf16[256,1024]{1,0:T(8,128)(2,1)S(1)}, bf16[256,1024]{1,0:T(8,128)(2,1)S(1)}, u32[]{:S(2)}, u32[]{:S(2)}) collective-permute-start(bf16[256,1024]{1,0:T(8,128)(2,1)S(1)} %get-tuple-element.63.refs_2_), channel_id=1, source_target_pairs={{0,8},{1,25},{2,10},{3,27},{4,12},{5,29},{6,14},{7,31},{8,16},{9,1... | collective-permute-start | bytes 1572872 | tf_op jit(solution)/shard_map/ppermute | solution.py:42
  41.0 13.8 %collective-permute-start.16 = (bf16[768,512]{1,0:T(8,128)(2,1)S(1)}, bf16[768,512]{1,0:T(8,128)(2,1)S(1)}, u32[]{:S(2)}, u32[]{:S(2)}) collective-permute-start(bf16[768,512]{1,0:T(8,128)(2,1)S(1)} %pad_maximum_fusion.1), channel_id=1, source_target_pairs={{0,8},{1,25},{2,10},{3,27},{4,12},{5,29},{6,14},{7,31},{8,16},{9,1... | collective-permute-start | bytes 2359304 | tf_op jit(solution)/shard_map/ppermute | solution.py:42
  42.4 12.6 %collective-permute-start.15 = (bf16[768,512]{1,0:T(8,128)(2,1)S(1)}, bf16[768,512]{1,0:T(8,128)(2,1)S(1)}, u32[]{:S(2)}, u32[]{:S(2)}) collective-permute-start(bf16[768,512]{1,0:T(8,128)(2,1)S(1)} %pad_maximum_fusion), channel_id=1, source_target_pairs={{0,32},{1,97},{2,34},{3,99},{4,36},{5,101},{6,38},{7,103},{8,40},{... | collective-permute-start | bytes 2359304 | tf_op jit(solution)/shard_map/ppermute | solution.py:42
  43.8 19.8 %collective-permute-start.19 = (bf16[4,768,256]{2,1,0:T(8,128)(2,1)S(1)}, bf16[4,768,256]{2,1,0:T(8,128)(2,1)S(1)}, u32[]{:S(2)}, u32[]{:S(2)}) collective-permute-start(bf16[4,768,256]{2,1,0:T(8,128)(2,1)S(1)} %get-tuple-element.71.refs_1_), channel_id=1, source_target_pairs={{0,2},{1,7},{2,4},{3,1},{4,6},{5,3},{6,0},{7,5},{8,10},{9,15},{10,... | collective-permute-start | bytes 4718600 | tf_op jit(solution)/shard_map/ppermute | solution.py:42
  46.6 16.6 %collective-permute-start.18 = (bf16[768,512]{1,0:T(8,128)(2,1)S(1)}, bf16[768,512]{1,0:T(8,128)(2,1)S(1)}, u32[]{:S(2)}, u32[]{:S(2)}) collective-permute-start(bf16[768,512]{1,0:T(8,128)(2,1)S(1)} %pad_maximum_fusion.3), channel_id=1, source_target_pairs={{0,8},{1,25},{2,10},{3,27},{4,12},{5,29},{6,14},{7,31},{8,16},{9,1... | collective-permute-start | bytes 2359304 | tf_op jit(solution)/shard_map/ppermute | solution.py:42
  48.0 15.4 %collective-permute-start.17 = (bf16[768,512]{1,0:T(8,128)(2,1)S(1)}, bf16[768,512]{1,0:T(8,128)(2,1)S(1)}, u32[]{:S(2)}, u32[]{:S(2)}) collective-permute-start(bf16[768,512]{1,0:T(8,128)(2,1)S(1)} %pad_maximum_fusion.2), channel_id=1, source_target_pairs={{0,32},{1,97},{2,34},{3,99},{4,36},{5,101},{6,38},{7,103},{8,40},{... | collective-permute-start | bytes 2359304 | tf_op jit(solution)/shard_map/ppermute | solution.py:42
  55.0 19.1 %collective-permute-start.21 = (bf16[768,512]{1,0:T(8,128)(2,1)S(1)}, bf16[768,512]{1,0:T(8,128)(2,1)S(1)}, u32[]{:S(2)}, u32[]{:S(2)}) collective-permute-start(bf16[768,512]{1,0:T(8,128)(2,1)S(1)} %get-tuple-element.74.refs_7_), channel_id=1, source_target_pairs={{0,32},{1,97},{2,34},{3,99},{4,36},{5,101},{6,38},{7,103},{8,40},{... | collective-permute-start | bytes 2359304 | tf_op jit(solution)/shard_map/ppermute | solution.py:42
  57.3 16.7 %collective-permute-start.22 = (bf16[768,512]{1,0:T(8,128)(2,1)S(1)}, bf16[768,512]{1,0:T(8,128)(2,1)S(1)}, u32[]{:S(2)}, u32[]{:S(2)}) collective-permute-start(bf16[768,512]{1,0:T(8,128)(2,1)S(1)} %get-tuple-element.75.refs_8_), channel_id=1, source_target_pairs={{0,8},{1,25},{2,10},{3,27},{4,12},{5,29},{6,14},{7,31},{8,16},{9,1... | collective-permute-start | bytes 2359304 | tf_op jit(solution)/shard_map/ppermute | solution.py:42
  63.6 20.8 %collective-permute-start.20 = (bf16[4,768,256]{2,1,0:T(8,128)(2,1)S(1)}, bf16[4,768,256]{2,1,0:T(8,128)(2,1)S(1)}, u32[]{:S(2)}, u32[]{:S(2)}) collective-permute-start(bf16[4,768,256]{2,1,0:T(8,128)(2,1)S(1)} %get-tuple-element.72.refs_2_), channel_id=1, source_target_pairs={{0,2},{1,7},{2,4},{3,1},{4,6},{5,3},{6,0},{7,5},{8,10},{9,15},{10,... | collective-permute-start | bytes 4718600 | tf_op jit(solution)/shard_map/ppermute | solution.py:42
  67.0 14.6 %collective-permute-start.23 = (bf16[768,512]{1,0:T(8,128)(2,1)S(1)}, bf16[768,512]{1,0:T(8,128)(2,1)S(1)}, u32[]{:S(2)}, u32[]{:S(2)}) collective-permute-start(bf16[768,512]{1,0:T(8,128)(2,1)S(1)} %get-tuple-element.77.refs_7_), channel_id=1, source_target_pairs={{0,32},{1,97},{2,34},{3,99},{4,36},{5,101},{6,38},{7,103},{8,40},{... | collective-permute-start | bytes 2359304 | tf_op jit(solution)/shard_map/ppermute | solution.py:42
  68.2 13.4 %collective-permute-start.24 = (bf16[768,512]{1,0:T(8,128)(2,1)S(1)}, bf16[768,512]{1,0:T(8,128)(2,1)S(1)}, u32[]{:S(2)}, u32[]{:S(2)}) collective-permute-start(bf16[768,512]{1,0:T(8,128)(2,1)S(1)} %get-tuple-element.78.refs_8_), channel_id=1, source_target_pairs={{0,8},{1,25},{2,10},{3,27},{4,12},{5,29},{6,14},{7,31},{8,16},{9,1... | collective-permute-start | bytes 2359304 | tf_op jit(solution)/shard_map/ppermute | solution.py:42
  74.0 14.6 %collective-permute-start.27 = (bf16[768,512]{1,0:T(8,128)(2,1)S(1)}, bf16[768,512]{1,0:T(8,128)(2,1)S(1)}, u32[]{:S(2)}, u32[]{:S(2)}) collective-permute-start(bf16[768,512]{1,0:T(8,128)(2,1)S(1)} %get-tuple-element.79.refs_9_), channel_id=1, source_target_pairs={{0,32},{1,97},{2,34},{3,99},{4,36},{5,101},{6,38},{7,103},{8,40},{... | collective-permute-start | bytes 2359304 | tf_op jit(solution)/shard_map/ppermute | solution.py:42
  74.2 14.5 %collective-permute-start.28 = (bf16[768,512]{1,0:T(8,128)(2,1)S(1)}, bf16[768,512]{1,0:T(8,128)(2,1)S(1)}, u32[]{:S(2)}, u32[]{:S(2)}) collective-permute-start(bf16[768,512]{1,0:T(8,128)(2,1)S(1)} %get-tuple-element.80.refs_10_), channel_id=1, source_target_pairs={{0,8},{1,25},{2,10},{3,27},{4,12},{5,29},{6,14},{7,31},{8,16},{9,1... | collective-permute-start | bytes 2359304 | tf_op jit(solution)/shard_map/ppermute | solution.py:42
  81.6 15.5 %collective-permute-start.25 = (bf16[768,512]{1,0:T(8,128)(2,1)S(1)}, bf16[768,512]{1,0:T(8,128)(2,1)S(1)}, u32[]{:S(2)}, u32[]{:S(2)}) collective-permute-start(bf16[768,512]{1,0:T(8,128)(2,1)S(1)} %get-tuple-element.83.refs_0_), channel_id=1, source_target_pairs={{0,32},{1,97},{2,34},{3,99},{4,36},{5,101},{6,38},{7,103},{8,40},{... | collective-permute-start | bytes 2359304 | tf_op jit(solution)/shard_map/ppermute | solution.py:42
  82.6 14.5 %collective-permute-start.26 = (bf16[768,512]{1,0:T(8,128)(2,1)S(1)}, bf16[768,512]{1,0:T(8,128)(2,1)S(1)}, u32[]{:S(2)}, u32[]{:S(2)}) collective-permute-start(bf16[768,512]{1,0:T(8,128)(2,1)S(1)} %get-tuple-element.84.refs_1_), channel_id=1, source_target_pairs={{0,8},{1,25},{2,10},{3,27},{4,12},{5,29},{6,14},{7,31},{8,16},{9,1... | collective-permute-start | bytes 2359304 | tf_op jit(solution)/shard_map/ppermute | solution.py:42
  90.2 7.9 %collective-permute-start.29 = (f32[768,1024]{1,0:T(8,128)S(1)}, f32[768,1024]{1,0:T(8,128)S(1)}, u32[]{:S(2)}, u32[]{:S(2)}) collective-permute-start(f32[768,1024]{1,0:T(8,128)S(1)} %shard_map.76), channel_id=1, source_target_pairs={{0,1},{1,0},{2,3},{3,2},{4,5},{5,4},{6,7},{7,6},{8,9},{9,8},{10,11... | collective-permute-start | bytes 9437192 | tf_op jit(solution)/shard_map/ppermute | solution.py:42
